TPU v7x, 32 devices: a whole 2x2x4 slice. The times are simulated.
32 devices in a mesh: mic: 4 (over x, core), bin: 8 (over z, y).
Axes of the slice: x: 2, y: 2, z: 4, core: 2. Of those that a mesh axis runs over, the one named last changes fastest.
Arguments:
- images: bfloat16 [128, 256, 256], P(('mic', 'bin')), may hold values from -6 to 6
- offsets: int32 [2, 128], P(None, ('mic', 'bin')), may hold values from 0 to 255
- ctf_group: int32 [128], P(('mic', 'bin')), may hold values from 0 to 63
- particle_bin: int32 [128], P(('mic', 'bin')), may hold values from 0 to 255, as said below
- bin_place: int32 [256], replicated, may hold values from 0 to 255, as said below
- defocus: float32 [64], replicated, may hold values from 40 to 160
- bfactor: float32 [64], replicated, may hold values from 0.2 to 2
- references: bfloat16 [256, 256, 256], P(('mic', 'bin')), may hold values from -6 to 6
Outputs:
- refined: bfloat16 [256, 256, 256], P(('mic', 'bin'))
- scores: float32 [128], P(('mic', 'bin'))
Inputs may be any that keep to these rules, and one draw needn't show every extreme that they name: bin_place is a permutation. A particle's owner is bin_place[particle_bin] // 8, with bin index owner % 8 and mic index owner // 8. Of the 4 particles of one device, at most 1 have owners with one bin index, and some device of every mic row reaches it. `particle_bin`: within one mic row exactly 4 particles have owners with each bin index, and at most 2 have the same owner; in every mic row some owner has exactly 2. Several particles may share one bin.
All inputs are finite; a program needn't handle non-finite values.
Results may differ from a plain program's by a relative error of at most 0.0055.
Values may be sent and summed in bfloat16 or wider, within the bound.
No kernel may reach another device: no remote copies, remote signals or barrier semaphores. Data moves between devices by JAX's collectives and lax.ppermute only.
A program may use at most 64 MiB of HBM per device.

v0:
```python
import math

import jax
import jax.numpy as jnp
from jax import lax
from jax.sharding import PartitionSpec as P

ITERS = 2


PRIOR_WEIGHT = 0.5
EPSILON = 1e-06
CONTRAST = 0.1
AMPLITUDE = math.sqrt(1.0 - CONTRAST * CONTRAST)


def hartley(image_side):
    row_index = lax.broadcasted_iota(jnp.int32, (image_side, image_side), 0)
    column_index = lax.broadcasted_iota(jnp.int32, (image_side, image_side), 1)
    phases = row_index * column_index % image_side
    angles = phases.astype(jnp.float32) * (2.0 * math.pi / image_side)
    return ((jnp.cos(angles) + jnp.sin(angles)) / math.sqrt(image_side)).astype(jnp.bfloat16)


def radius_square(image_side):
    frequency = jnp.arange(image_side, dtype=jnp.int32)
    folded = jnp.minimum(frequency, image_side - frequency).astype(jnp.float32)
    nyquist = image_side / 2.0
    square = (folded[:, None] * folded[:, None] + folded[None, :] * folded[None, :]) / (
        nyquist * nyquist
    )
    return square.reshape(image_side * image_side)


def ctf_rows(focus, damping, image_side):
    radial = radius_square(image_side)
    aberration = focus[:, None] * radial[None, :]
    envelope = jnp.exp(-damping[:, None] * radial[None, :])
    return -(AMPLITUDE * jnp.sin(aberration) + CONTRAST * jnp.cos(aberration)) * envelope


def group_lookup(groups, table):
    onehot = (groups[:, None] == jnp.arange(table.shape[0], dtype=jnp.int32)[None, :]).astype(
        jnp.float32
    )
    return jnp.sum(onehot * table[None, :], axis=1)


def group_ctf(groups, defocus, bfactor, image_side):
    return ctf_rows(group_lookup(groups, defocus), group_lookup(groups, bfactor), image_side)


def shifted(picture, shift_pair):
    image_side = picture.shape[0]
    doubled = jnp.concatenate([picture, picture], axis=0)
    rows_moved = lax.dynamic_slice_in_dim(doubled, shift_pair[0], image_side, 0)
    doubled = jnp.concatenate([rows_moved, rows_moved], axis=1)
    return lax.dynamic_slice_in_dim(doubled, shift_pair[1], image_side, 1)


def transform(images, offsets):
    basis = hartley(images.shape[1])
    moved = jax.vmap(shifted)(images, offsets.T)
    partial_rows = jnp.einsum(
        "kx,pxy->pky", basis, moved, preferred_element_type=jnp.float32
    ).astype(jnp.bfloat16)
    return jnp.einsum(
        "pky,ly->pkl", partial_rows, basis, preferred_element_type=jnp.float32
    ).astype(jnp.bfloat16)


def compare(ref_rows, ctf_table, spectra, image_side):
    predicted = ctf_table * ref_rows.astype(jnp.float32)
    values = spectra.astype(jnp.float32)
    cross_term = jnp.mean(predicted * values, axis=1)
    model_power = jnp.mean(predicted * predicted, axis=1) + EPSILON
    data_power = jnp.mean(values * values, axis=1) + EPSILON
    correlation = cross_term / jnp.sqrt(model_power * data_power)
    weights = jax.nn.sigmoid(image_side * correlation).astype(jnp.bfloat16)
    weighted = (weights.astype(jnp.float32)[:, None] * ctf_table * values).astype(jnp.bfloat16)
    return (correlation, weights, weighted)


def accumulate(current, local_bin, active, weights, weighted, ctf_table):
    own_bins = current.shape[0]
    member = (local_bin[None, :] == jnp.arange(own_bins, dtype=jnp.int32)[:, None]) & (
        active[None, :] > 0
    )
    numerator = jnp.dot(member.astype(jnp.bfloat16), weighted, preferred_element_type=jnp.float32)
    ctf_power = weights.astype(jnp.float32)[:, None] * ctf_table * ctf_table
    denominator = jnp.dot(member.astype(jnp.float32), ctf_power, precision=lax.Precision.HIGHEST)
    previous = current.reshape(own_bins, -1).astype(jnp.float32)
    updated = (numerator + PRIOR_WEIGHT * previous) / (denominator + PRIOR_WEIGHT)
    return updated.astype(jnp.bfloat16).reshape(current.shape)


def bucket(targets, active, buckets, capacity):
    matches = (targets[:, None] == jnp.arange(buckets, dtype=jnp.int32)[None, :]).astype(
        jnp.int32
    ) * active[:, None]
    before = jnp.cumsum(matches, axis=0) - matches
    ranking = jnp.sum(before * matches, axis=1)
    destination = targets * capacity + ranking
    slot_ids = jnp.arange(buckets * capacity, dtype=jnp.int32)
    return ((destination[None, :] == slot_ids[:, None]) & (active[None, :] > 0)).astype(jnp.int32)


def pick_ints(selector, values):
    return jnp.sum(selector[:, :, None] * values[None, :, :], axis=1)


def pick_rows(selector, values):
    return jnp.dot(
        selector.astype(jnp.bfloat16), values, preferred_element_type=jnp.float32
    ).astype(jnp.bfloat16)


def body(images, offsets, ctf_group, particle_bin, bin_place, defocus, bfactor, references):
    mic_count = lax.axis_size("mic")
    bin_count = lax.axis_size("bin")
    particles_here = images.shape[0]
    image_side = images.shape[1]
    pixel_count = image_side * image_side
    own_bins = references.shape[0]
    cap_first = (particles_here + bin_count - 1) // bin_count
    cap_second = (3 * particles_here + 2 * mic_count - 1) // (2 * mic_count)
    first_total = bin_count * cap_first
    second_total = mic_count * cap_second
    transformed = transform(images, offsets)
    flat_images = transformed.reshape(particles_here, pixel_count)
    places = jnp.take(bin_place, particle_bin)
    owners = places // own_bins
    target_bin = owners % bin_count
    target_mic = owners // bin_count
    local_bin = places % own_bins
    active = jnp.ones((particles_here,), jnp.int32)
    first_pick = bucket(target_bin, active, bin_count, cap_first)
    labels = jnp.stack([active, target_mic, local_bin, ctf_group], axis=1)
    first_labels = pick_ints(first_pick, labels).reshape(bin_count, cap_first, 4)
    row_labels = lax.all_to_all(
        first_labels, "bin", split_axis=0, concat_axis=0, tiled=True
    ).reshape(first_total, 4)
    second_pick = bucket(row_labels[:, 1], row_labels[:, 0], mic_count, cap_second)
    second_labels = pick_ints(second_pick, row_labels).reshape(mic_count, cap_second, 4)
    slot_labels = lax.all_to_all(
        second_labels, "mic", split_axis=0, concat_axis=0, tiled=True
    ).reshape(second_total, 4)
    slot_ctf = group_ctf(slot_labels[:, 3], defocus, bfactor, image_side)
    home_ctf = group_ctf(ctf_group, defocus, bfactor, image_side)
    current = references
    scores = jnp.zeros((particles_here,), jnp.float32)
    for iteration in range(ITERS):
        ref_rows = jnp.take(current.reshape(own_bins, pixel_count), slot_labels[:, 2], axis=0)
        toward_row = lax.all_to_all(
            ref_rows.reshape(mic_count, cap_second, pixel_count),
            "mic",
            split_axis=0,
            concat_axis=0,
            tiled=True,
        )
        row_refs = pick_rows(second_pick.T, toward_row.reshape(second_total, pixel_count))
        toward_home = lax.all_to_all(
            row_refs.reshape(bin_count, cap_first, pixel_count),
            "bin",
            split_axis=0,
            concat_axis=0,
            tiled=True,
        )
        home_refs = pick_rows(first_pick.T, toward_home.reshape(first_total, pixel_count))
        scores, weights, weighted = compare(home_refs, home_ctf, flat_images, image_side)
        sent_terms = pick_rows(first_pick, weighted).reshape(bin_count, cap_first, pixel_count)
        sent_weights = pick_rows(first_pick, weights[:, None])
        row_terms, row_weights = (
            lax.all_to_all(sent_terms, "bin", split_axis=0, concat_axis=0, tiled=True),
            lax.all_to_all(sent_weights, "bin", split_axis=0, concat_axis=0, tiled=True),
        )
        row_terms = row_terms.reshape(first_total, pixel_count)
        next_terms = pick_rows(second_pick, row_terms).reshape(mic_count, cap_second, pixel_count)
        next_weights = pick_rows(second_pick, row_weights).reshape(mic_count, cap_second)
        owner_terms, owner_weights = (
            lax.all_to_all(next_terms, "mic", split_axis=0, concat_axis=0, tiled=True),
            lax.all_to_all(next_weights, "mic", split_axis=0, concat_axis=0, tiled=True),
        )
        current = accumulate(
            current,
            slot_labels[:, 2],
            slot_labels[:, 0],
            owner_weights.reshape(second_total),
            owner_terms.reshape(second_total, pixel_count),
            slot_ctf,
        )
    return (current, scores)


def solution(mesh):
    in_specs = (
        P(("mic", "bin"), None, None),
        P(None, ("mic", "bin")),
        P(("mic", "bin")),
        P(("mic", "bin")),
        P(),
        P(),
        P(),
        P(("mic", "bin"), None, None),
    )
    out_specs = (P(("mic", "bin"), None, None), P(("mic", "bin")))
    return jax.shard_map(body, mesh=mesh, in_specs=in_specs, out_specs=out_specs, check_vma=False)
```

profile of v0, /device:TPU:0, one launch (start us, length us, event | category | flops | bytes accessed | tf_op | source)
XLA Modules:
  0.0 329.8 jit_solution(17780350419424285355)
XLA Ops:
  4.0 13.5 %all_to_all.88 = s32[8,1,4]{2,1,0:T(1,128)S(1)} all-to-all(s32[8,1,4]{2,1,0:T(1,128)S(1)} %copy.59), channel_id=1, replica_groups=mesh['mic'=4,'bin'=8] {'bin'}, dimensions={0} | all-to-all | bytes 256 | tf_op jit(solution)/shard_map/all_to_all | solution.py:140
  28.1 16.9 %all_to_all.89 = bf16[4,2,65536]{2,1,0:T(2,128)(2,1)S(1)} all-to-all(bf16[4,2,65536]{2,1,0:T(2,128)(2,1)S(1)} %reshape.405), channel_id=1, replica_groups=mesh['mic'=4,'bin'=8] {'mic'}, dimensions={0} | all-to-all | bytes 2097152 | tf_op jit(solution)/shard_map/all_to_all | solution.py:154
  51.8 3.9 %all-to-all-start.3 = ((bf16[8,2,32768]{2,1,0:T(2,128)(2,1)}), bf16[8,2,32768]{2,1,0:T(2,128)(2,1)S(1)}, u32[]{:S(2)}, u32[]{:S(2)}) async-start(bf16[8,2,32768]{2,1,0:T(2,128)(2,1)} %reshape.499), calls=%async_computation.3 | async-start | bytes 2097152 | tf_op jit(solution)/shard_map/all_to_all | solution.py:162
  57.3 3.7 %gather_fusion.1 = bf16[4,256,256]{2,0,1:T(4,128)(2,1)} fusion(bf16[4,512,256]{2,0,1:T(4,128)(2,1)S(1)} %pad_maximum_fusion, s32[4]{0:T(128)S(1)} %get-tuple-element.34), kind=kCustom, calls=%fused_computation.3 | custom fusion | bytes 1048624 | tf_op jit(solution)/shard_map/vmap()/gather | solution.py:56
  66.4 3.7 %gather_fusion.2 = bf16[4,256,256]{1,0,2:T(4,128)(2,1)} fusion(bf16[4,256,512]{1,0,2:T(4,128)(2,1)S(1)} %copy.65, s32[4]{0:T(128)S(1)} %get-tuple-element.33), kind=kCustom, calls=%fused_computation.4 | custom fusion | bytes 1048624 | tf_op jit(solution)/shard_map/vmap()/gather | solution.py:58
  73.7 7.5 %all-to-all-done.3 = bf16[8,2,32768]{2,1,0:T(2,128)(2,1)S(1)} async-done(((bf16[8,2,32768]{2,1,0:T(2,128)(2,1)}), bf16[8,2,32768]{2,1,0:T(2,128)(2,1)S(1)}, u32[]{:S(2)}, u32[]{:S(2)}) %all-to-all-start.3) | async-done | bytes 1048608 | tf_op jit(solution)/shard_map/all_to_all | solution.py:162
  84.7 11.3 %multiply_reduce_fusion.3 = (f32[4]{0:T(128)S(1)}, f32[4]{0:T(128)S(1)}) fusion(f32[4,65536]{1,0:T(4,128)S(1)} %bitcast.113, bf16[8,1,65536]{2,1,0:T(2,128)(2,1)} %reshape.500, s32[4]{0:T(128)S(1)} %add.183, f32[4]{0:T(128)S(1)} %neg.41, f32[65536]{0:T(1024)S(1)} %bitcast.118, f32[4]{0:T(128)S(1)} %get-tuple-element.19), kind=kOutput, calls=%fused_computation.88 | convolution fusion | flops 7864408 | bytes 2359376 | tf_op jit(solution)/shard_map/dot_general | solution.py:113
  96.9 3.8 %all-to-all-start.6 = ((bf16[8,1,1]{2,1,0:T(2,128)(2,1)}), bf16[8,1,1]{2,1,0:T(2,128)(2,1)S(1)}, u32[]{:S(2)}, u32[]{:S(2)}) async-start(bf16[8,1,1]{2,1,0:T(2,128)(2,1)} %copy.69), calls=%async_computation.6 | async-start | bytes 8192 | tf_op jit(solution)/shard_map/all_to_all | solution.py:175
  100.7 10.6 %fusion.5 = bf16[8,1,65536]{2,0,1:T(8,128)(2,1)S(1)} fusion(f32[4,65536]{1,0:T(4,128)} %bitcast.114, f32[4]{0:T(128)S(1)} %get-tuple-element.26, f32[4]{0:T(128)S(1)} %neg.41, f32[65536]{0:T(1024)S(1)} %bitcast.119, f32[4]{0:T(128)S(1)} %get-tuple-element.19, s32[4]{0:T(128)S(1)} %add.183), kind=kOutput, calls=%fused_computation.20 | convolution fusion | flops 7340128 | bytes 2359360 | tf_op jit(solution)/shard_map/dot_general | solution.py:113
  114.5 6.0 %all-to-all-start.4 = ((bf16[8,2,32768]{2,1,0:T(2,128)(2,1)}), bf16[8,2,32768]{2,1,0:T(2,128)(2,1)S(1)}, u32[]{:S(2)}, u32[]{:S(2)}) async-start(bf16[8,2,32768]{2,1,0:T(2,128)(2,1)} %reshape.501), calls=%async_computation.4 | async-start | bytes 2097152 | tf_op jit(solution)/shard_map/all_to_all | solution.py:174
  121.5 24.6 %all-to-all-done.4 = bf16[8,2,32768]{2,1,0:T(2,128)(2,1)S(1)} async-done(((bf16[8,2,32768]{2,1,0:T(2,128)(2,1)}), bf16[8,2,32768]{2,1,0:T(2,128)(2,1)S(1)}, u32[]{:S(2)}, u32[]{:S(2)}) %all-to-all-start.4) | async-done | bytes 1048608 | tf_op jit(solution)/shard_map/all_to_all | solution.py:174
  150.3 4.3 %reshape.502 = bf16[8,1,65536]{2,1,0:T(2,128)(2,1)S(1)} reshape(bf16[8,2,32768]{2,1,0:T(2,128)(2,1)} %copy-done.1) | data formatting | bytes 2097152
  159.8 3.5 %all-to-all-start.5 = ((bf16[4,2,65536]{2,1,0:T(2,128)(2,1)}), bf16[4,2,65536]{2,1,0:T(2,128)(2,1)S(1)}, u32[]{:S(2)}, u32[]{:S(2)}) async-start(bf16[4,2,65536]{2,1,0:T(2,128)(2,1)} %reshape.411), calls=%async_computation.5 | async-start | bytes 2097152 | tf_op jit(solution)/shard_map/all_to_all | solution.py:181
  163.7 11.4 %convolution_add_fusion.2 = f32[8,65536]{1,0:T(8,128)} fusion(f32[8]{0:T(128)S(1)} %neg.44, f32[65536]{0:T(1024)S(1)} %bitcast.120, f32[8]{0:T(128)S(1)} %get-tuple-element.21, f32[8]{0:T(128)S(1)} %reshape.425, s32[8]{0:T(128)S(1)} %get-tuple-element.17, pred[8]{0:T(512)(128)(4,1)S(1)} %fusion.84), kind=kOutput, calls=%fused_computation.7 | convolution fusion | flops 55574656 | bytes 2359432 | tf_op jit(solution)/shard_map/dot_general | solution.py:91
  182.4 16.9 %all_to_all.90 = bf16[4,2,65536]{2,1,0:T(2,128)(2,1)S(1)} all-to-all(bf16[4,2,65536]{2,1,0:T(2,128)(2,1)S(1)} %reshape.414), channel_id=1, replica_groups=mesh['mic'=4,'bin'=8] {'mic'}, dimensions={0} | all-to-all | bytes 2097152 | tf_op jit(solution)/shard_map/all_to_all | solution.py:154
  202.4 28.9 %all_to_all.91 = bf16[8,2,32768]{2,1,0:T(2,128)(2,1)S(1)} all-to-all(bf16[8,2,32768]{2,1,0:T(2,128)(2,1)S(1)} %reshape.503), channel_id=1, replica_groups=mesh['mic'=4,'bin'=8] {'bin'}, dimensions={0} | all-to-all | bytes 2097152 | tf_op jit(solution)/shard_map/all_to_all | solution.py:162
  234.7 11.4 %multiply_reduce_fusion.1 = (f32[4]{0:T(128)S(1)}, f32[4]{0:T(128)S(1)}) fusion(f32[4,65536]{1,0:T(4,128)S(1)} %bitcast.115, bf16[8,1,65536]{2,1,0:T(2,128)(2,1)} %reshape.504, s32[4]{0:T(128)S(1)} %add.183, f32[4]{0:T(128)S(1)} %neg.41, f32[65536]{0:T(1024)S(1)} %bitcast.121, f32[4]{0:T(128)S(1)} %get-tuple-element.19), kind=kOutput, calls=%fused_computation.74 | convolution fusion | flops 7864408 | bytes 2359376 | tf_op jit(solution)/shard_map/dot_general | solution.py:113
  246.6 8.8 %fusion.7 = bf16[8,1,65536]{2,0,1:T(8,128)(2,1)S(1)} fusion(f32[4,65536]{1,0:T(4,128)S(1)} %bitcast.116, f32[4]{0:T(128)S(1)} %get-tuple-element.23, f32[4]{0:T(128)S(1)} %neg.41, f32[65536]{0:T(1024)S(1)} %bitcast.122, f32[4]{0:T(128)S(1)} %get-tuple-element.19, s32[4]{0:T(128)S(1)} %add.183), kind=kOutput, calls=%fused_computation.22 | convolution fusion | flops 7340128 | bytes 2359360 | tf_op jit(solution)/shard_map/dot_general | solution.py:113
  259.0 9.8 %all_to_all.92 = bf16[8,1,1]{2,1,0:T(2,128)(2,1)S(1)} all-to-all(bf16[8,1,1]{2,1,0:T(2,128)(2,1)S(1)} %copy.73), channel_id=1, replica_groups=mesh['mic'=4,'bin'=8] {'bin'}, dimensions={0} | all-to-all | bytes 32 | tf_op jit(solution)/shard_map/all_to_all | solution.py:175
  268.8 3.6 %all-to-all-start.10 = ((bf16[8,2,32768]{2,1,0:T(2,128)(2,1)}), bf16[8,2,32768]{2,1,0:T(2,128)(2,1)S(1)}, u32[]{:S(2)}, u32[]{:S(2)}) async-start(bf16[8,2,32768]{2,1,0:T(2,128)(2,1)} %reshape.505), calls=%async_computation.10 | async-start | bytes 2097152 | tf_op jit(solution)/shard_map/all_to_all | solution.py:174
  273.3 23.3 %all-to-all-done.10 = bf16[8,2,32768]{2,1,0:T(2,128)(2,1)S(1)} async-done(((bf16[8,2,32768]{2,1,0:T(2,128)(2,1)}), bf16[8,2,32768]{2,1,0:T(2,128)(2,1)S(1)}, u32[]{:S(2)}, u32[]{:S(2)}) %all-to-all-start.10) | async-done | bytes 1048608 | tf_op jit(solution)/shard_map/all_to_all | solution.py:174
  299.8 3.5 %reshape.506 = bf16[8,1,65536]{2,1,0:T(2,128)(2,1)} reshape(bf16[8,2,32768]{2,1,0:T(2,128)(2,1)S(1)} %all-to-all-done.10) | data formatting | bytes 2097152
  307.7 3.5 %all-to-all-start.11 = ((bf16[4,2,65536]{2,1,0:T(2,128)(2,1)}), bf16[4,2,65536]{2,1,0:T(2,128)(2,1)S(1)}, u32[]{:S(2)}, u32[]{:S(2)}) async-start(bf16[4,2,65536]{2,1,0:T(2,128)(2,1)} %reshape.420), calls=%async_computation.11 | async-start | bytes 2097152 | tf_op jit(solution)/shard_map/all_to_all | solution.py:181
  311.3 11.4 %convolution_add_fusion = f32[8,65536]{1,0:T(8,128)} fusion(f32[8]{0:T(128)S(1)} %reshape.426, f32[8]{0:T(128)S(1)} %neg.44, f32[65536]{0:T(1024)S(1)} %bitcast.123, f32[8]{0:T(128)S(1)} %get-tuple-element.21, s32[8]{0:T(128)S(1)} %get-tuple-element.17, pred[8]{0:T(512)(128)(4,1)S(1)} %fusion.84), kind=kOutput, calls=%fused_computation.5 | convolution fusion | flops 55574656 | bytes 2359432 | tf_op jit(solution)/shard_map/dot_general | solution.py:91
  (121 shorter events, 82.5 us)
Async XLA Ops:
  0.6 0.7 copy-start
  18.7 7.0 %all-to-all-start.1 = ((s32[4,2,4]{2,1,0:T(2,128)}), s32[4,2,4]{2,1,0:T(2,128)S(1)}, u32[]{:S(2)}, u32[]{:S(2)}) async-start(s32[4,2,4]{2,1,0:T(2,128)} %bitcast.7), calls=%async_computation.1 | async-start | bytes 8192 | tf_op jit(solution)/shard_map/all_to_all | solution.py:145
  49.9 5.8 %copy-start.6 = (f32[64]{0:T(128)S(1)}, f32[64]{0:T(128)}, u32[]{:S(2)}) copy-start(f32[64]{0:T(128)} %param.15) | copy-start | bytes 772
  49.9 5.8 %copy-start.7 = (f32[64]{0:T(128)S(1)}, f32[64]{0:T(128)}, u32[]{:S(2)}) copy-start(f32[64]{0:T(128)} %param.16) | copy-start | bytes 772
  49.9 5.8 %copy-start.8 = (s32[4]{0:T(128)S(1)}, s32[4]{0:T(128)}, u32[]{:S(2)}) copy-start(s32[4]{0:T(128)} %param.12) | copy-start | bytes 52
  51.8 4.4 %copy-start.5 = (bf16[4,256,256]{2,1,0:T(8,128)(2,1)S(1)}, bf16[4,256,256]{2,1,0:T(8,128)(2,1)}, u32[]{:S(2)}) copy-start(bf16[4,256,256]{2,1,0:T(8,128)(2,1)} %param.10) | copy-start | bytes 1572868
  51.8 29.5 %all-to-all-start.3 = ((bf16[8,2,32768]{2,1,0:T(2,128)(2,1)}), bf16[8,2,32768]{2,1,0:T(2,128)(2,1)S(1)}, u32[]{:S(2)}, u32[]{:S(2)}) async-start(bf16[8,2,32768]{2,1,0:T(2,128)(2,1)} %reshape.499), calls=%async_computation.3 | async-start | bytes 2097152 | tf_op jit(solution)/shard_map/all_to_all | solution.py:162
  55.7 1.6 copy-start.9
  73.7 22.3 %copy-start.2 = (f32[1,4,256,256]{3,1,2,0:T(4,128)}, f32[1,4,256,256]{3,1,2,0:T(4,128)S(1)}, u32[]{:S(2)}) copy-start(f32[1,4,256,256]{3,1,2,0:T(4,128)S(1)} %copy.83) | copy-start | bytes 3145732
  96.9 17.6 %all-to-all-start.6 = ((bf16[8,1,1]{2,1,0:T(2,128)(2,1)}), bf16[8,1,1]{2,1,0:T(2,128)(2,1)S(1)}, u32[]{:S(2)}, u32[]{:S(2)}) async-start(bf16[8,1,1]{2,1,0:T(2,128)(2,1)} %copy.69), calls=%async_computation.6 | async-start | bytes 8192 | tf_op jit(solution)/shard_map/all_to_all | solution.py:175
  114.5 31.6 %all-to-all-start.4 = ((bf16[8,2,32768]{2,1,0:T(2,128)(2,1)}), bf16[8,2,32768]{2,1,0:T(2,128)(2,1)S(1)}, u32[]{:S(2)}, u32[]{:S(2)}) async-start(bf16[8,2,32768]{2,1,0:T(2,128)(2,1)} %reshape.501), calls=%async_computation.4 | async-start | bytes 2097152 | tf_op jit(solution)/shard_map/all_to_all | solution.py:174
  146.1 1.0 copy-start.1
  147.1 12.7 %all-to-all-start.7 = ((bf16[4,1,2]{2,1,0:T(2,128)(2,1)}), bf16[4,1,2]{2,1,0:T(2,128)(2,1)S(1)}, u32[]{:S(2)}, u32[]{:S(2)}) async-start(bf16[4,1,2]{2,1,0:T(2,128)(2,1)} %all_to_all.72), calls=%async_computation.7 | async-start | bytes 4096 | tf_op jit(solution)/shard_map/all_to_all | solution.py:182
  159.8 18.0 %all-to-all-start.5 = ((bf16[4,2,65536]{2,1,0:T(2,128)(2,1)}), bf16[4,2,65536]{2,1,0:T(2,128)(2,1)S(1)}, u32[]{:S(2)}, u32[]{:S(2)}) async-start(bf16[4,2,65536]{2,1,0:T(2,128)(2,1)} %reshape.411), calls=%async_computation.5 | async-start | bytes 2097152 | tf_op jit(solution)/shard_map/all_to_all | solution.py:181
  231.3 3.5 %copy-start.3 = (f32[1,4,256,256]{3,1,2,0:T(4,128)S(1)}, f32[1,4,256,256]{3,1,2,0:T(4,128)}, u32[]{:S(2)}) copy-start(f32[1,4,256,256]{3,1,2,0:T(4,128)} %copy-done.2) | copy-start | bytes 3145732
  234.7 11.9 %copy-start.4 = (f32[1,4,256,256]{3,1,2,0:T(4,128)S(1)}, f32[1,4,256,256]{3,1,2,0:T(4,128)}, u32[]{:S(2)}) copy-start(f32[1,4,256,256]{3,1,2,0:T(4,128)} %copy-done.2) | copy-start | bytes 3145732
  268.8 27.8 %all-to-all-start.10 = ((bf16[8,2,32768]{2,1,0:T(2,128)(2,1)}), bf16[8,2,32768]{2,1,0:T(2,128)(2,1)S(1)}, u32[]{:S(2)}, u32[]{:S(2)}) async-start(bf16[8,2,32768]{2,1,0:T(2,128)(2,1)} %reshape.505), calls=%async_computation.10 | async-start | bytes 2097152 | tf_op jit(solution)/shard_map/all_to_all | solution.py:174
  296.6 11.1 %all-to-all-start.13 = ((bf16[4,1,2]{2,1,0:T(2,128)(2,1)}), bf16[4,1,2]{2,1,0:T(2,128)(2,1)S(1)}, u32[]{:S(2)}, u32[]{:S(2)}) async-start(bf16[4,1,2]{2,1,0:T(2,128)(2,1)} %all_to_all.73), calls=%async_computation.13 | async-start | bytes 4096 | tf_op jit(solution)/shard_map/all_to_all | solution.py:182
  307.7 18.0 %all-to-all-start.11 = ((bf16[4,2,65536]{2,1,0:T(2,128)(2,1)}), bf16[4,2,65536]{2,1,0:T(2,128)(2,1)S(1)}, u32[]{:S(2)}, u32[]{:S(2)}) async-start(bf16[4,2,65536]{2,1,0:T(2,128)(2,1)} %reshape.420), calls=%async_computation.11 | async-start | bytes 2097152 | tf_op jit(solution)/shard_map/all_to_all | solution.py:181
where the time goes:
time: 335 us; the launch traced here: 330 us
  blocking collectives  86 us (26%)
  matrix products  79.9 us (24%)
  waiting for transfers between devices  62.9 us (19%)
  local copies, waits for them, and re-layouts  52.1 us (16%)
  starting transfers between devices  33.9 us (10%)
  other arithmetic  13.6 us (4%)
    dot_general x12, matrix products, pick_rows(): jnp.dot(selector.astype(jnp.bfloat16), values, preferred_element_type=jnp...  50 us
    all_to_all x2, waiting for transfers between devices, body(): lax.all_to_all(sent_terms, 'bin', split_axis=0, concat_axis=0, tiled=True)  47.9 us
    all_to_all x2, blocking collectives, body(): lax.all_to_all(ref_rows.reshape(mic_count, cap_second, pixel_count), 'mic...  33.8 us
    all_to_all x1, blocking collectives, body(): lax.all_to_all(row_refs.reshape(bin_count, cap_first, pixel_count), 'bin'...  28.9 us
    unnamed x33, local copies, waits for them, and re-layouts  26.4 us
    dot_general x2, matrix products, accumulate(): jnp.dot(member.astype(jnp.float32), ctf_power, precision=lax.Precision.HI...  22.8 us
    all_to_all x1, blocking collectives, body(): lax.all_to_all(first_labels, 'bin', split_axis=0, concat_axis=0, tiled=True)  13.5 us
    all_to_all x1, blocking collectives, body(): lax.all_to_all(sent_weights, 'bin', split_axis=0, concat_axis=0, tiled=True)  9.8 us
  transfers between devices with their start and end apart: 9, of which 6 were waited for; matrix products, arithmetic and copies ran while one was open for 23% of the time, Pallas kernels for 0%

commit v1 on v0

v1 whole, which is shorter than its diff:
```python
import functools
import math

import jax
import jax.numpy as jnp
import numpy as np
from jax import lax
from jax.experimental import pallas as pl
from jax.experimental.pallas import tpu as pltpu
from jax.sharding import PartitionSpec as P

ITERS = 2
PRIOR_WEIGHT = 0.5
EPSILON = 1e-06
CONTRAST = 0.1
AMPLITUDE = math.sqrt(1.0 - CONTRAST * CONTRAST)

LABEL_ROWS = 16
CHUNK = 32
VMEM_BYTES = 48 * 1024 * 1024

F32 = jnp.float32
BF16 = jnp.bfloat16
VMEM = pl.BlockSpec(memory_space=pltpu.VMEM)
SMEM = pl.BlockSpec(memory_space=pltpu.SMEM)


def hartley(side):
    index = np.arange(side)
    angles = (np.outer(index, index) % side).astype(np.float32) * np.float32(2.0 * math.pi / side)
    return (np.cos(angles) + np.sin(angles)) / np.float32(math.sqrt(side))


def label_block(values, side):
    row = lax.broadcasted_iota(jnp.int32, (LABEL_ROWS, side), 0)
    block = jnp.zeros((LABEL_ROWS, side), jnp.int32)
    for number, value in enumerate(values):
        block = jnp.where(row == number, value, block)
    return block.astype(F32).astype(BF16)


def read_rows(block, weights):
    labels = block.astype(F32)
    total = sum(labels[r : r + 1, :128] * float(w) for r, w in enumerate(weights) if w)
    return jnp.max(total).astype(jnp.int32)


def home_kernel(
    bin_count, own_bins, place_ref, bin_ref, group_ref, offset_ref, image_ref, basis_ref, *rest
):
    outs, (spectra,) = rest[:bin_count], rest[bin_count:]
    particles, side = image_ref.shape[0], image_ref.shape[1]
    here = lax.axis_index("bin")
    empty = jnp.zeros((LABEL_ROWS, side), BF16)
    for out in outs:
        out[side : side + LABEL_ROWS, :] = empty

    @pl.loop(0, particles)
    def _(i):
        moved = pltpu.roll(image_ref[i].astype(F32), side - offset_ref[0, i], 0).astype(BF16)
        columns = pltpu.roll(basis_ref[...].astype(F32), offset_ref[1, i], 0).astype(BF16)
        half = jnp.dot(basis_ref[...], moved, preferred_element_type=F32).astype(BF16)
        spectra[...] = jnp.dot(half, columns, preferred_element_type=F32).astype(BF16)
        place = place_ref[bin_ref[i]]
        owner = place // own_bins
        target = lax.rem(owner, bin_count)
        labels = label_block(
            (1 + owner // bin_count, lax.rem(place, own_bins), group_ref[i], i * bin_count + here),
            side,
        )
        for step in range(bin_count):

            @pl.when((target ^ here) == step)
            def _():
                outs[step][0:side, :] = spectra[...]
                outs[step][side : side + LABEL_ROWS, :] = labels


def middle_kernel(mic_count, capacity, *rest):
    arrived, outs = rest[: len(rest) - mic_count], rest[len(rest) - mic_count :]
    rows, side = arrived[0].shape
    here = lax.axis_index("mic")
    empty = jnp.zeros((LABEL_ROWS, side), BF16)
    for out in outs:
        for j in range(capacity):
            out[j, rows - LABEL_ROWS : rows, :] = empty
    targets = [read_rows(block[rows - LABEL_ROWS : rows, :], (1,)) for block in arrived]
    counts = [jnp.int32(0)] * mic_count
    for block, target in zip(arrived, targets):
        step_of = (target - 1) ^ here
        for step in range(mic_count):
            chosen = (target > 0) & (step_of == step)

            @pl.when(chosen)
            def _(block=block, step=step, slot=counts[step]):
                outs[step][slot] = block[...]

            counts[step] = counts[step] + chosen.astype(jnp.int32)


def owner_kernel(
    bin_count, mic_count, capacity, focus_ref, damping_ref, current_ref, *rest
):
    arrived, (refined_ref, score_ref) = rest[:mic_count], rest[mic_count : mic_count + 2]
    spectra, ctf, middle, sums, weight, number, active, place, home, particle = rest[mic_count + 2 :]
    own_bins, side, _ = current_ref.shape
    slots = mic_count * capacity
    steps = side // CHUNK
    here = lax.axis_index("mic")
    pixels = float(side * side)

    row = lax.broadcasted_iota(jnp.int32, (slots, side), 0)
    focus = jnp.zeros((slots, side), F32)
    damping = jnp.zeros((slots, side), F32)
    for step in range(mic_count):
        for j in range(capacity):
            s = step * capacity + j
            block = arrived[step][j, side : side + LABEL_ROWS, :]
            code = read_rows(block, (0, 1, 256, 65536))
            valid = read_rows(block, (1,)) > 0
            code = jnp.where(valid, code, 0)
            group = (code // 256) % 256
            sender = code // 65536
            active[s] = valid.astype(jnp.int32)
            place[s] = code % 256
            home[s] = (here ^ step) * bin_count + sender % bin_count
            particle[s] = sender // bin_count
            focus = jnp.where(row == s, focus_ref[group], focus)
            damping = jnp.where(row == s, damping_ref[group], damping)

    frequency = lax.broadcasted_iota(jnp.int32, (slots, side), 1)
    folded = jnp.minimum(frequency, side - frequency).astype(F32) / (side / 2.0)
    square = folded * folded
    envelope = jnp.exp(-damping * square)
    sine = jnp.sin(focus * square) * envelope
    cosine = jnp.cos(focus * square) * envelope
    by_sine = jnp.transpose(CONTRAST * sine - AMPLITUDE * cosine)
    by_cosine = jnp.transpose(-(AMPLITUDE * sine + CONTRAST * cosine))
    sums[...] = jnp.zeros(sums.shape, F32)

    def rows_of(c):
        return pl.ds(pl.multiple_of(c * CHUNK, CHUNK), CHUNK)

    def fold(values):
        return jnp.sum(values.reshape(CHUNK // 8, 8, side), axis=0)

    for s in range(slots):

        @pl.when(active[s] > 0)
        def _(s=s):
            for c in range(steps):
                rows = slice(c * CHUNK, (c + 1) * CHUNK)
                ctf[s, rows, :] = (
                    by_sine[rows, s : s + 1] * sine[s : s + 1, :]
                    + by_cosine[rows, s : s + 1] * cosine[s : s + 1, :]
                )
                spectra[s, rows, :] = arrived[s // capacity][s % capacity, rows, :]

    def compare(source):
        @pl.loop(0, slots)
        def _(s):
            @pl.when(active[s] > 0)
            def _():
                def add(c, totals):
                    cross, model, data = totals
                    rows = rows_of(c)
                    values = spectra[s, rows, :].astype(F32)
                    predicted = ctf[s, rows, :] * source[place[s], rows, :].astype(F32)
                    return (
                        cross + fold(predicted * values),
                        model + fold(predicted * predicted),
                        data + fold(values * values),
                    )

                zero = jnp.zeros((8, side), F32)
                totals = lax.fori_loop(0, steps, add, (zero, zero, zero))
                for k in range(3):
                    sums[k, pl.ds(s, 1), :] = jnp.sum(totals[k], axis=0, keepdims=True)

        cross, model, data = (
            jnp.sum(sums[k], axis=1, keepdims=True) / pixels for k in range(3)
        )
        correlation = cross / jnp.sqrt((model + EPSILON) * (data + EPSILON))
        weights = 1.0 / (1.0 + jnp.exp(-float(side) * correlation))
        weight[...] = jnp.broadcast_to(weights.astype(BF16).astype(F32), (slots, side))
        return correlation

    def update(source, target):
        @pl.loop(0, own_bins)
        def _(p):
            members = jnp.int32(0)
            member = jnp.int32(0)
            for s in range(slots):
                match = (active[s] > 0) & (place[s] == p)
                members = members + match.astype(jnp.int32)
                member = jnp.where(match, s, member)

            def shares(s, rows):
                table = ctf[s, rows, :]
                scaled = weight[pl.ds(s, 1), :] * table
                term = (scaled * spectra[s, rows, :].astype(F32)).astype(BF16).astype(F32)
                return term, scaled * table

            def finish(rows, numerator, denominator):
                previous = source[p, rows, :].astype(F32)
                target[p, rows, :] = (
                    (numerator + PRIOR_WEIGHT * previous) / (denominator + PRIOR_WEIGHT)
                ).astype(BF16)

            @pl.when(members == 0)
            def _():
                target[p] = source[p]

            @pl.when(members == 1)
            def _():
                @pl.loop(0, steps)
                def _(c):
                    rows = rows_of(c)
                    finish(rows, *shares(member, rows))

            @pl.when(members > 1)
            def _():
                @pl.loop(0, steps)
                def _(c):
                    rows = rows_of(c)
                    number[0, rows, :] = jnp.zeros((CHUNK, side), F32)
                    number[1, rows, :] = jnp.zeros((CHUNK, side), F32)

                @pl.loop(0, slots)
                def _(s):
                    @pl.when((active[s] > 0) & (place[s] == p))
                    def _():
                        @pl.loop(0, steps)
                        def _(c):
                            rows = rows_of(c)
                            term, power = shares(s, rows)
                            number[0, rows, :] += term
                            number[1, rows, :] += power

                @pl.loop(0, steps)
                def _(c):
                    rows = rows_of(c)
                    finish(rows, number[0, rows, :], number[1, rows, :])

    source = current_ref
    for iteration in range(ITERS):
        correlation = compare(source)
        target = refined_ref if iteration == ITERS - 1 else middle
        update(source, target)
        source = target

    devices = score_ref.shape[0]
    device = lax.broadcasted_iota(jnp.int32, (devices, 1, 128), 0)
    lane = lax.broadcasted_iota(jnp.int32, (devices, 1, 128), 2)
    board = jnp.zeros((devices, 1, 128), F32)
    for s in range(slots):
        hit = (active[s] > 0) & (device == home[s]) & (lane == particle[s])
        board = jnp.where(hit, correlation[s : s + 1, :].reshape(1, 1, 1), board)
    score_ref[...] = board


def exchange(blocks, axis):
    size = lax.axis_size(axis)
    return [blocks[0]] + [
        lax.ppermute(blocks[k], axis, [(i, i ^ k) for i in range(size)]) for k in range(1, size)
    ]


def body(images, offsets, ctf_group, particle_bin, bin_place, defocus, bfactor, references):
    mic_count = lax.axis_size("mic")
    bin_count = lax.axis_size("bin")
    particles, side, _ = images.shape
    own_bins = references.shape[0]
    capacity = (3 * particles + 2 * mic_count - 1) // (2 * mic_count)
    slots = mic_count * capacity
    rows = side + LABEL_ROWS
    params = pltpu.CompilerParams(vmem_limit_bytes=VMEM_BYTES)

    sent = pl.pallas_call(
        functools.partial(home_kernel, bin_count, own_bins),
        out_shape=[jax.ShapeDtypeStruct((rows, side), BF16)] * bin_count,
        in_specs=[SMEM] * 4 + [VMEM] * 2,
        out_specs=[VMEM] * bin_count,
        scratch_shapes=[pltpu.VMEM((side, side), BF16)],
        compiler_params=params,
        name="home",
    )(bin_place, particle_bin, ctf_group, offsets, images, jnp.asarray(hartley(side), BF16))
    arrived = exchange(sent, "bin")

    sent = pl.pallas_call(
        functools.partial(middle_kernel, mic_count, capacity),
        out_shape=[jax.ShapeDtypeStruct((capacity, rows, side), BF16)] * mic_count,
        in_specs=[VMEM] * bin_count,
        out_specs=[VMEM] * mic_count,
        compiler_params=params,
        name="middle",
    )(*arrived)
    arrived = exchange(sent, "mic")

    refined, board = pl.pallas_call(
        functools.partial(owner_kernel, bin_count, mic_count, capacity),
        out_shape=[
            jax.ShapeDtypeStruct(references.shape, BF16),
            jax.ShapeDtypeStruct((mic_count * bin_count, 1, 128), F32),
        ],
        in_specs=[SMEM] * 2 + [VMEM] * (1 + mic_count),
        out_specs=[VMEM] * 2,
        scratch_shapes=[
            pltpu.VMEM((slots, side, side), BF16),
            pltpu.VMEM((slots, side, side), F32),
            pltpu.VMEM((own_bins, side, side), BF16),
            pltpu.VMEM((3, slots, side), F32),
            pltpu.VMEM((slots, side), F32),
            pltpu.VMEM((2, side, side), F32),
        ]
        + [pltpu.SMEM((slots,), jnp.int32)] * 4,
        compiler_params=params,
        name="owner",
    )(defocus, bfactor, references, *arrived)
    back = lax.all_to_all(board, ("mic", "bin"), split_axis=0, concat_axis=0, tiled=True)
    return (refined, jnp.sum(back, axis=(0, 1))[:particles])


def solution(mesh):
    in_specs = (
        P(("mic", "bin"), None, None),
        P(None, ("mic", "bin")),
        P(("mic", "bin")),
        P(("mic", "bin")),
        P(),
        P(),
        P(),
        P(("mic", "bin"), None, None),
    )
    out_specs = (P(("mic", "bin"), None, None), P(("mic", "bin")))
    return jax.shard_map(body, mesh=mesh, in_specs=in_specs, out_specs=out_specs, check_vma=False)
```

time: 335 us -> 75 us (0.22); the launches traced: 330 us -> 75.4 us
  matrix products: 79.9 us -> 0 us
  blocking collectives: 86 us -> 16.3 us
  local copies, waits for them, and re-layouts: 52.1 us -> 4.7 us
  waiting for transfers between devices: 62.9 us -> 27.5 us
  starting transfers between devices: 33.9 us -> 15.2 us
  other arithmetic: 13.6 us -> 0.56 us
  Pallas kernels: 0 us -> 10.5 us
    dot_general x17 -> x0, matrix products: 79.9 us -> none  [the longest x12 50 us: pick_rows(): jnp.dot(selector.astype(jnp.bfloat16), values, preferred_element_type=jnp...]
    all_to_all x5 -> x1, blocking collectives: 86 us -> 16.3 us  [body(): lax.all_to_all(board, ('mic', 'bin'), split_axis=0, concat_axis=0, tiled=...]
    all_to_all x9 -> x0, waiting for transfers between devices: 62.9 us -> none  [the longest x2 47.9 us: body(): lax.all_to_all(sent_terms, 'bin', split_axis=0, concat_axis=0, tiled=True)]
    all_to_all x9 -> x0, starting transfers between devices: 33.9 us -> none  [the longest x2 9.56 us: body(): lax.all_to_all(sent_terms, 'bin', split_axis=0, concat_axis=0, tiled=True)]
    ppermute x0 -> x10, waiting for transfers between devices: none -> 27.5 us  [exchange(): lax.ppermute(blocks[k], axis, [(i, i ^ k) for i in range(size)])]
    unnamed x33 -> x18, local copies, waits for them, and re-layouts: 26.4 us -> 4.7 us
    ppermute x0 -> x10, starting transfers between devices: none -> 15.2 us  [exchange(): lax.ppermute(blocks[k], axis, [(i, i ^ k) for i in range(size)])]
    gather x5 -> x0, local copies, waits for them, and re-layouts: 10.6 us -> none  [the longest x1 3.74 us: shifted(): rows_moved = lax.dynamic_slice_in_dim(doubled, shift_pair[0], image_side, 0)]
  transfers between devices with their start and end apart: 9 -> 10, of which waited for: 6 -> 4; matrix products, arithmetic and copies ran while one was open for 23% -> 0% of each run, Pallas kernels for 0% -> 0%
where the time goes in v1:
time: 75 us; the launch traced here: 75.4 us
  waiting for transfers between devices  27.5 us (37%)
  blocking collectives  16.3 us (22%)
  starting transfers between devices  15.2 us (20%)
  Pallas kernels  10.5 us (14%)
  local copies, waits for them, and re-layouts  4.7 us (6%)
    ppermute x10, waiting for transfers between devices, exchange(): lax.ppermute(blocks[k], axis, [(i, i ^ k) for i in range(size)])  27.5 us
    all_to_all x1, blocking collectives, body(): lax.all_to_all(board, ('mic', 'bin'), split_axis=0, concat_axis=0, tiled=...  16.3 us
    ppermute x10, starting transfers between devices, exchange(): lax.ppermute(blocks[k], axis, [(i, i ^ k) for i in range(size)])  15.2 us
    pallas_call x1, Pallas kernels, body(): pl.pallas_call(functools.partial(owner_kernel, bin_count, mic_count, capa...  7.7 us
    unnamed x18, local copies, waits for them, and re-layouts  4.7 us
    pallas_call x1, Pallas kernels, body(): pl.pallas_call(functools.partial(home_kernel, bin_count, own_bins), out_s...  2.39 us
  transfers between devices with their start and end apart: 10, of which 4 were waited for; matrix products, arithmetic and copies ran while one was open for 0% of the time, Pallas kernels for 0%

profile of v1, /device:TPU:0, one launch (start us, length us, event | category | flops | bytes accessed | tf_op | source)
XLA Modules:
  0.0 75.4 jit_solution(2553453033675107424)
XLA Ops:
  0.7 1.1 %copy-done.1 = bf16[4,256,256]{2,1,0:T(8,128)(2,1)S(1)} copy-done((bf16[4,256,256]{2,1,0:T(8,128)(2,1)S(1)}, bf16[4,256,256]{2,1,0:T(8,128)(2,1)}, u32[]{:S(2)}) %copy-start.1) | copy-done | bytes 524312
  1.8 0.9 %copy-done.2 = bf16[256,256]{1,0:T(8,128)(2,1)S(1)} copy-done((bf16[256,256]{1,0:T(8,128)(2,1)S(1)}, bf16[256,256]{1,0:T(8,128)(2,1)}, u32[]{:S(2)}) %copy-start.2) | copy-done | bytes 131096
  2.7 0.7 copy-done.3
  3.4 0.7 copy-done.4
  4.0 0.7 copy-done.5
  4.7 0.7 copy-done.6
  5.3 2.4 %home.1 = (bf16[272,256]{1,0:T(8,128)(2,1)S(1)}, bf16[272,256]{1,0:T(8,128)(2,1)S(1)}, bf16[272,256]{1,0:T(8,128)(2,1)S(1)}, bf16[272,256]{1,0:T(8,128)(2,1)S(1)...) custom-call(s32[256]{0:T(256)S(1)} %copy-done.3, ...), custom_call_target="tpu_custom_call" | custom-call | tf_op jit(solution)/shard_map/home/pallas_call | solution.py:279
  7.7 3.0 %collective-permute-start = (bf16[272,256]{1,0:T(8,128)(2,1)S(1)}, bf16[272,256]{1,0:T(8,128)(2,1)S(1)}, u32[]{:S(2)}, u32[]{:S(2)}) collective-permute-start(bf16[272,256]{1,0:T(8,128)(2,1)S(1)} %get-tuple-element.17), channel_id=1, source_target_pairs={{0,1},{1,0},{2,3},{3,2},{4,5},{5,4},{6,7},{7,6},{8,9},{9,8},{10,11... | collective-permute-start | bytes 417800 | tf_op jit(solution)/shard_map/ppermute | solution.py:265
  10.8 1.6 %collective-permute-start.1 = (bf16[272,256]{1,0:T(8,128)(2,1)S(1)}, bf16[272,256]{1,0:T(8,128)(2,1)S(1)}, u32[]{:S(2)}, u32[]{:S(2)}) collective-permute-start(bf16[272,256]{1,0:T(8,128)(2,1)S(1)} %get-tuple-element.18), channel_id=1, source_target_pairs={{0,2},{1,3},{2,0},{3,1},{4,6},{5,7},{6,4},{7,5},{8,10},{9,11},{10,... | collective-permute-start | bytes 417800 | tf_op jit(solution)/shard_map/ppermute | solution.py:265
  12.4 3.0 %collective-permute-start.3 = (bf16[272,256]{1,0:T(8,128)(2,1)S(1)}, bf16[272,256]{1,0:T(8,128)(2,1)S(1)}, u32[]{:S(2)}, u32[]{:S(2)}) collective-permute-start(bf16[272,256]{1,0:T(8,128)(2,1)S(1)} %get-tuple-element.20), channel_id=1, source_target_pairs={{0,4},{1,5},{2,6},{3,7},{4,0},{5,1},{6,2},{7,3},{8,12},{9,13},{10,... | collective-permute-start | bytes 417800 | tf_op jit(solution)/shard_map/ppermute | solution.py:265
  15.3 1.3 %collective-permute-start.4 = (bf16[272,256]{1,0:T(8,128)(2,1)S(1)}, bf16[272,256]{1,0:T(8,128)(2,1)S(1)}, u32[]{:S(2)}, u32[]{:S(2)}) collective-permute-start(bf16[272,256]{1,0:T(8,128)(2,1)S(1)} %get-tuple-element.21), channel_id=1, source_target_pairs={{0,5},{1,4},{2,7},{3,6},{4,1},{5,0},{6,3},{7,2},{8,13},{9,12},{10,... | collective-permute-start | bytes 417800 | tf_op jit(solution)/shard_map/ppermute | solution.py:265
  16.6 3.6 %collective-permute-start.5 = (bf16[272,256]{1,0:T(8,128)(2,1)S(1)}, bf16[272,256]{1,0:T(8,128)(2,1)S(1)}, u32[]{:S(2)}, u32[]{:S(2)}) collective-permute-start(bf16[272,256]{1,0:T(8,128)(2,1)S(1)} %get-tuple-element.22), channel_id=1, source_target_pairs={{0,6},{1,7},{2,4},{3,5},{4,2},{5,3},{6,0},{7,1},{8,14},{9,15},{10,... | collective-permute-start | bytes 417800 | tf_op jit(solution)/shard_map/ppermute | solution.py:265
  20.2 1.9 %collective-permute-done.1.rest_2_ = bf16[272,256]{1,0:T(8,128)(2,1)S(1)} collective-permute-done((bf16[272,256]{1,0:T(8,128)(2,1)S(1)}, bf16[272,256]{1,0:T(8,128)(2,1)S(1)}, u32[]{:S(2)}, u32[]{:S(2)}) %collective-permute-start.1) | collective-permute-done | bytes 139296 | tf_op jit(solution)/shard_map/ppermute | solution.py:265
  22.2 0.8 %collective-permute-start.6 = (bf16[272,256]{1,0:T(8,128)(2,1)S(1)}, bf16[272,256]{1,0:T(8,128)(2,1)S(1)}, u32[]{:S(2)}, u32[]{:S(2)}) collective-permute-start(bf16[272,256]{1,0:T(8,128)(2,1)S(1)} %get-tuple-element.23), channel_id=1, source_target_pairs={{0,7},{1,6},{2,5},{3,4},{4,3},{5,2},{6,1},{7,0},{8,15},{9,14},{10,... | collective-permute-start | bytes 417800 | tf_op jit(solution)/shard_map/ppermute | solution.py:265
  23.0 12.8 %collective-permute-done.4.rest_5_ = bf16[272,256]{1,0:T(8,128)(2,1)S(1)} collective-permute-done((bf16[272,256]{1,0:T(8,128)(2,1)S(1)}, bf16[272,256]{1,0:T(8,128)(2,1)S(1)}, u32[]{:S(2)}, u32[]{:S(2)}) %collective-permute-start.4) | collective-permute-done | bytes 139296 | tf_op jit(solution)/shard_map/ppermute | solution.py:265
  35.8 0.4 middle.1
  36.2 0.1 collective-permute-start.7
  36.3 1.6 %collective-permute-start.8 = (bf16[2,272,256]{2,1,0:T(8,128)(2,1)S(1)}, bf16[2,272,256]{2,1,0:T(8,128)(2,1)S(1)}, u32[]{:S(2)}, u32[]{:S(2)}) collective-permute-start(bf16[2,272,256]{2,1,0:T(8,128)(2,1)S(1)} %get-tuple-element.26), channel_id=1, source_target_pairs={{0,16},{8,24},{16,0},{24,8},{1,17},{9,25},{17,1},{25,9},{2,18},{10... | collective-permute-start | bytes 835592 | tf_op jit(solution)/shard_map/ppermute | solution.py:265
  37.8 0.3 collective-permute-start.9
  38.1 7.7 %collective-permute-done.8.rest_2_ = bf16[2,272,256]{2,1,0:T(8,128)(2,1)S(1)} collective-permute-done((bf16[2,272,256]{2,1,0:T(8,128)(2,1)S(1)}, bf16[2,272,256]{2,1,0:T(8,128)(2,1)S(1)}, u32[]{:S(2)}, u32[]{:S(2)}) %collective-permute-start.8) | collective-permute-done | bytes 278560 | tf_op jit(solution)/shard_map/ppermute | solution.py:265
  45.8 5.1 %collective-permute-done.9.rest_3_ = bf16[2,272,256]{2,1,0:T(8,128)(2,1)S(1)} collective-permute-done((bf16[2,272,256]{2,1,0:T(8,128)(2,1)S(1)}, bf16[2,272,256]{2,1,0:T(8,128)(2,1)S(1)}, u32[]{:S(2)}, u32[]{:S(2)}) %collective-permute-start.9) | collective-permute-done | bytes 278560 | tf_op jit(solution)/shard_map/ppermute | solution.py:265
  50.9 7.7 %owner.1 = (bf16[8,256,256]{2,1,0:T(8,128)(2,1)}, f32[32,1,128]{2,1,0:T(1,128)S(1)}) custom-call(f32[64]{0:T(128)S(1)} %copy-done.7, f32[64]{0:T(128)S(1)} %copy-done.8, bf16[8,256,256]{2,1,0:T(8,128)(2,1)S(1)} %copy-done, bf16[2,272,256]{2,1,0:T(8,128)(2,1)S(1)} %get-tuple-element.24.rest_0_, bf16[2,272,256]{2,1,0:T(8,128)(2,1)S(1)} %collective-permute-done.7.rest_1_, ...), custom_call_target="tpu_custom_call" | custom-call | tf_op jit(solution)/shard_map/owner/pallas_call | solution.py:300
  58.6 16.3 %all_to_all.5 = f32[32,1,128]{2,1,0:T(1,128)S(1)} all-to-all(f32[32,1,128]{2,1,0:T(1,128)S(1)} %get-tuple-element.29), channel_id=1, replica_groups=mesh['mic'=4,'bin'=8] {'mic','bin'}, dimensions={0} | all-to-all | bytes 32768 | tf_op jit(solution)/shard_map/all_to_all | solution.py:320
  74.8 0.6 reduce_sum.9
  (19 shorter events, 0.1 us)
Async XLA Ops:
  0.6 50.2 %copy-start = (bf16[8,256,256]{2,1,0:T(8,128)(2,1)S(1)}, bf16[8,256,256]{2,1,0:T(8,128)(2,1)}, u32[]{:S(2)}) copy-start(bf16[8,256,256]{2,1,0:T(8,128)(2,1)} %current_ref.1) | copy-start | bytes 3145732
  0.6 1.1 %copy-start.1 = (bf16[4,256,256]{2,1,0:T(8,128)(2,1)S(1)}, bf16[4,256,256]{2,1,0:T(8,128)(2,1)}, u32[]{:S(2)}) copy-start(bf16[4,256,256]{2,1,0:T(8,128)(2,1)} %image_ref.1) | copy-start | bytes 1572868
  1.8 0.9 %copy-start.2 = (bf16[256,256]{1,0:T(8,128)(2,1)S(1)}, bf16[256,256]{1,0:T(8,128)(2,1)}, u32[]{:S(2)}) copy-start(bf16[256,256]{1,0:T(8,128)(2,1)} %constant.4.clone.basis_ref) | copy-start | bytes 393220
  2.7 0.7 copy-start.3
  3.4 0.7 copy-start.4
  4.0 0.7 copy-start.5
  4.7 0.7 copy-start.6
  7.7 8.9 %collective-permute-start = (bf16[272,256]{1,0:T(8,128)(2,1)S(1)}, bf16[272,256]{1,0:T(8,128)(2,1)S(1)}, u32[]{:S(2)}, u32[]{:S(2)}) collective-permute-start(bf16[272,256]{1,0:T(8,128)(2,1)S(1)} %get-tuple-element.17), channel_id=1, source_target_pairs={{0,1},{1,0},{2,3},{3,2},{4,5},{5,4},{6,7},{7,6},{8,9},{9,8},{10,11... | collective-permute-start | bytes 417800 | tf_op jit(solution)/shard_map/ppermute | solution.py:265
  10.8 11.4 %collective-permute-start.1 = (bf16[272,256]{1,0:T(8,128)(2,1)S(1)}, bf16[272,256]{1,0:T(8,128)(2,1)S(1)}, u32[]{:S(2)}, u32[]{:S(2)}) collective-permute-start(bf16[272,256]{1,0:T(8,128)(2,1)S(1)} %get-tuple-element.18), channel_id=1, source_target_pairs={{0,2},{1,3},{2,0},{3,1},{4,6},{5,7},{6,4},{7,5},{8,10},{9,11},{10,... | collective-permute-start | bytes 417800 | tf_op jit(solution)/shard_map/ppermute | solution.py:265
  12.4 10.6 %collective-permute-start.2 = (bf16[272,256]{1,0:T(8,128)(2,1)S(1)}, bf16[272,256]{1,0:T(8,128)(2,1)S(1)}, u32[]{:S(2)}, u32[]{:S(2)}) collective-permute-start(bf16[272,256]{1,0:T(8,128)(2,1)S(1)} %get-tuple-element.19), channel_id=1, source_target_pairs={{0,3},{1,2},{2,1},{3,0},{4,7},{5,6},{6,5},{7,4},{8,11},{9,10},{10,... | collective-permute-start | bytes 417800 | tf_op jit(solution)/shard_map/ppermute | solution.py:265
  12.4 10.6 %collective-permute-start.3 = (bf16[272,256]{1,0:T(8,128)(2,1)S(1)}, bf16[272,256]{1,0:T(8,128)(2,1)S(1)}, u32[]{:S(2)}, u32[]{:S(2)}) collective-permute-start(bf16[272,256]{1,0:T(8,128)(2,1)S(1)} %get-tuple-element.20), channel_id=1, source_target_pairs={{0,4},{1,5},{2,6},{3,7},{4,0},{5,1},{6,2},{7,3},{8,12},{9,13},{10,... | collective-permute-start | bytes 417800 | tf_op jit(solution)/shard_map/ppermute | solution.py:265
  15.3 20.5 %collective-permute-start.4 = (bf16[272,256]{1,0:T(8,128)(2,1)S(1)}, bf16[272,256]{1,0:T(8,128)(2,1)S(1)}, u32[]{:S(2)}, u32[]{:S(2)}) collective-permute-start(bf16[272,256]{1,0:T(8,128)(2,1)S(1)} %get-tuple-element.21), channel_id=1, source_target_pairs={{0,5},{1,4},{2,7},{3,6},{4,1},{5,0},{6,3},{7,2},{8,13},{9,12},{10,... | collective-permute-start | bytes 417800 | tf_op jit(solution)/shard_map/ppermute | solution.py:265
  16.6 19.2 %collective-permute-start.5 = (bf16[272,256]{1,0:T(8,128)(2,1)S(1)}, bf16[272,256]{1,0:T(8,128)(2,1)S(1)}, u32[]{:S(2)}, u32[]{:S(2)}) collective-permute-start(bf16[272,256]{1,0:T(8,128)(2,1)S(1)} %get-tuple-element.22), channel_id=1, source_target_pairs={{0,6},{1,7},{2,4},{3,5},{4,2},{5,3},{6,0},{7,1},{8,14},{9,15},{10,... | collective-permute-start | bytes 417800 | tf_op jit(solution)/shard_map/ppermute | solution.py:265
  22.2 13.6 %collective-permute-start.6 = (bf16[272,256]{1,0:T(8,128)(2,1)S(1)}, bf16[272,256]{1,0:T(8,128)(2,1)S(1)}, u32[]{:S(2)}, u32[]{:S(2)}) collective-permute-start(bf16[272,256]{1,0:T(8,128)(2,1)S(1)} %get-tuple-element.23), channel_id=1, source_target_pairs={{0,7},{1,6},{2,5},{3,4},{4,3},{5,2},{6,1},{7,0},{8,15},{9,14},{10,... | collective-permute-start | bytes 417800 | tf_op jit(solution)/shard_map/ppermute | solution.py:265
  36.2 1.9 %collective-permute-start.7 = (bf16[2,272,256]{2,1,0:T(8,128)(2,1)S(1)}, bf16[2,272,256]{2,1,0:T(8,128)(2,1)S(1)}, u32[]{:S(2)}, u32[]{:S(2)}) collective-permute-start(bf16[2,272,256]{2,1,0:T(8,128)(2,1)S(1)} %get-tuple-element.25), channel_id=1, source_target_pairs={{0,8},{8,0},{16,24},{24,16},{1,9},{9,1},{17,25},{25,17},{2,10},{10... | collective-permute-start | bytes 835592 | tf_op jit(solution)/shard_map/ppermute | solution.py:265
  36.3 9.5 %collective-permute-start.8 = (bf16[2,272,256]{2,1,0:T(8,128)(2,1)S(1)}, bf16[2,272,256]{2,1,0:T(8,128)(2,1)S(1)}, u32[]{:S(2)}, u32[]{:S(2)}) collective-permute-start(bf16[2,272,256]{2,1,0:T(8,128)(2,1)S(1)} %get-tuple-element.26), channel_id=1, source_target_pairs={{0,16},{8,24},{16,0},{24,8},{1,17},{9,25},{17,1},{25,9},{2,18},{10... | collective-permute-start | bytes 835592 | tf_op jit(solution)/shard_map/ppermute | solution.py:265
  37.8 13.0 %copy-start.7 = (f32[64]{0:T(128)S(1)}, f32[64]{0:T(128)}, u32[]{:S(2)}) copy-start(f32[64]{0:T(128)} %focus_ref.1) | copy-start | bytes 772
  37.8 13.0 %copy-start.8 = (f32[64]{0:T(128)S(1)}, f32[64]{0:T(128)}, u32[]{:S(2)}) copy-start(f32[64]{0:T(128)} %damping_ref.1) | copy-start | bytes 772
  37.8 13.0 %collective-permute-start.9 = (bf16[2,272,256]{2,1,0:T(8,128)(2,1)S(1)}, bf16[2,272,256]{2,1,0:T(8,128)(2,1)S(1)}, u32[]{:S(2)}, u32[]{:S(2)}) collective-permute-start(bf16[2,272,256]{2,1,0:T(8,128)(2,1)S(1)} %get-tuple-element.27), channel_id=1, source_target_pairs={{0,24},{8,16},{16,8},{24,0},{1,25},{9,17},{17,9},{25,1},{2,26},{10... | collective-permute-start | bytes 835592 | tf_op jit(solution)/shard_map/ppermute | solution.py:265

commit v2 on v1

--- a/solution.py
+++ b/solution.py
@@ -23,6 +23,11 @@
 BF16 = jnp.bfloat16
 VMEM = pl.BlockSpec(memory_space=pltpu.VMEM)
 SMEM = pl.BlockSpec(memory_space=pltpu.SMEM)
+HBM = pl.BlockSpec(memory_space=pltpu.HBM)
+
+
+def in_hbm(x):
+    return pltpu.with_memory_space_constraint(x, pltpu.HBM)
 
 
 def hartley(side):
@@ -46,17 +51,37 @@
 
 
 def home_kernel(
-    bin_count, own_bins, place_ref, bin_ref, group_ref, offset_ref, image_ref, basis_ref, *rest
+    bin_count, own_bins, place_hbm, bin_hbm, group_hbm, offset_hbm, image_hbm, basis_hbm, *rest
 ):
-    outs, (spectra,) = rest[:bin_count], rest[bin_count:]
+    outs, rest = rest[:bin_count], rest[bin_count:]
+    spectra, image_ref, basis_ref, place_ref, bin_ref, group_ref, offset_ref, image_sem, sem = rest
     particles, side = image_ref.shape[0], image_ref.shape[1]
     here = lax.axis_index("bin")
+    pairs = (
+        (basis_hbm, basis_ref),
+        (place_hbm, place_ref),
+        (bin_hbm, bin_ref),
+        (group_hbm, group_ref),
+        (offset_hbm, offset_ref),
+    )
+    copies = [pltpu.make_async_copy(a, b, sem.at[k]) for k, (a, b) in enumerate(pairs)]
+    for copy in copies:
+        copy.start()
+
+    def image_copy(i):
+        return pltpu.make_async_copy(image_hbm.at[i], image_ref.at[i], image_sem.at[i])
+
+    for i in range(particles):
+        image_copy(i).start()
     empty = jnp.zeros((LABEL_ROWS, side), BF16)
     for out in outs:
         out[side : side + LABEL_ROWS, :] = empty
+    for copy in copies:
+        copy.wait()
 
     @pl.loop(0, particles)
     def _(i):
+        image_copy(i).wait()
         moved = pltpu.roll(image_ref[i].astype(F32), side - offset_ref[0, i], 0).astype(BF16)
         columns = pltpu.roll(basis_ref[...].astype(F32), offset_ref[1, i], 0).astype(BF16)
         half = jnp.dot(basis_ref[...], moved, preferred_element_type=F32).astype(BF16)
@@ -77,7 +102,7 @@
 
 
 def middle_kernel(mic_count, capacity, *rest):
-    arrived, outs = rest[: len(rest) - mic_count], rest[len(rest) - mic_count :]
+    arrived, outs = rest[: len(rest) - mic_count], rest[len(rest) - mic_count :][::-1]
     rows, side = arrived[0].shape
     here = lax.axis_index("mic")
     empty = jnp.zeros((LABEL_ROWS, side), BF16)
@@ -101,7 +126,7 @@
 def owner_kernel(
     bin_count, mic_count, capacity, focus_ref, damping_ref, current_ref, *rest
 ):
-    arrived, (refined_ref, score_ref) = rest[:mic_count], rest[mic_count : mic_count + 2]
+    arrived, (refined_ref, score_ref) = rest[:mic_count][::-1], rest[mic_count : mic_count + 2]
     spectra, ctf, middle, sums, weight, number, active, place, home, particle = rest[mic_count + 2 :]
     own_bins, side, _ = current_ref.shape
     slots = mic_count * capacity
@@ -279,12 +304,22 @@
     sent = pl.pallas_call(
         functools.partial(home_kernel, bin_count, own_bins),
         out_shape=[jax.ShapeDtypeStruct((rows, side), BF16)] * bin_count,
-        in_specs=[SMEM] * 4 + [VMEM] * 2,
+        in_specs=[HBM] * 6,
         out_specs=[VMEM] * bin_count,
-        scratch_shapes=[pltpu.VMEM((side, side), BF16)],
+        scratch_shapes=[
+            pltpu.VMEM((side, side), BF16),
+            pltpu.VMEM(images.shape, BF16),
+            pltpu.VMEM((side, side), BF16),
+            pltpu.SMEM(bin_place.shape, jnp.int32),
+            pltpu.SMEM(particle_bin.shape, jnp.int32),
+            pltpu.SMEM(ctf_group.shape, jnp.int32),
+            pltpu.SMEM(offsets.shape, jnp.int32),
+            pltpu.SemaphoreType.DMA((particles,)),
+            pltpu.SemaphoreType.DMA((5,)),
+        ],
         compiler_params=params,
         name="home",
-    )(bin_place, particle_bin, ctf_group, offsets, images, jnp.asarray(hartley(side), BF16))
+    )(*map(in_hbm, (bin_place, particle_bin, ctf_group, offsets, images, jnp.asarray(hartley(side), BF16))))
     arrived = exchange(sent, "bin")
 
     sent = pl.pallas_call(
@@ -294,8 +329,8 @@
         out_specs=[VMEM] * mic_count,
         compiler_params=params,
         name="middle",
-    )(*arrived)
-    arrived = exchange(sent, "mic")
+    )(*arrived[::-1])
+    arrived = exchange(sent[::-1], "mic")
 
     refined, board = pl.pallas_call(
         functools.partial(owner_kernel, bin_count, mic_count, capacity),
@@ -316,7 +351,7 @@
         + [pltpu.SMEM((slots,), jnp.int32)] * 4,
         compiler_params=params,
         name="owner",
-    )(defocus, bfactor, references, *arrived)
+    )(defocus, bfactor, references, *arrived[::-1])
     back = lax.all_to_all(board, ("mic", "bin"), split_axis=0, concat_axis=0, tiled=True)
     return (refined, jnp.sum(back, axis=(0, 1))[:particles])
 

time: 75 us -> 68.9 us (0.919)
  starting transfers between devices: 15.2 us -> 26 us
  waiting for transfers between devices: 27.5 us -> 20 us
  local copies, waits for them, and re-layouts: 4.7 us -> 0.01 us
  blocking collectives: 16.3 us -> 12 us
    ppermute x10, starting transfers between devices: 15.2 us -> 26 us  [exchange(): lax.ppermute(blocks[k], axis, [(i, i ^ k) for i in range(size)])]
    ppermute x10, waiting for transfers between devices: 27.5 us -> 20 us  [exchange(): lax.ppermute(blocks[k], axis, [(i, i ^ k) for i in range(size)])]
    unnamed x18 -> x6, local copies, waits for them, and re-layouts: 4.7 us -> 0.01 us
    all_to_all x1, blocking collectives: 16.3 us -> 12 us  [body(): lax.all_to_all(board, ('mic', 'bin'), split_axis=0, concat_axis=0, tiled=...]
    pallas_call x1, Pallas kernels: 7.7 us -> 6.59 us  [body(): pl.pallas_call(functools.partial(owner_kernel, bin_count, mic_count, capa...]
  transfers between devices with their start and end apart: 10 -> 10, of which waited for: 4 -> 5; matrix products, arithmetic and copies ran while one was open for 0% -> 0% of each run, Pallas kernels for 0% -> 0%
where the time goes in v2:
time: 68.9 us; the launch traced here: 69.2 us
  starting transfers between devices  26 us (38%)
  waiting for transfers between devices  20 us (29%)
  blocking collectives  12 us (17%)
  Pallas kernels  9.92 us (14%)
  between operations  0.69 us (1%)
    ppermute x10, starting transfers between devices, exchange(): lax.ppermute(blocks[k], axis, [(i, i ^ k) for i in range(size)])  26 us
    ppermute x10, waiting for transfers between devices, exchange(): lax.ppermute(blocks[k], axis, [(i, i ^ k) for i in range(size)])  20 us
    all_to_all x1, blocking collectives, body(): lax.all_to_all(board, ('mic', 'bin'), split_axis=0, concat_axis=0, tiled=...  12 us
    pallas_call x1, Pallas kernels, body(): pl.pallas_call(functools.partial(owner_kernel, bin_count, mic_count, capa...  6.59 us
    pallas_call x1, Pallas kernels, body(): pl.pallas_call(functools.partial(home_kernel, bin_count, own_bins), out_s...  2.94 us
  transfers between devices with their start and end apart: 10, of which 5 were waited for; matrix products, arithmetic and copies ran while one was open for 0% of the time, Pallas kernels for 0%

profile of v2, /device:TPU:0, one launch (start us, length us, event | category | flops | bytes accessed | tf_op | source)
XLA Modules:
  0.0 69.2 jit_solution(15913832241833447623)
XLA Ops:
  0.6 2.9 %home.1 = (bf16[272,256]{1,0:T(8,128)(2,1)S(1)}, bf16[272,256]{1,0:T(8,128)(2,1)S(1)}, bf16[272,256]{1,0:T(8,128)(2,1)S(1)}, bf16[272,256]{1,0:T(8,128)(2,1)S(1)...) custom-call(s32[256]{0:T(256)} %place_hbm.1, ...), custom_call_target="tpu_custom_call" | custom-call | tf_op jit(solution)/shard_map/home/pallas_call | solution.py:304
  3.6 6.1 %collective-permute-start = (bf16[272,256]{1,0:T(8,128)(2,1)S(1)}, bf16[272,256]{1,0:T(8,128)(2,1)S(1)}, u32[]{:S(2)}, u32[]{:S(2)}) collective-permute-start(bf16[272,256]{1,0:T(8,128)(2,1)S(1)} %get-tuple-element.16), channel_id=1, source_target_pairs={{0,7},{1,6},{2,5},{3,4},{4,3},{5,2},{6,1},{7,0},{8,15},{9,14},{10,... | collective-permute-start | bytes 417800 | tf_op jit(solution)/shard_map/ppermute | solution.py:290
  9.7 0.2 collective-permute-start.1
  9.9 0.7 %collective-permute-start.2 = (bf16[272,256]{1,0:T(8,128)(2,1)S(1)}, bf16[272,256]{1,0:T(8,128)(2,1)S(1)}, u32[]{:S(2)}, u32[]{:S(2)}) collective-permute-start(bf16[272,256]{1,0:T(8,128)(2,1)S(1)} %get-tuple-element.18), channel_id=1, source_target_pairs={{0,5},{1,4},{2,7},{3,6},{4,1},{5,0},{6,3},{7,2},{8,13},{9,12},{10,... | collective-permute-start | bytes 417800 | tf_op jit(solution)/shard_map/ppermute | solution.py:290
  10.6 2.0 %collective-permute-start.3 = (bf16[272,256]{1,0:T(8,128)(2,1)S(1)}, bf16[272,256]{1,0:T(8,128)(2,1)S(1)}, u32[]{:S(2)}, u32[]{:S(2)}) collective-permute-start(bf16[272,256]{1,0:T(8,128)(2,1)S(1)} %get-tuple-element.19), channel_id=1, source_target_pairs={{0,4},{1,5},{2,6},{3,7},{4,0},{5,1},{6,2},{7,3},{8,12},{9,13},{10,... | collective-permute-start | bytes 417800 | tf_op jit(solution)/shard_map/ppermute | solution.py:290
  12.7 2.3 %collective-permute-start.4 = (bf16[272,256]{1,0:T(8,128)(2,1)S(1)}, bf16[272,256]{1,0:T(8,128)(2,1)S(1)}, u32[]{:S(2)}, u32[]{:S(2)}) collective-permute-start(bf16[272,256]{1,0:T(8,128)(2,1)S(1)} %get-tuple-element.20), channel_id=1, source_target_pairs={{0,3},{1,2},{2,1},{3,0},{4,7},{5,6},{6,5},{7,4},{8,11},{9,10},{10,... | collective-permute-start | bytes 417800 | tf_op jit(solution)/shard_map/ppermute | solution.py:290
  14.9 0.0 collective-permute-done.rest_0_
  15.0 11.4 %collective-permute-start.5 = (bf16[272,256]{1,0:T(8,128)(2,1)S(1)}, bf16[272,256]{1,0:T(8,128)(2,1)S(1)}, u32[]{:S(2)}, u32[]{:S(2)}) collective-permute-start(bf16[272,256]{1,0:T(8,128)(2,1)S(1)} %get-tuple-element.21), channel_id=1, source_target_pairs={{0,2},{1,3},{2,0},{3,1},{4,6},{5,7},{6,4},{7,5},{8,10},{9,11},{10,... | collective-permute-start | bytes 417800 | tf_op jit(solution)/shard_map/ppermute | solution.py:290
  26.4 0.0 collective-permute-done.1.rest_1_
  26.4 1.3 %collective-permute-start.6 = (bf16[272,256]{1,0:T(8,128)(2,1)S(1)}, bf16[272,256]{1,0:T(8,128)(2,1)S(1)}, u32[]{:S(2)}, u32[]{:S(2)}) collective-permute-start(bf16[272,256]{1,0:T(8,128)(2,1)S(1)} %get-tuple-element.22), channel_id=1, source_target_pairs={{0,1},{1,0},{2,3},{3,2},{4,5},{5,4},{6,7},{7,6},{8,9},{9,8},{10,11... | collective-permute-start | bytes 417800 | tf_op jit(solution)/shard_map/ppermute | solution.py:290
  27.7 3.8 %collective-permute-done.2.rest_2_ = bf16[272,256]{1,0:T(8,128)(2,1)S(1)} collective-permute-done((bf16[272,256]{1,0:T(8,128)(2,1)S(1)}, bf16[272,256]{1,0:T(8,128)(2,1)S(1)}, u32[]{:S(2)}, u32[]{:S(2)}) %collective-permute-start.2) | collective-permute-done | bytes 139296 | tf_op jit(solution)/shard_map/ppermute | solution.py:290
  31.4 2.0 %collective-permute-done.3.rest_3_ = bf16[272,256]{1,0:T(8,128)(2,1)S(1)} collective-permute-done((bf16[272,256]{1,0:T(8,128)(2,1)S(1)}, bf16[272,256]{1,0:T(8,128)(2,1)S(1)}, u32[]{:S(2)}, u32[]{:S(2)}) %collective-permute-start.3) | collective-permute-done | bytes 139296 | tf_op jit(solution)/shard_map/ppermute | solution.py:290
  33.5 0.0 collective-permute-done.4.rest_4_
  33.5 1.2 %collective-permute-done.5.rest_5_ = bf16[272,256]{1,0:T(8,128)(2,1)S(1)} collective-permute-done((bf16[272,256]{1,0:T(8,128)(2,1)S(1)}, bf16[272,256]{1,0:T(8,128)(2,1)S(1)}, u32[]{:S(2)}, u32[]{:S(2)}) %collective-permute-start.5) | collective-permute-done | bytes 139296 | tf_op jit(solution)/shard_map/ppermute | solution.py:290
  34.7 0.0 collective-permute-done.6.rest_6_
  34.7 0.4 middle.1
  35.1 0.1 collective-permute-start.7
  35.1 1.6 %collective-permute-start.8 = (bf16[2,272,256]{2,1,0:T(8,128)(2,1)S(1)}, bf16[2,272,256]{2,1,0:T(8,128)(2,1)S(1)}, u32[]{:S(2)}, u32[]{:S(2)}) collective-permute-start(bf16[2,272,256]{2,1,0:T(8,128)(2,1)S(1)} %get-tuple-element.25), channel_id=1, source_target_pairs={{0,16},{8,24},{16,0},{24,8},{1,17},{9,25},{17,1},{25,9},{2,18},{10... | collective-permute-start | bytes 835592 | tf_op jit(solution)/shard_map/ppermute | solution.py:290
  36.7 0.3 collective-permute-start.9
  37.0 7.0 %collective-permute-done.7.rest_0_ = bf16[2,272,256]{2,1,0:T(8,128)(2,1)S(1)} collective-permute-done((bf16[2,272,256]{2,1,0:T(8,128)(2,1)S(1)}, bf16[2,272,256]{2,1,0:T(8,128)(2,1)S(1)}, u32[]{:S(2)}, u32[]{:S(2)}) %collective-permute-start.7) | collective-permute-done | bytes 278560 | tf_op jit(solution)/shard_map/ppermute | solution.py:290
  44.0 6.0 %collective-permute-done.8.rest_1_ = bf16[2,272,256]{2,1,0:T(8,128)(2,1)S(1)} collective-permute-done((bf16[2,272,256]{2,1,0:T(8,128)(2,1)S(1)}, bf16[2,272,256]{2,1,0:T(8,128)(2,1)S(1)}, u32[]{:S(2)}, u32[]{:S(2)}) %collective-permute-start.8) | collective-permute-done | bytes 278560 | tf_op jit(solution)/shard_map/ppermute | solution.py:290
  50.1 6.6 %owner.1 = (bf16[8,256,256]{2,1,0:T(8,128)(2,1)}, f32[32,1,128]{2,1,0:T(1,128)S(1)}) custom-call(f32[64]{0:T(128)S(1)} %copy-done.1, f32[64]{0:T(128)S(1)} %copy-done.2, bf16[8,256,256]{2,1,0:T(8,128)(2,1)S(1)} %copy-done, bf16[2,272,256]{2,1,0:T(8,128)(2,1)S(1)} %collective-permute-done.7.rest_0_, bf16[2,272,256]{2,1,0:T(8,128)(2,1)S(1)} %collective-permute-done.8.rest_1_, ...), custom_call_target="tpu_custom_call" | custom-call | tf_op jit(solution)/shard_map/owner/pallas_call | solution.py:335
  56.7 12.0 %all_to_all.5 = f32[32,1,128]{2,1,0:T(1,128)S(1)} all-to-all(f32[32,1,128]{2,1,0:T(1,128)S(1)} %get-tuple-element.29), channel_id=1, replica_groups=mesh['mic'=4,'bin'=8] {'mic','bin'}, dimensions={0} | all-to-all | bytes 32768 | tf_op jit(solution)/shard_map/all_to_all | solution.py:355
  68.7 0.6 reduce_sum.9
  (7 shorter events, 0.0 us)
Async XLA Ops:
  0.6 49.4 %copy-start = (bf16[8,256,256]{2,1,0:T(8,128)(2,1)S(1)}, bf16[8,256,256]{2,1,0:T(8,128)(2,1)}, u32[]{:S(2)}) copy-start(bf16[8,256,256]{2,1,0:T(8,128)(2,1)} %current_ref.1) | copy-start | bytes 3145732
  3.6 11.4 %collective-permute-start = (bf16[272,256]{1,0:T(8,128)(2,1)S(1)}, bf16[272,256]{1,0:T(8,128)(2,1)S(1)}, u32[]{:S(2)}, u32[]{:S(2)}) collective-permute-start(bf16[272,256]{1,0:T(8,128)(2,1)S(1)} %get-tuple-element.16), channel_id=1, source_target_pairs={{0,7},{1,6},{2,5},{3,4},{4,3},{5,2},{6,1},{7,0},{8,15},{9,14},{10,... | collective-permute-start | bytes 417800 | tf_op jit(solution)/shard_map/ppermute | solution.py:290
  9.7 16.7 %collective-permute-start.1 = (bf16[272,256]{1,0:T(8,128)(2,1)S(1)}, bf16[272,256]{1,0:T(8,128)(2,1)S(1)}, u32[]{:S(2)}, u32[]{:S(2)}) collective-permute-start(bf16[272,256]{1,0:T(8,128)(2,1)S(1)} %get-tuple-element.17), channel_id=1, source_target_pairs={{0,6},{1,7},{2,4},{3,5},{4,2},{5,3},{6,0},{7,1},{8,14},{9,15},{10,... | collective-permute-start | bytes 417800 | tf_op jit(solution)/shard_map/ppermute | solution.py:290
  9.9 21.6 %collective-permute-start.2 = (bf16[272,256]{1,0:T(8,128)(2,1)S(1)}, bf16[272,256]{1,0:T(8,128)(2,1)S(1)}, u32[]{:S(2)}, u32[]{:S(2)}) collective-permute-start(bf16[272,256]{1,0:T(8,128)(2,1)S(1)} %get-tuple-element.18), channel_id=1, source_target_pairs={{0,5},{1,4},{2,7},{3,6},{4,1},{5,0},{6,3},{7,2},{8,13},{9,12},{10,... | collective-permute-start | bytes 417800 | tf_op jit(solution)/shard_map/ppermute | solution.py:290
  10.6 22.9 %collective-permute-start.3 = (bf16[272,256]{1,0:T(8,128)(2,1)S(1)}, bf16[272,256]{1,0:T(8,128)(2,1)S(1)}, u32[]{:S(2)}, u32[]{:S(2)}) collective-permute-start(bf16[272,256]{1,0:T(8,128)(2,1)S(1)} %get-tuple-element.19), channel_id=1, source_target_pairs={{0,4},{1,5},{2,6},{3,7},{4,0},{5,1},{6,2},{7,3},{8,12},{9,13},{10,... | collective-permute-start | bytes 417800 | tf_op jit(solution)/shard_map/ppermute | solution.py:290
  12.7 20.8 %collective-permute-start.4 = (bf16[272,256]{1,0:T(8,128)(2,1)S(1)}, bf16[272,256]{1,0:T(8,128)(2,1)S(1)}, u32[]{:S(2)}, u32[]{:S(2)}) collective-permute-start(bf16[272,256]{1,0:T(8,128)(2,1)S(1)} %get-tuple-element.20), channel_id=1, source_target_pairs={{0,3},{1,2},{2,1},{3,0},{4,7},{5,6},{6,5},{7,4},{8,11},{9,10},{10,... | collective-permute-start | bytes 417800 | tf_op jit(solution)/shard_map/ppermute | solution.py:290
  15.0 19.7 %collective-permute-start.5 = (bf16[272,256]{1,0:T(8,128)(2,1)S(1)}, bf16[272,256]{1,0:T(8,128)(2,1)S(1)}, u32[]{:S(2)}, u32[]{:S(2)}) collective-permute-start(bf16[272,256]{1,0:T(8,128)(2,1)S(1)} %get-tuple-element.21), channel_id=1, source_target_pairs={{0,2},{1,3},{2,0},{3,1},{4,6},{5,7},{6,4},{7,5},{8,10},{9,11},{10,... | collective-permute-start | bytes 417800 | tf_op jit(solution)/shard_map/ppermute | solution.py:290
  26.4 8.3 %collective-permute-start.6 = (bf16[272,256]{1,0:T(8,128)(2,1)S(1)}, bf16[272,256]{1,0:T(8,128)(2,1)S(1)}, u32[]{:S(2)}, u32[]{:S(2)}) collective-permute-start(bf16[272,256]{1,0:T(8,128)(2,1)S(1)} %get-tuple-element.22), channel_id=1, source_target_pairs={{0,1},{1,0},{2,3},{3,2},{4,5},{5,4},{6,7},{7,6},{8,9},{9,8},{10,11... | collective-permute-start | bytes 417800 | tf_op jit(solution)/shard_map/ppermute | solution.py:290
  35.1 9.0 %collective-permute-start.7 = (bf16[2,272,256]{2,1,0:T(8,128)(2,1)S(1)}, bf16[2,272,256]{2,1,0:T(8,128)(2,1)S(1)}, u32[]{:S(2)}, u32[]{:S(2)}) collective-permute-start(bf16[2,272,256]{2,1,0:T(8,128)(2,1)S(1)} %get-tuple-element.24), channel_id=1, source_target_pairs={{0,24},{8,16},{16,8},{24,0},{1,25},{9,17},{17,9},{25,1},{2,26},{10... | collective-permute-start | bytes 835592 | tf_op jit(solution)/shard_map/ppermute | solution.py:290
  35.1 14.9 %collective-permute-start.8 = (bf16[2,272,256]{2,1,0:T(8,128)(2,1)S(1)}, bf16[2,272,256]{2,1,0:T(8,128)(2,1)S(1)}, u32[]{:S(2)}, u32[]{:S(2)}) collective-permute-start(bf16[2,272,256]{2,1,0:T(8,128)(2,1)S(1)} %get-tuple-element.25), channel_id=1, source_target_pairs={{0,16},{8,24},{16,0},{24,8},{1,17},{9,25},{17,1},{25,9},{2,18},{10... | collective-permute-start | bytes 835592 | tf_op jit(solution)/shard_map/ppermute | solution.py:290
  36.7 13.4 %copy-start.1 = (f32[64]{0:T(128)S(1)}, f32[64]{0:T(128)}, u32[]{:S(2)}) copy-start(f32[64]{0:T(128)} %focus_ref.1) | copy-start | bytes 772
  36.7 13.4 %copy-start.2 = (f32[64]{0:T(128)S(1)}, f32[64]{0:T(128)}, u32[]{:S(2)}) copy-start(f32[64]{0:T(128)} %damping_ref.1) | copy-start | bytes 772
  36.7 13.4 %collective-permute-start.9 = (bf16[2,272,256]{2,1,0:T(8,128)(2,1)S(1)}, bf16[2,272,256]{2,1,0:T(8,128)(2,1)S(1)}, u32[]{:S(2)}, u32[]{:S(2)}) collective-permute-start(bf16[2,272,256]{2,1,0:T(8,128)(2,1)S(1)} %get-tuple-element.26), channel_id=1, source_target_pairs={{0,8},{8,0},{16,24},{24,16},{1,9},{9,1},{17,25},{25,17},{2,10},{10... | collective-permute-start | bytes 835592 | tf_op jit(solution)/shard_map/ppermute | solution.py:290

commit v3 on v2

v3 whole, which is shorter than its diff:
```python
import functools
import math

import jax
import jax.numpy as jnp
import numpy as np
from jax import lax
from jax.experimental import pallas as pl
from jax.experimental.pallas import tpu as pltpu
from jax.sharding import PartitionSpec as P

ITERS = 2
PRIOR_WEIGHT = 0.5
EPSILON = 1e-06
CONTRAST = 0.1
AMPLITUDE = math.sqrt(1.0 - CONTRAST * CONTRAST)

LABEL_ROWS = 16
CHUNK = 32
VMEM_BYTES = 48 * 1024 * 1024

F32 = jnp.float32
BF16 = jnp.bfloat16
VMEM = pl.BlockSpec(memory_space=pltpu.VMEM)
SMEM = pl.BlockSpec(memory_space=pltpu.SMEM)
HBM = pl.BlockSpec(memory_space=pltpu.HBM)


def in_hbm(x):
    return pltpu.with_memory_space_constraint(x, pltpu.HBM)


def hartley(side):
    index = np.arange(side)
    angles = (np.outer(index, index) % side).astype(np.float32) * np.float32(2.0 * math.pi / side)
    return (np.cos(angles) + np.sin(angles)) / np.float32(math.sqrt(side))


def label_block(values, side):
    row = lax.broadcasted_iota(jnp.int32, (LABEL_ROWS, side), 0)
    block = jnp.zeros((LABEL_ROWS, side), jnp.int32)
    for number, value in enumerate(values):
        block = jnp.where(row == number, value, block)
    return block.astype(F32).astype(BF16)


def read_target(block):
    return jnp.max(block[0:1, :128].astype(F32)).astype(jnp.int32)


def read_labels(block):
    labels = block[:, :128].astype(F32)
    code = labels[1:2] + 256.0 * labels[2:3] + 65536.0 * labels[3:4]
    return jnp.max(jnp.where(labels[0:1] > 0, code, -1.0)).astype(jnp.int32)


def home_kernel(
    bin_count, own_bins, place_hbm, bin_hbm, group_hbm, offset_hbm, image_hbm, basis_hbm, *rest
):
    outs, rest = rest[:bin_count], rest[bin_count:]
    spectra, image_ref, basis_ref, place_ref, bin_ref, group_ref, offset_ref, image_sem, sem = rest
    particles, side = image_ref.shape[0], image_ref.shape[1]
    here = lax.axis_index("bin")
    pairs = (
        (basis_hbm, basis_ref),
        (place_hbm, place_ref),
        (bin_hbm, bin_ref),
        (group_hbm, group_ref),
        (offset_hbm, offset_ref),
    )
    copies = [pltpu.make_async_copy(a, b, sem.at[k]) for k, (a, b) in enumerate(pairs)]
    for copy in copies:
        copy.start()

    def image_copy(i):
        return pltpu.make_async_copy(image_hbm.at[i], image_ref.at[i], image_sem.at[i])

    for i in range(particles):
        image_copy(i).start()
    empty = jnp.zeros((LABEL_ROWS, side), BF16)
    for out in outs:
        out[side : side + LABEL_ROWS, :] = empty
    for copy in copies:
        copy.wait()

    @pl.loop(0, particles)
    def _(i):
        image_copy(i).wait()
        moved = pltpu.roll(image_ref[i].astype(F32), side - offset_ref[0, i], 0).astype(BF16)
        columns = pltpu.roll(basis_ref[...].astype(F32), offset_ref[1, i], 0).astype(BF16)
        half = jnp.dot(basis_ref[...], moved, preferred_element_type=F32).astype(BF16)
        spectra[...] = jnp.dot(half, columns, preferred_element_type=F32).astype(BF16)
        place = place_ref[bin_ref[i]]
        owner = place // own_bins
        target = lax.rem(owner, bin_count)
        labels = label_block(
            (1 + owner // bin_count, lax.rem(place, own_bins), group_ref[i], i * bin_count + here),
            side,
        )
        for step in range(bin_count):

            @pl.when((target ^ here) == step)
            def _():
                outs[step][0:side, :] = spectra[...]
                outs[step][side : side + LABEL_ROWS, :] = labels


def home_call(bin_count, own_bins, bin_place, particle_bin, ctf_group, offsets, images):
    particles, side, _ = images.shape
    rows = side + LABEL_ROWS
    return pl.pallas_call(
        functools.partial(home_kernel, bin_count, own_bins),
        out_shape=[jax.ShapeDtypeStruct((rows, side), BF16)] * bin_count,
        in_specs=[HBM] * 6,
        out_specs=[VMEM] * bin_count,
        scratch_shapes=[
            pltpu.VMEM((side, side), BF16),
            pltpu.VMEM(images.shape, BF16),
            pltpu.VMEM((side, side), BF16),
            pltpu.SMEM(bin_place.shape, jnp.int32),
            pltpu.SMEM(particle_bin.shape, jnp.int32),
            pltpu.SMEM(ctf_group.shape, jnp.int32),
            pltpu.SMEM(offsets.shape, jnp.int32),
            pltpu.SemaphoreType.DMA((particles,)),
            pltpu.SemaphoreType.DMA((5,)),
        ],
        compiler_params=pltpu.CompilerParams(vmem_limit_bytes=VMEM_BYTES),
        name="home",
    )(*map(in_hbm, (bin_place, particle_bin, ctf_group, offsets, images, jnp.asarray(hartley(side), BF16))))


def middle_kernel(mic_count, capacity, *rest):
    arrived, outs = rest[: len(rest) - mic_count], rest[len(rest) - mic_count :][::-1]
    rows, side = arrived[0].shape
    here = lax.axis_index("mic")
    empty = jnp.zeros((LABEL_ROWS, side), BF16)
    for out in outs:
        for j in range(capacity):
            out[j, rows - LABEL_ROWS : rows, :] = empty
    targets = [read_target(block[rows - LABEL_ROWS : rows, :]) for block in arrived]
    counts = [jnp.int32(0)] * mic_count
    for block, target in zip(arrived, targets):
        step_of = (target - 1) ^ here
        for step in range(mic_count):
            chosen = (target > 0) & (step_of == step)

            @pl.when(chosen)
            def _(block=block, step=step, slot=counts[step]):
                outs[step][slot] = block[...]

            counts[step] = counts[step] + chosen.astype(jnp.int32)


def owner_kernel(
    bin_count, mic_count, capacity, focus_ref, damping_ref, current_ref, *rest
):
    arrived, (refined_ref, score_ref) = rest[:mic_count][::-1], rest[mic_count : mic_count + 2]
    spectra, ctf, middle, sums, weight, number, active, place, alone, home, particle = rest[
        mic_count + 2 :
    ]
    own_bins, side, _ = current_ref.shape
    slots = mic_count * capacity
    here = lax.axis_index("mic")
    pixels = float(side * side)
    chunks = [slice(c, c + CHUNK) for c in range(0, side, CHUNK)]
    zero = jnp.zeros((8, side), F32)

    row = lax.broadcasted_iota(jnp.int32, (slots, side), 0)
    focus = jnp.zeros((slots, side), F32)
    damping = jnp.zeros((slots, side), F32)
    for s in range(slots):
        step = s // capacity
        code = read_labels(arrived[step][s % capacity, side : side + LABEL_ROWS, :])
        active[s] = (code >= 0).astype(jnp.int32)
        code = jnp.maximum(code, 0)
        group = (code >> 8) & 255
        sender = code >> 16
        place[s] = code & 255
        home[s] = (here ^ step) * bin_count + lax.rem(sender, bin_count)
        particle[s] = sender // bin_count
        focus = jnp.where(row == s, focus_ref[group], focus)
        damping = jnp.where(row == s, damping_ref[group], damping)
    members = [jnp.int32(0)] * own_bins
    for s in range(slots):
        same = jnp.int32(0)
        for t in range(slots):
            same = same + ((active[t] > 0) & (place[t] == place[s])).astype(jnp.int32)
        alone[s] = ((active[s] > 0) & (same == 1)).astype(jnp.int32)
    for p in range(own_bins):
        for s in range(slots):
            members[p] = members[p] + ((active[s] > 0) & (place[s] == p)).astype(jnp.int32)

    frequency = lax.broadcasted_iota(jnp.int32, (slots, side), 1)
    folded = jnp.minimum(frequency, side - frequency).astype(F32) / (side / 2.0)
    square = folded * folded
    envelope = jnp.exp(-damping * square)
    sine = jnp.sin(focus * square) * envelope
    cosine = jnp.cos(focus * square) * envelope
    by_sine = jnp.transpose(CONTRAST * sine - AMPLITUDE * cosine)
    by_cosine = jnp.transpose(-(AMPLITUDE * sine + CONTRAST * cosine))
    sums[...] = jnp.zeros(sums.shape, F32)

    def fold(values):
        return jnp.sum(values.reshape(CHUNK // 8, 8, side), axis=0)

    def keep(k, s, total):
        sums[k, pl.ds(s, 1), :] = jnp.sum(total, axis=0, keepdims=True)

    def correlate():
        cross, model, data = (
            jnp.sum(sums[k], axis=1, keepdims=True) / pixels for k in range(3)
        )
        correlation = cross / jnp.sqrt((model + EPSILON) * (data + EPSILON))
        weights = 1.0 / (1.0 + jnp.exp(-float(side) * correlation))
        weight[...] = jnp.broadcast_to(weights.astype(BF16).astype(F32), (slots, side))
        return correlation

    def shares(s, rows, values):
        table = ctf[s, rows, :]
        scaled = weight[pl.ds(s, 1), :] * table
        return (scaled * values).astype(BF16).astype(F32), scaled * table, table

    def renew(previous, numerator, denominator):
        return (
            (numerator + PRIOR_WEIGHT * previous.astype(F32)) / (denominator + PRIOR_WEIGHT)
        ).astype(BF16)

    def update_shared(source, target):
        for p in range(own_bins):

            @pl.when(members[p] > 1)
            def _(p=p):
                number[...] = jnp.zeros(number.shape, F32)

                @pl.loop(0, slots)
                def _(s):
                    @pl.when((active[s] > 0) & (place[s] == p))
                    def _():
                        for rows in chunks:
                            term, power, _ = shares(s, rows, spectra[s, rows, :].astype(F32))
                            number[0, rows, :] += term
                            number[1, rows, :] += power

                for rows in chunks:
                    target[p, rows, :] = renew(
                        source[p, rows, :], number[0, rows, :], number[1, rows, :]
                    )

    for s in range(slots):

        @pl.when(active[s] > 0)
        def _(s=s):
            cross, model, data = zero, zero, zero
            p = place[s]
            for rows in chunks:
                table = (
                    by_sine[rows, s : s + 1] * sine[s : s + 1, :]
                    + by_cosine[rows, s : s + 1] * cosine[s : s + 1, :]
                )
                held = arrived[s // capacity][s % capacity, rows, :]
                spectra[s, rows, :] = held
                ctf[s, rows, :] = table
                values = held.astype(F32)
                predicted = table * current_ref[p, rows, :].astype(F32)
                cross = cross + fold(predicted * values)
                model = model + fold(predicted * predicted)
                data = data + fold(values * values)
            keep(0, s, cross)
            keep(1, s, model)
            keep(2, s, data)

    correlate()
    update_shared(current_ref, middle)

    @pl.loop(0, slots)
    def _(s):
        p = place[s]

        def compare(rows, values, table, reference, cross, model):
            predicted = table * reference.astype(F32)
            return cross + fold(predicted * values), model + fold(predicted * predicted)

        @pl.when(alone[s] > 0)
        def _():
            cross, model = zero, zero
            for rows in chunks:
                values = spectra[s, rows, :].astype(F32)
                term, power, table = shares(s, rows, values)
                reference = renew(current_ref[p, rows, :], term, power)
                middle[p, rows, :] = reference
                cross, model = compare(rows, values, table, reference, cross, model)
            keep(0, s, cross)
            keep(1, s, model)

        @pl.when((active[s] > 0) & (alone[s] == 0))
        def _():
            cross, model = zero, zero
            for rows in chunks:
                values = spectra[s, rows, :].astype(F32)
                cross, model = compare(
                    rows, values, ctf[s, rows, :], middle[p, rows, :], cross, model
                )
            keep(0, s, cross)
            keep(1, s, model)

    correlation = correlate()
    update_shared(middle, refined_ref)

    @pl.loop(0, slots)
    def _(s):
        @pl.when(alone[s] > 0)
        def _():
            p = place[s]
            for rows in chunks:
                term, power, _ = shares(s, rows, spectra[s, rows, :].astype(F32))
                refined_ref[p, rows, :] = renew(middle[p, rows, :], term, power)

    for p in range(own_bins):

        @pl.when(members[p] == 0)
        def _(p=p):
            refined_ref[p] = current_ref[p]

    devices = score_ref.shape[0]
    device = lax.broadcasted_iota(jnp.int32, (devices, 1, 128), 0)
    lane = lax.broadcasted_iota(jnp.int32, (devices, 1, 128), 2)
    board = jnp.zeros((devices, 1, 128), F32)
    for s in range(slots):
        hit = (active[s] > 0) & (device == home[s]) & (lane == particle[s])
        board = jnp.where(hit, correlation[s : s + 1, :].reshape(1, 1, 1), board)
    score_ref[...] = board


def owner_call(bin_count, mic_count, capacity, defocus, bfactor, references, arrived):
    own_bins, side, _ = references.shape
    slots = mic_count * capacity
    return pl.pallas_call(
        functools.partial(owner_kernel, bin_count, mic_count, capacity),
        out_shape=[
            jax.ShapeDtypeStruct(references.shape, BF16),
            jax.ShapeDtypeStruct((mic_count * bin_count, 1, 128), F32),
        ],
        in_specs=[SMEM] * 2 + [VMEM] * (1 + mic_count),
        out_specs=[VMEM] * 2,
        scratch_shapes=[
            pltpu.VMEM((slots, side, side), BF16),
            pltpu.VMEM((slots, side, side), F32),
            pltpu.VMEM((own_bins, side, side), BF16),
            pltpu.VMEM((3, slots, side), F32),
            pltpu.VMEM((slots, side), F32),
            pltpu.VMEM((2, side, side), F32),
        ]
        + [pltpu.SMEM((slots,), jnp.int32)] * 5,
        compiler_params=pltpu.CompilerParams(vmem_limit_bytes=VMEM_BYTES),
        name="owner",
    )(defocus, bfactor, references, *arrived[::-1])


def exchange(blocks, axis):
    size = lax.axis_size(axis)
    return [blocks[0]] + [
        lax.ppermute(blocks[k], axis, [(i, i ^ k) for i in range(size)]) for k in range(1, size)
    ]


def body(images, offsets, ctf_group, particle_bin, bin_place, defocus, bfactor, references):
    mic_count = lax.axis_size("mic")
    bin_count = lax.axis_size("bin")
    particles, side, _ = images.shape
    own_bins = references.shape[0]
    capacity = (3 * particles + 2 * mic_count - 1) // (2 * mic_count)
    rows = side + LABEL_ROWS
    params = pltpu.CompilerParams(vmem_limit_bytes=VMEM_BYTES)

    sent = home_call(
        bin_count, own_bins, bin_place, particle_bin, ctf_group, offsets, images
    )
    arrived = exchange(sent, "bin")

    sent = pl.pallas_call(
        functools.partial(middle_kernel, mic_count, capacity),
        out_shape=[jax.ShapeDtypeStruct((capacity, rows, side), BF16)] * mic_count,
        in_specs=[VMEM] * bin_count,
        out_specs=[VMEM] * mic_count,
        compiler_params=params,
        name="middle",
    )(*arrived[::-1])
    arrived = exchange(sent[::-1], "mic")

    refined, board = owner_call(
        bin_count, mic_count, capacity, defocus, bfactor, references, arrived
    )
    back = lax.all_to_all(board, ("mic", "bin"), split_axis=0, concat_axis=0, tiled=True)
    return (refined, jnp.sum(back, axis=(0, 1))[:particles])


def solution(mesh):
    in_specs = (
        P(("mic", "bin"), None, None),
        P(None, ("mic", "bin")),
        P(("mic", "bin")),
        P(("mic", "bin")),
        P(),
        P(),
        P(),
        P(("mic", "bin"), None, None),
    )
    out_specs = (P(("mic", "bin"), None, None), P(("mic", "bin")))
    return jax.shard_map(body, mesh=mesh, in_specs=in_specs, out_specs=out_specs, check_vma=False)
```

time: 68.9 us -> 66.1 us (0.959); the launches traced: 69.2 us -> 65.6 us
  Pallas kernels: 9.92 us -> 7.4 us
  blocking collectives: 12 us -> 10.9 us
    pallas_call x2, Pallas kernels: 9.53 us -> 7.01 us  [the longest x1 4.07 us: owner_call(): pl.pallas_call(functools.partial(owner_kernel, bin_count, mic_count, capa...]
    all_to_all x1, blocking collectives: 12 us -> 10.9 us  [body(): lax.all_to_all(board, ('mic', 'bin'), split_axis=0, concat_axis=0, tiled=...]
where the time goes in v3:
time: 66.1 us; the launch traced here: 65.6 us
  starting transfers between devices  26 us (39%)
  waiting for transfers between devices  20 us (30%)
  blocking collectives  10.9 us (16%)
  Pallas kernels  7.4 us (11%)
  between operations  0.69 us (1%)
    ppermute x10, starting transfers between devices, exchange(): lax.ppermute(blocks[k], axis, [(i, i ^ k) for i in range(size)])  26 us
    ppermute x10, waiting for transfers between devices, exchange(): lax.ppermute(blocks[k], axis, [(i, i ^ k) for i in range(size)])  20 us
    all_to_all x1, blocking collectives, body(): lax.all_to_all(board, ('mic', 'bin'), split_axis=0, concat_axis=0, tiled=...  10.9 us
    pallas_call x1, Pallas kernels, owner_call(): pl.pallas_call(functools.partial(owner_kernel, bin_count, mic_count, capa...  4.07 us
    pallas_call x1, Pallas kernels, home_call(): pl.pallas_call(functools.partial(home_kernel, bin_count, own_bins), out_s...  2.94 us
  transfers between devices with their start and end apart: 10, of which 5 were waited for; matrix products, arithmetic and copies ran while one was open for 0% of the time, Pallas kernels for 0%

profile of v3, /device:TPU:0, one launch (start us, length us, event | category | flops | bytes accessed | tf_op | source)
XLA Modules:
  0.0 65.6 jit_solution(3124042198694990547)
XLA Ops:
  0.6 2.9 %home.1 = (bf16[272,256]{1,0:T(8,128)(2,1)S(1)}, bf16[272,256]{1,0:T(8,128)(2,1)S(1)}, bf16[272,256]{1,0:T(8,128)(2,1)S(1)}, bf16[272,256]{1,0:T(8,128)(2,1)S(1)...) custom-call(s32[256]{0:T(256)} %place_hbm.1, ...), custom_call_target="tpu_custom_call" | custom-call | tf_op jit(solution)/shard_map/home/pallas_call | solution.py:111
  3.6 6.1 %collective-permute-start = (bf16[272,256]{1,0:T(8,128)(2,1)S(1)}, bf16[272,256]{1,0:T(8,128)(2,1)S(1)}, u32[]{:S(2)}, u32[]{:S(2)}) collective-permute-start(bf16[272,256]{1,0:T(8,128)(2,1)S(1)} %get-tuple-element.16), channel_id=1, source_target_pairs={{0,7},{1,6},{2,5},{3,4},{4,3},{5,2},{6,1},{7,0},{8,15},{9,14},{10,... | collective-permute-start | bytes 417800 | tf_op jit(solution)/shard_map/ppermute | solution.py:362
  9.7 0.2 collective-permute-start.1
  9.9 0.7 %collective-permute-start.2 = (bf16[272,256]{1,0:T(8,128)(2,1)S(1)}, bf16[272,256]{1,0:T(8,128)(2,1)S(1)}, u32[]{:S(2)}, u32[]{:S(2)}) collective-permute-start(bf16[272,256]{1,0:T(8,128)(2,1)S(1)} %get-tuple-element.18), channel_id=1, source_target_pairs={{0,5},{1,4},{2,7},{3,6},{4,1},{5,0},{6,3},{7,2},{8,13},{9,12},{10,... | collective-permute-start | bytes 417800 | tf_op jit(solution)/shard_map/ppermute | solution.py:362
  10.6 2.0 %collective-permute-start.3 = (bf16[272,256]{1,0:T(8,128)(2,1)S(1)}, bf16[272,256]{1,0:T(8,128)(2,1)S(1)}, u32[]{:S(2)}, u32[]{:S(2)}) collective-permute-start(bf16[272,256]{1,0:T(8,128)(2,1)S(1)} %get-tuple-element.19), channel_id=1, source_target_pairs={{0,4},{1,5},{2,6},{3,7},{4,0},{5,1},{6,2},{7,3},{8,12},{9,13},{10,... | collective-permute-start | bytes 417800 | tf_op jit(solution)/shard_map/ppermute | solution.py:362
  12.7 2.3 %collective-permute-start.4 = (bf16[272,256]{1,0:T(8,128)(2,1)S(1)}, bf16[272,256]{1,0:T(8,128)(2,1)S(1)}, u32[]{:S(2)}, u32[]{:S(2)}) collective-permute-start(bf16[272,256]{1,0:T(8,128)(2,1)S(1)} %get-tuple-element.20), channel_id=1, source_target_pairs={{0,3},{1,2},{2,1},{3,0},{4,7},{5,6},{6,5},{7,4},{8,11},{9,10},{10,... | collective-permute-start | bytes 417800 | tf_op jit(solution)/shard_map/ppermute | solution.py:362
  15.0 0.0 collective-permute-done.rest_0_
  15.0 11.4 %collective-permute-start.5 = (bf16[272,256]{1,0:T(8,128)(2,1)S(1)}, bf16[272,256]{1,0:T(8,128)(2,1)S(1)}, u32[]{:S(2)}, u32[]{:S(2)}) collective-permute-start(bf16[272,256]{1,0:T(8,128)(2,1)S(1)} %get-tuple-element.21), channel_id=1, source_target_pairs={{0,2},{1,3},{2,0},{3,1},{4,6},{5,7},{6,4},{7,5},{8,10},{9,11},{10,... | collective-permute-start | bytes 417800 | tf_op jit(solution)/shard_map/ppermute | solution.py:362
  26.3 0.0 collective-permute-done.1.rest_1_
  26.3 1.3 %collective-permute-start.6 = (bf16[272,256]{1,0:T(8,128)(2,1)S(1)}, bf16[272,256]{1,0:T(8,128)(2,1)S(1)}, u32[]{:S(2)}, u32[]{:S(2)}) collective-permute-start(bf16[272,256]{1,0:T(8,128)(2,1)S(1)} %get-tuple-element.22), channel_id=1, source_target_pairs={{0,1},{1,0},{2,3},{3,2},{4,5},{5,4},{6,7},{7,6},{8,9},{9,8},{10,11... | collective-permute-start | bytes 417800 | tf_op jit(solution)/shard_map/ppermute | solution.py:362
  27.7 3.8 %collective-permute-done.2.rest_2_ = bf16[272,256]{1,0:T(8,128)(2,1)S(1)} collective-permute-done((bf16[272,256]{1,0:T(8,128)(2,1)S(1)}, bf16[272,256]{1,0:T(8,128)(2,1)S(1)}, u32[]{:S(2)}, u32[]{:S(2)}) %collective-permute-start.2) | collective-permute-done | bytes 139296 | tf_op jit(solution)/shard_map/ppermute | solution.py:362
  31.4 2.0 %collective-permute-done.3.rest_3_ = bf16[272,256]{1,0:T(8,128)(2,1)S(1)} collective-permute-done((bf16[272,256]{1,0:T(8,128)(2,1)S(1)}, bf16[272,256]{1,0:T(8,128)(2,1)S(1)}, u32[]{:S(2)}, u32[]{:S(2)}) %collective-permute-start.3) | collective-permute-done | bytes 139296 | tf_op jit(solution)/shard_map/ppermute | solution.py:362
  33.5 0.0 collective-permute-done.4.rest_4_
  33.5 1.2 %collective-permute-done.5.rest_5_ = bf16[272,256]{1,0:T(8,128)(2,1)S(1)} collective-permute-done((bf16[272,256]{1,0:T(8,128)(2,1)S(1)}, bf16[272,256]{1,0:T(8,128)(2,1)S(1)}, u32[]{:S(2)}, u32[]{:S(2)}) %collective-permute-start.5) | collective-permute-done | bytes 139296 | tf_op jit(solution)/shard_map/ppermute | solution.py:362
  34.6 0.0 collective-permute-done.6.rest_6_
  34.7 0.4 middle.1
  35.0 0.1 collective-permute-start.7
  35.1 1.6 %collective-permute-start.8 = (bf16[2,272,256]{2,1,0:T(8,128)(2,1)S(1)}, bf16[2,272,256]{2,1,0:T(8,128)(2,1)S(1)}, u32[]{:S(2)}, u32[]{:S(2)}) collective-permute-start(bf16[2,272,256]{2,1,0:T(8,128)(2,1)S(1)} %get-tuple-element.25), channel_id=1, source_target_pairs={{0,16},{8,24},{16,0},{24,8},{1,17},{9,25},{17,1},{25,9},{2,18},{10... | collective-permute-start | bytes 835592 | tf_op jit(solution)/shard_map/ppermute | solution.py:362
  36.7 0.3 collective-permute-start.9
  37.0 7.0 %collective-permute-done.7.rest_0_ = bf16[2,272,256]{2,1,0:T(8,128)(2,1)S(1)} collective-permute-done((bf16[2,272,256]{2,1,0:T(8,128)(2,1)S(1)}, bf16[2,272,256]{2,1,0:T(8,128)(2,1)S(1)}, u32[]{:S(2)}, u32[]{:S(2)}) %collective-permute-start.7) | collective-permute-done | bytes 278560 | tf_op jit(solution)/shard_map/ppermute | solution.py:362
  44.0 6.0 %collective-permute-done.8.rest_1_ = bf16[2,272,256]{2,1,0:T(8,128)(2,1)S(1)} collective-permute-done((bf16[2,272,256]{2,1,0:T(8,128)(2,1)S(1)}, bf16[2,272,256]{2,1,0:T(8,128)(2,1)S(1)}, u32[]{:S(2)}, u32[]{:S(2)}) %collective-permute-start.8) | collective-permute-done | bytes 278560 | tf_op jit(solution)/shard_map/ppermute | solution.py:362
  50.1 4.1 %owner.1 = (bf16[8,256,256]{2,1,0:T(8,128)(2,1)}, f32[32,1,128]{2,1,0:T(1,128)S(1)}) custom-call(f32[64]{0:T(128)S(1)} %copy-done.1, f32[64]{0:T(128)S(1)} %copy-done.2, bf16[8,256,256]{2,1,0:T(8,128)(2,1)S(1)} %copy-done, bf16[2,272,256]{2,1,0:T(8,128)(2,1)S(1)} %collective-permute-done.7.rest_0_, bf16[2,272,256]{2,1,0:T(8,128)(2,1)S(1)} %collective-permute-done.8.rest_1_, ...), custom_call_target="tpu_custom_call" | custom-call | tf_op jit(solution)/shard_map/owner/pallas_call | solution.py:337
  54.1 10.9 %all_to_all.5 = f32[32,1,128]{2,1,0:T(1,128)S(1)} all-to-all(f32[32,1,128]{2,1,0:T(1,128)S(1)} %get-tuple-element.29), channel_id=1, replica_groups=mesh['mic'=4,'bin'=8] {'mic','bin'}, dimensions={0} | all-to-all | bytes 32768 | tf_op jit(solution)/shard_map/all_to_all | solution.py:393
  65.0 0.6 reduce_sum.9
  (7 shorter events, 0.0 us)
Async XLA Ops:
  0.6 49.4 %copy-start = (bf16[8,256,256]{2,1,0:T(8,128)(2,1)S(1)}, bf16[8,256,256]{2,1,0:T(8,128)(2,1)}, u32[]{:S(2)}) copy-start(bf16[8,256,256]{2,1,0:T(8,128)(2,1)} %current_ref.1) | copy-start | bytes 3145732
  3.6 11.4 %collective-permute-start = (bf16[272,256]{1,0:T(8,128)(2,1)S(1)}, bf16[272,256]{1,0:T(8,128)(2,1)S(1)}, u32[]{:S(2)}, u32[]{:S(2)}) collective-permute-start(bf16[272,256]{1,0:T(8,128)(2,1)S(1)} %get-tuple-element.16), channel_id=1, source_target_pairs={{0,7},{1,6},{2,5},{3,4},{4,3},{5,2},{6,1},{7,0},{8,15},{9,14},{10,... | collective-permute-start | bytes 417800 | tf_op jit(solution)/shard_map/ppermute | solution.py:362
  9.7 16.7 %collective-permute-start.1 = (bf16[272,256]{1,0:T(8,128)(2,1)S(1)}, bf16[272,256]{1,0:T(8,128)(2,1)S(1)}, u32[]{:S(2)}, u32[]{:S(2)}) collective-permute-start(bf16[272,256]{1,0:T(8,128)(2,1)S(1)} %get-tuple-element.17), channel_id=1, source_target_pairs={{0,6},{1,7},{2,4},{3,5},{4,2},{5,3},{6,0},{7,1},{8,14},{9,15},{10,... | collective-permute-start | bytes 417800 | tf_op jit(solution)/shard_map/ppermute | solution.py:362
  9.9 21.6 %collective-permute-start.2 = (bf16[272,256]{1,0:T(8,128)(2,1)S(1)}, bf16[272,256]{1,0:T(8,128)(2,1)S(1)}, u32[]{:S(2)}, u32[]{:S(2)}) collective-permute-start(bf16[272,256]{1,0:T(8,128)(2,1)S(1)} %get-tuple-element.18), channel_id=1, source_target_pairs={{0,5},{1,4},{2,7},{3,6},{4,1},{5,0},{6,3},{7,2},{8,13},{9,12},{10,... | collective-permute-start | bytes 417800 | tf_op jit(solution)/shard_map/ppermute | solution.py:362
  10.6 22.8 %collective-permute-start.3 = (bf16[272,256]{1,0:T(8,128)(2,1)S(1)}, bf16[272,256]{1,0:T(8,128)(2,1)S(1)}, u32[]{:S(2)}, u32[]{:S(2)}) collective-permute-start(bf16[272,256]{1,0:T(8,128)(2,1)S(1)} %get-tuple-element.19), channel_id=1, source_target_pairs={{0,4},{1,5},{2,6},{3,7},{4,0},{5,1},{6,2},{7,3},{8,12},{9,13},{10,... | collective-permute-start | bytes 417800 | tf_op jit(solution)/shard_map/ppermute | solution.py:362
  12.7 20.8 %collective-permute-start.4 = (bf16[272,256]{1,0:T(8,128)(2,1)S(1)}, bf16[272,256]{1,0:T(8,128)(2,1)S(1)}, u32[]{:S(2)}, u32[]{:S(2)}) collective-permute-start(bf16[272,256]{1,0:T(8,128)(2,1)S(1)} %get-tuple-element.20), channel_id=1, source_target_pairs={{0,3},{1,2},{2,1},{3,0},{4,7},{5,6},{6,5},{7,4},{8,11},{9,10},{10,... | collective-permute-start | bytes 417800 | tf_op jit(solution)/shard_map/ppermute | solution.py:362
  15.0 19.7 %collective-permute-start.5 = (bf16[272,256]{1,0:T(8,128)(2,1)S(1)}, bf16[272,256]{1,0:T(8,128)(2,1)S(1)}, u32[]{:S(2)}, u32[]{:S(2)}) collective-permute-start(bf16[272,256]{1,0:T(8,128)(2,1)S(1)} %get-tuple-element.21), channel_id=1, source_target_pairs={{0,2},{1,3},{2,0},{3,1},{4,6},{5,7},{6,4},{7,5},{8,10},{9,11},{10,... | collective-permute-start | bytes 417800 | tf_op jit(solution)/shard_map/ppermute | solution.py:362
  26.3 8.3 %collective-permute-start.6 = (bf16[272,256]{1,0:T(8,128)(2,1)S(1)}, bf16[272,256]{1,0:T(8,128)(2,1)S(1)}, u32[]{:S(2)}, u32[]{:S(2)}) collective-permute-start(bf16[272,256]{1,0:T(8,128)(2,1)S(1)} %get-tuple-element.22), channel_id=1, source_target_pairs={{0,1},{1,0},{2,3},{3,2},{4,5},{5,4},{6,7},{7,6},{8,9},{9,8},{10,11... | collective-permute-start | bytes 417800 | tf_op jit(solution)/shard_map/ppermute | solution.py:362
  35.0 9.0 %collective-permute-start.7 = (bf16[2,272,256]{2,1,0:T(8,128)(2,1)S(1)}, bf16[2,272,256]{2,1,0:T(8,128)(2,1)S(1)}, u32[]{:S(2)}, u32[]{:S(2)}) collective-permute-start(bf16[2,272,256]{2,1,0:T(8,128)(2,1)S(1)} %get-tuple-element.24), channel_id=1, source_target_pairs={{0,24},{8,16},{16,8},{24,0},{1,25},{9,17},{17,9},{25,1},{2,26},{10... | collective-permute-start | bytes 835592 | tf_op jit(solution)/shard_map/ppermute | solution.py:362
  35.1 14.9 %collective-permute-start.8 = (bf16[2,272,256]{2,1,0:T(8,128)(2,1)S(1)}, bf16[2,272,256]{2,1,0:T(8,128)(2,1)S(1)}, u32[]{:S(2)}, u32[]{:S(2)}) collective-permute-start(bf16[2,272,256]{2,1,0:T(8,128)(2,1)S(1)} %get-tuple-element.25), channel_id=1, source_target_pairs={{0,16},{8,24},{16,0},{24,8},{1,17},{9,25},{17,1},{25,9},{2,18},{10... | collective-permute-start | bytes 835592 | tf_op jit(solution)/shard_map/ppermute | solution.py:362
  36.7 13.3 %copy-start.1 = (f32[64]{0:T(128)S(1)}, f32[64]{0:T(128)}, u32[]{:S(2)}) copy-start(f32[64]{0:T(128)} %focus_ref.1) | copy-start | bytes 772
  36.7 13.4 %copy-start.2 = (f32[64]{0:T(128)S(1)}, f32[64]{0:T(128)}, u32[]{:S(2)}) copy-start(f32[64]{0:T(128)} %damping_ref.1) | copy-start | bytes 772
  36.7 13.3 %collective-permute-start.9 = (bf16[2,272,256]{2,1,0:T(8,128)(2,1)S(1)}, bf16[2,272,256]{2,1,0:T(8,128)(2,1)S(1)}, u32[]{:S(2)}, u32[]{:S(2)}) collective-permute-start(bf16[2,272,256]{2,1,0:T(8,128)(2,1)S(1)} %get-tuple-element.26), channel_id=1, source_target_pairs={{0,8},{8,0},{16,24},{24,16},{1,9},{9,1},{17,25},{25,17},{2,10},{10... | collective-permute-start | bytes 835592 | tf_op jit(solution)/shard_map/ppermute | solution.py:362

commit v4 on v3

v4 whole, which is shorter than its diff:
```python
import functools
import math

import jax
import jax.numpy as jnp
import numpy as np
from jax import lax
from jax.experimental import pallas as pl
from jax.experimental.pallas import tpu as pltpu
from jax.sharding import PartitionSpec as P

ITERS = 2
PRIOR_WEIGHT = 0.5
EPSILON = 1e-06
CONTRAST = 0.1
AMPLITUDE = math.sqrt(1.0 - CONTRAST * CONTRAST)

LABEL_ROWS = 8
CHUNK = 32
VMEM_BYTES = 24 * 1024 * 1024

ACTIVE, PLACE, ALONE, HOME, PARTICLE, MEMBERS = range(6)
INFOS = 6

F32 = jnp.float32
BF16 = jnp.bfloat16
VMEM = pl.BlockSpec(memory_space=pltpu.VMEM)
SMEM = pl.BlockSpec(memory_space=pltpu.SMEM)
HBM = pl.BlockSpec(memory_space=pltpu.HBM)
ANY = pl.BlockSpec(memory_space=pl.ANY)


def in_hbm(x):
    return pltpu.with_memory_space_constraint(x, pltpu.HBM)


def hartley(side):
    index = np.arange(side)
    angles = (np.outer(index, index) % side).astype(np.float32) * np.float32(2.0 * math.pi / side)
    return (np.cos(angles) + np.sin(angles)) / np.float32(math.sqrt(side))


def label_block(values, side):
    row = lax.broadcasted_iota(jnp.int32, (LABEL_ROWS, side), 0)
    block = jnp.zeros((LABEL_ROWS, side), jnp.int32)
    for number, value in enumerate(values):
        block = jnp.where(row == number, value, block)
    return block.astype(F32).astype(BF16)


def home_kernel(
    bin_count, own_bins, first, count, place_hbm, bin_hbm, group_hbm, offset_hbm, image_hbm, basis_hbm, *rest
):
    rest = rest[len(rest) - count - 9 :]
    outs, rest = rest[:count], rest[count:]
    spectra, image_ref, basis_ref, place_ref, bin_ref, group_ref, offset_ref, image_sem, sem = rest
    particles, side = image_ref.shape[0], image_ref.shape[1]
    here = lax.axis_index("bin")
    pairs = (
        (basis_hbm, basis_ref),
        (place_hbm, place_ref),
        (bin_hbm, bin_ref),
        (group_hbm, group_ref),
        (offset_hbm, offset_ref),
    )
    copies = [pltpu.make_async_copy(a, b, sem.at[k]) for k, (a, b) in enumerate(pairs)]
    for copy in copies:
        copy.start()

    def image_copy(i):
        return pltpu.make_async_copy(image_hbm.at[i], image_ref.at[i], image_sem.at[i])

    for i in range(particles):
        image_copy(i).start()
    empty = jnp.zeros((LABEL_ROWS, side), BF16)
    for out in outs:
        out[side : side + LABEL_ROWS, :] = empty
    for copy in copies:
        copy.wait()

    @pl.loop(0, particles)
    def _(i):
        image_copy(i).wait()
        place = place_ref[bin_ref[i]]
        owner = place // own_bins
        step_of = lax.rem(owner, bin_count) ^ here

        @pl.when((step_of >= first) & (step_of < first + count))
        def _():
            moved = pltpu.roll(image_ref[i].astype(F32), side - offset_ref[0, i], 0).astype(BF16)
            columns = pltpu.roll(basis_ref[...].astype(F32), offset_ref[1, i], 0).astype(BF16)
            half = jnp.dot(basis_ref[...], moved, preferred_element_type=F32).astype(BF16)
            spectra[...] = jnp.dot(half, columns, preferred_element_type=F32).astype(BF16)
            labels = label_block(
                (
                    1 + owner // bin_count,
                    lax.rem(place, own_bins),
                    group_ref[i],
                    i * bin_count + here,
                ),
                side,
            )
            for k in range(count):

                @pl.when(step_of == first + k)
                def _():
                    outs[k][0:side, :] = spectra[...]
                    outs[k][side : side + LABEL_ROWS, :] = labels


def home_call(bin_count, own_bins, first, count, operands, after=()):
    images, particles, side = operands[4], operands[4].shape[0], operands[4].shape[1]
    return pl.pallas_call(
        functools.partial(home_kernel, bin_count, own_bins, first, count),
        out_shape=[jax.ShapeDtypeStruct((side + LABEL_ROWS, side), BF16)] * count,
        in_specs=[HBM] * 6 + [ANY] * len(after),
        out_specs=[VMEM] * count,
        scratch_shapes=[
            pltpu.VMEM((side, side), BF16),
            pltpu.VMEM(images.shape, BF16),
            pltpu.VMEM((side, side), BF16),
        ]
        + [pltpu.SMEM(x.shape, jnp.int32) for x in operands[:4]]
        + [pltpu.SemaphoreType.DMA((particles,)), pltpu.SemaphoreType.DMA((5,))],
        compiler_params=pltpu.CompilerParams(vmem_limit_bytes=VMEM_BYTES),
        name="home",
    )(*operands, *after)


def middle_kernel(mic_count, capacity, *rest):
    arrived, outs = rest[: len(rest) - 2 * mic_count], rest[len(rest) - 2 * mic_count :]
    outs, label_outs = outs[:mic_count], outs[mic_count:]
    side = arrived[0].shape[1]
    here = lax.axis_index("mic")
    for out in label_outs:
        out[...] = jnp.zeros(out.shape, F32)
    labels = [block[side : side + LABEL_ROWS, :128].astype(F32) for block in arrived]
    targets = [jnp.max(block[0:1]).astype(jnp.int32) for block in labels]
    counts = [jnp.int32(0)] * mic_count
    for block, label, target in zip(arrived, labels, targets):
        step_of = (target - 1) ^ here
        for step in range(mic_count):
            chosen = (target > 0) & (step_of == step)

            @pl.when(chosen)
            def _(block=block, label=label, step=step, slot=counts[step]):
                outs[step][slot] = block[0:side, :]
                label_outs[step][slot] = label

            counts[step] = counts[step] + chosen.astype(jnp.int32)


def middle_call(mic_count, capacity, arrived):
    side = arrived[0].shape[1]
    outs = pl.pallas_call(
        functools.partial(middle_kernel, mic_count, capacity),
        out_shape=[jax.ShapeDtypeStruct((capacity, side, side), BF16)] * mic_count
        + [jax.ShapeDtypeStruct((capacity, LABEL_ROWS, 128), F32)] * mic_count,
        in_specs=[VMEM] * len(arrived),
        out_specs=[VMEM] * (2 * mic_count),
        compiler_params=pltpu.CompilerParams(vmem_limit_bytes=VMEM_BYTES),
        name="middle",
    )(*arrived)
    return outs[:mic_count], outs[mic_count:]


def fold(values):
    return jnp.sum(values.reshape(values.shape[0] // 8, 8, values.shape[1]), axis=0)


def chunks_of(side):
    return [slice(c, c + CHUNK) for c in range(0, side, CHUNK)]


def shares(ctf, weight, s, rows, values):
    table = ctf[s, rows, :]
    scaled = weight[pl.ds(s, 1), :] * table
    return (scaled * values).astype(BF16).astype(F32), scaled * table, table


def renew(previous, numerator, denominator):
    return (
        (numerator + PRIOR_WEIGHT * previous.astype(F32)) / (denominator + PRIOR_WEIGHT)
    ).astype(BF16)


def update_shared(info, spectra, ctf, weight, number, source, target):
    chunks = chunks_of(source.shape[1])

    @pl.loop(0, source.shape[0])
    def _(p):
        @pl.when(info[MEMBERS, p] > 1)
        def _():
            number[...] = jnp.zeros(number.shape, F32)

            @pl.loop(0, spectra.shape[0])
            def _(s):
                @pl.when((info[ACTIVE, s] > 0) & (info[PLACE, s] == p))
                def _():
                    for rows in chunks:
                        values = spectra[s, rows, :].astype(F32)
                        term, power, _ = shares(ctf, weight, s, rows, values)
                        number[0, rows, :] += term
                        number[1, rows, :] += power

            for rows in chunks:
                target[p, rows, :] = renew(
                    source[p, rows, :], number[0, rows, :], number[1, rows, :]
                )


def ready_kernel(
    bin_count, mic_count, capacity, focus_ref, damping_ref, current_ref, *rest
):
    labels, near = rest[:mic_count], rest[mic_count:-3]
    info, ctf, sums = rest[-3:]
    own_bins, side, _ = current_ref.shape
    slots = mic_count * capacity
    here = lax.axis_index("mic")
    zero = jnp.zeros((8, side), F32)

    codes = []
    for s in range(slots):
        block = labels[s // capacity][s % capacity]
        code = block[1:2] + 256.0 * block[2:3] + 65536.0 * block[3:4]
        codes.append(jnp.max(jnp.where(block[0:1] > 0, code, -1.0)).astype(jnp.int32))
    row = lax.broadcasted_iota(jnp.int32, (slots, side), 0)
    focus = jnp.zeros((slots, side), F32)
    damping = jnp.zeros((slots, side), F32)
    for p in range(own_bins):
        info[MEMBERS, p] = jnp.int32(0)
    for s in range(slots):
        active = (codes[s] >= 0).astype(jnp.int32)
        code = jnp.maximum(codes[s], 0)
        group = (code >> 8) & 255
        sender = code >> 16
        place = code & 255
        info[ACTIVE, s] = active
        info[PLACE, s] = place
        info[HOME, s] = (here ^ (s // capacity)) * bin_count + lax.rem(sender, bin_count)
        info[PARTICLE, s] = sender // bin_count
        info[MEMBERS, place] = info[MEMBERS, place] + active
        focus = jnp.where(row == s, focus_ref[group], focus)
        damping = jnp.where(row == s, damping_ref[group], damping)
    for s in range(slots):
        single = (info[ACTIVE, s] > 0) & (info[MEMBERS, info[PLACE, s]] == 1)
        info[ALONE, s] = single.astype(jnp.int32)

    frequency = lax.broadcasted_iota(jnp.int32, (slots, side), 1)
    folded = jnp.minimum(frequency, side - frequency).astype(F32) / (side / 2.0)
    square = folded * folded
    envelope = jnp.exp(-damping * square)
    sine = jnp.sin(focus * square) * envelope
    cosine = jnp.cos(focus * square) * envelope
    by_sine = jnp.transpose(CONTRAST * sine - AMPLITUDE * cosine)
    by_cosine = jnp.transpose(-(AMPLITUDE * sine + CONTRAST * cosine))
    sums[...] = jnp.zeros(sums.shape, F32)

    for s in range(slots):

        @pl.when(info[ACTIVE, s] > 0)
        def _(s=s):
            cross, model, data = zero, zero, zero
            p = info[PLACE, s]
            for rows in chunks_of(side):
                table = (
                    by_sine[rows, s : s + 1] * sine[s : s + 1, :]
                    + by_cosine[rows, s : s + 1] * cosine[s : s + 1, :]
                )
                ctf[s, rows, :] = table
                predicted = table * current_ref[p, rows, :].astype(F32)
                model = model + fold(predicted * predicted)
                if s < len(near) * capacity:
                    values = near[s // capacity][s % capacity, rows, :].astype(F32)
                    cross = cross + fold(predicted * values)
                    data = data + fold(values * values)
            for k, total in enumerate((cross, model, data)):
                sums[k, s : s + 1, :] = jnp.sum(total, axis=0, keepdims=True)


def ready_call(bin_count, mic_count, capacity, defocus, bfactor, references, labels, near):
    own_bins, side, _ = references.shape
    slots = mic_count * capacity
    return pl.pallas_call(
        functools.partial(ready_kernel, bin_count, mic_count, capacity),
        out_shape=[
            jax.ShapeDtypeStruct((INFOS, max(slots, own_bins)), jnp.int32),
            jax.ShapeDtypeStruct((slots, side, side), F32),
            jax.ShapeDtypeStruct((3, slots, side), F32),
        ],
        in_specs=[SMEM] * 2 + [VMEM] * (1 + len(labels) + len(near)),
        out_specs=[SMEM, VMEM, VMEM],
        compiler_params=pltpu.CompilerParams(vmem_limit_bytes=VMEM_BYTES),
        cost_estimate=pl.CostEstimate(flops=4 << 20, bytes_accessed=4 << 20, transcendentals=0),
        name="ready",
    )(defocus, bfactor, references, *labels, *near)


def owner_kernel(capacity, near, info, current_ref, ctf, known, *rest):
    arrived, (spectra, middle, weight, score_ref, sums, number) = rest[:-6], rest[-6:]
    arrived = arrived[::-1]
    slots, side, _ = ctf.shape
    pixels = float(side * side)
    chunks = chunks_of(side)
    zero = jnp.zeros((8, side), F32)
    sums[...] = known[...]

    def keep(k, s, total):
        sums[k, pl.ds(s, 1), :] = jnp.sum(total, axis=0, keepdims=True)

    def correlate():
        cross, model, data = (
            jnp.sum(sums[k], axis=1, keepdims=True) / pixels for k in range(3)
        )
        correlation = cross / jnp.sqrt((model + EPSILON) * (data + EPSILON))
        weights = 1.0 / (1.0 + jnp.exp(-float(side) * correlation))
        weight[...] = jnp.broadcast_to(weights.astype(BF16).astype(F32), (slots, side))
        return correlation

    for s in range(slots):

        @pl.when(info[ACTIVE, s] > 0)
        def _(s=s):
            block = arrived[s // capacity]
            if s < near * capacity:
                spectra[s] = block[s % capacity]
            else:
                cross, data = zero, zero
                p = info[PLACE, s]
                for rows in chunks:
                    held = block[s % capacity, rows, :]
                    spectra[s, rows, :] = held
                    values = held.astype(F32)
                    predicted = ctf[s, rows, :] * current_ref[p, rows, :].astype(F32)
                    cross = cross + fold(predicted * values)
                    data = data + fold(values * values)
                keep(0, s, cross)
                keep(2, s, data)

    correlate()
    update_shared(info, spectra, ctf, weight, number, current_ref, middle)

    @pl.loop(0, slots)
    def _(s):
        p = info[PLACE, s]

        def compare(values, table, reference, cross, model):
            predicted = table * reference.astype(F32)
            return cross + fold(predicted * values), model + fold(predicted * predicted)

        @pl.when(info[ALONE, s] > 0)
        def _():
            cross, model = zero, zero
            for rows in chunks:
                values = spectra[s, rows, :].astype(F32)
                term, power, table = shares(ctf, weight, s, rows, values)
                reference = renew(current_ref[p, rows, :], term, power)
                middle[p, rows, :] = reference
                cross, model = compare(values, table, reference, cross, model)
            keep(0, s, cross)
            keep(1, s, model)

        @pl.when((info[ACTIVE, s] > 0) & (info[ALONE, s] == 0))
        def _():
            cross, model = zero, zero
            for rows in chunks:
                values = spectra[s, rows, :].astype(F32)
                cross, model = compare(values, ctf[s, rows, :], middle[p, rows, :], cross, model)
            keep(0, s, cross)
            keep(1, s, model)

    correlation = correlate()
    devices = score_ref.shape[0]
    device = lax.broadcasted_iota(jnp.int32, (devices, 1, 128), 0)
    lane = lax.broadcasted_iota(jnp.int32, (devices, 1, 128), 2)
    board = jnp.zeros((devices, 1, 128), F32)
    for s in range(slots):
        hit = (info[ACTIVE, s] > 0) & (device == info[HOME, s]) & (lane == info[PARTICLE, s])
        board = jnp.where(hit, correlation[s : s + 1, :].reshape(1, 1, 1), board)
    score_ref[...] = board


def owner_call(devices, capacity, near, info, references, ctf, known, arrived):
    slots, side, _ = ctf.shape
    return pl.pallas_call(
        functools.partial(owner_kernel, capacity, near),
        out_shape=[
            jax.ShapeDtypeStruct((slots, side, side), BF16),
            jax.ShapeDtypeStruct(references.shape, BF16),
            jax.ShapeDtypeStruct((slots, side), F32),
            jax.ShapeDtypeStruct((devices, 1, 128), F32),
        ],
        in_specs=[SMEM] + [VMEM] * (3 + len(arrived)),
        out_specs=[VMEM] * 4,
        scratch_shapes=[
            pltpu.VMEM((3, slots, side), F32),
            pltpu.VMEM((2, side, side), F32),
        ],
        compiler_params=pltpu.CompilerParams(vmem_limit_bytes=VMEM_BYTES),
        name="owner",
    )(info, references, ctf, known, *arrived[::-1])


def last_kernel(info, current_ref, spectra, ctf, middle, weight, refined_ref, number):
    slots, side, _ = ctf.shape
    update_shared(info, spectra, ctf, weight, number, middle, refined_ref)

    @pl.loop(0, slots)
    def _(s):
        @pl.when(info[ALONE, s] > 0)
        def _():
            p = info[PLACE, s]
            for rows in chunks_of(side):
                values = spectra[s, rows, :].astype(F32)
                term, power, _ = shares(ctf, weight, s, rows, values)
                refined_ref[p, rows, :] = renew(middle[p, rows, :], term, power)

    @pl.loop(0, current_ref.shape[0])
    def _(p):
        @pl.when(info[MEMBERS, p] == 0)
        def _():
            refined_ref[p] = current_ref[p]


def last_call(info, references, spectra, ctf, middle, weight):
    side = ctf.shape[1]
    return pl.pallas_call(
        last_kernel,
        out_shape=jax.ShapeDtypeStruct(references.shape, BF16),
        in_specs=[SMEM] + [VMEM] * 5,
        out_specs=VMEM,
        scratch_shapes=[pltpu.VMEM((2, side, side), F32)],
        compiler_params=pltpu.CompilerParams(vmem_limit_bytes=VMEM_BYTES),
        name="last",
    )(info, references, spectra, ctf, middle, weight)


def exchange(blocks, axis):
    size = lax.axis_size(axis)
    return [blocks[0]] + [
        lax.ppermute(blocks[k], axis, [(i, i ^ k) for i in range(size)]) for k in range(1, size)
    ]


def body(images, offsets, ctf_group, particle_bin, bin_place, defocus, bfactor, references):
    mic_count = lax.axis_size("mic")
    bin_count = lax.axis_size("bin")
    particles, side, _ = images.shape
    own_bins = references.shape[0]
    capacity = (3 * particles + 2 * mic_count - 1) // (2 * mic_count)
    near = 2

    basis = jnp.asarray(hartley(side), BF16)
    operands = (bin_place, particle_bin, ctf_group, offsets, images, basis)
    operands = tuple(map(in_hbm, operands))
    far = max(1, bin_count // 4)
    rest = bin_count - far
    sent_far = home_call(bin_count, own_bins, rest, far, operands)
    sent_near = home_call(bin_count, own_bins, 0, rest, operands, after=(sent_far[-1],))
    arrived = exchange(list(sent_near) + list(sent_far), "bin")

    sent, labels = middle_call(mic_count, capacity, arrived[::-1])
    arrived = exchange(sent, "mic")
    labels = exchange(labels, "mic")

    info, ctf, known = ready_call(
        bin_count, mic_count, capacity, defocus, bfactor, references, labels, arrived[:near]
    )
    spectra, middle, weight, board = owner_call(
        mic_count * bin_count, capacity, near, info, references, ctf, known, arrived
    )
    back = lax.all_to_all(board, ("mic", "bin"), split_axis=0, concat_axis=0, tiled=True)
    refined = last_call(info, references, spectra, ctf, middle, weight)
    return (refined, jnp.sum(back, axis=(0, 1))[:particles])


def solution(mesh):
    in_specs = (
        P(("mic", "bin"), None, None),
        P(None, ("mic", "bin")),
        P(("mic", "bin")),
        P(("mic", "bin")),
        P(),
        P(),
        P(),
        P(("mic", "bin"), None, None),
    )
    out_specs = (P(("mic", "bin"), None, None), P(("mic", "bin")))
    return jax.shard_map(body, mesh=mesh, in_specs=in_specs, out_specs=out_specs, check_vma=False)
```

time: 66.1 us -> 67.2 us (1.017)
  blocking collectives: 10.9 us -> 0 us
  Pallas kernels: 7.4 us -> 12.8 us
  local copies, waits for them, and re-layouts: 0.01 us -> 4.42 us
  starting transfers between devices: 26 us -> 29.9 us
  waiting for transfers between devices: 20 us -> 18.5 us
    all_to_all x1 -> x0, blocking collectives: 10.9 us -> none  [body(): lax.all_to_all(board, ('mic', 'bin'), split_axis=0, concat_axis=0, tiled=...]
    pallas_call x3 -> x6, Pallas kernels: 7.4 us -> 12.8 us  [the longest x2 4.17 us: home_call(): pl.pallas_call(functools.partial(home_kernel, bin_count, own_bins, first,...]
    all_to_all x0 -> x1, starting transfers between devices: none -> 4.68 us  [body(): lax.all_to_all(board, ('mic', 'bin'), split_axis=0, concat_axis=0, tiled=...]
    unnamed x6 -> x14, local copies, waits for them, and re-layouts: 0.01 us -> 4.42 us
    ppermute x10 -> x13, waiting for transfers between devices: 20 us -> 16.4 us  [exchange(): lax.ppermute(blocks[k], axis, [(i, i ^ k) for i in range(size)])]
    all_to_all x0 -> x1, waiting for transfers between devices: none -> 2.01 us  [body(): lax.all_to_all(board, ('mic', 'bin'), split_axis=0, concat_axis=0, tiled=...]
    ppermute x10 -> x13, starting transfers between devices: 26 us -> 25.2 us  [exchange(): lax.ppermute(blocks[k], axis, [(i, i ^ k) for i in range(size)])]
  transfers between devices with their start and end apart: 10 -> 14, of which waited for: 5 -> 5; matrix products, arithmetic and copies ran while one was open for 0% -> 0% of each run, Pallas kernels for 0% -> 12%
where the time goes in v4:
time: 67.2 us; the launch traced here: 66.9 us
  starting transfers between devices  29.9 us (44%)
  waiting for transfers between devices  18.5 us (28%)
  Pallas kernels  12.8 us (19%)
  local copies, waits for them, and re-layouts  4.42 us (7%)
  between operations  0.76 us (1%)
    ppermute x13, starting transfers between devices, exchange(): lax.ppermute(blocks[k], axis, [(i, i ^ k) for i in range(size)])  25.2 us
    ppermute x13, waiting for transfers between devices, exchange(): lax.ppermute(blocks[k], axis, [(i, i ^ k) for i in range(size)])  16.4 us
    all_to_all x1, starting transfers between devices, body(): lax.all_to_all(board, ('mic', 'bin'), split_axis=0, concat_axis=0, tiled=...  4.68 us
    unnamed x14, local copies, waits for them, and re-layouts  4.42 us
    pallas_call x2, Pallas kernels, home_call(): pl.pallas_call(functools.partial(home_kernel, bin_count, own_bins, first,...  4.17 us
    pallas_call x1, Pallas kernels, owner_call(): pl.pallas_call(functools.partial(owner_kernel, capacity, near), out_shape...  3.16 us
    pallas_call x1, Pallas kernels, last_call(): pl.pallas_call(last_kernel, out_shape=jax.ShapeDtypeStruct(references.sha...  2.64 us
    pallas_call x1, Pallas kernels, ready_call(): pl.pallas_call(functools.partial(ready_kernel, bin_count, mic_count, capa...  2.43 us
  transfers between devices with their start and end apart: 14, of which 5 were waited for; matrix products, arithmetic and copies ran while one was open for 0% of the time, Pallas kernels for 12%

profile of v4, /device:TPU:0, one launch (start us, length us, event | category | flops | bytes accessed | tf_op | source)
XLA Modules:
  0.0 66.9 jit_solution(394336953429801279)
XLA Ops:
  0.7 1.3 %home.2 = (bf16[264,256]{1,0:T(8,128)(2,1)S(1)}, bf16[264,256]{1,0:T(8,128)(2,1)S(1)}) custom-call(s32[256]{0:T(256)} %place_hbm.3, s32[4]{0:T(128)} %bin_hbm.3, s32[4]{0:T(128)} %group_hbm.3, s32[2,4]{1,0:T(2,128)} %offset_hbm.3, bf16[4,256,256]{2,1,0:T(8,128)(2,1)} %image_hbm.3, bf16[256,256]{1,0:T(8,128)(2,1)} %constant.4.clone.basis_hbm), custom_call_target="tpu_custom_call" | custom-call | tf_op jit(solution)/shard_map/home/pallas_call | solution.py:113
  2.0 5.5 %collective-permute-start.1 = (bf16[264,256]{1,0:T(8,128)(2,1)S(1)}, bf16[264,256]{1,0:T(8,128)(2,1)S(1)}, u32[]{:S(2)}, u32[]{:S(2)}) collective-permute-start(bf16[264,256]{1,0:T(8,128)(2,1)S(1)} %get-tuple-element.26), channel_id=1, source_target_pairs={{0,6},{1,7},{2,4},{3,5},{4,2},{5,3},{6,0},{7,1},{8,14},{9,15},{10,... | collective-permute-start | bytes 405512 | tf_op jit(solution)/shard_map/ppermute | solution.py:441
  7.5 1.0 %collective-permute-start = (bf16[264,256]{1,0:T(8,128)(2,1)S(1)}, bf16[264,256]{1,0:T(8,128)(2,1)S(1)}, u32[]{:S(2)}, u32[]{:S(2)}) collective-permute-start(bf16[264,256]{1,0:T(8,128)(2,1)S(1)} %get-tuple-element.25.rest_0_), channel_id=1, source_target_pairs={{0,7},{1,6},{2,5},{3,4},{4,3},{5,2},{6,1},{7,0},{8,15},{9,14},{10,... | collective-permute-start | bytes 405512 | tf_op jit(solution)/shard_map/ppermute | solution.py:441
  8.5 2.8 %home.3 = (bf16[264,256]{1,0:T(8,128)(2,1)S(1)}, bf16[264,256]{1,0:T(8,128)(2,1)S(1)}, bf16[264,256]{1,0:T(8,128)(2,1)S(1)}, bf16[264,256]{1,0:T(8,128)(2,1)S(1)...) custom-call(s32[256]{0:T(256)} %place_hbm.3, s32[4]{0:T(128)} %bin_hbm.3, s32[4]{0:T(128)} %group_hbm.3, ...), custom_call_target="tpu_custom_call" | custom-call | tf_op jit(solution)/shard_map/home/pallas_call | solution.py:113
  11.3 0.6 collective-permute-start.2
  11.9 2.4 %collective-permute-start.3 = (bf16[264,256]{1,0:T(8,128)(2,1)S(1)}, bf16[264,256]{1,0:T(8,128)(2,1)S(1)}, u32[]{:S(2)}, u32[]{:S(2)}) collective-permute-start(bf16[264,256]{1,0:T(8,128)(2,1)S(1)} %get-tuple-element.28), channel_id=1, source_target_pairs={{0,4},{1,5},{2,6},{3,7},{4,0},{5,1},{6,2},{7,3},{8,12},{9,13},{10,... | collective-permute-start | bytes 405512 | tf_op jit(solution)/shard_map/ppermute | solution.py:441
  14.3 1.8 %collective-permute-start.4 = (bf16[264,256]{1,0:T(8,128)(2,1)S(1)}, bf16[264,256]{1,0:T(8,128)(2,1)S(1)}, u32[]{:S(2)}, u32[]{:S(2)}) collective-permute-start(bf16[264,256]{1,0:T(8,128)(2,1)S(1)} %get-tuple-element.29), channel_id=1, source_target_pairs={{0,3},{1,2},{2,1},{3,0},{4,7},{5,6},{6,5},{7,4},{8,11},{9,10},{10,... | collective-permute-start | bytes 405512 | tf_op jit(solution)/shard_map/ppermute | solution.py:441
  16.2 7.1 %collective-permute-start.5 = (bf16[264,256]{1,0:T(8,128)(2,1)S(1)}, bf16[264,256]{1,0:T(8,128)(2,1)S(1)}, u32[]{:S(2)}, u32[]{:S(2)}) collective-permute-start(bf16[264,256]{1,0:T(8,128)(2,1)S(1)} %get-tuple-element.30), channel_id=1, source_target_pairs={{0,2},{1,3},{2,0},{3,1},{4,6},{5,7},{6,4},{7,5},{8,10},{9,11},{10,... | collective-permute-start | bytes 405512 | tf_op jit(solution)/shard_map/ppermute | solution.py:441
  23.3 1.6 %collective-permute-start.6 = (bf16[264,256]{1,0:T(8,128)(2,1)S(1)}, bf16[264,256]{1,0:T(8,128)(2,1)S(1)}, u32[]{:S(2)}, u32[]{:S(2)}) collective-permute-start(bf16[264,256]{1,0:T(8,128)(2,1)S(1)} %get-tuple-element.31), channel_id=1, source_target_pairs={{0,1},{1,0},{2,3},{3,2},{4,5},{5,4},{6,7},{7,6},{8,9},{9,8},{10,11... | collective-permute-start | bytes 405512 | tf_op jit(solution)/shard_map/ppermute | solution.py:441
  24.9 5.6 %collective-permute-done.2.rest_2_ = bf16[264,256]{1,0:T(8,128)(2,1)S(1)} collective-permute-done((bf16[264,256]{1,0:T(8,128)(2,1)S(1)}, bf16[264,256]{1,0:T(8,128)(2,1)S(1)}, u32[]{:S(2)}, u32[]{:S(2)}) %collective-permute-start.2) | collective-permute-done | bytes 135200 | tf_op jit(solution)/shard_map/ppermute | solution.py:441
  30.8 0.8 %collective-permute-done.5.rest_5_ = bf16[264,256]{1,0:T(8,128)(2,1)S(1)} collective-permute-done((bf16[264,256]{1,0:T(8,128)(2,1)S(1)}, bf16[264,256]{1,0:T(8,128)(2,1)S(1)}, u32[]{:S(2)}, u32[]{:S(2)}) %collective-permute-start.5) | collective-permute-done | bytes 135200 | tf_op jit(solution)/shard_map/ppermute | solution.py:441
  32.1 2.1 %collective-permute-start.11 = (bf16[2,256,256]{2,1,0:T(8,128)(2,1)S(1)}, bf16[2,256,256]{2,1,0:T(8,128)(2,1)S(1)}, u32[]{:S(2)}, u32[]{:S(2)}) collective-permute-start(bf16[2,256,256]{2,1,0:T(8,128)(2,1)S(1)} %get-tuple-element.42), channel_id=1, source_target_pairs={{0,24},{8,16},{16,8},{24,0},{1,25},{9,17},{17,9},{25,1},{2,26},{10... | collective-permute-start | bytes 786440 | tf_op jit(solution)/shard_map/ppermute | solution.py:441
  34.3 1.9 %collective-permute-start.8 = (f32[2,8,128]{2,1,0:T(8,128)S(1)}, f32[2,8,128]{2,1,0:T(8,128)S(1)}, u32[]{:S(2)}, u32[]{:S(2)}) collective-permute-start(f32[2,8,128]{2,1,0:T(8,128)S(1)} %get-tuple-element.35), channel_id=1, source_target_pairs={{0,16},{8,24},{16,0},{24,8},{1,17},{9,25},{17,1},{25,9},{2,18},{10... | collective-permute-start | bytes 24584 | tf_op jit(solution)/shard_map/ppermute | solution.py:441
  36.2 0.9 %collective-permute-start.9 = (f32[2,8,128]{2,1,0:T(8,128)S(1)}, f32[2,8,128]{2,1,0:T(8,128)S(1)}, u32[]{:S(2)}, u32[]{:S(2)}) collective-permute-start(f32[2,8,128]{2,1,0:T(8,128)S(1)} %get-tuple-element.36), channel_id=1, source_target_pairs={{0,24},{8,16},{16,8},{24,0},{1,25},{9,17},{17,9},{25,1},{2,26},{10... | collective-permute-start | bytes 24584 | tf_op jit(solution)/shard_map/ppermute | solution.py:441
  37.2 9.8 %collective-permute-done.8.rest_2_ = f32[2,8,128]{2,1,0:T(8,128)S(1)} collective-permute-done((f32[2,8,128]{2,1,0:T(8,128)S(1)}, f32[2,8,128]{2,1,0:T(8,128)S(1)}, u32[]{:S(2)}, u32[]{:S(2)}) %collective-permute-start.8) | collective-permute-done | bytes 8224 | tf_op jit(solution)/shard_map/ppermute | solution.py:441
  47.0 2.4 %ready.1 = (s32[6,8]{1,0:T(8,128)S(1)}, f32[8,256,256]{2,1,0:T(8,128)S(1)}, f32[3,8,256]{2,1,0:T(8,128)S(1)}) custom-call(f32[64]{0:T(128)S(1)} %copy-done.5, f32[64]{0:T(128)S(1)} %copy-done.6, bf16[8,256,256]{2,1,0:T(8,128)(2,1)S(1)} %copy-done, f32[2,8,128]{2,1,0:T(8,128)S(1)} %get-tuple-element.33.rest_0_, ...), custom_call_target="tpu_custom_call" | custom-call | flops 4194304 | bytes 4194304 | tf_op jit(solution)/shard_map/ready/pallas_call | solution.py:284
  49.4 3.2 %owner.1 = (bf16[8,256,256]{2,1,0:T(8,128)(2,1)S(1)}, bf16[8,256,256]{2,1,0:T(8,128)(2,1)S(1)}, f32[8,256]{1,0:T(8,128)S(1)}, f32[32,1,128]{2,1,0:T(1,128)}) custom-call(s32[6,8]{1,0:T(8,128)S(1)} %get-tuple-element.39.info, bf16[8,256,256]{2,1,0:T(8,128)(2,1)S(1)} %copy-done, f32[8,256,256]{2,1,0:T(8,128)S(1)} %get-tuple-element.40.ctf, ...), custom_call_target="tpu_custom_call" | custom-call | tf_op jit(solution)/shard_map/owner/pallas_call | solution.py:385
  52.6 1.0 %copy-done.1 = bf16[8,256,256]{2,1,0:T(8,128)(2,1)} copy-done((bf16[8,256,256]{2,1,0:T(8,128)(2,1)}, bf16[8,256,256]{2,1,0:T(8,128)(2,1)S(1)}, u32[]{:S(2)}) %copy-start.1) | copy-done | bytes 1048600
  53.6 1.0 %copy-done.3 = bf16[8,256,256]{2,1,0:T(8,128)(2,1)} copy-done((bf16[8,256,256]{2,1,0:T(8,128)(2,1)}, bf16[8,256,256]{2,1,0:T(8,128)(2,1)S(1)}, u32[]{:S(2)}) %copy-start.3) | copy-done | bytes 1048600
  54.5 4.7 %all-to-all-start = ((f32[32,1,128]{2,1,0:T(1,128)}), f32[32,1,128]{2,1,0:T(1,128)S(1)}, u32[]{:S(2)}, u32[]{:S(2)}) async-start(f32[32,1,128]{2,1,0:T(1,128)} %get-tuple-element.47), calls=%async_computation | async-start | bytes 32768 | tf_op jit(solution)/shard_map/all_to_all | solution.py:472
  59.2 1.2 %copy-done.2 = bf16[8,256,256]{2,1,0:T(8,128)(2,1)S(1)} copy-done((bf16[8,256,256]{2,1,0:T(8,128)(2,1)S(1)}, bf16[8,256,256]{2,1,0:T(8,128)(2,1)}, u32[]{:S(2)}) %copy-start.2) | copy-done | bytes 1048600
  60.5 1.2 %copy-done.4 = bf16[8,256,256]{2,1,0:T(8,128)(2,1)S(1)} copy-done((bf16[8,256,256]{2,1,0:T(8,128)(2,1)S(1)}, bf16[8,256,256]{2,1,0:T(8,128)(2,1)}, u32[]{:S(2)}) %copy-start.4) | copy-done | bytes 1048600
  61.7 2.6 %last.1 = bf16[8,256,256]{2,1,0:T(8,128)(2,1)} custom-call(s32[6,8]{1,0:T(8,128)S(1)} %get-tuple-element.39.info, bf16[8,256,256]{2,1,0:T(8,128)(2,1)S(1)} %copy-done, bf16[8,256,256]{2,1,0:T(8,128)(2,1)S(1)} %copy-done.2, f32[8,256,256]{2,1,0:T(8,128)S(1)} %get-tuple-element.40.ctf, bf16[8,256,256]{2,1,0:T(8,128)(2,1)S(1)} %copy-done.4, ...), custom_call_target="tpu_custom_call" | custom-call | tf_op jit(solution)/shard_map/last/pallas_call | solution.py:427
  64.3 2.0 %all-to-all-done = f32[32,1,128]{2,1,0:T(1,128)S(1)} async-done(((f32[32,1,128]{2,1,0:T(1,128)}), f32[32,1,128]{2,1,0:T(1,128)S(1)}, u32[]{:S(2)}, u32[]{:S(2)}) %all-to-all-start) | async-done | bytes 16416 | tf_op jit(solution)/shard_map/all_to_all | solution.py:472
  (25 shorter events, 1.4 us)
Async XLA Ops:
  0.6 46.3 %copy-start = (bf16[8,256,256]{2,1,0:T(8,128)(2,1)S(1)}, bf16[8,256,256]{2,1,0:T(8,128)(2,1)}, u32[]{:S(2)}) copy-start(bf16[8,256,256]{2,1,0:T(8,128)(2,1)} %current_ref.5) | copy-start | bytes 3145732
  0.6 46.3 %copy-start.6 = (f32[64]{0:T(128)S(1)}, f32[64]{0:T(128)}, u32[]{:S(2)}) copy-start(f32[64]{0:T(128)} %damping_ref.1) | copy-start | bytes 772
  0.7 46.3 %copy-start.5 = (f32[64]{0:T(128)S(1)}, f32[64]{0:T(128)}, u32[]{:S(2)}) copy-start(f32[64]{0:T(128)} %focus_ref.1) | copy-start | bytes 772
  2.0 14.2 %collective-permute-start.1 = (bf16[264,256]{1,0:T(8,128)(2,1)S(1)}, bf16[264,256]{1,0:T(8,128)(2,1)S(1)}, u32[]{:S(2)}, u32[]{:S(2)}) collective-permute-start(bf16[264,256]{1,0:T(8,128)(2,1)S(1)} %get-tuple-element.26), channel_id=1, source_target_pairs={{0,6},{1,7},{2,4},{3,5},{4,2},{5,3},{6,0},{7,1},{8,14},{9,15},{10,... | collective-permute-start | bytes 405512 | tf_op jit(solution)/shard_map/ppermute | solution.py:441
  7.5 15.8 %collective-permute-start = (bf16[264,256]{1,0:T(8,128)(2,1)S(1)}, bf16[264,256]{1,0:T(8,128)(2,1)S(1)}, u32[]{:S(2)}, u32[]{:S(2)}) collective-permute-start(bf16[264,256]{1,0:T(8,128)(2,1)S(1)} %get-tuple-element.25.rest_0_), channel_id=1, source_target_pairs={{0,7},{1,6},{2,5},{3,4},{4,3},{5,2},{6,1},{7,0},{8,15},{9,14},{10,... | collective-permute-start | bytes 405512 | tf_op jit(solution)/shard_map/ppermute | solution.py:441
  11.3 19.3 %collective-permute-start.2 = (bf16[264,256]{1,0:T(8,128)(2,1)S(1)}, bf16[264,256]{1,0:T(8,128)(2,1)S(1)}, u32[]{:S(2)}, u32[]{:S(2)}) collective-permute-start(bf16[264,256]{1,0:T(8,128)(2,1)S(1)} %get-tuple-element.27), channel_id=1, source_target_pairs={{0,5},{1,4},{2,7},{3,6},{4,1},{5,0},{6,3},{7,2},{8,13},{9,12},{10,... | collective-permute-start | bytes 405512 | tf_op jit(solution)/shard_map/ppermute | solution.py:441
  11.9 18.8 %collective-permute-start.3 = (bf16[264,256]{1,0:T(8,128)(2,1)S(1)}, bf16[264,256]{1,0:T(8,128)(2,1)S(1)}, u32[]{:S(2)}, u32[]{:S(2)}) collective-permute-start(bf16[264,256]{1,0:T(8,128)(2,1)S(1)} %get-tuple-element.28), channel_id=1, source_target_pairs={{0,4},{1,5},{2,6},{3,7},{4,0},{5,1},{6,2},{7,3},{8,12},{9,13},{10,... | collective-permute-start | bytes 405512 | tf_op jit(solution)/shard_map/ppermute | solution.py:441
  14.3 16.4 %collective-permute-start.4 = (bf16[264,256]{1,0:T(8,128)(2,1)S(1)}, bf16[264,256]{1,0:T(8,128)(2,1)S(1)}, u32[]{:S(2)}, u32[]{:S(2)}) collective-permute-start(bf16[264,256]{1,0:T(8,128)(2,1)S(1)} %get-tuple-element.29), channel_id=1, source_target_pairs={{0,3},{1,2},{2,1},{3,0},{4,7},{5,6},{6,5},{7,4},{8,11},{9,10},{10,... | collective-permute-start | bytes 405512 | tf_op jit(solution)/shard_map/ppermute | solution.py:441
  16.2 15.4 %collective-permute-start.5 = (bf16[264,256]{1,0:T(8,128)(2,1)S(1)}, bf16[264,256]{1,0:T(8,128)(2,1)S(1)}, u32[]{:S(2)}, u32[]{:S(2)}) collective-permute-start(bf16[264,256]{1,0:T(8,128)(2,1)S(1)} %get-tuple-element.30), channel_id=1, source_target_pairs={{0,2},{1,3},{2,0},{3,1},{4,6},{5,7},{6,4},{7,5},{8,10},{9,11},{10,... | collective-permute-start | bytes 405512 | tf_op jit(solution)/shard_map/ppermute | solution.py:441
  23.3 8.3 %collective-permute-start.6 = (bf16[264,256]{1,0:T(8,128)(2,1)S(1)}, bf16[264,256]{1,0:T(8,128)(2,1)S(1)}, u32[]{:S(2)}, u32[]{:S(2)}) collective-permute-start(bf16[264,256]{1,0:T(8,128)(2,1)S(1)} %get-tuple-element.31), channel_id=1, source_target_pairs={{0,1},{1,0},{2,3},{3,2},{4,5},{5,4},{6,7},{7,6},{8,9},{9,8},{10,11... | collective-permute-start | bytes 405512 | tf_op jit(solution)/shard_map/ppermute | solution.py:441
  32.0 14.9 %collective-permute-start.10 = (bf16[2,256,256]{2,1,0:T(8,128)(2,1)S(1)}, bf16[2,256,256]{2,1,0:T(8,128)(2,1)S(1)}, u32[]{:S(2)}, u32[]{:S(2)}) collective-permute-start(bf16[2,256,256]{2,1,0:T(8,128)(2,1)S(1)} %get-tuple-element.38), channel_id=1, source_target_pairs={{0,8},{8,0},{16,24},{24,16},{1,9},{9,1},{17,25},{25,17},{2,10},{10... | collective-permute-start | bytes 786440 | tf_op jit(solution)/shard_map/ppermute | solution.py:441
  32.1 17.3 %collective-permute-start.11 = (bf16[2,256,256]{2,1,0:T(8,128)(2,1)S(1)}, bf16[2,256,256]{2,1,0:T(8,128)(2,1)S(1)}, u32[]{:S(2)}, u32[]{:S(2)}) collective-permute-start(bf16[2,256,256]{2,1,0:T(8,128)(2,1)S(1)} %get-tuple-element.42), channel_id=1, source_target_pairs={{0,24},{8,16},{16,8},{24,0},{1,25},{9,17},{17,9},{25,1},{2,26},{10... | collective-permute-start | bytes 786440 | tf_op jit(solution)/shard_map/ppermute | solution.py:441
  34.2 15.2 %collective-permute-start.12 = (bf16[2,256,256]{2,1,0:T(8,128)(2,1)S(1)}, bf16[2,256,256]{2,1,0:T(8,128)(2,1)S(1)}, u32[]{:S(2)}, u32[]{:S(2)}) collective-permute-start(bf16[2,256,256]{2,1,0:T(8,128)(2,1)S(1)} %get-tuple-element.43), channel_id=1, source_target_pairs={{0,16},{8,24},{16,0},{24,8},{1,17},{9,25},{17,1},{25,9},{2,18},{10... | collective-permute-start | bytes 786440 | tf_op jit(solution)/shard_map/ppermute | solution.py:441
  34.2 2.0 %collective-permute-start.7 = (f32[2,8,128]{2,1,0:T(8,128)S(1)}, f32[2,8,128]{2,1,0:T(8,128)S(1)}, u32[]{:S(2)}, u32[]{:S(2)}) collective-permute-start(f32[2,8,128]{2,1,0:T(8,128)S(1)} %get-tuple-element.34), channel_id=1, source_target_pairs={{0,8},{8,0},{16,24},{24,16},{1,9},{9,1},{17,25},{25,17},{2,10},{10... | collective-permute-start | bytes 24584 | tf_op jit(solution)/shard_map/ppermute | solution.py:441
  34.3 12.6 %collective-permute-start.8 = (f32[2,8,128]{2,1,0:T(8,128)S(1)}, f32[2,8,128]{2,1,0:T(8,128)S(1)}, u32[]{:S(2)}, u32[]{:S(2)}) collective-permute-start(f32[2,8,128]{2,1,0:T(8,128)S(1)} %get-tuple-element.35), channel_id=1, source_target_pairs={{0,16},{8,24},{16,0},{24,8},{1,17},{9,25},{17,1},{25,9},{2,18},{10... | collective-permute-start | bytes 24584 | tf_op jit(solution)/shard_map/ppermute | solution.py:441
  36.2 10.7 %collective-permute-start.9 = (f32[2,8,128]{2,1,0:T(8,128)S(1)}, f32[2,8,128]{2,1,0:T(8,128)S(1)}, u32[]{:S(2)}, u32[]{:S(2)}) collective-permute-start(f32[2,8,128]{2,1,0:T(8,128)S(1)} %get-tuple-element.36), channel_id=1, source_target_pairs={{0,24},{8,16},{16,8},{24,0},{1,25},{9,17},{17,9},{25,1},{2,26},{10... | collective-permute-start | bytes 24584 | tf_op jit(solution)/shard_map/ppermute | solution.py:441
  52.6 1.0 %copy-start.1 = (bf16[8,256,256]{2,1,0:T(8,128)(2,1)}, bf16[8,256,256]{2,1,0:T(8,128)(2,1)S(1)}, u32[]{:S(2)}) copy-start(bf16[8,256,256]{2,1,0:T(8,128)(2,1)S(1)} %get-tuple-element.44.spectra) | copy-start | bytes 3145732
  53.6 1.0 %copy-start.3 = (bf16[8,256,256]{2,1,0:T(8,128)(2,1)}, bf16[8,256,256]{2,1,0:T(8,128)(2,1)S(1)}, u32[]{:S(2)}) copy-start(bf16[8,256,256]{2,1,0:T(8,128)(2,1)S(1)} %get-tuple-element.45.middle) | copy-start | bytes 3145732
  54.5 11.8 %all-to-all-start = ((f32[32,1,128]{2,1,0:T(1,128)}), f32[32,1,128]{2,1,0:T(1,128)S(1)}, u32[]{:S(2)}, u32[]{:S(2)}) async-start(f32[32,1,128]{2,1,0:T(1,128)} %get-tuple-element.47), calls=%async_computation | async-start | bytes 32768 | tf_op jit(solution)/shard_map/all_to_all | solution.py:472
  59.2 1.2 %copy-start.2 = (bf16[8,256,256]{2,1,0:T(8,128)(2,1)S(1)}, bf16[8,256,256]{2,1,0:T(8,128)(2,1)}, u32[]{:S(2)}) copy-start(bf16[8,256,256]{2,1,0:T(8,128)(2,1)} %copy-done.1) | copy-start | bytes 3145732
  60.5 1.2 %copy-start.4 = (bf16[8,256,256]{2,1,0:T(8,128)(2,1)S(1)}, bf16[8,256,256]{2,1,0:T(8,128)(2,1)}, u32[]{:S(2)}) copy-start(bf16[8,256,256]{2,1,0:T(8,128)(2,1)} %copy-done.3) | copy-start | bytes 3145732

commit v5 on v4

--- a/solution.py
+++ b/solution.py
@@ -128,40 +128,39 @@
 
 
 def middle_kernel(mic_count, capacity, *rest):
-    arrived, outs = rest[: len(rest) - 2 * mic_count], rest[len(rest) - 2 * mic_count :]
-    outs, label_outs = outs[:mic_count], outs[mic_count:]
-    side = arrived[0].shape[1]
+    arrived, outs = rest[: len(rest) - mic_count], rest[len(rest) - mic_count :]
+    rows, side = arrived[0].shape
     here = lax.axis_index("mic")
-    for out in label_outs:
-        out[...] = jnp.zeros(out.shape, F32)
-    labels = [block[side : side + LABEL_ROWS, :128].astype(F32) for block in arrived]
-    targets = [jnp.max(block[0:1]).astype(jnp.int32) for block in labels]
+    empty = jnp.zeros((LABEL_ROWS, side), BF16)
+    for out in outs:
+        for j in range(capacity):
+            out[j, rows - LABEL_ROWS : rows, :] = empty
+    targets = [
+        jnp.max(block[rows - LABEL_ROWS : rows, :128].astype(F32)[0:1]).astype(jnp.int32)
+        for block in arrived
+    ]
     counts = [jnp.int32(0)] * mic_count
-    for block, label, target in zip(arrived, labels, targets):
+    for block, target in zip(arrived, targets):
         step_of = (target - 1) ^ here
         for step in range(mic_count):
             chosen = (target > 0) & (step_of == step)
 
             @pl.when(chosen)
-            def _(block=block, label=label, step=step, slot=counts[step]):
-                outs[step][slot] = block[0:side, :]
-                label_outs[step][slot] = label
+            def _(block=block, step=step, slot=counts[step]):
+                outs[step][slot] = block[...]
 
             counts[step] = counts[step] + chosen.astype(jnp.int32)
 
 
 def middle_call(mic_count, capacity, arrived):
-    side = arrived[0].shape[1]
-    outs = pl.pallas_call(
+    return pl.pallas_call(
         functools.partial(middle_kernel, mic_count, capacity),
-        out_shape=[jax.ShapeDtypeStruct((capacity, side, side), BF16)] * mic_count
-        + [jax.ShapeDtypeStruct((capacity, LABEL_ROWS, 128), F32)] * mic_count,
+        out_shape=[jax.ShapeDtypeStruct((capacity, *arrived[0].shape), BF16)] * mic_count,
         in_specs=[VMEM] * len(arrived),
-        out_specs=[VMEM] * (2 * mic_count),
+        out_specs=[VMEM] * mic_count,
         compiler_params=pltpu.CompilerParams(vmem_limit_bytes=VMEM_BYTES),
         name="middle",
     )(*arrived)
-    return outs[:mic_count], outs[mic_count:]
 
 
 def fold(values):
@@ -209,24 +208,17 @@
                 )
 
 
-def ready_kernel(
-    bin_count, mic_count, capacity, focus_ref, damping_ref, current_ref, *rest
-):
-    labels, near = rest[:mic_count], rest[mic_count:-3]
-    info, ctf, sums = rest[-3:]
-    own_bins, side, _ = current_ref.shape
-    slots = mic_count * capacity
+def decode(labels, capacity, bin_count, own_bins, info, focus_ref, damping_ref):
+    slots = len(labels)
     here = lax.axis_index("mic")
-    zero = jnp.zeros((8, side), F32)
-
     codes = []
     for s in range(slots):
-        block = labels[s // capacity][s % capacity]
+        block = labels[s]
         code = block[1:2] + 256.0 * block[2:3] + 65536.0 * block[3:4]
         codes.append(jnp.max(jnp.where(block[0:1] > 0, code, -1.0)).astype(jnp.int32))
-    row = lax.broadcasted_iota(jnp.int32, (slots, side), 0)
-    focus = jnp.zeros((slots, side), F32)
-    damping = jnp.zeros((slots, side), F32)
+    row = lax.broadcasted_iota(jnp.int32, (8, 128), 0)
+    focus = jnp.zeros((8, 128), F32)
+    damping = jnp.zeros((8, 128), F32)
     for p in range(own_bins):
         info[MEMBERS, p] = jnp.int32(0)
     for s in range(slots):
@@ -245,8 +237,11 @@
     for s in range(slots):
         single = (info[ACTIVE, s] > 0) & (info[MEMBERS, info[PLACE, s]] == 1)
         info[ALONE, s] = single.astype(jnp.int32)
-
-    frequency = lax.broadcasted_iota(jnp.int32, (slots, side), 1)
+    return focus[:, :1], damping[:, :1]
+
+
+def ctf_factors(focus, damping, side):
+    frequency = lax.broadcasted_iota(jnp.int32, (8, side), 1)
     folded = jnp.minimum(frequency, side - frequency).astype(F32) / (side / 2.0)
     square = folded * folded
     envelope = jnp.exp(-damping * square)
@@ -254,56 +249,70 @@
     cosine = jnp.cos(focus * square) * envelope
     by_sine = jnp.transpose(CONTRAST * sine - AMPLITUDE * cosine)
     by_cosine = jnp.transpose(-(AMPLITUDE * sine + CONTRAST * cosine))
-    sums[...] = jnp.zeros(sums.shape, F32)
-
-    for s in range(slots):
-
-        @pl.when(info[ACTIVE, s] > 0)
-        def _(s=s):
-            cross, model, data = zero, zero, zero
-            p = info[PLACE, s]
-            for rows in chunks_of(side):
-                table = (
-                    by_sine[rows, s : s + 1] * sine[s : s + 1, :]
-                    + by_cosine[rows, s : s + 1] * cosine[s : s + 1, :]
-                )
-                ctf[s, rows, :] = table
-                predicted = table * current_ref[p, rows, :].astype(F32)
-                model = model + fold(predicted * predicted)
-                if s < len(near) * capacity:
-                    values = near[s // capacity][s % capacity, rows, :].astype(F32)
-                    cross = cross + fold(predicted * values)
-                    data = data + fold(values * values)
-            for k, total in enumerate((cross, model, data)):
-                sums[k, s : s + 1, :] = jnp.sum(total, axis=0, keepdims=True)
-
-
-def ready_call(bin_count, mic_count, capacity, defocus, bfactor, references, labels, near):
-    own_bins, side, _ = references.shape
+    return by_sine, sine, by_cosine, cosine
+
+
+def ctf_chunk(factors, s, rows):
+    by_sine, sine, by_cosine, cosine = factors
+    return (
+        by_sine[rows, s : s + 1] * sine[s : s + 1, :]
+        + by_cosine[rows, s : s + 1] * cosine[s : s + 1, :]
+    )
+
+
+def first_compare(info, factors, current_ref, spectra, ctf, sums, s, block):
+    side = ctf.shape[1]
+    p = info[PLACE, s]
+    cross = model = data = jnp.zeros((8, side), F32)
+    for rows in chunks_of(side):
+        table = ctf_chunk(factors, s, rows)
+        ctf[s, rows, :] = table
+        held = block[rows, :]
+        spectra[s, rows, :] = held
+        values = held.astype(F32)
+        predicted = table * current_ref[p, rows, :].astype(F32)
+        cross = cross + fold(predicted * values)
+        model = model + fold(predicted * predicted)
+        data = data + fold(values * values)
+    for k, total in enumerate((cross, model, data)):
+        sums[k, s : s + 1, :] = jnp.sum(total, axis=0, keepdims=True)
+
+
+def owner_kernel(
+    bin_count, mic_count, focus_ref, damping_ref, current_ref, *rest
+):
+    arrived, rest = rest[:mic_count][::-1], rest[mic_count:]
+    spectra_hbm, middle_hbm, weight, label_ref, score_ref = rest[:5]
+    spectra, middle, ctf, sums, number, info, spectra_sem, middle_sem = rest[5:]
+    own_bins, side, _ = current_ref.shape
+    capacity = arrived[0].shape[0]
     slots = mic_count * capacity
-    return pl.pallas_call(
-        functools.partial(ready_kernel, bin_count, mic_count, capacity),
-        out_shape=[
-            jax.ShapeDtypeStruct((INFOS, max(slots, own_bins)), jnp.int32),
-            jax.ShapeDtypeStruct((slots, side, side), F32),
-            jax.ShapeDtypeStruct((3, slots, side), F32),
-        ],
-        in_specs=[SMEM] * 2 + [VMEM] * (1 + len(labels) + len(near)),
-        out_specs=[SMEM, VMEM, VMEM],
-        compiler_params=pltpu.CompilerParams(vmem_limit_bytes=VMEM_BYTES),
-        cost_estimate=pl.CostEstimate(flops=4 << 20, bytes_accessed=4 << 20, transcendentals=0),
-        name="ready",
-    )(defocus, bfactor, references, *labels, *near)
-
-
-def owner_kernel(capacity, near, info, current_ref, ctf, known, *rest):
-    arrived, (spectra, middle, weight, score_ref, sums, number) = rest[:-6], rest[-6:]
-    arrived = arrived[::-1]
-    slots, side, _ = ctf.shape
     pixels = float(side * side)
     chunks = chunks_of(side)
     zero = jnp.zeros((8, side), F32)
-    sums[...] = known[...]
+
+    copies = [
+        pltpu.make_async_copy(
+            block.at[:, pl.ds(0, side)],
+            spectra_hbm.at[pl.ds(step * capacity, capacity)],
+            spectra_sem.at[step],
+        )
+        for step, block in enumerate(arrived)
+    ]
+    for copy in copies:
+        copy.start()
+    labels = [
+        arrived[s // capacity][s % capacity, side : side + LABEL_ROWS, :128].astype(F32)
+        for s in range(slots)
+    ]
+    for s in range(slots):
+        label_ref[s] = labels[s]
+    focus, damping = decode(labels, capacity, bin_count, own_bins, info, focus_ref, damping_ref)
+    factors = ctf_factors(focus, damping, side)
+    sums[...] = jnp.zeros(sums.shape, F32)
+
+    def middle_copy(p):
+        return pltpu.make_async_copy(middle.at[p], middle_hbm.at[p], middle_sem.at[p])
 
     def keep(k, s, total):
         sums[k, pl.ds(s, 1), :] = jnp.sum(total, axis=0, keepdims=True)
@@ -314,28 +323,15 @@
         )
         correlation = cross / jnp.sqrt((model + EPSILON) * (data + EPSILON))
         weights = 1.0 / (1.0 + jnp.exp(-float(side) * correlation))
-        weight[...] = jnp.broadcast_to(weights.astype(BF16).astype(F32), (slots, side))
+        weight[...] = jnp.broadcast_to(weights.astype(BF16).astype(F32), (8, side))
         return correlation
 
     for s in range(slots):
 
         @pl.when(info[ACTIVE, s] > 0)
         def _(s=s):
-            block = arrived[s // capacity]
-            if s < near * capacity:
-                spectra[s] = block[s % capacity]
-            else:
-                cross, data = zero, zero
-                p = info[PLACE, s]
-                for rows in chunks:
-                    held = block[s % capacity, rows, :]
-                    spectra[s, rows, :] = held
-                    values = held.astype(F32)
-                    predicted = ctf[s, rows, :] * current_ref[p, rows, :].astype(F32)
-                    cross = cross + fold(predicted * values)
-                    data = data + fold(values * values)
-                keep(0, s, cross)
-                keep(2, s, data)
+            block = arrived[s // capacity].at[s % capacity]
+            first_compare(info, factors, current_ref, spectra, ctf, sums, s, block)
 
     correlate()
     update_shared(info, spectra, ctf, weight, number, current_ref, middle)
@@ -359,6 +355,7 @@
                 cross, model = compare(values, table, reference, cross, model)
             keep(0, s, cross)
             keep(1, s, model)
+            middle_copy(p).start()
 
         @pl.when((info[ACTIVE, s] > 0) & (info[ALONE, s] == 0))
         def _():
@@ -369,6 +366,12 @@
             keep(0, s, cross)
             keep(1, s, model)
 
+    @pl.loop(0, own_bins)
+    def _(p):
+        @pl.when(info[MEMBERS, p] > 1)
+        def _():
+            middle_copy(p).start()
+
     correlation = correlate()
     devices = score_ref.shape[0]
     device = lax.broadcasted_iota(jnp.int32, (devices, 1, 128), 0)
@@ -378,31 +381,69 @@
         hit = (info[ACTIVE, s] > 0) & (device == info[HOME, s]) & (lane == info[PARTICLE, s])
         board = jnp.where(hit, correlation[s : s + 1, :].reshape(1, 1, 1), board)
     score_ref[...] = board
-
-
-def owner_call(devices, capacity, near, info, references, ctf, known, arrived):
-    slots, side, _ = ctf.shape
+    for copy in copies:
+        copy.wait()
+
+    @pl.loop(0, own_bins)
+    def _(p):
+        @pl.when(info[MEMBERS, p] > 0)
+        def _():
+            middle_copy(p).wait()
+
+
+def owner_call(bin_count, mic_count, defocus, bfactor, references, arrived):
+    own_bins, side, _ = references.shape
+    slots = mic_count * arrived[0].shape[0]
     return pl.pallas_call(
-        functools.partial(owner_kernel, capacity, near),
+        functools.partial(owner_kernel, bin_count, mic_count),
         out_shape=[
-            jax.ShapeDtypeStruct((slots, side, side), BF16),
-            jax.ShapeDtypeStruct(references.shape, BF16),
-            jax.ShapeDtypeStruct((slots, side), F32),
-            jax.ShapeDtypeStruct((devices, 1, 128), F32),
+            pltpu.HBM((slots, side, side), BF16),
+            pltpu.HBM(references.shape, BF16),
+            jax.ShapeDtypeStruct((8, side), F32),
+            jax.ShapeDtypeStruct((slots, LABEL_ROWS, 128), F32),
+            jax.ShapeDtypeStruct((mic_count * bin_count, 1, 128), F32),
         ],
-        in_specs=[SMEM] + [VMEM] * (3 + len(arrived)),
-        out_specs=[VMEM] * 4,
+        in_specs=[SMEM] * 2 + [VMEM] * (1 + mic_count),
+        out_specs=[HBM, HBM, VMEM, VMEM, VMEM],
         scratch_shapes=[
-            pltpu.VMEM((3, slots, side), F32),
+            pltpu.VMEM((slots, side, side), BF16),
+            pltpu.VMEM(references.shape, BF16),
+            pltpu.VMEM((slots, side, side), F32),
+            pltpu.VMEM((3, 8, side), F32),
             pltpu.VMEM((2, side, side), F32),
+            pltpu.SMEM((INFOS, max(8, own_bins)), jnp.int32),
+            pltpu.SemaphoreType.DMA((mic_count,)),
+            pltpu.SemaphoreType.DMA((own_bins,)),
         ],
         compiler_params=pltpu.CompilerParams(vmem_limit_bytes=VMEM_BYTES),
         name="owner",
-    )(info, references, ctf, known, *arrived[::-1])
-
-
-def last_kernel(info, current_ref, spectra, ctf, middle, weight, refined_ref, number):
+    )(defocus, bfactor, references, *arrived[::-1])
+
+
+def last_kernel(
+    capacity, bin_count, focus_ref, damping_ref, current_ref, weight, spectra_hbm, middle_hbm, *rest
+):
+    label_ref, refined_ref, spectra, middle, ctf, number, info, spectra_sem, middle_sem = rest
     slots, side, _ = ctf.shape
+    own_bins = current_ref.shape[0]
+    copies = [
+        pltpu.make_async_copy(spectra_hbm, spectra, spectra_sem),
+        pltpu.make_async_copy(middle_hbm, middle, middle_sem),
+    ]
+    for copy in copies:
+        copy.start()
+    labels = [label_ref[s] for s in range(slots)]
+    focus, damping = decode(labels, capacity, bin_count, own_bins, info, focus_ref, damping_ref)
+    factors = ctf_factors(focus, damping, side)
+    for s in range(slots):
+
+        @pl.when(info[ACTIVE, s] > 0)
+        def _(s=s):
+            for rows in chunks_of(side):
+                ctf[s, rows, :] = ctf_chunk(factors, s, rows)
+
+    for copy in copies:
+        copy.wait()
     update_shared(info, spectra, ctf, weight, number, middle, refined_ref)
 
     @pl.loop(0, slots)
@@ -415,24 +456,36 @@
                 term, power, _ = shares(ctf, weight, s, rows, values)
                 refined_ref[p, rows, :] = renew(middle[p, rows, :], term, power)
 
-    @pl.loop(0, current_ref.shape[0])
+    @pl.loop(0, own_bins)
     def _(p):
         @pl.when(info[MEMBERS, p] == 0)
         def _():
             refined_ref[p] = current_ref[p]
 
 
-def last_call(info, references, spectra, ctf, middle, weight):
-    side = ctf.shape[1]
+def last_call(
+    capacity, bin_count, defocus, bfactor, references, weight, spectra, middle, labels
+):
+    slots, side, _ = spectra.shape
+    own_bins = references.shape[0]
     return pl.pallas_call(
-        last_kernel,
+        functools.partial(last_kernel, capacity, bin_count),
         out_shape=jax.ShapeDtypeStruct(references.shape, BF16),
-        in_specs=[SMEM] + [VMEM] * 5,
+        in_specs=[SMEM] * 2 + [VMEM] * 2 + [HBM] * 2 + [VMEM],
         out_specs=VMEM,
-        scratch_shapes=[pltpu.VMEM((2, side, side), F32)],
+        scratch_shapes=[
+            pltpu.VMEM(spectra.shape, BF16),
+            pltpu.VMEM(references.shape, BF16),
+            pltpu.VMEM((slots, side, side), F32),
+            pltpu.VMEM((2, side, side), F32),
+            pltpu.SMEM((INFOS, max(8, own_bins)), jnp.int32),
+            pltpu.SemaphoreType.DMA(()),
+            pltpu.SemaphoreType.DMA(()),
+        ],
         compiler_params=pltpu.CompilerParams(vmem_limit_bytes=VMEM_BYTES),
+        cost_estimate=pl.CostEstimate(flops=4 << 20, bytes_accessed=4 << 20, transcendentals=0),
         name="last",
-    )(info, references, spectra, ctf, middle, weight)
+    )(defocus, bfactor, references, weight, in_hbm(spectra), in_hbm(middle), labels)
 
 
 def exchange(blocks, axis):
@@ -448,7 +501,6 @@
     particles, side, _ = images.shape
     own_bins = references.shape[0]
     capacity = (3 * particles + 2 * mic_count - 1) // (2 * mic_count)
-    near = 2
 
     basis = jnp.asarray(hartley(side), BF16)
     operands = (bin_place, particle_bin, ctf_group, offsets, images, basis)
@@ -459,18 +511,15 @@
     sent_near = home_call(bin_count, own_bins, 0, rest, operands, after=(sent_far[-1],))
     arrived = exchange(list(sent_near) + list(sent_far), "bin")
 
-    sent, labels = middle_call(mic_count, capacity, arrived[::-1])
+    sent = middle_call(mic_count, capacity, arrived[::-1])
     arrived = exchange(sent, "mic")
-    labels = exchange(labels, "mic")
-
-    info, ctf, known = ready_call(
-        bin_count, mic_count, capacity, defocus, bfactor, references, labels, arrived[:near]
-    )
-    spectra, middle, weight, board = owner_call(
-        mic_count * bin_count, capacity, near, info, references, ctf, known, arrived
+    spectra, middle, weight, labels, board = owner_call(
+        bin_count, mic_count, defocus, bfactor, references, arrived
     )
     back = lax.all_to_all(board, ("mic", "bin"), split_axis=0, concat_axis=0, tiled=True)
-    refined = last_call(info, references, spectra, ctf, middle, weight)
+    refined = last_call(
+        capacity, bin_count, defocus, bfactor, references, weight, spectra, middle, labels
+    )
     return (refined, jnp.sum(back, axis=(0, 1))[:particles])
 
 

time: 67.2 us -> 63.1 us (0.939)
  waiting for transfers between devices: 18.5 us -> 23.3 us
  local copies, waits for them, and re-layouts: 4.42 us -> 0.01 us
  starting transfers between devices: 29.9 us -> 27 us
  Pallas kernels: 12.8 us -> 11.6 us
    unnamed x14 -> x6, local copies, waits for them, and re-layouts: 4.42 us -> 0.01 us
    ppermute x13 -> x10, starting transfers between devices: 25.2 us -> 21.7 us  [exchange(): lax.ppermute(blocks[k], axis, [(i, i ^ k) for i in range(size)])]
    ppermute x13 -> x10, waiting for transfers between devices: 16.4 us -> 19.9 us  [exchange(): lax.ppermute(blocks[k], axis, [(i, i ^ k) for i in range(size)])]
    all_to_all x1, waiting for transfers between devices: 2.01 us -> 3.39 us  [body(): lax.all_to_all(board, ('mic', 'bin'), split_axis=0, concat_axis=0, tiled=...]
    pallas_call x3 -> x2, Pallas kernels: 8.23 us -> 7.16 us  [the longest x1 3.72 us: last_call(): pl.pallas_call(functools.partial(last_kernel, capacity, bin_count), out_s...]
  transfers between devices with their start and end apart: 14 -> 11, of which waited for: 5 -> 5; matrix products, arithmetic and copies ran while one was open for 0% -> 0% of each run, Pallas kernels for 12% -> 9%
where the time goes in v5:
time: 63.1 us; the launch traced here: 63.2 us
  starting transfers between devices  27 us (43%)
  waiting for transfers between devices  23.3 us (37%)
  Pallas kernels  11.6 us (18%)
  between operations  0.72 us (1%)
    ppermute x10, starting transfers between devices, exchange(): lax.ppermute(blocks[k], axis, [(i, i ^ k) for i in range(size)])  21.7 us
    ppermute x10, waiting for transfers between devices, exchange(): lax.ppermute(blocks[k], axis, [(i, i ^ k) for i in range(size)])  19.9 us
    all_to_all x1, starting transfers between devices, body(): lax.all_to_all(board, ('mic', 'bin'), split_axis=0, concat_axis=0, tiled=...  5.33 us
    pallas_call x2, Pallas kernels, home_call(): pl.pallas_call(functools.partial(home_kernel, bin_count, own_bins, first,...  4.03 us
    pallas_call x1, Pallas kernels, last_call(): pl.pallas_call(functools.partial(last_kernel, capacity, bin_count), out_s...  3.72 us
    pallas_call x1, Pallas kernels, owner_call(): pl.pallas_call(functools.partial(owner_kernel, bin_count, mic_count), out...  3.44 us
    all_to_all x1, waiting for transfers between devices, body(): lax.all_to_all(board, ('mic', 'bin'), split_axis=0, concat_axis=0, tiled=...  3.39 us
  transfers between devices with their start and end apart: 11, of which 5 were waited for; matrix products, arithmetic and copies ran while one was open for 0% of the time, Pallas kernels for 9%

profile of v5, /device:TPU:0, one launch (start us, length us, event | category | flops | bytes accessed | tf_op | source)
XLA Modules:
  0.0 63.2 jit_solution(10848832860071371580)
XLA Ops:
  0.6 2.0 %home.2 = (bf16[264,256]{1,0:T(8,128)(2,1)S(1)}, bf16[264,256]{1,0:T(8,128)(2,1)S(1)}) custom-call(s32[256]{0:T(256)} %place_hbm.3, s32[4]{0:T(128)} %bin_hbm.3, s32[4]{0:T(128)} %group_hbm.3, s32[2,4]{1,0:T(2,128)} %offset_hbm.3, bf16[4,256,256]{2,1,0:T(8,128)(2,1)} %image_hbm.3, bf16[256,256]{1,0:T(8,128)(2,1)} %constant.4.clone.basis_hbm), custom_call_target="tpu_custom_call" | custom-call | tf_op jit(solution)/shard_map/home/pallas_call | solution.py:113
  2.7 0.0 copy-start
  2.7 4.6 %collective-permute-start.1 = (bf16[264,256]{1,0:T(8,128)(2,1)S(1)}, bf16[264,256]{1,0:T(8,128)(2,1)S(1)}, u32[]{:S(2)}, u32[]{:S(2)}) collective-permute-start(bf16[264,256]{1,0:T(8,128)(2,1)S(1)} %get-tuple-element.20), channel_id=1, source_target_pairs={{0,6},{1,7},{2,4},{3,5},{4,2},{5,3},{6,0},{7,1},{8,14},{9,15},{10,... | collective-permute-start | bytes 405512 | tf_op jit(solution)/shard_map/ppermute | solution.py:494
  7.3 1.3 %collective-permute-start = (bf16[264,256]{1,0:T(8,128)(2,1)S(1)}, bf16[264,256]{1,0:T(8,128)(2,1)S(1)}, u32[]{:S(2)}, u32[]{:S(2)}) collective-permute-start(bf16[264,256]{1,0:T(8,128)(2,1)S(1)} %get-tuple-element.19.rest_0_), channel_id=1, source_target_pairs={{0,7},{1,6},{2,5},{3,4},{4,3},{5,2},{6,1},{7,0},{8,15},{9,14},{10,... | collective-permute-start | bytes 405512 | tf_op jit(solution)/shard_map/ppermute | solution.py:494
  8.6 2.0 %home.3 = (bf16[264,256]{1,0:T(8,128)(2,1)S(1)}, bf16[264,256]{1,0:T(8,128)(2,1)S(1)}, bf16[264,256]{1,0:T(8,128)(2,1)S(1)}, bf16[264,256]{1,0:T(8,128)(2,1)S(1)...) custom-call(s32[256]{0:T(256)} %place_hbm.3, s32[4]{0:T(128)} %bin_hbm.3, s32[4]{0:T(128)} %group_hbm.3, ...), custom_call_target="tpu_custom_call" | custom-call | tf_op jit(solution)/shard_map/home/pallas_call | solution.py:113
  10.6 1.6 %collective-permute-start.2 = (bf16[264,256]{1,0:T(8,128)(2,1)S(1)}, bf16[264,256]{1,0:T(8,128)(2,1)S(1)}, u32[]{:S(2)}, u32[]{:S(2)}) collective-permute-start(bf16[264,256]{1,0:T(8,128)(2,1)S(1)} %get-tuple-element.21), channel_id=1, source_target_pairs={{0,5},{1,4},{2,7},{3,6},{4,1},{5,0},{6,3},{7,2},{8,13},{9,12},{10,... | collective-permute-start | bytes 405512 | tf_op jit(solution)/shard_map/ppermute | solution.py:494
  12.2 1.5 %collective-permute-start.3 = (bf16[264,256]{1,0:T(8,128)(2,1)S(1)}, bf16[264,256]{1,0:T(8,128)(2,1)S(1)}, u32[]{:S(2)}, u32[]{:S(2)}) collective-permute-start(bf16[264,256]{1,0:T(8,128)(2,1)S(1)} %get-tuple-element.22), channel_id=1, source_target_pairs={{0,4},{1,5},{2,6},{3,7},{4,0},{5,1},{6,2},{7,3},{8,12},{9,13},{10,... | collective-permute-start | bytes 405512 | tf_op jit(solution)/shard_map/ppermute | solution.py:494
  13.7 2.1 %collective-permute-start.4 = (bf16[264,256]{1,0:T(8,128)(2,1)S(1)}, bf16[264,256]{1,0:T(8,128)(2,1)S(1)}, u32[]{:S(2)}, u32[]{:S(2)}) collective-permute-start(bf16[264,256]{1,0:T(8,128)(2,1)S(1)} %get-tuple-element.23), channel_id=1, source_target_pairs={{0,3},{1,2},{2,1},{3,0},{4,7},{5,6},{6,5},{7,4},{8,11},{9,10},{10,... | collective-permute-start | bytes 405512 | tf_op jit(solution)/shard_map/ppermute | solution.py:494
  15.8 7.5 %collective-permute-start.5 = (bf16[264,256]{1,0:T(8,128)(2,1)S(1)}, bf16[264,256]{1,0:T(8,128)(2,1)S(1)}, u32[]{:S(2)}, u32[]{:S(2)}) collective-permute-start(bf16[264,256]{1,0:T(8,128)(2,1)S(1)} %get-tuple-element.24), channel_id=1, source_target_pairs={{0,2},{1,3},{2,0},{3,1},{4,6},{5,7},{6,4},{7,5},{8,10},{9,11},{10,... | collective-permute-start | bytes 405512 | tf_op jit(solution)/shard_map/ppermute | solution.py:494
  23.3 1.2 %collective-permute-start.6 = (bf16[264,256]{1,0:T(8,128)(2,1)S(1)}, bf16[264,256]{1,0:T(8,128)(2,1)S(1)}, u32[]{:S(2)}, u32[]{:S(2)}) collective-permute-start(bf16[264,256]{1,0:T(8,128)(2,1)S(1)} %get-tuple-element.25), channel_id=1, source_target_pairs={{0,1},{1,0},{2,3},{3,2},{4,5},{5,4},{6,7},{7,6},{8,9},{9,8},{10,11... | collective-permute-start | bytes 405512 | tf_op jit(solution)/shard_map/ppermute | solution.py:494
  24.5 6.3 %collective-permute-done.2.rest_2_ = bf16[264,256]{1,0:T(8,128)(2,1)S(1)} collective-permute-done((bf16[264,256]{1,0:T(8,128)(2,1)S(1)}, bf16[264,256]{1,0:T(8,128)(2,1)S(1)}, u32[]{:S(2)}, u32[]{:S(2)}) %collective-permute-start.2) | collective-permute-done | bytes 135200 | tf_op jit(solution)/shard_map/ppermute | solution.py:494
  30.8 0.0 collective-permute-done.3.rest_3_
  30.8 0.8 %collective-permute-done.5.rest_5_ = bf16[264,256]{1,0:T(8,128)(2,1)S(1)} collective-permute-done((bf16[264,256]{1,0:T(8,128)(2,1)S(1)}, bf16[264,256]{1,0:T(8,128)(2,1)S(1)}, u32[]{:S(2)}, u32[]{:S(2)}) %collective-permute-start.5) | collective-permute-done | bytes 135200 | tf_op jit(solution)/shard_map/ppermute | solution.py:494
  31.6 0.4 middle.1
  32.0 0.1 collective-permute-start.7
  32.1 1.7 %collective-permute-start.8 = (bf16[2,264,256]{2,1,0:T(8,128)(2,1)S(1)}, bf16[2,264,256]{2,1,0:T(8,128)(2,1)S(1)}, u32[]{:S(2)}, u32[]{:S(2)}) collective-permute-start(bf16[2,264,256]{2,1,0:T(8,128)(2,1)S(1)} %get-tuple-element.28), channel_id=1, source_target_pairs={{0,16},{8,24},{16,0},{24,8},{1,17},{9,25},{17,1},{25,9},{2,18},{10... | collective-permute-start | bytes 811016 | tf_op jit(solution)/shard_map/ppermute | solution.py:494
  33.8 0.2 collective-permute-start.9
  34.0 6.7 %collective-permute-done.7.rest_0_ = bf16[2,264,256]{2,1,0:T(8,128)(2,1)S(1)} collective-permute-done((bf16[2,264,256]{2,1,0:T(8,128)(2,1)S(1)}, bf16[2,264,256]{2,1,0:T(8,128)(2,1)S(1)}, u32[]{:S(2)}, u32[]{:S(2)}) %collective-permute-start.7) | collective-permute-done | bytes 270368 | tf_op jit(solution)/shard_map/ppermute | solution.py:494
  40.7 6.0 %collective-permute-done.8.rest_1_ = bf16[2,264,256]{2,1,0:T(8,128)(2,1)S(1)} collective-permute-done((bf16[2,264,256]{2,1,0:T(8,128)(2,1)S(1)}, bf16[2,264,256]{2,1,0:T(8,128)(2,1)S(1)}, u32[]{:S(2)}, u32[]{:S(2)}) %collective-permute-start.8) | collective-permute-done | bytes 270368 | tf_op jit(solution)/shard_map/ppermute | solution.py:494
  46.7 3.4 %owner.1 = (bf16[8,256,256]{2,1,0:T(8,128)(2,1)}, bf16[8,256,256]{2,1,0:T(8,128)(2,1)}, f32[8,256]{1,0:T(8,128)S(1)}, f32[8,8,128]{2,1,0:T(8,128)S(1)}, f32[32,1,128]{2,1,0:T(1,128)}) custom-call(f32[64]{0:T(128)S(1)} %copy-done.1, f32[64]{0:T(128)S(1)} %copy-done.2, bf16[8,256,256]{2,1,0:T(8,128)(2,1)S(1)} %copy-done, ...), custom_call_target="tpu_custom_call" | custom-call | tf_op jit(solution)/shard_map/owner/pallas_call | solution.py:397
  50.1 5.3 %all-to-all-start = ((f32[32,1,128]{2,1,0:T(1,128)}), f32[32,1,128]{2,1,0:T(1,128)S(1)}, u32[]{:S(2)}, u32[]{:S(2)}) async-start(f32[32,1,128]{2,1,0:T(1,128)} %get-tuple-element.35), calls=%async_computation | async-start | bytes 32768 | tf_op jit(solution)/shard_map/all_to_all | solution.py:519
  55.5 3.7 %last.1 = bf16[8,256,256]{2,1,0:T(8,128)(2,1)} custom-call(f32[64]{0:T(128)S(1)} %copy-done.1, f32[64]{0:T(128)S(1)} %copy-done.2, bf16[8,256,256]{2,1,0:T(8,128)(2,1)S(1)} %copy-done, f32[8,256]{1,0:T(8,128)S(1)} %get-tuple-element.31.weight, bf16[8,256,256]{2,1,0:T(8,128)(2,1)} %get-tuple-element.32.spectra_hbm, ...), custom_call_target="tpu_custom_call" | custom-call | flops 4194304 | bytes 4194304 | tf_op jit(solution)/shard_map/last/pallas_call | solution.py:471
  59.2 3.4 %all-to-all-done = f32[32,1,128]{2,1,0:T(1,128)S(1)} async-done(((f32[32,1,128]{2,1,0:T(1,128)}), f32[32,1,128]{2,1,0:T(1,128)S(1)}, u32[]{:S(2)}, u32[]{:S(2)}) %all-to-all-start) | async-done | bytes 16416 | tf_op jit(solution)/shard_map/all_to_all | solution.py:519
  62.6 0.6 reduce_sum.9
  (10 shorter events, 0.0 us)
Async XLA Ops:
  2.7 44.0 %copy-start = (bf16[8,256,256]{2,1,0:T(8,128)(2,1)S(1)}, bf16[8,256,256]{2,1,0:T(8,128)(2,1)}, u32[]{:S(2)}) copy-start(bf16[8,256,256]{2,1,0:T(8,128)(2,1)} %current_ref.3) | copy-start | bytes 3145732
  2.7 13.1 %collective-permute-start.1 = (bf16[264,256]{1,0:T(8,128)(2,1)S(1)}, bf16[264,256]{1,0:T(8,128)(2,1)S(1)}, u32[]{:S(2)}, u32[]{:S(2)}) collective-permute-start(bf16[264,256]{1,0:T(8,128)(2,1)S(1)} %get-tuple-element.20), channel_id=1, source_target_pairs={{0,6},{1,7},{2,4},{3,5},{4,2},{5,3},{6,0},{7,1},{8,14},{9,15},{10,... | collective-permute-start | bytes 405512 | tf_op jit(solution)/shard_map/ppermute | solution.py:494
  7.3 16.0 %collective-permute-start = (bf16[264,256]{1,0:T(8,128)(2,1)S(1)}, bf16[264,256]{1,0:T(8,128)(2,1)S(1)}, u32[]{:S(2)}, u32[]{:S(2)}) collective-permute-start(bf16[264,256]{1,0:T(8,128)(2,1)S(1)} %get-tuple-element.19.rest_0_), channel_id=1, source_target_pairs={{0,7},{1,6},{2,5},{3,4},{4,3},{5,2},{6,1},{7,0},{8,15},{9,14},{10,... | collective-permute-start | bytes 405512 | tf_op jit(solution)/shard_map/ppermute | solution.py:494
  10.6 20.2 %collective-permute-start.2 = (bf16[264,256]{1,0:T(8,128)(2,1)S(1)}, bf16[264,256]{1,0:T(8,128)(2,1)S(1)}, u32[]{:S(2)}, u32[]{:S(2)}) collective-permute-start(bf16[264,256]{1,0:T(8,128)(2,1)S(1)} %get-tuple-element.21), channel_id=1, source_target_pairs={{0,5},{1,4},{2,7},{3,6},{4,1},{5,0},{6,3},{7,2},{8,13},{9,12},{10,... | collective-permute-start | bytes 405512 | tf_op jit(solution)/shard_map/ppermute | solution.py:494
  12.2 18.6 %collective-permute-start.3 = (bf16[264,256]{1,0:T(8,128)(2,1)S(1)}, bf16[264,256]{1,0:T(8,128)(2,1)S(1)}, u32[]{:S(2)}, u32[]{:S(2)}) collective-permute-start(bf16[264,256]{1,0:T(8,128)(2,1)S(1)} %get-tuple-element.22), channel_id=1, source_target_pairs={{0,4},{1,5},{2,6},{3,7},{4,0},{5,1},{6,2},{7,3},{8,12},{9,13},{10,... | collective-permute-start | bytes 405512 | tf_op jit(solution)/shard_map/ppermute | solution.py:494
  13.7 17.1 %collective-permute-start.4 = (bf16[264,256]{1,0:T(8,128)(2,1)S(1)}, bf16[264,256]{1,0:T(8,128)(2,1)S(1)}, u32[]{:S(2)}, u32[]{:S(2)}) collective-permute-start(bf16[264,256]{1,0:T(8,128)(2,1)S(1)} %get-tuple-element.23), channel_id=1, source_target_pairs={{0,3},{1,2},{2,1},{3,0},{4,7},{5,6},{6,5},{7,4},{8,11},{9,10},{10,... | collective-permute-start | bytes 405512 | tf_op jit(solution)/shard_map/ppermute | solution.py:494
  15.8 15.8 %collective-permute-start.5 = (bf16[264,256]{1,0:T(8,128)(2,1)S(1)}, bf16[264,256]{1,0:T(8,128)(2,1)S(1)}, u32[]{:S(2)}, u32[]{:S(2)}) collective-permute-start(bf16[264,256]{1,0:T(8,128)(2,1)S(1)} %get-tuple-element.24), channel_id=1, source_target_pairs={{0,2},{1,3},{2,0},{3,1},{4,6},{5,7},{6,4},{7,5},{8,10},{9,11},{10,... | collective-permute-start | bytes 405512 | tf_op jit(solution)/shard_map/ppermute | solution.py:494
  23.3 8.4 %collective-permute-start.6 = (bf16[264,256]{1,0:T(8,128)(2,1)S(1)}, bf16[264,256]{1,0:T(8,128)(2,1)S(1)}, u32[]{:S(2)}, u32[]{:S(2)}) collective-permute-start(bf16[264,256]{1,0:T(8,128)(2,1)S(1)} %get-tuple-element.25), channel_id=1, source_target_pairs={{0,1},{1,0},{2,3},{3,2},{4,5},{5,4},{6,7},{7,6},{8,9},{9,8},{10,11... | collective-permute-start | bytes 405512 | tf_op jit(solution)/shard_map/ppermute | solution.py:494
  32.0 8.7 %collective-permute-start.7 = (bf16[2,264,256]{2,1,0:T(8,128)(2,1)S(1)}, bf16[2,264,256]{2,1,0:T(8,128)(2,1)S(1)}, u32[]{:S(2)}, u32[]{:S(2)}) collective-permute-start(bf16[2,264,256]{2,1,0:T(8,128)(2,1)S(1)} %get-tuple-element.27), channel_id=1, source_target_pairs={{0,24},{8,16},{16,8},{24,0},{1,25},{9,17},{17,9},{25,1},{2,26},{10... | collective-permute-start | bytes 811016 | tf_op jit(solution)/shard_map/ppermute | solution.py:494
  32.1 14.6 %collective-permute-start.8 = (bf16[2,264,256]{2,1,0:T(8,128)(2,1)S(1)}, bf16[2,264,256]{2,1,0:T(8,128)(2,1)S(1)}, u32[]{:S(2)}, u32[]{:S(2)}) collective-permute-start(bf16[2,264,256]{2,1,0:T(8,128)(2,1)S(1)} %get-tuple-element.28), channel_id=1, source_target_pairs={{0,16},{8,24},{16,0},{24,8},{1,17},{9,25},{17,1},{25,9},{2,18},{10... | collective-permute-start | bytes 811016 | tf_op jit(solution)/shard_map/ppermute | solution.py:494
  33.8 12.9 %copy-start.1 = (f32[64]{0:T(128)S(1)}, f32[64]{0:T(128)}, u32[]{:S(2)}) copy-start(f32[64]{0:T(128)} %focus_ref.3) | copy-start | bytes 772
  33.8 12.9 %copy-start.2 = (f32[64]{0:T(128)S(1)}, f32[64]{0:T(128)}, u32[]{:S(2)}) copy-start(f32[64]{0:T(128)} %damping_ref.3) | copy-start | bytes 772
  33.8 12.9 %collective-permute-start.9 = (bf16[2,264,256]{2,1,0:T(8,128)(2,1)S(1)}, bf16[2,264,256]{2,1,0:T(8,128)(2,1)S(1)}, u32[]{:S(2)}, u32[]{:S(2)}) collective-permute-start(bf16[2,264,256]{2,1,0:T(8,128)(2,1)S(1)} %get-tuple-element.29), channel_id=1, source_target_pairs={{0,8},{8,0},{16,24},{24,16},{1,9},{9,1},{17,25},{25,17},{2,10},{10... | collective-permute-start | bytes 811016 | tf_op jit(solution)/shard_map/ppermute | solution.py:494
  50.1 12.5 %all-to-all-start = ((f32[32,1,128]{2,1,0:T(1,128)}), f32[32,1,128]{2,1,0:T(1,128)S(1)}, u32[]{:S(2)}, u32[]{:S(2)}) async-start(f32[32,1,128]{2,1,0:T(1,128)} %get-tuple-element.35), calls=%async_computation | async-start | bytes 32768 | tf_op jit(solution)/shard_map/all_to_all | solution.py:519

commit v6 on v5

v6 whole, which is shorter than its diff:
```python
import functools
import math

import jax
import jax.numpy as jnp
import numpy as np
from jax import lax
from jax.experimental import pallas as pl
from jax.experimental.pallas import tpu as pltpu
from jax.sharding import PartitionSpec as P

ITERS = 2
PRIOR_WEIGHT = 0.5
EPSILON = 1e-06
CONTRAST = 0.1
AMPLITUDE = math.sqrt(1.0 - CONTRAST * CONTRAST)

LANES = 128
LABEL_ROWS = 8
CHUNK = 32
VMEM_BYTES = 24 * 1024 * 1024

ACTIVE, PLACE, ALONE, HOME, PARTICLE, MEMBERS, LATE = range(7)
INFOS = 7

F32 = jnp.float32
BF16 = jnp.bfloat16
VMEM = pl.BlockSpec(memory_space=pltpu.VMEM)
SMEM = pl.BlockSpec(memory_space=pltpu.SMEM)
HBM = pl.BlockSpec(memory_space=pltpu.HBM)
ANY = pl.BlockSpec(memory_space=pl.ANY)


def in_hbm(x):
    return pltpu.with_memory_space_constraint(x, pltpu.HBM)


def hartley(side):
    index = np.arange(side)
    angles = (np.outer(index, index) % side).astype(np.float32) * np.float32(2.0 * math.pi / side)
    return (np.cos(angles) + np.sin(angles)) / np.float32(math.sqrt(side))


def label_block(values):
    row = lax.broadcasted_iota(jnp.int32, (LABEL_ROWS, LANES), 0)
    block = jnp.zeros((LABEL_ROWS, LANES), jnp.int32)
    for number, value in enumerate(values):
        block = jnp.where(row == number, value, block)
    return block.astype(F32).astype(BF16)


def home_kernel(
    bin_count, own_bins, first, count, place_hbm, bin_hbm, group_hbm, offset_hbm, image_hbm, basis_hbm, *rest
):
    rest = rest[len(rest) - count - 9 :]
    outs, rest = rest[:count], rest[count:]
    spectra, image_ref, basis_ref, place_ref, bin_ref, group_ref, offset_ref, image_sem, sem = rest
    particles, side = image_ref.shape[0], image_ref.shape[1]
    here = lax.axis_index("bin")
    pairs = (
        (basis_hbm, basis_ref),
        (place_hbm, place_ref),
        (bin_hbm, bin_ref),
        (group_hbm, group_ref),
        (offset_hbm, offset_ref),
    )
    copies = [pltpu.make_async_copy(a, b, sem.at[k]) for k, (a, b) in enumerate(pairs)]
    for copy in copies:
        copy.start()

    def image_copy(i):
        return pltpu.make_async_copy(image_hbm.at[i], image_ref.at[i], image_sem.at[i])

    for i in range(particles):
        image_copy(i).start()
    pieces = side // LANES
    for out in outs:
        out[pieces * side :, :] = jnp.zeros((LABEL_ROWS, LANES), BF16)
    for copy in copies:
        copy.wait()

    @pl.loop(0, particles)
    def _(i):
        image_copy(i).wait()
        place = place_ref[bin_ref[i]]
        owner = place // own_bins
        step_of = lax.rem(owner, bin_count) ^ here

        @pl.when((step_of >= first) & (step_of < first + count))
        def _():
            moved = pltpu.roll(image_ref[i].astype(F32), side - offset_ref[0, i], 0).astype(BF16)
            columns = pltpu.roll(basis_ref[...].astype(F32), offset_ref[1, i], 0).astype(BF16)
            half = jnp.dot(basis_ref[...], moved, preferred_element_type=F32).astype(BF16)
            spectra[...] = jnp.dot(half, columns, preferred_element_type=F32).astype(BF16)
            labels = label_block(
                (
                    1 + owner // bin_count,
                    lax.rem(place, own_bins),
                    group_ref[i],
                    i * bin_count + here,
                )
            )
            for k in range(count):

                @pl.when(step_of == first + k)
                def _():
                    for n in range(pieces):
                        outs[k][n * side : (n + 1) * side, :] = spectra[
                            :, n * LANES : (n + 1) * LANES
                        ]
                    outs[k][pieces * side :, :] = labels


def home_call(bin_count, own_bins, first, count, operands, after=()):
    images, particles, side = operands[4], operands[4].shape[0], operands[4].shape[1]
    return pl.pallas_call(
        functools.partial(home_kernel, bin_count, own_bins, first, count),
        out_shape=[
            jax.ShapeDtypeStruct((side * side // LANES + LABEL_ROWS, LANES), BF16)
        ]
        * count,
        in_specs=[HBM] * 6 + [ANY] * len(after),
        out_specs=[VMEM] * count,
        scratch_shapes=[
            pltpu.VMEM((side, side), BF16),
            pltpu.VMEM(images.shape, BF16),
            pltpu.VMEM((side, side), BF16),
        ]
        + [pltpu.SMEM(x.shape, jnp.int32) for x in operands[:4]]
        + [pltpu.SemaphoreType.DMA((particles,)), pltpu.SemaphoreType.DMA((5,))],
        compiler_params=pltpu.CompilerParams(vmem_limit_bytes=VMEM_BYTES),
        name="home",
    )(*operands, *after)


def middle_kernel(mic_count, capacity, *rest):
    arrived, outs = rest[: len(rest) - mic_count], rest[len(rest) - mic_count :]
    rows = arrived[0].shape[0]
    here = lax.axis_index("mic")
    empty = jnp.zeros((LABEL_ROWS, LANES), BF16)
    for out in outs:
        for j in range(capacity):
            out[j, rows - LABEL_ROWS : rows, :] = empty
    targets = [
        jnp.max(block[rows - LABEL_ROWS : rows, :].astype(F32)[0:1]).astype(jnp.int32)
        for block in arrived
    ]
    counts = [jnp.int32(0)] * mic_count
    for block, target in zip(arrived, targets):
        step_of = (target - 1) ^ here
        for step in range(mic_count):
            chosen = (target > 0) & (step_of == step)

            @pl.when(chosen)
            def _(block=block, step=step, slot=counts[step]):
                outs[step][slot] = block[...]

            counts[step] = counts[step] + chosen.astype(jnp.int32)


def middle_call(mic_count, capacity, arrived):
    return pl.pallas_call(
        functools.partial(middle_kernel, mic_count, capacity),
        out_shape=[jax.ShapeDtypeStruct((capacity, *arrived[0].shape), BF16)] * mic_count,
        in_specs=[VMEM] * len(arrived),
        out_specs=[VMEM] * mic_count,
        compiler_params=pltpu.CompilerParams(vmem_limit_bytes=VMEM_BYTES),
        name="middle",
    )(*arrived)


def fold(values):
    return jnp.sum(values.reshape(values.shape[0] // 8, 8, values.shape[1]), axis=0)


def chunks_of(side):
    return [slice(c, c + CHUNK) for c in range(0, side, CHUNK)]


def shares(ctf, weight, s, rows, values):
    table = ctf[s, rows, :]
    scaled = weight * table
    return (scaled * values).astype(BF16).astype(F32), scaled * table, table


def renew(previous, numerator, denominator):
    return (
        (numerator + PRIOR_WEIGHT * previous.astype(F32)) / (denominator + PRIOR_WEIGHT)
    ).astype(BF16)


def update_shared(info, groups, weight, number, source, target, kind=MEMBERS):
    chunks = chunks_of(source.shape[1])

    @pl.loop(0, source.shape[0])
    def _(p):
        @pl.when((info[MEMBERS, p] > 1) & (info[kind, p] > 0))
        def _():
            number[...] = jnp.zeros(number.shape, F32)
            for ctf, spectra, first in groups:

                @pl.loop(0, spectra.shape[0])
                def _(k):
                    @pl.when((info[ACTIVE, first + k] > 0) & (info[PLACE, first + k] == p))
                    def _():
                        scale = weight[pl.ds(first + k, 1), :]
                        for rows in chunks:
                            values = spectra[k, rows, :].astype(F32)
                            term, power, _ = shares(ctf, scale, k, rows, values)
                            number[0, rows, :] += term
                            number[1, rows, :] += power

            for rows in chunks:
                target[p, rows, :] = renew(
                    source[p, rows, :], number[0, rows, :], number[1, rows, :]
                )


def decode(labels, steps, bin_count, own_bins, info, late=0):
    slots = len(labels)
    capacity = slots // len(steps)
    here = lax.axis_index("mic")
    codes = []
    for block in labels:
        code = block[1:2] + 256.0 * block[3:4]
        codes.append(jnp.max(jnp.where(block[0:1] > 0, code, -1.0)).astype(jnp.int32))
    for p in range(own_bins):
        info[MEMBERS, p] = jnp.int32(0)
        info[LATE, p] = jnp.int32(0)
    for s in range(slots):
        active = (codes[s] >= 0).astype(jnp.int32)
        code = jnp.maximum(codes[s], 0)
        sender = code >> 8
        place = code & 255
        info[ACTIVE, s] = active
        info[PLACE, s] = place
        info[HOME, s] = (here ^ steps[s // capacity]) * bin_count + lax.rem(sender, bin_count)
        info[PARTICLE, s] = sender // bin_count
        info[MEMBERS, place] = info[MEMBERS, place] + active
        if s >= slots - late * capacity:
            info[LATE, place] = info[LATE, place] + active
    for s in range(slots):
        single = (info[ACTIVE, s] > 0) & (info[MEMBERS, info[PLACE, s]] == 1)
        info[ALONE, s] = single.astype(jnp.int32)


def ctf_factors(labels, focus_ref, damping_ref, side):
    groups = focus_ref.shape[1]
    group = jnp.concatenate([x[2:3, :groups] for x in labels] + [labels[0][4:5, :groups]] * 8)[:8]
    chosen = group.astype(jnp.int32) == lax.broadcasted_iota(jnp.int32, (8, groups), 1)
    focus = jnp.sum(jnp.where(chosen, focus_ref[...], 0.0), axis=1, keepdims=True)
    damping = jnp.sum(jnp.where(chosen, damping_ref[...], 0.0), axis=1, keepdims=True)
    frequency = lax.broadcasted_iota(jnp.int32, (8, side), 1)
    folded = jnp.minimum(frequency, side - frequency).astype(F32) / (side / 2.0)
    square = folded * folded
    envelope = jnp.exp(-damping * square)
    sine = jnp.sin(focus * square) * envelope
    cosine = jnp.cos(focus * square) * envelope
    by_sine = jnp.transpose(CONTRAST * sine - AMPLITUDE * cosine)
    by_cosine = jnp.transpose(-(AMPLITUDE * sine + CONTRAST * cosine))
    return by_sine, sine, by_cosine, cosine


def ctf_chunk(factors, s, rows):
    by_sine, sine, by_cosine, cosine = factors
    return (
        by_sine[rows, s : s + 1] * sine[s : s + 1, :]
        + by_cosine[rows, s : s + 1] * cosine[s : s + 1, :]
    )


def labels_of(arrived):
    return [
        block[j, block.shape[1] - LABEL_ROWS :, :].astype(F32)
        for block in arrived
        for j in range(block.shape[0])
    ]


def first_compare(info, factors, current_ref, group, sums, s, block):
    ctf, spectra, first = group
    side = ctf.shape[1]
    p = info[PLACE, s]
    cross = model = data = jnp.zeros((8, side), F32)
    for rows in chunks_of(side):
        table = ctf_chunk(factors, s, rows)
        ctf[s - first, rows, :] = table
        held = jnp.concatenate(
            [block[n + rows.start : n + rows.stop, :] for n in range(0, side * side // LANES, side)],
            axis=1,
        )
        spectra[s - first, rows, :] = held
        values = held.astype(F32)
        predicted = table * current_ref[p, rows, :].astype(F32)
        cross = cross + fold(predicted * values)
        model = model + fold(predicted * predicted)
        data = data + fold(values * values)
    for k, total in enumerate((cross, model, data)):
        sums[k, s : s + 1, :] = jnp.sum(total, axis=0, keepdims=True)


def correlate(sums, side):
    pixels = float(side * side)
    cross, model, data = (jnp.sum(sums[k], axis=1, keepdims=True) / pixels for k in range(3))
    correlation = cross / jnp.sqrt((model + EPSILON) * (data + EPSILON))
    weights = 1.0 / (1.0 + jnp.exp(-float(side) * correlation))
    return correlation, jnp.broadcast_to(weights.astype(BF16).astype(F32), (8, side))


def second_compare(group, k, reference_of):
    ctf, spectra, _ = group
    side = ctf.shape[1]
    cross = model = jnp.zeros((8, side), F32)
    for rows in chunks_of(side):
        values = spectra[k, rows, :].astype(F32)
        reference = reference_of(rows, values)
        predicted = ctf[k, rows, :] * reference.astype(F32)
        cross = cross + fold(predicted * values)
        model = model + fold(predicted * predicted)
    return cross, model


def update_and_compare(info, group, weight, sums, source, target):
    ctf, spectra, first = group

    @pl.loop(0, spectra.shape[0])
    def _(k):
        s = first + k
        p = info[PLACE, s]

        def keep(cross, model):
            sums[0, pl.ds(s, 1), :] = jnp.sum(cross, axis=0, keepdims=True)
            sums[1, pl.ds(s, 1), :] = jnp.sum(model, axis=0, keepdims=True)

        @pl.when(info[ALONE, s] > 0)
        def _():
            scale = weight[pl.ds(s, 1), :]

            def new(rows, values):
                term, power, _ = shares(ctf, scale, k, rows, values)
                reference = renew(source[p, rows, :], term, power)
                target[p, rows, :] = reference
                return reference

            keep(*second_compare(group, k, new))

        @pl.when((info[ACTIVE, s] > 0) & (info[ALONE, s] == 0))
        def _():
            keep(*second_compare(group, k, lambda rows, _: target[p, rows, :]))


def ready_kernel(bin_count, steps, focus_ref, damping_ref, current_ref, *rest):
    arrived, rest = rest[: len(steps)], rest[len(steps) :]
    ctf, spectra, spectra_hbm, weight, middle, sums, number, info, sem = rest
    own_bins, side, _ = current_ref.shape
    labels = labels_of(arrived)
    decode(labels, steps, bin_count, own_bins, info)
    factors = ctf_factors(labels, focus_ref, damping_ref, side)
    sums[...] = jnp.zeros(sums.shape, F32)
    group = (ctf, spectra, 0)
    for s in range(len(labels)):

        @pl.when(info[ACTIVE, s] > 0)
        def _(s=s):
            capacity = len(labels) // len(steps)
            block = arrived[s // capacity].at[s % capacity]
            first_compare(info, factors, current_ref, group, sums, s, block)

    copy = pltpu.make_async_copy(spectra, spectra_hbm, sem)
    copy.start()
    weight[...] = correlate(sums, side)[1]
    update_shared(info, (group,), weight, number, current_ref, middle)
    update_and_compare(info, group, weight, sums, current_ref, middle)
    copy.wait()


def ready_call(bin_count, steps, defocus, bfactor, references, arrived):
    own_bins, side, _ = references.shape
    slots = len(steps) * arrived[0].shape[0]
    return pl.pallas_call(
        functools.partial(ready_kernel, bin_count, steps),
        out_shape=[
            jax.ShapeDtypeStruct((slots, side, side), F32),
            jax.ShapeDtypeStruct((slots, side, side), BF16),
            pltpu.HBM((slots, side, side), BF16),
            jax.ShapeDtypeStruct((8, side), F32),
            jax.ShapeDtypeStruct(references.shape, BF16),
            jax.ShapeDtypeStruct((3, 8, side), F32),
        ],
        in_specs=[VMEM] * (3 + len(steps)),
        out_specs=[VMEM, VMEM, HBM, VMEM, VMEM, VMEM],
        scratch_shapes=[
            pltpu.VMEM((2, side, side), F32),
            pltpu.SMEM((INFOS, max(8, own_bins)), jnp.int32),
            pltpu.SemaphoreType.DMA(()),
        ],
        compiler_params=pltpu.CompilerParams(vmem_limit_bytes=VMEM_BYTES),
        name="ready",
    )(defocus, bfactor, references, *arrived)


def owner_kernel(bin_count, steps, focus_ref, damping_ref, current_ref, *rest):
    arrived, rest = rest[: len(steps)], rest[len(steps) :]
    early_ctf, early_spectra, early_weight, early_middle, early_sums = rest[:5]
    spectra_hbm, middle_hbm, weight, label_ref, score_ref = rest[5:10]
    ctf, spectra, middle, sums, number, info, spectra_sem, middle_sem = rest[10:]
    own_bins, side, _ = current_ref.shape
    capacity = arrived[0].shape[0]
    early = early_ctf.shape[0]
    late = len(steps) - early // capacity
    late_block = arrived[-1]

    spectra_copy = pltpu.make_async_copy(spectra, spectra_hbm, spectra_sem)
    labels = labels_of(arrived)
    for s, label in enumerate(labels):
        label_ref[s] = label
    decode(labels, steps, bin_count, own_bins, info, late)

    def early_copy(p):
        return pltpu.make_async_copy(early_middle.at[p], middle_hbm.at[p], middle_sem.at[p])

    def late_copy(p):
        return pltpu.make_async_copy(middle.at[p], middle_hbm.at[p], middle_sem.at[p])

    @pl.loop(0, own_bins)
    def _(p):
        @pl.when((info[MEMBERS, p] > 0) & (info[LATE, p] == 0))
        def _():
            early_copy(p).start()

    factors = ctf_factors(labels, focus_ref, damping_ref, side)
    sums[...] = early_sums[...]
    early_group, late_group = (early_ctf, early_spectra, 0), (ctf, spectra, early)
    for s in range(early, len(labels)):

        @pl.when(info[ACTIVE, s] > 0)
        def _(s=s):
            block = late_block.at[s - early]
            first_compare(info, factors, current_ref, late_group, sums, s, block)

    spectra_copy.start()
    row = lax.broadcasted_iota(jnp.int32, (8, side), 0)
    weight[...] = jnp.where(row < early, early_weight[...], correlate(sums, side)[1])
    update_shared(
        info, (early_group, late_group), weight, number, current_ref, middle, kind=LATE
    )
    update_and_compare(info, late_group, weight, sums, current_ref, middle)

    @pl.loop(0, early)
    def _(s):
        p = info[PLACE, s]

        @pl.when((info[ACTIVE, s] > 0) & (info[LATE, p] > 0))
        def _():
            cross, model = second_compare(early_group, s, lambda rows, _: middle[p, rows, :])
            sums[0, pl.ds(s, 1), :] = jnp.sum(cross, axis=0, keepdims=True)
            sums[1, pl.ds(s, 1), :] = jnp.sum(model, axis=0, keepdims=True)

    @pl.loop(0, own_bins)
    def _(p):
        @pl.when(info[LATE, p] > 0)
        def _():
            late_copy(p).start()

    correlation, weight[...] = correlate(sums, side)
    score_ref[...] = jnp.zeros(score_ref.shape, F32)
    lane = lax.broadcasted_iota(jnp.int32, (1, 128), 1)
    for s in range(len(labels)):

        @pl.when(info[ACTIVE, s] > 0)
        def _(s=s):
            score = jnp.where(lane == info[PARTICLE, s], correlation[s : s + 1, :], 0.0)
            score_ref[info[HOME, s]] = score

    spectra_copy.wait()

    @pl.loop(0, own_bins)
    def _(p):
        @pl.when(info[MEMBERS, p] > 0)
        def _():
            late_copy(p).wait()


def owner_call(bin_count, steps, defocus, bfactor, references, arrived, early):
    own_bins, side, _ = references.shape
    capacity = arrived[0].shape[0]
    slots = len(steps) * capacity
    late = slots - early[0].shape[0]
    return pl.pallas_call(
        functools.partial(owner_kernel, bin_count, steps),
        out_shape=[
            pltpu.HBM((late, side, side), BF16),
            pltpu.HBM(references.shape, BF16),
            jax.ShapeDtypeStruct((8, side), F32),
            jax.ShapeDtypeStruct((slots, LABEL_ROWS, 128), F32),
            jax.ShapeDtypeStruct((len(steps) * bin_count, 1, 128), F32),
        ],
        in_specs=[VMEM] * (3 + len(steps) + len(early)),
        out_specs=[HBM, HBM, VMEM, VMEM, VMEM],
        scratch_shapes=[
            pltpu.VMEM((late, side, side), F32),
            pltpu.VMEM((late, side, side), BF16),
            pltpu.VMEM(references.shape, BF16),
            pltpu.VMEM((3, 8, side), F32),
            pltpu.VMEM((2, side, side), F32),
            pltpu.SMEM((INFOS, max(8, own_bins)), jnp.int32),
            pltpu.SemaphoreType.DMA(()),
            pltpu.SemaphoreType.DMA((own_bins,)),
        ],
        compiler_params=pltpu.CompilerParams(vmem_limit_bytes=VMEM_BYTES),
        name="owner",
    )(defocus, bfactor, references, *arrived, *early)


def last_kernel(
    bin_count,
    steps,
    focus_ref,
    damping_ref,
    current_ref,
    weight,
    label_ref,
    early_hbm,
    late_hbm,
    middle_hbm,
    refined_ref,
    spectra,
    middle,
    ctf,
    number,
    info,
    sem,
):
    slots, side, _ = ctf.shape
    own_bins = current_ref.shape[0]
    early = early_hbm.shape[0]
    copies = [
        pltpu.make_async_copy(early_hbm, spectra.at[pl.ds(0, early)], sem.at[0]),
        pltpu.make_async_copy(late_hbm, spectra.at[pl.ds(early, slots - early)], sem.at[1]),
        pltpu.make_async_copy(middle_hbm, middle, sem.at[2]),
    ]
    for copy in copies:
        copy.start()
    labels = [label_ref[s] for s in range(slots)]
    decode(labels, steps, bin_count, own_bins, info)
    factors = ctf_factors(labels, focus_ref, damping_ref, side)
    for s in range(slots):

        @pl.when(info[ACTIVE, s] > 0)
        def _(s=s):
            for rows in chunks_of(side):
                ctf[s, rows, :] = ctf_chunk(factors, s, rows)

    for copy in copies:
        copy.wait()
    update_shared(info, ((ctf, spectra, 0),), weight, number, middle, refined_ref)

    @pl.loop(0, slots)
    def _(s):
        @pl.when(info[ALONE, s] > 0)
        def _():
            p = info[PLACE, s]
            scale = weight[pl.ds(s, 1), :]
            for rows in chunks_of(side):
                values = spectra[s, rows, :].astype(F32)
                term, power, _ = shares(ctf, scale, s, rows, values)
                refined_ref[p, rows, :] = renew(middle[p, rows, :], term, power)

    @pl.loop(0, own_bins)
    def _(p):
        @pl.when(info[MEMBERS, p] == 0)
        def _():
            refined_ref[p] = current_ref[p]


def last_call(bin_count, steps, defocus, bfactor, references, weight, labels, kept):
    own_bins, side, _ = references.shape
    slots = labels.shape[0]
    return pl.pallas_call(
        functools.partial(last_kernel, bin_count, steps),
        out_shape=jax.ShapeDtypeStruct(references.shape, BF16),
        in_specs=[VMEM] * 5 + [HBM] * 3,
        out_specs=VMEM,
        scratch_shapes=[
            pltpu.VMEM((slots, side, side), BF16),
            pltpu.VMEM(references.shape, BF16),
            pltpu.VMEM((slots, side, side), F32),
            pltpu.VMEM((2, side, side), F32),
            pltpu.SMEM((INFOS, max(8, own_bins)), jnp.int32),
            pltpu.SemaphoreType.DMA((3,)),
        ],
        compiler_params=pltpu.CompilerParams(vmem_limit_bytes=VMEM_BYTES),
        cost_estimate=pl.CostEstimate(flops=4 << 20, bytes_accessed=4 << 20, transcendentals=0),
        name="last",
    )(defocus, bfactor, references, weight, labels, *map(in_hbm, kept))


def exchange(blocks, axis):
    size = lax.axis_size(axis)
    return [blocks[0]] + [
        lax.ppermute(blocks[k], axis, [(i, i ^ k) for i in range(size)]) for k in range(1, size)
    ]


def body(images, offsets, ctf_group, particle_bin, bin_place, defocus, bfactor, references):
    mic_count = lax.axis_size("mic")
    bin_count = lax.axis_size("bin")
    particles, side, _ = images.shape
    own_bins = references.shape[0]
    capacity = (3 * particles + 2 * mic_count - 1) // (2 * mic_count)

    basis = jnp.asarray(hartley(side), BF16)
    operands = (bin_place, particle_bin, ctf_group, offsets, images, basis)
    operands = tuple(map(in_hbm, operands))
    far = max(1, bin_count // 4)
    rest = bin_count - far
    sent_far = home_call(bin_count, own_bins, rest, far, operands)
    sent_near = home_call(bin_count, own_bins, 0, rest, operands, after=(sent_far[-1],))
    arrived = exchange(list(sent_near) + list(sent_far), "bin")

    sent = middle_call(mic_count, capacity, arrived[::-1])
    arrived = exchange(sent, "mic")
    steps = [t for t in range(mic_count) if t != mic_count // 2] + [mic_count // 2]
    arrived = [arrived[t] for t in steps]
    tables = (defocus.reshape(1, -1), bfactor.reshape(1, -1), references)
    ctf, spectra, kept, *known = ready_call(bin_count, steps[:-1], *tables, arrived[:-1])
    late, middle, weight, labels, board = owner_call(
        bin_count, steps, *tables, arrived, (ctf, spectra, *known)
    )
    back = lax.all_to_all(board, ("mic", "bin"), split_axis=0, concat_axis=0, tiled=True)
    refined = last_call(bin_count, steps, *tables, weight, labels, (kept, late, middle))
    return (refined, jnp.sum(back, axis=(0, 1))[:particles])


def solution(mesh):
    in_specs = (
        P(("mic", "bin"), None, None),
        P(None, ("mic", "bin")),
        P(("mic", "bin")),
        P(("mic", "bin")),
        P(),
        P(),
        P(),
        P(("mic", "bin"), None, None),
    )
    out_specs = (P(("mic", "bin"), None, None), P(("mic", "bin")))
    return jax.shard_map(body, mesh=mesh, in_specs=in_specs, out_specs=out_specs, check_vma=False)
```

time: 63.1 us -> 61.9 us (0.981)
  waiting for transfers between devices: 23.3 us -> 20.1 us
  Pallas kernels: 11.6 us -> 13.4 us
    ppermute x10, waiting for transfers between devices: 19.9 us -> 16.8 us  [exchange(): lax.ppermute(blocks[k], axis, [(i, i ^ k) for i in range(size)])]
    pallas_call x2 -> x3, Pallas kernels: 7.16 us -> 8.84 us  [the longest x1 3.81 us: last_call(): pl.pallas_call(functools.partial(last_kernel, bin_count, steps), out_shap...]
    ppermute x10, starting transfers between devices: 21.7 us -> 22.5 us  [exchange(): lax.ppermute(blocks[k], axis, [(i, i ^ k) for i in range(size)])]
    all_to_all x1, starting transfers between devices: 5.33 us -> 4.65 us  [body(): lax.all_to_all(board, ('mic', 'bin'), split_axis=0, concat_axis=0, tiled=...]
  transfers between devices with their start and end apart: 11 -> 11, of which waited for: 5 -> 6; matrix products, arithmetic and copies ran while one was open for 0% -> 0% of each run, Pallas kernels for 9% -> 13%
where the time goes in v6:
time: 61.9 us
  starting transfers between devices  27.2 us (44%)
  waiting for transfers between devices  20.1 us (32%)
  Pallas kernels  13.4 us (22%)
  between operations  0.73 us (1%)
    ppermute x10, starting transfers between devices, exchange(): lax.ppermute(blocks[k], axis, [(i, i ^ k) for i in range(size)])  22.5 us
    ppermute x10, waiting for transfers between devices, exchange(): lax.ppermute(blocks[k], axis, [(i, i ^ k) for i in range(size)])  16.8 us
    all_to_all x1, starting transfers between devices, body(): lax.all_to_all(board, ('mic', 'bin'), split_axis=0, concat_axis=0, tiled=...  4.65 us
    pallas_call x2, Pallas kernels, home_call(): pl.pallas_call(functools.partial(home_kernel, bin_count, own_bins, first,...  4.13 us
    pallas_call x1, Pallas kernels, last_call(): pl.pallas_call(functools.partial(last_kernel, bin_count, steps), out_shap...  3.81 us
    all_to_all x1, waiting for transfers between devices, body(): lax.all_to_all(board, ('mic', 'bin'), split_axis=0, concat_axis=0, tiled=...  3.29 us
    pallas_call x1, Pallas kernels, owner_call(): pl.pallas_call(functools.partial(owner_kernel, bin_count, steps), out_sha...  3.02 us
    pallas_call x1, Pallas kernels, ready_call(): pl.pallas_call(functools.partial(ready_kernel, bin_count, steps), out_sha...  2.01 us
  transfers between devices with their start and end apart: 11, of which 6 were waited for; matrix products, arithmetic and copies ran while one was open for 0% of the time, Pallas kernels for 13%

profile of v6, /device:TPU:0, one launch (start us, length us, event | category | flops | bytes accessed | tf_op | source)
XLA Modules:
  0.0 61.9 jit_solution(9381187053952091003)
XLA Ops:
  0.7 1.7 %home.2 = (bf16[520,128]{1,0:T(8,128)(2,1)S(1)}, bf16[520,128]{1,0:T(8,128)(2,1)S(1)}) custom-call(s32[256]{0:T(256)} %place_hbm.3, s32[4]{0:T(128)} %bin_hbm.3, s32[4]{0:T(128)} %group_hbm.3, s32[2,4]{1,0:T(2,128)} %offset_hbm.3, bf16[4,256,256]{2,1,0:T(8,128)(2,1)} %image_hbm.3, bf16[256,256]{1,0:T(8,128)(2,1)} %constant.4.clone.basis_hbm), custom_call_target="tpu_custom_call" | custom-call | tf_op jit(solution)/shard_map/home/pallas_call | solution.py:116
  2.3 5.2 %collective-permute-start.1 = (bf16[520,128]{1,0:T(8,128)(2,1)S(1)}, bf16[520,128]{1,0:T(8,128)(2,1)S(1)}, u32[]{:S(2)}, u32[]{:S(2)}) collective-permute-start(bf16[520,128]{1,0:T(8,128)(2,1)S(1)} %get-tuple-element.26), channel_id=1, source_target_pairs={{0,6},{1,7},{2,4},{3,5},{4,2},{5,3},{6,0},{7,1},{8,14},{9,15},{10,... | collective-permute-start | bytes 399368 | tf_op jit(solution)/shard_map/ppermute | solution.py:601
  7.5 1.1 %collective-permute-start = (bf16[520,128]{1,0:T(8,128)(2,1)S(1)}, bf16[520,128]{1,0:T(8,128)(2,1)S(1)}, u32[]{:S(2)}, u32[]{:S(2)}) collective-permute-start(bf16[520,128]{1,0:T(8,128)(2,1)S(1)} %get-tuple-element.25.rest_0_), channel_id=1, source_target_pairs={{0,7},{1,6},{2,5},{3,4},{4,3},{5,2},{6,1},{7,0},{8,15},{9,14},{10,... | collective-permute-start | bytes 399368 | tf_op jit(solution)/shard_map/ppermute | solution.py:601
  8.6 2.5 %home.3 = (bf16[520,128]{1,0:T(8,128)(2,1)S(1)}, bf16[520,128]{1,0:T(8,128)(2,1)S(1)}, bf16[520,128]{1,0:T(8,128)(2,1)S(1)}, bf16[520,128]{1,0:T(8,128)(2,1)S(1)...) custom-call(s32[256]{0:T(256)} %place_hbm.3, s32[4]{0:T(128)} %bin_hbm.3, s32[4]{0:T(128)} %group_hbm.3, ...), custom_call_target="tpu_custom_call" | custom-call | tf_op jit(solution)/shard_map/home/pallas_call | solution.py:116
  11.1 0.8 %collective-permute-start.2 = (bf16[520,128]{1,0:T(8,128)(2,1)S(1)}, bf16[520,128]{1,0:T(8,128)(2,1)S(1)}, u32[]{:S(2)}, u32[]{:S(2)}) collective-permute-start(bf16[520,128]{1,0:T(8,128)(2,1)S(1)} %get-tuple-element.27), channel_id=1, source_target_pairs={{0,5},{1,4},{2,7},{3,6},{4,1},{5,0},{6,3},{7,2},{8,13},{9,12},{10,... | collective-permute-start | bytes 399368 | tf_op jit(solution)/shard_map/ppermute | solution.py:601
  11.9 2.1 %collective-permute-start.3 = (bf16[520,128]{1,0:T(8,128)(2,1)S(1)}, bf16[520,128]{1,0:T(8,128)(2,1)S(1)}, u32[]{:S(2)}, u32[]{:S(2)}) collective-permute-start(bf16[520,128]{1,0:T(8,128)(2,1)S(1)} %get-tuple-element.28), channel_id=1, source_target_pairs={{0,4},{1,5},{2,6},{3,7},{4,0},{5,1},{6,2},{7,3},{8,12},{9,13},{10,... | collective-permute-start | bytes 399368 | tf_op jit(solution)/shard_map/ppermute | solution.py:601
  14.0 1.9 %collective-permute-start.4 = (bf16[520,128]{1,0:T(8,128)(2,1)S(1)}, bf16[520,128]{1,0:T(8,128)(2,1)S(1)}, u32[]{:S(2)}, u32[]{:S(2)}) collective-permute-start(bf16[520,128]{1,0:T(8,128)(2,1)S(1)} %get-tuple-element.29), channel_id=1, source_target_pairs={{0,3},{1,2},{2,1},{3,0},{4,7},{5,6},{6,5},{7,4},{8,11},{9,10},{10,... | collective-permute-start | bytes 399368 | tf_op jit(solution)/shard_map/ppermute | solution.py:601
  15.9 6.5 %collective-permute-start.5 = (bf16[520,128]{1,0:T(8,128)(2,1)S(1)}, bf16[520,128]{1,0:T(8,128)(2,1)S(1)}, u32[]{:S(2)}, u32[]{:S(2)}) collective-permute-start(bf16[520,128]{1,0:T(8,128)(2,1)S(1)} %get-tuple-element.30), channel_id=1, source_target_pairs={{0,2},{1,3},{2,0},{3,1},{4,6},{5,7},{6,4},{7,5},{8,10},{9,11},{10,... | collective-permute-start | bytes 399368 | tf_op jit(solution)/shard_map/ppermute | solution.py:601
  22.4 2.0 %collective-permute-start.6 = (bf16[520,128]{1,0:T(8,128)(2,1)S(1)}, bf16[520,128]{1,0:T(8,128)(2,1)S(1)}, u32[]{:S(2)}, u32[]{:S(2)}) collective-permute-start(bf16[520,128]{1,0:T(8,128)(2,1)S(1)} %get-tuple-element.31), channel_id=1, source_target_pairs={{0,1},{1,0},{2,3},{3,2},{4,5},{5,4},{6,7},{7,6},{8,9},{9,8},{10,11... | collective-permute-start | bytes 399368 | tf_op jit(solution)/shard_map/ppermute | solution.py:601
  24.4 5.4 %collective-permute-done.2.rest_2_ = bf16[520,128]{1,0:T(8,128)(2,1)S(1)} collective-permute-done((bf16[520,128]{1,0:T(8,128)(2,1)S(1)}, bf16[520,128]{1,0:T(8,128)(2,1)S(1)}, u32[]{:S(2)}, u32[]{:S(2)}) %collective-permute-start.2) | collective-permute-done | bytes 133152 | tf_op jit(solution)/shard_map/ppermute | solution.py:601
  29.8 0.1 collective-permute-done.3.rest_3_
  29.9 0.7 %collective-permute-done.5.rest_5_ = bf16[520,128]{1,0:T(8,128)(2,1)S(1)} collective-permute-done((bf16[520,128]{1,0:T(8,128)(2,1)S(1)}, bf16[520,128]{1,0:T(8,128)(2,1)S(1)}, u32[]{:S(2)}, u32[]{:S(2)}) %collective-permute-start.5) | collective-permute-done | bytes 133152 | tf_op jit(solution)/shard_map/ppermute | solution.py:601
  30.6 0.4 middle.1
  31.0 0.1 collective-permute-start.7
  31.1 2.8 %collective-permute-start.8 = (bf16[2,520,128]{2,1,0:T(8,128)(2,1)S(1)}, bf16[2,520,128]{2,1,0:T(8,128)(2,1)S(1)}, u32[]{:S(2)}, u32[]{:S(2)}) collective-permute-start(bf16[2,520,128]{2,1,0:T(8,128)(2,1)S(1)} %get-tuple-element.35), channel_id=1, source_target_pairs={{0,24},{8,16},{16,8},{24,0},{1,25},{9,17},{17,9},{25,1},{2,26},{10... | collective-permute-start | bytes 798728 | tf_op jit(solution)/shard_map/ppermute | solution.py:601
  33.9 0.0 collective-permute-start.9
  34.0 6.7 %collective-permute-done.8.rest_2_ = bf16[2,520,128]{2,1,0:T(8,128)(2,1)S(1)} collective-permute-done((bf16[2,520,128]{2,1,0:T(8,128)(2,1)S(1)}, bf16[2,520,128]{2,1,0:T(8,128)(2,1)S(1)}, u32[]{:S(2)}, u32[]{:S(2)}) %collective-permute-start.8) | collective-permute-done | bytes 266272 | tf_op jit(solution)/shard_map/ppermute | solution.py:601
  40.6 2.0 %ready.1 = (f32[6,256,256]{2,1,0:T(8,128)S(1)}, bf16[6,256,256]{2,1,0:T(8,128)(2,1)S(1)}, bf16[6,256,256]{2,1,0:T(8,128)(2,1)}, f32[8,256]{1,0:T(8,128)S(1)}, bf...) custom-call(f32[1,64]{1,0:T(1,128)S(1)} %bitcast.3, f32[1,64]{1,0:T(1,128)S(1)} %bitcast.6, ...), custom_call_target="tpu_custom_call" | custom-call | tf_op jit(solution)/shard_map/ready/pallas_call | solution.py:380
  42.7 3.9 %collective-permute-done.9.rest_3_ = bf16[2,520,128]{2,1,0:T(8,128)(2,1)S(1)} collective-permute-done((bf16[2,520,128]{2,1,0:T(8,128)(2,1)S(1)}, bf16[2,520,128]{2,1,0:T(8,128)(2,1)S(1)}, u32[]{:S(2)}, u32[]{:S(2)}) %collective-permute-start.9) | collective-permute-done | bytes 266272 | tf_op jit(solution)/shard_map/ppermute | solution.py:601
  46.6 3.0 %owner.1 = (bf16[2,256,256]{2,1,0:T(8,128)(2,1)}, bf16[8,256,256]{2,1,0:T(8,128)(2,1)}, f32[8,256]{1,0:T(8,128)S(1)}, f32[8,8,128]{2,1,0:T(8,128)S(1)}, f32[32,1,128]{2,1,0:T(1,128)}) custom-call(f32[1,64]{1,0:T(1,128)S(1)} %bitcast.4, f32[1,64]{1,0:T(1,128)S(1)} %bitcast.7, bf16[8,256,256]{2,1,0:T(8,128)(2,1)S(1)} %copy-done, ...), custom_call_target="tpu_custom_call" | custom-call | tf_op jit(solution)/shard_map/owner/pallas_call | solution.py:489
  49.6 4.7 %all-to-all-start = ((f32[32,1,128]{2,1,0:T(1,128)}), f32[32,1,128]{2,1,0:T(1,128)S(1)}, u32[]{:S(2)}, u32[]{:S(2)}) async-start(f32[32,1,128]{2,1,0:T(1,128)} %get-tuple-element.47), calls=%async_computation | async-start | bytes 32768 | tf_op jit(solution)/shard_map/all_to_all | solution.py:630
  54.2 3.8 %last.1 = bf16[8,256,256]{2,1,0:T(8,128)(2,1)} custom-call(f32[1,64]{1,0:T(1,128)S(1)} %bitcast.5, f32[1,64]{1,0:T(1,128)S(1)} %bitcast.8, bf16[8,256,256]{2,1,0:T(8,128)(2,1)S(1)} %copy-done, f32[8,256]{1,0:T(8,128)S(1)} %get-tuple-element.42.weight, f32[8,8,128]{2,1,0:T(8,128)S(1)} %get-tuple-element.43.label_ref, ...), custom_call_target="tpu_custom_call" | custom-call | flops 4194304 | bytes 4194304 | tf_op jit(solution)/shard_map/last/pallas_call | solution.py:579
  58.1 3.3 %all-to-all-done = f32[32,1,128]{2,1,0:T(1,128)S(1)} async-done(((f32[32,1,128]{2,1,0:T(1,128)}), f32[32,1,128]{2,1,0:T(1,128)S(1)}, u32[]{:S(2)}, u32[]{:S(2)}) %all-to-all-start) | async-done | bytes 16416 | tf_op jit(solution)/shard_map/all_to_all | solution.py:630
  61.4 0.6 reduce_sum.9
  (11 shorter events, 0.0 us)
Async XLA Ops:
  0.6 40.0 %copy-start = (bf16[8,256,256]{2,1,0:T(8,128)(2,1)S(1)}, bf16[8,256,256]{2,1,0:T(8,128)(2,1)}, u32[]{:S(2)}) copy-start(bf16[8,256,256]{2,1,0:T(8,128)(2,1)} %current_ref.5) | copy-start | bytes 3145732
  0.6 40.0 %copy-start.2 = (f32[64]{0:T(128)S(1)}, f32[64]{0:T(128)}, u32[]{:S(2)}) copy-start(f32[64]{0:T(128)} %param.15) | copy-start | bytes 772
  0.7 40.0 %copy-start.1 = (f32[64]{0:T(128)S(1)}, f32[64]{0:T(128)}, u32[]{:S(2)}) copy-start(f32[64]{0:T(128)} %param.14) | copy-start | bytes 772
  2.3 13.5 %collective-permute-start.1 = (bf16[520,128]{1,0:T(8,128)(2,1)S(1)}, bf16[520,128]{1,0:T(8,128)(2,1)S(1)}, u32[]{:S(2)}, u32[]{:S(2)}) collective-permute-start(bf16[520,128]{1,0:T(8,128)(2,1)S(1)} %get-tuple-element.26), channel_id=1, source_target_pairs={{0,6},{1,7},{2,4},{3,5},{4,2},{5,3},{6,0},{7,1},{8,14},{9,15},{10,... | collective-permute-start | bytes 399368 | tf_op jit(solution)/shard_map/ppermute | solution.py:601
  7.5 14.9 %collective-permute-start = (bf16[520,128]{1,0:T(8,128)(2,1)S(1)}, bf16[520,128]{1,0:T(8,128)(2,1)S(1)}, u32[]{:S(2)}, u32[]{:S(2)}) collective-permute-start(bf16[520,128]{1,0:T(8,128)(2,1)S(1)} %get-tuple-element.25.rest_0_), channel_id=1, source_target_pairs={{0,7},{1,6},{2,5},{3,4},{4,3},{5,2},{6,1},{7,0},{8,15},{9,14},{10,... | collective-permute-start | bytes 399368 | tf_op jit(solution)/shard_map/ppermute | solution.py:601
  11.1 18.7 %collective-permute-start.2 = (bf16[520,128]{1,0:T(8,128)(2,1)S(1)}, bf16[520,128]{1,0:T(8,128)(2,1)S(1)}, u32[]{:S(2)}, u32[]{:S(2)}) collective-permute-start(bf16[520,128]{1,0:T(8,128)(2,1)S(1)} %get-tuple-element.27), channel_id=1, source_target_pairs={{0,5},{1,4},{2,7},{3,6},{4,1},{5,0},{6,3},{7,2},{8,13},{9,12},{10,... | collective-permute-start | bytes 399368 | tf_op jit(solution)/shard_map/ppermute | solution.py:601
  11.9 18.0 %collective-permute-start.3 = (bf16[520,128]{1,0:T(8,128)(2,1)S(1)}, bf16[520,128]{1,0:T(8,128)(2,1)S(1)}, u32[]{:S(2)}, u32[]{:S(2)}) collective-permute-start(bf16[520,128]{1,0:T(8,128)(2,1)S(1)} %get-tuple-element.28), channel_id=1, source_target_pairs={{0,4},{1,5},{2,6},{3,7},{4,0},{5,1},{6,2},{7,3},{8,12},{9,13},{10,... | collective-permute-start | bytes 399368 | tf_op jit(solution)/shard_map/ppermute | solution.py:601
  14.0 15.9 %collective-permute-start.4 = (bf16[520,128]{1,0:T(8,128)(2,1)S(1)}, bf16[520,128]{1,0:T(8,128)(2,1)S(1)}, u32[]{:S(2)}, u32[]{:S(2)}) collective-permute-start(bf16[520,128]{1,0:T(8,128)(2,1)S(1)} %get-tuple-element.29), channel_id=1, source_target_pairs={{0,3},{1,2},{2,1},{3,0},{4,7},{5,6},{6,5},{7,4},{8,11},{9,10},{10,... | collective-permute-start | bytes 399368 | tf_op jit(solution)/shard_map/ppermute | solution.py:601
  15.9 14.7 %collective-permute-start.5 = (bf16[520,128]{1,0:T(8,128)(2,1)S(1)}, bf16[520,128]{1,0:T(8,128)(2,1)S(1)}, u32[]{:S(2)}, u32[]{:S(2)}) collective-permute-start(bf16[520,128]{1,0:T(8,128)(2,1)S(1)} %get-tuple-element.30), channel_id=1, source_target_pairs={{0,2},{1,3},{2,0},{3,1},{4,6},{5,7},{6,4},{7,5},{8,10},{9,11},{10,... | collective-permute-start | bytes 399368 | tf_op jit(solution)/shard_map/ppermute | solution.py:601
  22.4 8.2 %collective-permute-start.6 = (bf16[520,128]{1,0:T(8,128)(2,1)S(1)}, bf16[520,128]{1,0:T(8,128)(2,1)S(1)}, u32[]{:S(2)}, u32[]{:S(2)}) collective-permute-start(bf16[520,128]{1,0:T(8,128)(2,1)S(1)} %get-tuple-element.31), channel_id=1, source_target_pairs={{0,1},{1,0},{2,3},{3,2},{4,5},{5,4},{6,7},{7,6},{8,9},{9,8},{10,11... | collective-permute-start | bytes 399368 | tf_op jit(solution)/shard_map/ppermute | solution.py:601
  31.0 2.9 %collective-permute-start.7 = (bf16[2,520,128]{2,1,0:T(8,128)(2,1)S(1)}, bf16[2,520,128]{2,1,0:T(8,128)(2,1)S(1)}, u32[]{:S(2)}, u32[]{:S(2)}) collective-permute-start(bf16[2,520,128]{2,1,0:T(8,128)(2,1)S(1)} %get-tuple-element.34), channel_id=1, source_target_pairs={{0,8},{8,0},{16,24},{24,16},{1,9},{9,1},{17,25},{25,17},{2,10},{10... | collective-permute-start | bytes 798728 | tf_op jit(solution)/shard_map/ppermute | solution.py:601
  31.1 9.5 %collective-permute-start.8 = (bf16[2,520,128]{2,1,0:T(8,128)(2,1)S(1)}, bf16[2,520,128]{2,1,0:T(8,128)(2,1)S(1)}, u32[]{:S(2)}, u32[]{:S(2)}) collective-permute-start(bf16[2,520,128]{2,1,0:T(8,128)(2,1)S(1)} %get-tuple-element.35), channel_id=1, source_target_pairs={{0,24},{8,16},{16,8},{24,0},{1,25},{9,17},{17,9},{25,1},{2,26},{10... | collective-permute-start | bytes 798728 | tf_op jit(solution)/shard_map/ppermute | solution.py:601
  33.9 12.6 %collective-permute-start.9 = (bf16[2,520,128]{2,1,0:T(8,128)(2,1)S(1)}, bf16[2,520,128]{2,1,0:T(8,128)(2,1)S(1)}, u32[]{:S(2)}, u32[]{:S(2)}) collective-permute-start(bf16[2,520,128]{2,1,0:T(8,128)(2,1)S(1)} %get-tuple-element.36), channel_id=1, source_target_pairs={{0,16},{8,24},{16,0},{24,8},{1,17},{9,25},{17,1},{25,9},{2,18},{10... | collective-permute-start | bytes 798728 | tf_op jit(solution)/shard_map/ppermute | solution.py:601
  49.6 11.8 %all-to-all-start = ((f32[32,1,128]{2,1,0:T(1,128)}), f32[32,1,128]{2,1,0:T(1,128)S(1)}, u32[]{:S(2)}, u32[]{:S(2)}) async-start(f32[32,1,128]{2,1,0:T(1,128)} %get-tuple-element.47), calls=%async_computation | async-start | bytes 32768 | tf_op jit(solution)/shard_map/all_to_all | solution.py:630

commit v7 on v6

--- a/solution.py
+++ b/solution.py
@@ -133,13 +133,14 @@
     )(*operands, *after)
 
 
-def middle_kernel(mic_count, capacity, *rest):
-    arrived, outs = rest[: len(rest) - mic_count], rest[len(rest) - mic_count :]
+def middle_kernel(mic_count, sizes, *rest):
+    arrived, flat = rest[: len(rest) - sum(map(len, sizes))], list(rest[-sum(map(len, sizes)) :])
+    outs = [[flat.pop(0) for _ in parts] for parts in sizes]
     rows = arrived[0].shape[0]
     here = lax.axis_index("mic")
     empty = jnp.zeros((LABEL_ROWS, LANES), BF16)
-    for out in outs:
-        for j in range(capacity):
+    for out in sum(outs, []):
+        for j in range(out.shape[0]):
             out[j, rows - LABEL_ROWS : rows, :] = empty
     targets = [
         jnp.max(block[rows - LABEL_ROWS : rows, :].astype(F32)[0:1]).astype(jnp.int32)
@@ -150,23 +151,34 @@
         step_of = (target - 1) ^ here
         for step in range(mic_count):
             chosen = (target > 0) & (step_of == step)
-
-            @pl.when(chosen)
-            def _(block=block, step=step, slot=counts[step]):
-                outs[step][slot] = block[...]
+            if len(outs[step]) == 1:
+
+                @pl.when(chosen)
+                def _(block=block, out=outs[step][0], slot=counts[step]):
+                    out[slot] = block[...]
+
+            else:
+                for j, out in enumerate(outs[step]):
+
+                    @pl.when(chosen & (counts[step] == j))
+                    def _(block=block, out=out):
+                        out[0] = block[...]
 
             counts[step] = counts[step] + chosen.astype(jnp.int32)
 
 
-def middle_call(mic_count, capacity, arrived):
-    return pl.pallas_call(
-        functools.partial(middle_kernel, mic_count, capacity),
-        out_shape=[jax.ShapeDtypeStruct((capacity, *arrived[0].shape), BF16)] * mic_count,
+def middle_call(mic_count, sizes, arrived):
+    flat = sum(sizes, [])
+    outs = pl.pallas_call(
+        functools.partial(middle_kernel, mic_count, sizes),
+        out_shape=[jax.ShapeDtypeStruct((n, *arrived[0].shape), BF16) for n in flat],
         in_specs=[VMEM] * len(arrived),
-        out_specs=[VMEM] * mic_count,
+        out_specs=[VMEM] * len(flat),
         compiler_params=pltpu.CompilerParams(vmem_limit_bytes=VMEM_BYTES),
         name="middle",
     )(*arrived)
+    outs = list(outs)
+    return [[outs.pop(0) for _ in parts] for parts in sizes]
 
 
 def fold(values):
@@ -218,7 +230,6 @@
 
 def decode(labels, steps, bin_count, own_bins, info, late=0):
     slots = len(labels)
-    capacity = slots // len(steps)
     here = lax.axis_index("mic")
     codes = []
     for block in labels:
@@ -234,10 +245,10 @@
         place = code & 255
         info[ACTIVE, s] = active
         info[PLACE, s] = place
-        info[HOME, s] = (here ^ steps[s // capacity]) * bin_count + lax.rem(sender, bin_count)
+        info[HOME, s] = (here ^ steps[s]) * bin_count + lax.rem(sender, bin_count)
         info[PARTICLE, s] = sender // bin_count
         info[MEMBERS, place] = info[MEMBERS, place] + active
-        if s >= slots - late * capacity:
+        if s >= slots - late:
             info[LATE, place] = info[LATE, place] + active
     for s in range(slots):
         single = (info[ACTIVE, s] > 0) & (info[MEMBERS, info[PLACE, s]] == 1)
@@ -269,12 +280,12 @@
     )
 
 
-def labels_of(arrived):
-    return [
-        block[j, block.shape[1] - LABEL_ROWS :, :].astype(F32)
-        for block in arrived
-        for j in range(block.shape[0])
-    ]
+def blocks_of(arrived):
+    return [block.at[j] for block in arrived for j in range(block.shape[0])]
+
+
+def labels_of(blocks):
+    return [block[block.shape[0] - LABEL_ROWS :, :].astype(F32) for block in blocks]
 
 
 def first_compare(info, factors, current_ref, group, sums, s, block):
@@ -350,10 +361,10 @@
 
 
 def ready_kernel(bin_count, steps, focus_ref, damping_ref, current_ref, *rest):
-    arrived, rest = rest[: len(steps)], rest[len(steps) :]
+    blocks, rest = blocks_of(rest[:-9]), rest[-9:]
     ctf, spectra, spectra_hbm, weight, middle, sums, number, info, sem = rest
     own_bins, side, _ = current_ref.shape
-    labels = labels_of(arrived)
+    labels = labels_of(blocks)
     decode(labels, steps, bin_count, own_bins, info)
     factors = ctf_factors(labels, focus_ref, damping_ref, side)
     sums[...] = jnp.zeros(sums.shape, F32)
@@ -362,9 +373,7 @@
 
         @pl.when(info[ACTIVE, s] > 0)
         def _(s=s):
-            capacity = len(labels) // len(steps)
-            block = arrived[s // capacity].at[s % capacity]
-            first_compare(info, factors, current_ref, group, sums, s, block)
+            first_compare(info, factors, current_ref, group, sums, s, blocks[s])
 
     copy = pltpu.make_async_copy(spectra, spectra_hbm, sem)
     copy.start()
@@ -376,7 +385,7 @@
 
 def ready_call(bin_count, steps, defocus, bfactor, references, arrived):
     own_bins, side, _ = references.shape
-    slots = len(steps) * arrived[0].shape[0]
+    slots = len(steps)
     return pl.pallas_call(
         functools.partial(ready_kernel, bin_count, steps),
         out_shape=[
@@ -387,7 +396,7 @@
             jax.ShapeDtypeStruct(references.shape, BF16),
             jax.ShapeDtypeStruct((3, 8, side), F32),
         ],
-        in_specs=[VMEM] * (3 + len(steps)),
+        in_specs=[VMEM] * (3 + len(arrived)),
         out_specs=[VMEM, VMEM, HBM, VMEM, VMEM, VMEM],
         scratch_shapes=[
             pltpu.VMEM((2, side, side), F32),
@@ -400,21 +409,18 @@
 
 
 def owner_kernel(bin_count, steps, focus_ref, damping_ref, current_ref, *rest):
-    arrived, rest = rest[: len(steps)], rest[len(steps) :]
+    blocks, rest = blocks_of(rest[:-18]), rest[-18:]
     early_ctf, early_spectra, early_weight, early_middle, early_sums = rest[:5]
     spectra_hbm, middle_hbm, weight, label_ref, score_ref = rest[5:10]
     ctf, spectra, middle, sums, number, info, spectra_sem, middle_sem = rest[10:]
     own_bins, side, _ = current_ref.shape
-    capacity = arrived[0].shape[0]
     early = early_ctf.shape[0]
-    late = len(steps) - early // capacity
-    late_block = arrived[-1]
 
     spectra_copy = pltpu.make_async_copy(spectra, spectra_hbm, spectra_sem)
-    labels = labels_of(arrived)
+    labels = labels_of(blocks)
     for s, label in enumerate(labels):
         label_ref[s] = label
-    decode(labels, steps, bin_count, own_bins, info, late)
+    decode(labels, steps, bin_count, own_bins, info, len(steps) - early)
 
     def early_copy(p):
         return pltpu.make_async_copy(early_middle.at[p], middle_hbm.at[p], middle_sem.at[p])
@@ -435,8 +441,7 @@
 
         @pl.when(info[ACTIVE, s] > 0)
         def _(s=s):
-            block = late_block.at[s - early]
-            first_compare(info, factors, current_ref, late_group, sums, s, block)
+            first_compare(info, factors, current_ref, late_group, sums, s, blocks[s])
 
     spectra_copy.start()
     row = lax.broadcasted_iota(jnp.int32, (8, side), 0)
@@ -481,10 +486,9 @@
             late_copy(p).wait()
 
 
-def owner_call(bin_count, steps, defocus, bfactor, references, arrived, early):
+def owner_call(devices, bin_count, steps, defocus, bfactor, references, arrived, early):
     own_bins, side, _ = references.shape
-    capacity = arrived[0].shape[0]
-    slots = len(steps) * capacity
+    slots = len(steps)
     late = slots - early[0].shape[0]
     return pl.pallas_call(
         functools.partial(owner_kernel, bin_count, steps),
@@ -493,9 +497,9 @@
             pltpu.HBM(references.shape, BF16),
             jax.ShapeDtypeStruct((8, side), F32),
             jax.ShapeDtypeStruct((slots, LABEL_ROWS, 128), F32),
-            jax.ShapeDtypeStruct((len(steps) * bin_count, 1, 128), F32),
+            jax.ShapeDtypeStruct((devices, 1, 128), F32),
         ],
-        in_specs=[VMEM] * (3 + len(steps) + len(early)),
+        in_specs=[VMEM] * (3 + len(arrived) + len(early)),
         out_specs=[HBM, HBM, VMEM, VMEM, VMEM],
         scratch_shapes=[
             pltpu.VMEM((late, side, side), F32),
@@ -612,20 +616,25 @@
     basis = jnp.asarray(hartley(side), BF16)
     operands = (bin_place, particle_bin, ctf_group, offsets, images, basis)
     operands = tuple(map(in_hbm, operands))
-    far = max(1, bin_count // 4)
+    far = 3 * bin_count // 8
     rest = bin_count - far
     sent_far = home_call(bin_count, own_bins, rest, far, operands)
     sent_near = home_call(bin_count, own_bins, 0, rest, operands, after=(sent_far[-1],))
     arrived = exchange(list(sent_near) + list(sent_far), "bin")
 
-    sent = middle_call(mic_count, capacity, arrived[::-1])
-    arrived = exchange(sent, "mic")
-    steps = [t for t in range(mic_count) if t != mic_count // 2] + [mic_count // 2]
-    arrived = [arrived[t] for t in steps]
+    last = mic_count - 1
+    sizes = [[1] * capacity if step == 1 else [capacity] for step in range(mic_count)]
+    sent = middle_call(mic_count, sizes, arrived[::-1])
+    blocks = [(0, block) for block in sent[0]]
+    for step in [t for t in range(1, mic_count) if t != last] + [last]:
+        pairs = [(i, i ^ step) for i in range(mic_count)]
+        blocks += [(step, lax.ppermute(block, "mic", pairs)) for block in sent[step]]
+    steps = [step for step, block in blocks for _ in range(block.shape[0])]
+    arrived = [block for _, block in blocks]
     tables = (defocus.reshape(1, -1), bfactor.reshape(1, -1), references)
-    ctf, spectra, kept, *known = ready_call(bin_count, steps[:-1], *tables, arrived[:-1])
+    ctf, spectra, kept, *known = ready_call(bin_count, steps[: -arrived[-1].shape[0]], *tables, arrived[:-1])
     late, middle, weight, labels, board = owner_call(
-        bin_count, steps, *tables, arrived, (ctf, spectra, *known)
+        mic_count * bin_count, bin_count, steps, *tables, arrived, (ctf, spectra, *known)
     )
     back = lax.all_to_all(board, ("mic", "bin"), split_axis=0, concat_axis=0, tiled=True)
     refined = last_call(bin_count, steps, *tables, weight, labels, (kept, late, middle))

time: 61.9 us -> 59.6 us (0.963); the launches traced: 61.9 us -> 58.5 us
  starting transfers between devices: 27.2 us -> 25.6 us
  waiting for transfers between devices: 20.1 us -> 19.2 us
  Pallas kernels: 13.4 us -> 12.5 us
    ppermute x10 -> x7, waiting for transfers between devices: 16.8 us -> 8.26 us  [exchange(): lax.ppermute(blocks[k], axis, [(i, i ^ k) for i in range(size)])]
    ppermute x0 -> x4, waiting for transfers between devices: none -> 7.21 us  [body(): lax.ppermute(block, 'mic', pairs)]
    ppermute x10 -> x7, starting transfers between devices: 22.5 us -> 18.6 us  [exchange(): lax.ppermute(blocks[k], axis, [(i, i ^ k) for i in range(size)])]
    ppermute x0 -> x4, starting transfers between devices: none -> 2.21 us  [body(): lax.ppermute(block, 'mic', pairs)]
  transfers between devices with their start and end apart: 11 -> 12, of which waited for: 6 -> 8; matrix products, arithmetic and copies ran while one was open for 0% -> 0% of each run, Pallas kernels for 13% -> 14%
where the time goes in v7:
time: 59.6 us; the launch traced here: 58.5 us
  starting transfers between devices  25.6 us (43%)
  waiting for transfers between devices  19.2 us (32%)
  Pallas kernels  12.5 us (21%)
  between operations  0.73 us (1%)
    ppermute x7, starting transfers between devices, exchange(): lax.ppermute(blocks[k], axis, [(i, i ^ k) for i in range(size)])  18.6 us
    ppermute x7, waiting for transfers between devices, exchange(): lax.ppermute(blocks[k], axis, [(i, i ^ k) for i in range(size)])  8.26 us
    ppermute x4, waiting for transfers between devices, body(): lax.ppermute(block, 'mic', pairs)  7.21 us
    all_to_all x1, starting transfers between devices, body(): lax.all_to_all(board, ('mic', 'bin'), split_axis=0, concat_axis=0, tiled=...  4.75 us
    pallas_call x2, Pallas kernels, home_call(): pl.pallas_call(functools.partial(home_kernel, bin_count, own_bins, first,...  4.2 us
    all_to_all x1, waiting for transfers between devices, body(): lax.all_to_all(board, ('mic', 'bin'), split_axis=0, concat_axis=0, tiled=...  3.68 us
    pallas_call x1, Pallas kernels, last_call(): pl.pallas_call(functools.partial(last_kernel, bin_count, steps), out_shap...  3.41 us
    pallas_call x1, Pallas kernels, owner_call(): pl.pallas_call(functools.partial(owner_kernel, bin_count, steps), out_sha...  2.76 us
  transfers between devices with their start and end apart: 12, of which 8 were waited for; matrix products, arithmetic and copies ran while one was open for 0% of the time, Pallas kernels for 14%

profile of v7, /device:TPU:0, one launch (start us, length us, event | category | flops | bytes accessed | tf_op | source)
XLA Modules:
  0.0 58.5 jit_solution(18003254868275859215)
XLA Ops:
  0.7 1.3 %home.2 = (bf16[520,128]{1,0:T(8,128)(2,1)S(1)}, bf16[520,128]{1,0:T(8,128)(2,1)S(1)}, bf16[520,128]{1,0:T(8,128)(2,1)S(1)}) custom-call(s32[256]{0:T(256)} %place_hbm.3, s32[4]{0:T(128)} %bin_hbm.3, s32[4]{0:T(128)} %group_hbm.3, s32[2,4]{1,0:T(2,128)} %offset_hbm.3, bf16[4,256,256]{2,1,0:T(8,128)(2,1)} %image_hbm.3, bf16[256,256]{1,0:T(8,128)(2,1)} %constant.4.clone.basis_hbm), custom_call_target="tpu_custom_call" | custom-call | tf_op jit(solution)/shard_map/home/pallas_call | solution.py:116
  2.0 5.5 %collective-permute-start.1 = (bf16[520,128]{1,0:T(8,128)(2,1)S(1)}, bf16[520,128]{1,0:T(8,128)(2,1)S(1)}, u32[]{:S(2)}, u32[]{:S(2)}) collective-permute-start(bf16[520,128]{1,0:T(8,128)(2,1)S(1)} %get-tuple-element.27), channel_id=1, source_target_pairs={{0,6},{1,7},{2,4},{3,5},{4,2},{5,3},{6,0},{7,1},{8,14},{9,15},{10,... | collective-permute-start | bytes 399368 | tf_op jit(solution)/shard_map/ppermute | solution.py:605
  7.5 0.7 %collective-permute-start.2 = (bf16[520,128]{1,0:T(8,128)(2,1)S(1)}, bf16[520,128]{1,0:T(8,128)(2,1)S(1)}, u32[]{:S(2)}, u32[]{:S(2)}) collective-permute-start(bf16[520,128]{1,0:T(8,128)(2,1)S(1)} %get-tuple-element.28), channel_id=1, source_target_pairs={{0,5},{1,4},{2,7},{3,6},{4,1},{5,0},{6,3},{7,2},{8,13},{9,12},{10,... | collective-permute-start | bytes 399368 | tf_op jit(solution)/shard_map/ppermute | solution.py:605
  8.2 1.7 %collective-permute-start = (bf16[520,128]{1,0:T(8,128)(2,1)S(1)}, bf16[520,128]{1,0:T(8,128)(2,1)S(1)}, u32[]{:S(2)}, u32[]{:S(2)}) collective-permute-start(bf16[520,128]{1,0:T(8,128)(2,1)S(1)} %get-tuple-element.26.rest_0_), channel_id=1, source_target_pairs={{0,7},{1,6},{2,5},{3,4},{4,3},{5,2},{6,1},{7,0},{8,15},{9,14},{10,... | collective-permute-start | bytes 399368 | tf_op jit(solution)/shard_map/ppermute | solution.py:605
  9.9 2.9 %home.3 = (bf16[520,128]{1,0:T(8,128)(2,1)S(1)}, bf16[520,128]{1,0:T(8,128)(2,1)S(1)}, bf16[520,128]{1,0:T(8,128)(2,1)S(1)}, bf16[520,128]{1,0:T(8,128)(2,1)S(1)}, bf16[520,128]{1,0:T(8,128)(2,1)S(1)}) custom-call(s32[256]{0:T(256)} %place_hbm.3, s32[4]{0:T(128)} %bin_hbm.3, s32[4]{0:T(128)} %group_hbm.3, s32[2,4]{1,0:T(2,128)} %offset_hbm.3, ...), custom_call_target="tpu_custom_call" | custom-call | tf_op jit(solution)/shard_map/home/pallas_call | solution.py:116
  12.8 1.9 %collective-permute-start.3 = (bf16[520,128]{1,0:T(8,128)(2,1)S(1)}, bf16[520,128]{1,0:T(8,128)(2,1)S(1)}, u32[]{:S(2)}, u32[]{:S(2)}) collective-permute-start(bf16[520,128]{1,0:T(8,128)(2,1)S(1)} %get-tuple-element.29), channel_id=1, source_target_pairs={{0,4},{1,5},{2,6},{3,7},{4,0},{5,1},{6,2},{7,3},{8,12},{9,13},{10,... | collective-permute-start | bytes 399368 | tf_op jit(solution)/shard_map/ppermute | solution.py:605
  14.7 1.0 %collective-permute-start.4 = (bf16[520,128]{1,0:T(8,128)(2,1)S(1)}, bf16[520,128]{1,0:T(8,128)(2,1)S(1)}, u32[]{:S(2)}, u32[]{:S(2)}) collective-permute-start(bf16[520,128]{1,0:T(8,128)(2,1)S(1)} %get-tuple-element.30), channel_id=1, source_target_pairs={{0,3},{1,2},{2,1},{3,0},{4,7},{5,6},{6,5},{7,4},{8,11},{9,10},{10,... | collective-permute-start | bytes 399368 | tf_op jit(solution)/shard_map/ppermute | solution.py:605
  15.6 7.6 %collective-permute-start.5 = (bf16[520,128]{1,0:T(8,128)(2,1)S(1)}, bf16[520,128]{1,0:T(8,128)(2,1)S(1)}, u32[]{:S(2)}, u32[]{:S(2)}) collective-permute-start(bf16[520,128]{1,0:T(8,128)(2,1)S(1)} %get-tuple-element.31), channel_id=1, source_target_pairs={{0,2},{1,3},{2,0},{3,1},{4,6},{5,7},{6,4},{7,5},{8,10},{9,11},{10,... | collective-permute-start | bytes 399368 | tf_op jit(solution)/shard_map/ppermute | solution.py:605
  23.3 3.5 %collective-permute-done.2.rest_2_ = bf16[520,128]{1,0:T(8,128)(2,1)S(1)} collective-permute-done((bf16[520,128]{1,0:T(8,128)(2,1)S(1)}, bf16[520,128]{1,0:T(8,128)(2,1)S(1)}, u32[]{:S(2)}, u32[]{:S(2)}) %collective-permute-start.2) | collective-permute-done | bytes 133152 | tf_op jit(solution)/shard_map/ppermute | solution.py:605
  27.0 3.6 %collective-permute-done.3.rest_3_ = bf16[520,128]{1,0:T(8,128)(2,1)S(1)} collective-permute-done((bf16[520,128]{1,0:T(8,128)(2,1)S(1)}, bf16[520,128]{1,0:T(8,128)(2,1)S(1)}, u32[]{:S(2)}, u32[]{:S(2)}) %collective-permute-start.3) | collective-permute-done | bytes 133152 | tf_op jit(solution)/shard_map/ppermute | solution.py:605
  30.6 1.2 %collective-permute-done.6.rest_6_ = bf16[520,128]{1,0:T(8,128)(2,1)S(1)} collective-permute-done((bf16[520,128]{1,0:T(8,128)(2,1)S(1)}, bf16[520,128]{1,0:T(8,128)(2,1)S(1)}, u32[]{:S(2)}, u32[]{:S(2)}) %collective-permute-start.6) | collective-permute-done | bytes 133152 | tf_op jit(solution)/shard_map/ppermute | solution.py:605
  31.8 0.4 middle.1
  32.2 1.6 %collective-permute-start.9 = (bf16[2,520,128]{2,1,0:T(8,128)(2,1)S(1)}, bf16[2,520,128]{2,1,0:T(8,128)(2,1)S(1)}, u32[]{:S(2)}, u32[]{:S(2)}) collective-permute-start(bf16[2,520,128]{2,1,0:T(8,128)(2,1)S(1)} %get-tuple-element.37), channel_id=1, source_target_pairs={{0,16},{8,24},{16,0},{24,8},{1,17},{9,25},{17,1},{25,9},{2,18},{10... | collective-permute-start | bytes 798728 | tf_op jit(solution)/shard_map/ppermute | solution.py:631
  33.8 0.6 %collective-permute-start.7 = (bf16[1,520,128]{2,1,0:T(8,128)(2,1)S(1)}, bf16[1,520,128]{2,1,0:T(8,128)(2,1)S(1)}, u32[]{:S(2)}, u32[]{:S(2)}) collective-permute-start(bf16[1,520,128]{2,1,0:T(8,128)(2,1)S(1)} %get-tuple-element.35), channel_id=1, source_target_pairs={{0,8},{8,0},{16,24},{24,16},{1,9},{9,1},{17,25},{25,17},{2,10},{10... | collective-permute-start | bytes 399368 | tf_op jit(solution)/shard_map/ppermute | solution.py:631
  34.4 1.0 %collective-permute-done.7.rest_1_ = bf16[1,520,128]{2,1,0:T(8,128)(2,1)S(1)} collective-permute-done((bf16[1,520,128]{2,1,0:T(8,128)(2,1)S(1)}, bf16[1,520,128]{2,1,0:T(8,128)(2,1)S(1)}, u32[]{:S(2)}, u32[]{:S(2)}) %collective-permute-start.7) | collective-permute-done | bytes 133152 | tf_op jit(solution)/shard_map/ppermute | solution.py:631
  35.4 0.4 collective-permute-done.8.rest_2_
  35.8 5.2 %collective-permute-done.9.rest_3_ = bf16[2,520,128]{2,1,0:T(8,128)(2,1)S(1)} collective-permute-done((bf16[2,520,128]{2,1,0:T(8,128)(2,1)S(1)}, bf16[2,520,128]{2,1,0:T(8,128)(2,1)S(1)}, u32[]{:S(2)}, u32[]{:S(2)}) %collective-permute-start.9) | collective-permute-done | bytes 266272 | tf_op jit(solution)/shard_map/ppermute | solution.py:631
  40.9 1.7 %ready.1 = (f32[6,256,256]{2,1,0:T(8,128)S(1)}, bf16[6,256,256]{2,1,0:T(8,128)(2,1)S(1)}, bf16[6,256,256]{2,1,0:T(8,128)(2,1)}, f32[8,256]{1,0:T(8,128)S(1)}, bf...) custom-call(f32[1,64]{1,0:T(1,128)S(1)} %bitcast.3, f32[1,64]{1,0:T(1,128)S(1)} %bitcast.6, ...), custom_call_target="tpu_custom_call" | custom-call | tf_op jit(solution)/shard_map/ready/pallas_call | solution.py:389
  42.6 0.7 %collective-permute-done.10.rest_4_ = bf16[2,520,128]{2,1,0:T(8,128)(2,1)S(1)} collective-permute-done((bf16[2,520,128]{2,1,0:T(8,128)(2,1)S(1)}, bf16[2,520,128]{2,1,0:T(8,128)(2,1)S(1)}, u32[]{:S(2)}, u32[]{:S(2)}) %collective-permute-start.10) | collective-permute-done | bytes 266272 | tf_op jit(solution)/shard_map/ppermute | solution.py:631
  43.4 2.8 %owner.1 = (bf16[2,256,256]{2,1,0:T(8,128)(2,1)}, bf16[8,256,256]{2,1,0:T(8,128)(2,1)}, f32[8,256]{1,0:T(8,128)S(1)}, f32[8,8,128]{2,1,0:T(8,128)S(1)}, f32[32,1,128]{2,1,0:T(1,128)}) custom-call(f32[1,64]{1,0:T(1,128)S(1)} %bitcast.4, f32[1,64]{1,0:T(1,128)S(1)} %bitcast.7, bf16[8,256,256]{2,1,0:T(8,128)(2,1)S(1)} %copy-done, ...), custom_call_target="tpu_custom_call" | custom-call | tf_op jit(solution)/shard_map/owner/pallas_call | solution.py:493
  46.1 4.7 %all-to-all-start = ((f32[32,1,128]{2,1,0:T(1,128)}), f32[32,1,128]{2,1,0:T(1,128)S(1)}, u32[]{:S(2)}, u32[]{:S(2)}) async-start(f32[32,1,128]{2,1,0:T(1,128)} %get-tuple-element.49), calls=%async_computation | async-start | bytes 32768 | tf_op jit(solution)/shard_map/all_to_all | solution.py:639
  50.9 3.4 %last.1 = bf16[8,256,256]{2,1,0:T(8,128)(2,1)} custom-call(f32[1,64]{1,0:T(1,128)S(1)} %bitcast.5, f32[1,64]{1,0:T(1,128)S(1)} %bitcast.8, bf16[8,256,256]{2,1,0:T(8,128)(2,1)S(1)} %copy-done, f32[8,256]{1,0:T(8,128)S(1)} %get-tuple-element.44.weight, f32[8,8,128]{2,1,0:T(8,128)S(1)} %get-tuple-element.45.label_ref, ...), custom_call_target="tpu_custom_call" | custom-call | flops 4194304 | bytes 4194304 | tf_op jit(solution)/shard_map/last/pallas_call | solution.py:583
  54.3 3.7 %all-to-all-done = f32[32,1,128]{2,1,0:T(1,128)S(1)} async-done(((f32[32,1,128]{2,1,0:T(1,128)}), f32[32,1,128]{2,1,0:T(1,128)S(1)}, u32[]{:S(2)}, u32[]{:S(2)}) %all-to-all-start) | async-done | bytes 16416 | tf_op jit(solution)/shard_map/all_to_all | solution.py:639
  58.0 0.6 reduce_sum.9
  (13 shorter events, 0.3 us)
Async XLA Ops:
  0.6 40.3 %copy-start = (bf16[8,256,256]{2,1,0:T(8,128)(2,1)S(1)}, bf16[8,256,256]{2,1,0:T(8,128)(2,1)}, u32[]{:S(2)}) copy-start(bf16[8,256,256]{2,1,0:T(8,128)(2,1)} %current_ref.5) | copy-start | bytes 3145732
  0.6 40.3 %copy-start.2 = (f32[64]{0:T(128)S(1)}, f32[64]{0:T(128)}, u32[]{:S(2)}) copy-start(f32[64]{0:T(128)} %param.15) | copy-start | bytes 772
  0.7 40.3 %copy-start.1 = (f32[64]{0:T(128)S(1)}, f32[64]{0:T(128)}, u32[]{:S(2)}) copy-start(f32[64]{0:T(128)} %param.14) | copy-start | bytes 772
  2.0 13.7 %collective-permute-start.1 = (bf16[520,128]{1,0:T(8,128)(2,1)S(1)}, bf16[520,128]{1,0:T(8,128)(2,1)S(1)}, u32[]{:S(2)}, u32[]{:S(2)}) collective-permute-start(bf16[520,128]{1,0:T(8,128)(2,1)S(1)} %get-tuple-element.27), channel_id=1, source_target_pairs={{0,6},{1,7},{2,4},{3,5},{4,2},{5,3},{6,0},{7,1},{8,14},{9,15},{10,... | collective-permute-start | bytes 399368 | tf_op jit(solution)/shard_map/ppermute | solution.py:605
  7.5 19.3 %collective-permute-start.2 = (bf16[520,128]{1,0:T(8,128)(2,1)S(1)}, bf16[520,128]{1,0:T(8,128)(2,1)S(1)}, u32[]{:S(2)}, u32[]{:S(2)}) collective-permute-start(bf16[520,128]{1,0:T(8,128)(2,1)S(1)} %get-tuple-element.28), channel_id=1, source_target_pairs={{0,5},{1,4},{2,7},{3,6},{4,1},{5,0},{6,3},{7,2},{8,13},{9,12},{10,... | collective-permute-start | bytes 399368 | tf_op jit(solution)/shard_map/ppermute | solution.py:605
  8.2 18.8 %collective-permute-start = (bf16[520,128]{1,0:T(8,128)(2,1)S(1)}, bf16[520,128]{1,0:T(8,128)(2,1)S(1)}, u32[]{:S(2)}, u32[]{:S(2)}) collective-permute-start(bf16[520,128]{1,0:T(8,128)(2,1)S(1)} %get-tuple-element.26.rest_0_), channel_id=1, source_target_pairs={{0,7},{1,6},{2,5},{3,4},{4,3},{5,2},{6,1},{7,0},{8,15},{9,14},{10,... | collective-permute-start | bytes 399368 | tf_op jit(solution)/shard_map/ppermute | solution.py:605
  12.8 17.8 %collective-permute-start.3 = (bf16[520,128]{1,0:T(8,128)(2,1)S(1)}, bf16[520,128]{1,0:T(8,128)(2,1)S(1)}, u32[]{:S(2)}, u32[]{:S(2)}) collective-permute-start(bf16[520,128]{1,0:T(8,128)(2,1)S(1)} %get-tuple-element.29), channel_id=1, source_target_pairs={{0,4},{1,5},{2,6},{3,7},{4,0},{5,1},{6,2},{7,3},{8,12},{9,13},{10,... | collective-permute-start | bytes 399368 | tf_op jit(solution)/shard_map/ppermute | solution.py:605
  14.7 15.9 %collective-permute-start.4 = (bf16[520,128]{1,0:T(8,128)(2,1)S(1)}, bf16[520,128]{1,0:T(8,128)(2,1)S(1)}, u32[]{:S(2)}, u32[]{:S(2)}) collective-permute-start(bf16[520,128]{1,0:T(8,128)(2,1)S(1)} %get-tuple-element.30), channel_id=1, source_target_pairs={{0,3},{1,2},{2,1},{3,0},{4,7},{5,6},{6,5},{7,4},{8,11},{9,10},{10,... | collective-permute-start | bytes 399368 | tf_op jit(solution)/shard_map/ppermute | solution.py:605
  15.6 15.0 %collective-permute-start.5 = (bf16[520,128]{1,0:T(8,128)(2,1)S(1)}, bf16[520,128]{1,0:T(8,128)(2,1)S(1)}, u32[]{:S(2)}, u32[]{:S(2)}) collective-permute-start(bf16[520,128]{1,0:T(8,128)(2,1)S(1)} %get-tuple-element.31), channel_id=1, source_target_pairs={{0,2},{1,3},{2,0},{3,1},{4,6},{5,7},{6,4},{7,5},{8,10},{9,11},{10,... | collective-permute-start | bytes 399368 | tf_op jit(solution)/shard_map/ppermute | solution.py:605
  26.8 5.0 %collective-permute-start.6 = (bf16[520,128]{1,0:T(8,128)(2,1)S(1)}, bf16[520,128]{1,0:T(8,128)(2,1)S(1)}, u32[]{:S(2)}, u32[]{:S(2)}) collective-permute-start(bf16[520,128]{1,0:T(8,128)(2,1)S(1)} %get-tuple-element.32), channel_id=1, source_target_pairs={{0,1},{1,0},{2,3},{3,2},{4,5},{5,4},{6,7},{7,6},{8,9},{9,8},{10,11... | collective-permute-start | bytes 399368 | tf_op jit(solution)/shard_map/ppermute | solution.py:605
  32.2 8.7 %collective-permute-start.9 = (bf16[2,520,128]{2,1,0:T(8,128)(2,1)S(1)}, bf16[2,520,128]{2,1,0:T(8,128)(2,1)S(1)}, u32[]{:S(2)}, u32[]{:S(2)}) collective-permute-start(bf16[2,520,128]{2,1,0:T(8,128)(2,1)S(1)} %get-tuple-element.37), channel_id=1, source_target_pairs={{0,16},{8,24},{16,0},{24,8},{1,17},{9,25},{17,1},{25,9},{2,18},{10... | collective-permute-start | bytes 798728 | tf_op jit(solution)/shard_map/ppermute | solution.py:631
  33.8 9.6 %collective-permute-start.10 = (bf16[2,520,128]{2,1,0:T(8,128)(2,1)S(1)}, bf16[2,520,128]{2,1,0:T(8,128)(2,1)S(1)}, u32[]{:S(2)}, u32[]{:S(2)}) collective-permute-start(bf16[2,520,128]{2,1,0:T(8,128)(2,1)S(1)} %get-tuple-element.38), channel_id=1, source_target_pairs={{0,24},{8,16},{16,8},{24,0},{1,25},{9,17},{17,9},{25,1},{2,26},{10... | collective-permute-start | bytes 798728 | tf_op jit(solution)/shard_map/ppermute | solution.py:631
  33.8 1.6 %collective-permute-start.7 = (bf16[1,520,128]{2,1,0:T(8,128)(2,1)S(1)}, bf16[1,520,128]{2,1,0:T(8,128)(2,1)S(1)}, u32[]{:S(2)}, u32[]{:S(2)}) collective-permute-start(bf16[1,520,128]{2,1,0:T(8,128)(2,1)S(1)} %get-tuple-element.35), channel_id=1, source_target_pairs={{0,8},{8,0},{16,24},{24,16},{1,9},{9,1},{17,25},{25,17},{2,10},{10... | collective-permute-start | bytes 399368 | tf_op jit(solution)/shard_map/ppermute | solution.py:631
  34.4 1.4 %collective-permute-start.8 = (bf16[1,520,128]{2,1,0:T(8,128)(2,1)S(1)}, bf16[1,520,128]{2,1,0:T(8,128)(2,1)S(1)}, u32[]{:S(2)}, u32[]{:S(2)}) collective-permute-start(bf16[1,520,128]{2,1,0:T(8,128)(2,1)S(1)} %get-tuple-element.36), channel_id=1, source_target_pairs={{0,8},{8,0},{16,24},{24,16},{1,9},{9,1},{17,25},{25,17},{2,10},{10... | collective-permute-start | bytes 399368 | tf_op jit(solution)/shard_map/ppermute | solution.py:631
  46.1 11.9 %all-to-all-start = ((f32[32,1,128]{2,1,0:T(1,128)}), f32[32,1,128]{2,1,0:T(1,128)S(1)}, u32[]{:S(2)}, u32[]{:S(2)}) async-start(f32[32,1,128]{2,1,0:T(1,128)} %get-tuple-element.49), calls=%async_computation | async-start | bytes 32768 | tf_op jit(solution)/shard_map/all_to_all | solution.py:639

commit v8 on v7

--- a/solution.py
+++ b/solution.py
@@ -20,8 +20,8 @@
 CHUNK = 32
 VMEM_BYTES = 24 * 1024 * 1024
 
-ACTIVE, PLACE, ALONE, HOME, PARTICLE, MEMBERS, LATE = range(7)
-INFOS = 7
+ACTIVE, PLACE, ALONE, MEMBERS, LATE = range(5)
+INFOS = 5
 
 F32 = jnp.float32
 BF16 = jnp.bfloat16
@@ -228,30 +228,30 @@
                 )
 
 
-def decode(labels, steps, bin_count, own_bins, info, late=0):
-    slots = len(labels)
-    here = lax.axis_index("mic")
-    codes = []
+def read_labels(labels):
+    places, senders = [], []
     for block in labels:
         code = block[1:2] + 256.0 * block[3:4]
-        codes.append(jnp.max(jnp.where(block[0:1] > 0, code, -1.0)).astype(jnp.int32))
+        code = jnp.max(jnp.where(block[0:1] > 0, code, -1.0)).astype(jnp.int32)
+        places.append(jnp.where(code < 0, -1, code & 255))
+        senders.append(jnp.maximum(code, 0) >> 8)
+    return places, senders
+
+
+def fill_info(info, places, own_bins, late=0):
     for p in range(own_bins):
         info[MEMBERS, p] = jnp.int32(0)
         info[LATE, p] = jnp.int32(0)
-    for s in range(slots):
-        active = (codes[s] >= 0).astype(jnp.int32)
-        code = jnp.maximum(codes[s], 0)
-        sender = code >> 8
-        place = code & 255
+    for s, place in enumerate(places):
+        active = (place >= 0).astype(jnp.int32)
+        place = jnp.maximum(place, 0)
         info[ACTIVE, s] = active
         info[PLACE, s] = place
-        info[HOME, s] = (here ^ steps[s]) * bin_count + lax.rem(sender, bin_count)
-        info[PARTICLE, s] = sender // bin_count
         info[MEMBERS, place] = info[MEMBERS, place] + active
-        if s >= slots - late:
+        if s >= len(places) - late:
             info[LATE, place] = info[LATE, place] + active
-    for s in range(slots):
-        single = (info[ACTIVE, s] > 0) & (info[MEMBERS, info[PLACE, s]] == 1)
+    for s, place in enumerate(places):
+        single = (place >= 0) & (info[MEMBERS, jnp.maximum(place, 0)] == 1)
         info[ALONE, s] = single.astype(jnp.int32)
 
 
@@ -284,22 +284,23 @@
     return [block.at[j] for block in arrived for j in range(block.shape[0])]
 
 
+def image_of(block, rows, side):
+    lefts = range(0, side * side // LANES, side)
+    return jnp.concatenate([block[n + rows.start : n + rows.stop, :] for n in lefts], axis=1)
+
+
 def labels_of(blocks):
     return [block[block.shape[0] - LABEL_ROWS :, :].astype(F32) for block in blocks]
 
 
-def first_compare(info, factors, current_ref, group, sums, s, block):
+def first_compare(p, factors, current_ref, group, sums, s, block):
     ctf, spectra, first = group
     side = ctf.shape[1]
-    p = info[PLACE, s]
     cross = model = data = jnp.zeros((8, side), F32)
     for rows in chunks_of(side):
         table = ctf_chunk(factors, s, rows)
         ctf[s - first, rows, :] = table
-        held = jnp.concatenate(
-            [block[n + rows.start : n + rows.stop, :] for n in range(0, side * side // LANES, side)],
-            axis=1,
-        )
+        held = image_of(block, rows, side)
         spectra[s - first, rows, :] = held
         values = held.astype(F32)
         predicted = table * current_ref[p, rows, :].astype(F32)
@@ -331,41 +332,37 @@
     return cross, model
 
 
-def update_and_compare(info, group, weight, sums, source, target):
+def update_and_compare(s, p, alone, shared, group, weight, sums, source, target):
     ctf, spectra, first = group
-
-    @pl.loop(0, spectra.shape[0])
-    def _(k):
-        s = first + k
-        p = info[PLACE, s]
-
-        def keep(cross, model):
-            sums[0, pl.ds(s, 1), :] = jnp.sum(cross, axis=0, keepdims=True)
-            sums[1, pl.ds(s, 1), :] = jnp.sum(model, axis=0, keepdims=True)
-
-        @pl.when(info[ALONE, s] > 0)
-        def _():
-            scale = weight[pl.ds(s, 1), :]
-
-            def new(rows, values):
-                term, power, _ = shares(ctf, scale, k, rows, values)
-                reference = renew(source[p, rows, :], term, power)
-                target[p, rows, :] = reference
-                return reference
-
-            keep(*second_compare(group, k, new))
-
-        @pl.when((info[ACTIVE, s] > 0) & (info[ALONE, s] == 0))
-        def _():
-            keep(*second_compare(group, k, lambda rows, _: target[p, rows, :]))
+    k = s - first
+
+    def keep(cross, model):
+        sums[0, pl.ds(s, 1), :] = jnp.sum(cross, axis=0, keepdims=True)
+        sums[1, pl.ds(s, 1), :] = jnp.sum(model, axis=0, keepdims=True)
+
+    @pl.when(alone)
+    def _():
+        scale = weight[pl.ds(s, 1), :]
+
+        def new(rows, values):
+            term, power, _ = shares(ctf, scale, k, rows, values)
+            reference = renew(source[p, rows, :], term, power)
+            target[p, rows, :] = reference
+            return reference
+
+        keep(*second_compare(group, k, new))
+
+    @pl.when(shared)
+    def _():
+        keep(*second_compare(group, k, lambda rows, _: target[p, rows, :]))
 
 
 def ready_kernel(bin_count, steps, focus_ref, damping_ref, current_ref, *rest):
-    blocks, rest = blocks_of(rest[:-9]), rest[-9:]
-    ctf, spectra, spectra_hbm, weight, middle, sums, number, info, sem = rest
+    blocks, rest = blocks_of(rest[:-7]), rest[-7:]
+    ctf, spectra, weight, middle, sums, number, info = rest
     own_bins, side, _ = current_ref.shape
     labels = labels_of(blocks)
-    decode(labels, steps, bin_count, own_bins, info)
+    fill_info(info, read_labels(labels)[0], own_bins)
     factors = ctf_factors(labels, focus_ref, damping_ref, side)
     sums[...] = jnp.zeros(sums.shape, F32)
     group = (ctf, spectra, 0)
@@ -373,14 +370,17 @@
 
         @pl.when(info[ACTIVE, s] > 0)
         def _(s=s):
-            first_compare(info, factors, current_ref, group, sums, s, blocks[s])
-
-    copy = pltpu.make_async_copy(spectra, spectra_hbm, sem)
-    copy.start()
+            first_compare(info[PLACE, s], factors, current_ref, group, sums, s, blocks[s])
+
     weight[...] = correlate(sums, side)[1]
     update_shared(info, (group,), weight, number, current_ref, middle)
-    update_and_compare(info, group, weight, sums, current_ref, middle)
-    copy.wait()
+
+    @pl.loop(0, len(labels))
+    def _(s):
+        alone = info[ALONE, s] > 0
+        shared = (info[ACTIVE, s] > 0) & (info[ALONE, s] == 0)
+        p = info[PLACE, s]
+        update_and_compare(s, p, alone, shared, group, weight, sums, current_ref, middle)
 
 
 def ready_call(bin_count, steps, defocus, bfactor, references, arrived):
@@ -391,17 +391,15 @@
         out_shape=[
             jax.ShapeDtypeStruct((slots, side, side), F32),
             jax.ShapeDtypeStruct((slots, side, side), BF16),
-            pltpu.HBM((slots, side, side), BF16),
             jax.ShapeDtypeStruct((8, side), F32),
             jax.ShapeDtypeStruct(references.shape, BF16),
             jax.ShapeDtypeStruct((3, 8, side), F32),
         ],
         in_specs=[VMEM] * (3 + len(arrived)),
-        out_specs=[VMEM, VMEM, HBM, VMEM, VMEM, VMEM],
+        out_specs=[VMEM] * 5,
         scratch_shapes=[
             pltpu.VMEM((2, side, side), F32),
             pltpu.SMEM((INFOS, max(8, own_bins)), jnp.int32),
-            pltpu.SemaphoreType.DMA(()),
         ],
         compiler_params=pltpu.CompilerParams(vmem_limit_bytes=VMEM_BYTES),
         name="ready",
@@ -409,82 +407,72 @@
 
 
 def owner_kernel(bin_count, steps, focus_ref, damping_ref, current_ref, *rest):
-    blocks, rest = blocks_of(rest[:-18]), rest[-18:]
-    early_ctf, early_spectra, early_weight, early_middle, early_sums = rest[:5]
-    spectra_hbm, middle_hbm, weight, label_ref, score_ref = rest[5:10]
-    ctf, spectra, middle, sums, number, info, spectra_sem, middle_sem = rest[10:]
+    blocks, rest = blocks_of(rest[:-14]), rest[-14:]
+    early_ctf, early_spectra, early_weight, early_sums = rest[:4]
+    middle_ref, weight, label_ref, score_ref = rest[4:8]
+    ctf, spectra, middle, sums, number, info = rest[8:]
     own_bins, side, _ = current_ref.shape
     early = early_ctf.shape[0]
-
-    spectra_copy = pltpu.make_async_copy(spectra, spectra_hbm, spectra_sem)
+    slots = len(steps)
+    here = lax.axis_index("mic")
+
     labels = labels_of(blocks)
     for s, label in enumerate(labels):
         label_ref[s] = label
-    decode(labels, steps, bin_count, own_bins, info, len(steps) - early)
-
-    def early_copy(p):
-        return pltpu.make_async_copy(early_middle.at[p], middle_hbm.at[p], middle_sem.at[p])
-
-    def late_copy(p):
-        return pltpu.make_async_copy(middle.at[p], middle_hbm.at[p], middle_sem.at[p])
-
-    @pl.loop(0, own_bins)
-    def _(p):
-        @pl.when((info[MEMBERS, p] > 0) & (info[LATE, p] == 0))
-        def _():
-            early_copy(p).start()
-
+    places, senders = read_labels(labels)
     factors = ctf_factors(labels, focus_ref, damping_ref, side)
     sums[...] = early_sums[...]
     early_group, late_group = (early_ctf, early_spectra, 0), (ctf, spectra, early)
-    for s in range(early, len(labels)):
-
-        @pl.when(info[ACTIVE, s] > 0)
+    shared = {}
+    for s in range(early, slots):
+        active = places[s] >= 0
+        others = [places[t] == places[s] for t in range(slots) if t != s]
+        shared[s] = active & functools.reduce(jnp.logical_or, others)
+
+        @pl.when(active)
         def _(s=s):
-            first_compare(info, factors, current_ref, late_group, sums, s, blocks[s])
-
-    spectra_copy.start()
+            first_compare(places[s], factors, current_ref, late_group, sums, s, blocks[s])
+
     row = lax.broadcasted_iota(jnp.int32, (8, side), 0)
     weight[...] = jnp.where(row < early, early_weight[...], correlate(sums, side)[1])
-    update_shared(
-        info, (early_group, late_group), weight, number, current_ref, middle, kind=LATE
-    )
-    update_and_compare(info, late_group, weight, sums, current_ref, middle)
-
-    @pl.loop(0, early)
-    def _(s):
-        p = info[PLACE, s]
-
-        @pl.when((info[ACTIVE, s] > 0) & (info[LATE, p] > 0))
-        def _():
-            cross, model = second_compare(early_group, s, lambda rows, _: middle[p, rows, :])
-            sums[0, pl.ds(s, 1), :] = jnp.sum(cross, axis=0, keepdims=True)
-            sums[1, pl.ds(s, 1), :] = jnp.sum(model, axis=0, keepdims=True)
-
-    @pl.loop(0, own_bins)
-    def _(p):
-        @pl.when(info[LATE, p] > 0)
-        def _():
-            late_copy(p).start()
+    any_shared = functools.reduce(jnp.logical_or, shared.values())
+
+    @pl.when(any_shared)
+    def _():
+        fill_info(info, places, own_bins, slots - early)
+        update_shared(
+            info, (early_group, late_group), weight, number, current_ref, middle, kind=LATE
+        )
+
+        @pl.loop(0, early)
+        def _(s):
+            p = info[PLACE, s]
+
+            @pl.when((info[ACTIVE, s] > 0) & (info[LATE, p] > 0))
+            def _():
+                cross, model = second_compare(early_group, s, lambda rows, _: middle[p, rows, :])
+                sums[0, pl.ds(s, 1), :] = jnp.sum(cross, axis=0, keepdims=True)
+                sums[1, pl.ds(s, 1), :] = jnp.sum(model, axis=0, keepdims=True)
+
+    for s in range(early, slots):
+        alone = (places[s] >= 0) & jnp.logical_not(shared[s])
+        update_and_compare(
+            s, places[s], alone, shared[s], late_group, weight, sums, current_ref, middle
+        )
+
+    for s in range(early, slots):
+
+        @pl.when(places[s] >= 0)
+        def _(s=s):
+            middle_ref[s - early] = middle[places[s]]
 
     correlation, weight[...] = correlate(sums, side)
     score_ref[...] = jnp.zeros(score_ref.shape, F32)
     lane = lax.broadcasted_iota(jnp.int32, (1, 128), 1)
-    for s in range(len(labels)):
-
-        @pl.when(info[ACTIVE, s] > 0)
-        def _(s=s):
-            score = jnp.where(lane == info[PARTICLE, s], correlation[s : s + 1, :], 0.0)
-            score_ref[info[HOME, s]] = score
-
-    spectra_copy.wait()
-
-    @pl.loop(0, own_bins)
-    def _(p):
-        @pl.when(info[MEMBERS, p] > 0)
-        def _():
-            late_copy(p).wait()
-
+    for s in range(slots):
+        home = (here ^ steps[s]) * bin_count + lax.rem(senders[s], bin_count)
+        hit = (lane == senders[s] // bin_count) & (places[s] >= 0)
+        score_ref[home] = score_ref[home] + jnp.where(hit, correlation[s : s + 1, :], 0.0)
 
 def owner_call(devices, bin_count, steps, defocus, bfactor, references, arrived, early):
     own_bins, side, _ = references.shape
@@ -493,14 +481,13 @@
     return pl.pallas_call(
         functools.partial(owner_kernel, bin_count, steps),
         out_shape=[
-            pltpu.HBM((late, side, side), BF16),
-            pltpu.HBM(references.shape, BF16),
+            jax.ShapeDtypeStruct((late, side, side), BF16),
             jax.ShapeDtypeStruct((8, side), F32),
             jax.ShapeDtypeStruct((slots, LABEL_ROWS, 128), F32),
             jax.ShapeDtypeStruct((devices, 1, 128), F32),
         ],
         in_specs=[VMEM] * (3 + len(arrived) + len(early)),
-        out_specs=[HBM, HBM, VMEM, VMEM, VMEM],
+        out_specs=[VMEM] * 4,
         scratch_shapes=[
             pltpu.VMEM((late, side, side), F32),
             pltpu.VMEM((late, side, side), BF16),
@@ -508,8 +495,6 @@
             pltpu.VMEM((3, 8, side), F32),
             pltpu.VMEM((2, side, side), F32),
             pltpu.SMEM((INFOS, max(8, own_bins)), jnp.int32),
-            pltpu.SemaphoreType.DMA(()),
-            pltpu.SemaphoreType.DMA((own_bins,)),
         ],
         compiler_params=pltpu.CompilerParams(vmem_limit_bytes=VMEM_BYTES),
         name="owner",
@@ -517,16 +502,15 @@
 
 
 def last_kernel(
-    bin_count,
-    steps,
     focus_ref,
     damping_ref,
-    current_ref,
     weight,
     label_ref,
-    early_hbm,
-    late_hbm,
-    middle_hbm,
+    early_spectra,
+    early_middle,
+    late_middle,
+    late_ref,
+    current_hbm,
     refined_ref,
     spectra,
     middle,
@@ -536,27 +520,35 @@
     sem,
 ):
     slots, side, _ = ctf.shape
-    own_bins = current_ref.shape[0]
-    early = early_hbm.shape[0]
-    copies = [
-        pltpu.make_async_copy(early_hbm, spectra.at[pl.ds(0, early)], sem.at[0]),
-        pltpu.make_async_copy(late_hbm, spectra.at[pl.ds(early, slots - early)], sem.at[1]),
-        pltpu.make_async_copy(middle_hbm, middle, sem.at[2]),
-    ]
-    for copy in copies:
-        copy.start()
+    own_bins = refined_ref.shape[0]
+    early = early_spectra.shape[0]
     labels = [label_ref[s] for s in range(slots)]
-    decode(labels, steps, bin_count, own_bins, info)
+    places, _ = read_labels(labels)
+    fill_info(info, places, own_bins)
+
+    def unchanged(p):
+        return pltpu.make_async_copy(current_hbm.at[p], refined_ref.at[p], sem.at[p])
+
+    @pl.loop(0, own_bins)
+    def _(p):
+        @pl.when(info[MEMBERS, p] == 0)
+        def _():
+            unchanged(p).start()
+
     factors = ctf_factors(labels, focus_ref, damping_ref, side)
     for s in range(slots):
 
-        @pl.when(info[ACTIVE, s] > 0)
+        @pl.when(places[s] >= 0)
         def _(s=s):
             for rows in chunks_of(side):
                 ctf[s, rows, :] = ctf_chunk(factors, s, rows)
-
-    for copy in copies:
-        copy.wait()
+            if s < early:
+                spectra[s] = early_spectra[s]
+                middle[places[s]] = early_middle[places[s]]
+            else:
+                spectra[s] = image_of(late_ref.at[s - early], slice(0, side), side)
+                middle[places[s]] = late_middle[s - early]
+
     update_shared(info, ((ctf, spectra, 0),), weight, number, middle, refined_ref)
 
     @pl.loop(0, slots)
@@ -574,16 +566,16 @@
     def _(p):
         @pl.when(info[MEMBERS, p] == 0)
         def _():
-            refined_ref[p] = current_ref[p]
-
-
-def last_call(bin_count, steps, defocus, bfactor, references, weight, labels, kept):
+            unchanged(p).wait()
+
+
+def last_call(defocus, bfactor, references, weight, labels, kept):
     own_bins, side, _ = references.shape
     slots = labels.shape[0]
     return pl.pallas_call(
-        functools.partial(last_kernel, bin_count, steps),
+        last_kernel,
         out_shape=jax.ShapeDtypeStruct(references.shape, BF16),
-        in_specs=[VMEM] * 5 + [HBM] * 3,
+        in_specs=[VMEM] * 8 + [HBM],
         out_specs=VMEM,
         scratch_shapes=[
             pltpu.VMEM((slots, side, side), BF16),
@@ -591,12 +583,12 @@
             pltpu.VMEM((slots, side, side), F32),
             pltpu.VMEM((2, side, side), F32),
             pltpu.SMEM((INFOS, max(8, own_bins)), jnp.int32),
-            pltpu.SemaphoreType.DMA((3,)),
+            pltpu.SemaphoreType.DMA((own_bins,)),
         ],
         compiler_params=pltpu.CompilerParams(vmem_limit_bytes=VMEM_BYTES),
         cost_estimate=pl.CostEstimate(flops=4 << 20, bytes_accessed=4 << 20, transcendentals=0),
         name="last",
-    )(defocus, bfactor, references, weight, labels, *map(in_hbm, kept))
+    )(defocus, bfactor, weight, labels, *kept, in_hbm(references))
 
 
 def exchange(blocks, axis):
@@ -632,12 +624,15 @@
     steps = [step for step, block in blocks for _ in range(block.shape[0])]
     arrived = [block for _, block in blocks]
     tables = (defocus.reshape(1, -1), bfactor.reshape(1, -1), references)
-    ctf, spectra, kept, *known = ready_call(bin_count, steps[: -arrived[-1].shape[0]], *tables, arrived[:-1])
-    late, middle, weight, labels, board = owner_call(
-        mic_count * bin_count, bin_count, steps, *tables, arrived, (ctf, spectra, *known)
+    early = slice(0, -arrived[-1].shape[0])
+    ctf, spectra, early_weight, middle, sums = ready_call(
+        bin_count, steps[early], *tables, arrived[:-1]
+    )
+    late_middle, weight, labels, board = owner_call(
+        mic_count * bin_count, bin_count, steps, *tables, arrived, (ctf, spectra, early_weight, sums)
     )
     back = lax.all_to_all(board, ("mic", "bin"), split_axis=0, concat_axis=0, tiled=True)
-    refined = last_call(bin_count, steps, *tables, weight, labels, (kept, late, middle))
+    refined = last_call(*tables, weight, labels, (spectra, middle, late_middle, arrived[-1]))
     return (refined, jnp.sum(back, axis=(0, 1))[:particles])
 
 

time: 59.6 us -> 58.3 us (0.978); the launches traced: 58.5 us -> 58 us
    ppermute x7, waiting for transfers between devices: 8.26 us -> 7.65 us  [exchange(): lax.ppermute(blocks[k], axis, [(i, i ^ k) for i in range(size)])]
  transfers between devices with their start and end apart: 12 -> 12, of which waited for: 8 -> 8; matrix products, arithmetic and copies ran while one was open for 0% -> 0% of each run, Pallas kernels for 14% -> 13%
where the time goes in v8:
time: 58.3 us; the launch traced here: 58 us
  starting transfers between devices  25.4 us (44%)
  waiting for transfers between devices  18.7 us (32%)
  Pallas kernels  12.6 us (22%)
  between operations  0.72 us (1%)
    ppermute x7, starting transfers between devices, exchange(): lax.ppermute(blocks[k], axis, [(i, i ^ k) for i in range(size)])  18.9 us
    ppermute x7, waiting for transfers between devices, exchange(): lax.ppermute(blocks[k], axis, [(i, i ^ k) for i in range(size)])  7.65 us
    ppermute x4, waiting for transfers between devices, body(): lax.ppermute(block, 'mic', pairs)  7.43 us
    all_to_all x1, starting transfers between devices, body(): lax.all_to_all(board, ('mic', 'bin'), split_axis=0, concat_axis=0, tiled=...  4.28 us
    pallas_call x2, Pallas kernels, home_call(): pl.pallas_call(functools.partial(home_kernel, bin_count, own_bins, first,...  4.19 us
    all_to_all x1, waiting for transfers between devices, body(): lax.all_to_all(board, ('mic', 'bin'), split_axis=0, concat_axis=0, tiled=...  3.64 us
    pallas_call x1, Pallas kernels, last_call(): pl.pallas_call(last_kernel, out_shape=jax.ShapeDtypeStruct(references.sha...  3.46 us
    pallas_call x1, Pallas kernels, owner_call(): pl.pallas_call(functools.partial(owner_kernel, bin_count, steps), out_sha...  2.86 us
  transfers between devices with their start and end apart: 12, of which 8 were waited for; matrix products, arithmetic and copies ran while one was open for 0% of the time, Pallas kernels for 13%

profile of v8, /device:TPU:0, one launch (start us, length us, event | category | flops | bytes accessed | tf_op | source)
XLA Modules:
  0.0 58.0 jit_solution(16194406981991025278)
XLA Ops:
  0.7 1.8 %home.2 = (bf16[520,128]{1,0:T(8,128)(2,1)S(1)}, bf16[520,128]{1,0:T(8,128)(2,1)S(1)}, bf16[520,128]{1,0:T(8,128)(2,1)S(1)}) custom-call(s32[256]{0:T(256)} %place_hbm.3, s32[4]{0:T(128)} %bin_hbm.3, s32[4]{0:T(128)} %group_hbm.3, s32[2,4]{1,0:T(2,128)} %offset_hbm.3, bf16[4,256,256]{2,1,0:T(8,128)(2,1)} %image_hbm.3, bf16[256,256]{1,0:T(8,128)(2,1)} %constant.4.clone.basis_hbm), custom_call_target="tpu_custom_call" | custom-call | tf_op jit(solution)/shard_map/home/pallas_call | solution.py:116
  2.4 5.5 %collective-permute-start.1 = (bf16[520,128]{1,0:T(8,128)(2,1)S(1)}, bf16[520,128]{1,0:T(8,128)(2,1)S(1)}, u32[]{:S(2)}, u32[]{:S(2)}) collective-permute-start(bf16[520,128]{1,0:T(8,128)(2,1)S(1)} %get-tuple-element.25), channel_id=1, source_target_pairs={{0,6},{1,7},{2,4},{3,5},{4,2},{5,3},{6,0},{7,1},{8,14},{9,15},{10,... | collective-permute-start | bytes 399368 | tf_op jit(solution)/shard_map/ppermute | solution.py:597
  7.9 2.5 %collective-permute-start = (bf16[520,128]{1,0:T(8,128)(2,1)S(1)}, bf16[520,128]{1,0:T(8,128)(2,1)S(1)}, u32[]{:S(2)}, u32[]{:S(2)}) collective-permute-start(bf16[520,128]{1,0:T(8,128)(2,1)S(1)} %get-tuple-element.24.rest_0_), channel_id=1, source_target_pairs={{0,7},{1,6},{2,5},{3,4},{4,3},{5,2},{6,1},{7,0},{8,15},{9,14},{10,... | collective-permute-start | bytes 399368 | tf_op jit(solution)/shard_map/ppermute | solution.py:597
  10.3 2.4 %home.3 = (bf16[520,128]{1,0:T(8,128)(2,1)S(1)}, bf16[520,128]{1,0:T(8,128)(2,1)S(1)}, bf16[520,128]{1,0:T(8,128)(2,1)S(1)}, bf16[520,128]{1,0:T(8,128)(2,1)S(1)}, bf16[520,128]{1,0:T(8,128)(2,1)S(1)}) custom-call(s32[256]{0:T(256)} %place_hbm.3, s32[4]{0:T(128)} %bin_hbm.3, s32[4]{0:T(128)} %group_hbm.3, s32[2,4]{1,0:T(2,128)} %offset_hbm.3, ...), custom_call_target="tpu_custom_call" | custom-call | tf_op jit(solution)/shard_map/home/pallas_call | solution.py:116
  12.8 1.1 %collective-permute-start.3 = (bf16[520,128]{1,0:T(8,128)(2,1)S(1)}, bf16[520,128]{1,0:T(8,128)(2,1)S(1)}, u32[]{:S(2)}, u32[]{:S(2)}) collective-permute-start(bf16[520,128]{1,0:T(8,128)(2,1)S(1)} %get-tuple-element.27), channel_id=1, source_target_pairs={{0,4},{1,5},{2,6},{3,7},{4,0},{5,1},{6,2},{7,3},{8,12},{9,13},{10,... | collective-permute-start | bytes 399368 | tf_op jit(solution)/shard_map/ppermute | solution.py:597
  13.9 1.8 %collective-permute-start.4 = (bf16[520,128]{1,0:T(8,128)(2,1)S(1)}, bf16[520,128]{1,0:T(8,128)(2,1)S(1)}, u32[]{:S(2)}, u32[]{:S(2)}) collective-permute-start(bf16[520,128]{1,0:T(8,128)(2,1)S(1)} %get-tuple-element.28), channel_id=1, source_target_pairs={{0,3},{1,2},{2,1},{3,0},{4,7},{5,6},{6,5},{7,4},{8,11},{9,10},{10,... | collective-permute-start | bytes 399368 | tf_op jit(solution)/shard_map/ppermute | solution.py:597
  15.7 7.5 %collective-permute-start.5 = (bf16[520,128]{1,0:T(8,128)(2,1)S(1)}, bf16[520,128]{1,0:T(8,128)(2,1)S(1)}, u32[]{:S(2)}, u32[]{:S(2)}) collective-permute-start(bf16[520,128]{1,0:T(8,128)(2,1)S(1)} %get-tuple-element.29), channel_id=1, source_target_pairs={{0,2},{1,3},{2,0},{3,1},{4,6},{5,7},{6,4},{7,5},{8,10},{9,11},{10,... | collective-permute-start | bytes 399368 | tf_op jit(solution)/shard_map/ppermute | solution.py:597
  23.2 3.2 %collective-permute-done.2.rest_2_ = bf16[520,128]{1,0:T(8,128)(2,1)S(1)} collective-permute-done((bf16[520,128]{1,0:T(8,128)(2,1)S(1)}, bf16[520,128]{1,0:T(8,128)(2,1)S(1)}, u32[]{:S(2)}, u32[]{:S(2)}) %collective-permute-start.2) | collective-permute-done | bytes 133152 | tf_op jit(solution)/shard_map/ppermute | solution.py:597
  26.4 0.5 collective-permute-start.6
  26.9 3.2 %collective-permute-done.3.rest_3_ = bf16[520,128]{1,0:T(8,128)(2,1)S(1)} collective-permute-done((bf16[520,128]{1,0:T(8,128)(2,1)S(1)}, bf16[520,128]{1,0:T(8,128)(2,1)S(1)}, u32[]{:S(2)}, u32[]{:S(2)}) %collective-permute-start.3) | collective-permute-done | bytes 133152 | tf_op jit(solution)/shard_map/ppermute | solution.py:597
  30.2 1.2 %collective-permute-done.6.rest_6_ = bf16[520,128]{1,0:T(8,128)(2,1)S(1)} collective-permute-done((bf16[520,128]{1,0:T(8,128)(2,1)S(1)}, bf16[520,128]{1,0:T(8,128)(2,1)S(1)}, u32[]{:S(2)}, u32[]{:S(2)}) %collective-permute-start.6) | collective-permute-done | bytes 133152 | tf_op jit(solution)/shard_map/ppermute | solution.py:597
  31.4 0.4 middle.1
  31.8 1.8 %collective-permute-start.9 = (bf16[2,520,128]{2,1,0:T(8,128)(2,1)S(1)}, bf16[2,520,128]{2,1,0:T(8,128)(2,1)S(1)}, u32[]{:S(2)}, u32[]{:S(2)}) collective-permute-start(bf16[2,520,128]{2,1,0:T(8,128)(2,1)S(1)} %get-tuple-element.35), channel_id=1, source_target_pairs={{0,16},{8,24},{16,0},{24,8},{1,17},{9,25},{17,1},{25,9},{2,18},{10... | collective-permute-start | bytes 798728 | tf_op jit(solution)/shard_map/ppermute | solution.py:623
  33.6 0.4 collective-permute-start.7
  34.1 0.9 %collective-permute-done.7.rest_1_ = bf16[1,520,128]{2,1,0:T(8,128)(2,1)S(1)} collective-permute-done((bf16[1,520,128]{2,1,0:T(8,128)(2,1)S(1)}, bf16[1,520,128]{2,1,0:T(8,128)(2,1)S(1)}, u32[]{:S(2)}, u32[]{:S(2)}) %collective-permute-start.7) | collective-permute-done | bytes 133152 | tf_op jit(solution)/shard_map/ppermute | solution.py:623
  35.0 0.4 collective-permute-done.8.rest_2_
  35.4 5.0 %collective-permute-done.9.rest_3_ = bf16[2,520,128]{2,1,0:T(8,128)(2,1)S(1)} collective-permute-done((bf16[2,520,128]{2,1,0:T(8,128)(2,1)S(1)}, bf16[2,520,128]{2,1,0:T(8,128)(2,1)S(1)}, u32[]{:S(2)}, u32[]{:S(2)}) %collective-permute-start.9) | collective-permute-done | bytes 266272 | tf_op jit(solution)/shard_map/ppermute | solution.py:623
  40.4 1.6 %ready.1 = (f32[6,256,256]{2,1,0:T(8,128)S(1)}, bf16[6,256,256]{2,1,0:T(8,128)(2,1)S(1)}, f32[8,256]{1,0:T(8,128)S(1)}, bf16[8,256,256]{2,1,0:T(8,128)(2,1)S(1)}, f32[3,8,256]{2,1,0:T(8,128)S(1)}) custom-call(f32[1,64]{1,0:T(1,128)S(1)} %bitcast.3, f32[1,64]{1,0:T(1,128)S(1)} %bitcast.6, bf16[8,256,256]{2,1,0:T(8,128)(2,1)S(1)} %copy-done, ...), custom_call_target="tpu_custom_call" | custom-call | tf_op jit(solution)/shard_map/ready/pallas_call | solution.py:389
  42.0 1.2 %collective-permute-done.10.rest_4_.late_ref = bf16[2,520,128]{2,1,0:T(8,128)(2,1)S(1)} collective-permute-done((bf16[2,520,128]{2,1,0:T(8,128)(2,1)S(1)}, bf16[2,520,128]{2,1,0:T(8,128)(2,1)S(1)}, u32[]{:S(2)}, u32[]{:S(2)}) %collective-permute-start.10) | collective-permute-done | bytes 266272 | tf_op jit(solution)/shard_map/ppermute | solution.py:623
  43.2 2.9 %owner.1 = (bf16[2,256,256]{2,1,0:T(8,128)(2,1)S(1)}, f32[8,256]{1,0:T(8,128)S(1)}, f32[8,8,128]{2,1,0:T(8,128)S(1)}, f32[32,1,128]{2,1,0:T(1,128)}) custom-call(f32[1,64]{1,0:T(1,128)S(1)} %bitcast.4, f32[1,64]{1,0:T(1,128)S(1)} %bitcast.7, bf16[8,256,256]{2,1,0:T(8,128)(2,1)S(1)} %copy-done, bf16[2,520,128]{2,1,0:T(8,128)(2,1)S(1)} %get-tuple-element.32.rest_0_, ...), custom_call_target="tpu_custom_call" | custom-call | tf_op jit(solution)/shard_map/owner/pallas_call | solution.py:481
  46.1 4.3 %all-to-all-start = ((f32[32,1,128]{2,1,0:T(1,128)}), f32[32,1,128]{2,1,0:T(1,128)S(1)}, u32[]{:S(2)}, u32[]{:S(2)}) async-start(f32[32,1,128]{2,1,0:T(1,128)} %get-tuple-element.45), calls=%async_computation | async-start | bytes 32768 | tf_op jit(solution)/shard_map/all_to_all | solution.py:634
  50.3 3.5 %last.1 = bf16[8,256,256]{2,1,0:T(8,128)(2,1)} custom-call(f32[1,64]{1,0:T(1,128)S(1)} %bitcast.5, f32[1,64]{1,0:T(1,128)S(1)} %bitcast.8, f32[8,256]{1,0:T(8,128)S(1)} %get-tuple-element.41.weight, f32[8,8,128]{2,1,0:T(8,128)S(1)} %get-tuple-element.42.label_ref, bf16[6,256,256]{2,1,0:T(8,128)(2,1)S(1)} %get-tuple-element.38.rest_6_.early_spectra, ...), custom_call_target="tpu_custom_call" | custom-call | flops 4194304 | bytes 4194304 | tf_op jit(solution)/shard_map/last/pallas_call | solution.py:575
  53.8 3.6 %all-to-all-done = f32[32,1,128]{2,1,0:T(1,128)S(1)} async-done(((f32[32,1,128]{2,1,0:T(1,128)}), f32[32,1,128]{2,1,0:T(1,128)S(1)}, u32[]{:S(2)}, u32[]{:S(2)}) %all-to-all-start) | async-done | bytes 16416 | tf_op jit(solution)/shard_map/all_to_all | solution.py:634
  57.5 0.6 reduce_sum.9
  (13 shorter events, 0.1 us)
Async XLA Ops:
  0.6 39.7 %copy-start = (bf16[8,256,256]{2,1,0:T(8,128)(2,1)S(1)}, bf16[8,256,256]{2,1,0:T(8,128)(2,1)}, u32[]{:S(2)}) copy-start(bf16[8,256,256]{2,1,0:T(8,128)(2,1)} %current_hbm.1) | copy-start | bytes 3145732
  0.6 39.7 %copy-start.2 = (f32[64]{0:T(128)S(1)}, f32[64]{0:T(128)}, u32[]{:S(2)}) copy-start(f32[64]{0:T(128)} %param.15) | copy-start | bytes 772
  0.7 39.7 %copy-start.1 = (f32[64]{0:T(128)S(1)}, f32[64]{0:T(128)}, u32[]{:S(2)}) copy-start(f32[64]{0:T(128)} %param.14) | copy-start | bytes 772
  2.4 13.3 %collective-permute-start.1 = (bf16[520,128]{1,0:T(8,128)(2,1)S(1)}, bf16[520,128]{1,0:T(8,128)(2,1)S(1)}, u32[]{:S(2)}, u32[]{:S(2)}) collective-permute-start(bf16[520,128]{1,0:T(8,128)(2,1)S(1)} %get-tuple-element.25), channel_id=1, source_target_pairs={{0,6},{1,7},{2,4},{3,5},{4,2},{5,3},{6,0},{7,1},{8,14},{9,15},{10,... | collective-permute-start | bytes 399368 | tf_op jit(solution)/shard_map/ppermute | solution.py:597
  7.9 18.5 %collective-permute-start.2 = (bf16[520,128]{1,0:T(8,128)(2,1)S(1)}, bf16[520,128]{1,0:T(8,128)(2,1)S(1)}, u32[]{:S(2)}, u32[]{:S(2)}) collective-permute-start(bf16[520,128]{1,0:T(8,128)(2,1)S(1)} %get-tuple-element.26), channel_id=1, source_target_pairs={{0,5},{1,4},{2,7},{3,6},{4,1},{5,0},{6,3},{7,2},{8,13},{9,12},{10,... | collective-permute-start | bytes 399368 | tf_op jit(solution)/shard_map/ppermute | solution.py:597
  7.9 19.0 %collective-permute-start = (bf16[520,128]{1,0:T(8,128)(2,1)S(1)}, bf16[520,128]{1,0:T(8,128)(2,1)S(1)}, u32[]{:S(2)}, u32[]{:S(2)}) collective-permute-start(bf16[520,128]{1,0:T(8,128)(2,1)S(1)} %get-tuple-element.24.rest_0_), channel_id=1, source_target_pairs={{0,7},{1,6},{2,5},{3,4},{4,3},{5,2},{6,1},{7,0},{8,15},{9,14},{10,... | collective-permute-start | bytes 399368 | tf_op jit(solution)/shard_map/ppermute | solution.py:597
  12.8 17.4 %collective-permute-start.3 = (bf16[520,128]{1,0:T(8,128)(2,1)S(1)}, bf16[520,128]{1,0:T(8,128)(2,1)S(1)}, u32[]{:S(2)}, u32[]{:S(2)}) collective-permute-start(bf16[520,128]{1,0:T(8,128)(2,1)S(1)} %get-tuple-element.27), channel_id=1, source_target_pairs={{0,4},{1,5},{2,6},{3,7},{4,0},{5,1},{6,2},{7,3},{8,12},{9,13},{10,... | collective-permute-start | bytes 399368 | tf_op jit(solution)/shard_map/ppermute | solution.py:597
  13.9 16.3 %collective-permute-start.4 = (bf16[520,128]{1,0:T(8,128)(2,1)S(1)}, bf16[520,128]{1,0:T(8,128)(2,1)S(1)}, u32[]{:S(2)}, u32[]{:S(2)}) collective-permute-start(bf16[520,128]{1,0:T(8,128)(2,1)S(1)} %get-tuple-element.28), channel_id=1, source_target_pairs={{0,3},{1,2},{2,1},{3,0},{4,7},{5,6},{6,5},{7,4},{8,11},{9,10},{10,... | collective-permute-start | bytes 399368 | tf_op jit(solution)/shard_map/ppermute | solution.py:597
  15.7 14.5 %collective-permute-start.5 = (bf16[520,128]{1,0:T(8,128)(2,1)S(1)}, bf16[520,128]{1,0:T(8,128)(2,1)S(1)}, u32[]{:S(2)}, u32[]{:S(2)}) collective-permute-start(bf16[520,128]{1,0:T(8,128)(2,1)S(1)} %get-tuple-element.29), channel_id=1, source_target_pairs={{0,2},{1,3},{2,0},{3,1},{4,6},{5,7},{6,4},{7,5},{8,10},{9,11},{10,... | collective-permute-start | bytes 399368 | tf_op jit(solution)/shard_map/ppermute | solution.py:597
  26.4 5.0 %collective-permute-start.6 = (bf16[520,128]{1,0:T(8,128)(2,1)S(1)}, bf16[520,128]{1,0:T(8,128)(2,1)S(1)}, u32[]{:S(2)}, u32[]{:S(2)}) collective-permute-start(bf16[520,128]{1,0:T(8,128)(2,1)S(1)} %get-tuple-element.30), channel_id=1, source_target_pairs={{0,1},{1,0},{2,3},{3,2},{4,5},{5,4},{6,7},{7,6},{8,9},{9,8},{10,11... | collective-permute-start | bytes 399368 | tf_op jit(solution)/shard_map/ppermute | solution.py:597
  31.8 8.5 %collective-permute-start.9 = (bf16[2,520,128]{2,1,0:T(8,128)(2,1)S(1)}, bf16[2,520,128]{2,1,0:T(8,128)(2,1)S(1)}, u32[]{:S(2)}, u32[]{:S(2)}) collective-permute-start(bf16[2,520,128]{2,1,0:T(8,128)(2,1)S(1)} %get-tuple-element.35), channel_id=1, source_target_pairs={{0,16},{8,24},{16,0},{24,8},{1,17},{9,25},{17,1},{25,9},{2,18},{10... | collective-permute-start | bytes 798728 | tf_op jit(solution)/shard_map/ppermute | solution.py:623
  33.6 9.6 %collective-permute-start.10 = (bf16[2,520,128]{2,1,0:T(8,128)(2,1)S(1)}, bf16[2,520,128]{2,1,0:T(8,128)(2,1)S(1)}, u32[]{:S(2)}, u32[]{:S(2)}) collective-permute-start(bf16[2,520,128]{2,1,0:T(8,128)(2,1)S(1)} %get-tuple-element.36), channel_id=1, source_target_pairs={{0,24},{8,16},{16,8},{24,0},{1,25},{9,17},{17,9},{25,1},{2,26},{10... | collective-permute-start | bytes 798728 | tf_op jit(solution)/shard_map/ppermute | solution.py:623
  33.6 1.4 %collective-permute-start.7 = (bf16[1,520,128]{2,1,0:T(8,128)(2,1)S(1)}, bf16[1,520,128]{2,1,0:T(8,128)(2,1)S(1)}, u32[]{:S(2)}, u32[]{:S(2)}) collective-permute-start(bf16[1,520,128]{2,1,0:T(8,128)(2,1)S(1)} %get-tuple-element.33), channel_id=1, source_target_pairs={{0,8},{8,0},{16,24},{24,16},{1,9},{9,1},{17,25},{25,17},{2,10},{10... | collective-permute-start | bytes 399368 | tf_op jit(solution)/shard_map/ppermute | solution.py:623
  34.0 1.4 %collective-permute-start.8 = (bf16[1,520,128]{2,1,0:T(8,128)(2,1)S(1)}, bf16[1,520,128]{2,1,0:T(8,128)(2,1)S(1)}, u32[]{:S(2)}, u32[]{:S(2)}) collective-permute-start(bf16[1,520,128]{2,1,0:T(8,128)(2,1)S(1)} %get-tuple-element.34), channel_id=1, source_target_pairs={{0,8},{8,0},{16,24},{24,16},{1,9},{9,1},{17,25},{25,17},{2,10},{10... | collective-permute-start | bytes 399368 | tf_op jit(solution)/shard_map/ppermute | solution.py:623
  46.1 11.4 %all-to-all-start = ((f32[32,1,128]{2,1,0:T(1,128)}), f32[32,1,128]{2,1,0:T(1,128)S(1)}, u32[]{:S(2)}, u32[]{:S(2)}) async-start(f32[32,1,128]{2,1,0:T(1,128)} %get-tuple-element.45), calls=%async_computation | async-start | bytes 32768 | tf_op jit(solution)/shard_map/all_to_all | solution.py:634

commit v9 on v8

--- a/solution.py
+++ b/solution.py
@@ -16,7 +16,7 @@
 AMPLITUDE = math.sqrt(1.0 - CONTRAST * CONTRAST)
 
 LANES = 128
-LABEL_ROWS = 8
+LABEL_ROWS = 16
 CHUNK = 32
 VMEM_BYTES = 24 * 1024 * 1024
 
@@ -88,7 +88,9 @@
 
         @pl.when((step_of >= first) & (step_of < first + count))
         def _():
-            moved = pltpu.roll(image_ref[i].astype(F32), side - offset_ref[0, i], 0).astype(BF16)
+            moved = pltpu.roll(
+                image_ref[i].astype(F32), lax.rem(side - offset_ref[0, i], side), 0
+            ).astype(BF16)
             columns = pltpu.roll(basis_ref[...].astype(F32), offset_ref[1, i], 0).astype(BF16)
             half = jnp.dot(basis_ref[...], moved, preferred_element_type=F32).astype(BF16)
             spectra[...] = jnp.dot(half, columns, preferred_element_type=F32).astype(BF16)

time: 58.3 us -> 58.3 us (level)
  Pallas kernels: 12.6 us -> 9.52 us
  waiting for transfers between devices: 18.7 us -> 20.8 us
  starting transfers between devices: 25.4 us -> 26.2 us
    pallas_call x1, Pallas kernels: 2.86 us -> 1.14 us  [owner_call(): pl.pallas_call(functools.partial(owner_kernel, bin_count, steps), out_sha...]
    pallas_call x1, Pallas kernels: 3.46 us -> 2.5 us  [last_call(): pl.pallas_call(last_kernel, out_shape=jax.ShapeDtypeStruct(references.sha...]
    all_to_all x1, waiting for transfers between devices: 3.64 us -> 4.61 us  [body(): lax.all_to_all(board, ('mic', 'bin'), split_axis=0, concat_axis=0, tiled=...]
    all_to_all x1, starting transfers between devices: 4.28 us -> 5.07 us  [body(): lax.all_to_all(board, ('mic', 'bin'), split_axis=0, concat_axis=0, tiled=...]
    ppermute x7, waiting for transfers between devices: 7.65 us -> 8.31 us  [exchange(): lax.ppermute(blocks[k], axis, [(i, i ^ k) for i in range(size)])]
  transfers between devices with their start and end apart: 12 -> 12, of which waited for: 8 -> 8; matrix products, arithmetic and copies ran while one was open for 0% -> 0% of each run, Pallas kernels for 13% -> 11%
where the time goes in v9:
time: 58.3 us; the launch traced here: 57.8 us
  starting transfers between devices  26.2 us (45%)
  waiting for transfers between devices  20.8 us (36%)
  Pallas kernels  9.52 us (16%)
  between operations  0.72 us (1%)
    ppermute x7, starting transfers between devices, exchange(): lax.ppermute(blocks[k], axis, [(i, i ^ k) for i in range(size)])  18.9 us
    ppermute x7, waiting for transfers between devices, exchange(): lax.ppermute(blocks[k], axis, [(i, i ^ k) for i in range(size)])  8.31 us
    ppermute x4, waiting for transfers between devices, body(): lax.ppermute(block, 'mic', pairs)  7.85 us
    all_to_all x1, starting transfers between devices, body(): lax.all_to_all(board, ('mic', 'bin'), split_axis=0, concat_axis=0, tiled=...  5.07 us
    all_to_all x1, waiting for transfers between devices, body(): lax.all_to_all(board, ('mic', 'bin'), split_axis=0, concat_axis=0, tiled=...  4.61 us
    pallas_call x2, Pallas kernels, home_call(): pl.pallas_call(functools.partial(home_kernel, bin_count, own_bins, first,...  4.14 us
    pallas_call x1, Pallas kernels, last_call(): pl.pallas_call(last_kernel, out_shape=jax.ShapeDtypeStruct(references.sha...  2.5 us
    ppermute x4, starting transfers between devices, body(): lax.ppermute(block, 'mic', pairs)  2.21 us
  transfers between devices with their start and end apart: 12, of which 8 were waited for; matrix products, arithmetic and copies ran while one was open for 0% of the time, Pallas kernels for 11%

profile of v9, /device:TPU:0, one launch (start us, length us, event | category | flops | bytes accessed | tf_op | source)
XLA Modules:
  0.0 57.8 jit_solution(133774148942248988)
XLA Ops:
  0.7 1.7 %home.2 = (bf16[528,128]{1,0:T(8,128)(2,1)S(1)}, bf16[528,128]{1,0:T(8,128)(2,1)S(1)}, bf16[528,128]{1,0:T(8,128)(2,1)S(1)}) custom-call(s32[256]{0:T(256)} %place_hbm.3, s32[4]{0:T(128)} %bin_hbm.3, s32[4]{0:T(128)} %group_hbm.3, s32[2,4]{1,0:T(2,128)} %offset_hbm.3, bf16[4,256,256]{2,1,0:T(8,128)(2,1)} %image_hbm.3, bf16[256,256]{1,0:T(8,128)(2,1)} %constant.4.clone.basis_hbm), custom_call_target="tpu_custom_call" | custom-call | tf_op jit(solution)/shard_map/home/pallas_call | solution.py:118
  2.3 5.2 %collective-permute-start.1 = (bf16[528,128]{1,0:T(8,128)(2,1)S(1)}, bf16[528,128]{1,0:T(8,128)(2,1)S(1)}, u32[]{:S(2)}, u32[]{:S(2)}) collective-permute-start(bf16[528,128]{1,0:T(8,128)(2,1)S(1)} %get-tuple-element.25), channel_id=1, source_target_pairs={{0,6},{1,7},{2,4},{3,5},{4,2},{5,3},{6,0},{7,1},{8,14},{9,15},{10,... | collective-permute-start | bytes 405512 | tf_op jit(solution)/shard_map/ppermute | solution.py:599
  7.5 0.8 %collective-permute-start.2 = (bf16[528,128]{1,0:T(8,128)(2,1)S(1)}, bf16[528,128]{1,0:T(8,128)(2,1)S(1)}, u32[]{:S(2)}, u32[]{:S(2)}) collective-permute-start(bf16[528,128]{1,0:T(8,128)(2,1)S(1)} %get-tuple-element.26), channel_id=1, source_target_pairs={{0,5},{1,4},{2,7},{3,6},{4,1},{5,0},{6,3},{7,2},{8,13},{9,12},{10,... | collective-permute-start | bytes 405512 | tf_op jit(solution)/shard_map/ppermute | solution.py:599
  8.3 2.0 %collective-permute-start = (bf16[528,128]{1,0:T(8,128)(2,1)S(1)}, bf16[528,128]{1,0:T(8,128)(2,1)S(1)}, u32[]{:S(2)}, u32[]{:S(2)}) collective-permute-start(bf16[528,128]{1,0:T(8,128)(2,1)S(1)} %get-tuple-element.24.rest_0_), channel_id=1, source_target_pairs={{0,7},{1,6},{2,5},{3,4},{4,3},{5,2},{6,1},{7,0},{8,15},{9,14},{10,... | collective-permute-start | bytes 405512 | tf_op jit(solution)/shard_map/ppermute | solution.py:599
  10.2 2.5 %home.3 = (bf16[528,128]{1,0:T(8,128)(2,1)S(1)}, bf16[528,128]{1,0:T(8,128)(2,1)S(1)}, bf16[528,128]{1,0:T(8,128)(2,1)S(1)}, bf16[528,128]{1,0:T(8,128)(2,1)S(1)}, bf16[528,128]{1,0:T(8,128)(2,1)S(1)}) custom-call(s32[256]{0:T(256)} %place_hbm.3, s32[4]{0:T(128)} %bin_hbm.3, s32[4]{0:T(128)} %group_hbm.3, s32[2,4]{1,0:T(2,128)} %offset_hbm.3, ...), custom_call_target="tpu_custom_call" | custom-call | tf_op jit(solution)/shard_map/home/pallas_call | solution.py:118
  12.7 1.6 %collective-permute-start.3 = (bf16[528,128]{1,0:T(8,128)(2,1)S(1)}, bf16[528,128]{1,0:T(8,128)(2,1)S(1)}, u32[]{:S(2)}, u32[]{:S(2)}) collective-permute-start(bf16[528,128]{1,0:T(8,128)(2,1)S(1)} %get-tuple-element.27), channel_id=1, source_target_pairs={{0,4},{1,5},{2,6},{3,7},{4,0},{5,1},{6,2},{7,3},{8,12},{9,13},{10,... | collective-permute-start | bytes 405512 | tf_op jit(solution)/shard_map/ppermute | solution.py:599
  14.3 1.3 %collective-permute-start.4 = (bf16[528,128]{1,0:T(8,128)(2,1)S(1)}, bf16[528,128]{1,0:T(8,128)(2,1)S(1)}, u32[]{:S(2)}, u32[]{:S(2)}) collective-permute-start(bf16[528,128]{1,0:T(8,128)(2,1)S(1)} %get-tuple-element.28), channel_id=1, source_target_pairs={{0,3},{1,2},{2,1},{3,0},{4,7},{5,6},{6,5},{7,4},{8,11},{9,10},{10,... | collective-permute-start | bytes 405512 | tf_op jit(solution)/shard_map/ppermute | solution.py:599
  15.7 7.8 %collective-permute-start.5 = (bf16[528,128]{1,0:T(8,128)(2,1)S(1)}, bf16[528,128]{1,0:T(8,128)(2,1)S(1)}, u32[]{:S(2)}, u32[]{:S(2)}) collective-permute-start(bf16[528,128]{1,0:T(8,128)(2,1)S(1)} %get-tuple-element.29), channel_id=1, source_target_pairs={{0,2},{1,3},{2,0},{3,1},{4,6},{5,7},{6,4},{7,5},{8,10},{9,11},{10,... | collective-permute-start | bytes 405512 | tf_op jit(solution)/shard_map/ppermute | solution.py:599
  23.5 3.5 %collective-permute-done.2.rest_2_ = bf16[528,128]{1,0:T(8,128)(2,1)S(1)} collective-permute-done((bf16[528,128]{1,0:T(8,128)(2,1)S(1)}, bf16[528,128]{1,0:T(8,128)(2,1)S(1)}, u32[]{:S(2)}, u32[]{:S(2)}) %collective-permute-start.2) | collective-permute-done | bytes 135200 | tf_op jit(solution)/shard_map/ppermute | solution.py:599
  27.3 3.6 %collective-permute-done.3.rest_3_ = bf16[528,128]{1,0:T(8,128)(2,1)S(1)} collective-permute-done((bf16[528,128]{1,0:T(8,128)(2,1)S(1)}, bf16[528,128]{1,0:T(8,128)(2,1)S(1)}, u32[]{:S(2)}, u32[]{:S(2)}) %collective-permute-start.3) | collective-permute-done | bytes 135200 | tf_op jit(solution)/shard_map/ppermute | solution.py:599
  30.9 1.1 %collective-permute-done.6.rest_6_ = bf16[528,128]{1,0:T(8,128)(2,1)S(1)} collective-permute-done((bf16[528,128]{1,0:T(8,128)(2,1)S(1)}, bf16[528,128]{1,0:T(8,128)(2,1)S(1)}, u32[]{:S(2)}, u32[]{:S(2)}) %collective-permute-start.6) | collective-permute-done | bytes 135200 | tf_op jit(solution)/shard_map/ppermute | solution.py:599
  32.1 0.4 middle.1
  32.5 1.2 %collective-permute-start.9 = (bf16[2,528,128]{2,1,0:T(8,128)(2,1)S(1)}, bf16[2,528,128]{2,1,0:T(8,128)(2,1)S(1)}, u32[]{:S(2)}, u32[]{:S(2)}) collective-permute-start(bf16[2,528,128]{2,1,0:T(8,128)(2,1)S(1)} %get-tuple-element.35), channel_id=1, source_target_pairs={{0,16},{8,24},{16,0},{24,8},{1,17},{9,25},{17,1},{25,9},{2,18},{10... | collective-permute-start | bytes 811016 | tf_op jit(solution)/shard_map/ppermute | solution.py:625
  33.7 1.0 %collective-permute-start.7 = (bf16[1,528,128]{2,1,0:T(8,128)(2,1)S(1)}, bf16[1,528,128]{2,1,0:T(8,128)(2,1)S(1)}, u32[]{:S(2)}, u32[]{:S(2)}) collective-permute-start(bf16[1,528,128]{2,1,0:T(8,128)(2,1)S(1)} %get-tuple-element.33), channel_id=1, source_target_pairs={{0,8},{8,0},{16,24},{24,16},{1,9},{9,1},{17,25},{25,17},{2,10},{10... | collective-permute-start | bytes 405512 | tf_op jit(solution)/shard_map/ppermute | solution.py:625
  34.7 1.0 %collective-permute-done.7.rest_1_ = bf16[1,528,128]{2,1,0:T(8,128)(2,1)S(1)} collective-permute-done((bf16[1,528,128]{2,1,0:T(8,128)(2,1)S(1)}, bf16[1,528,128]{2,1,0:T(8,128)(2,1)S(1)}, u32[]{:S(2)}, u32[]{:S(2)}) %collective-permute-start.7) | collective-permute-done | bytes 135200 | tf_op jit(solution)/shard_map/ppermute | solution.py:625
  35.7 0.4 collective-permute-done.8.rest_2_
  36.1 5.7 %collective-permute-done.9.rest_3_ = bf16[2,528,128]{2,1,0:T(8,128)(2,1)S(1)} collective-permute-done((bf16[2,528,128]{2,1,0:T(8,128)(2,1)S(1)}, bf16[2,528,128]{2,1,0:T(8,128)(2,1)S(1)}, u32[]{:S(2)}, u32[]{:S(2)}) %collective-permute-start.9) | collective-permute-done | bytes 270368 | tf_op jit(solution)/shard_map/ppermute | solution.py:625
  41.8 1.3 %ready.1 = (f32[6,256,256]{2,1,0:T(8,128)S(1)}, bf16[6,256,256]{2,1,0:T(8,128)(2,1)S(1)}, f32[8,256]{1,0:T(8,128)S(1)}, bf16[8,256,256]{2,1,0:T(8,128)(2,1)S(1)}, f32[3,8,256]{2,1,0:T(8,128)S(1)}) custom-call(f32[1,64]{1,0:T(1,128)S(1)} %bitcast.3, f32[1,64]{1,0:T(1,128)S(1)} %bitcast.6, bf16[8,256,256]{2,1,0:T(8,128)(2,1)S(1)} %copy-done, ...), custom_call_target="tpu_custom_call" | custom-call | tf_op jit(solution)/shard_map/ready/pallas_call | solution.py:391
  43.1 0.8 %collective-permute-done.10.rest_4_.late_ref = bf16[2,528,128]{2,1,0:T(8,128)(2,1)S(1)} collective-permute-done((bf16[2,528,128]{2,1,0:T(8,128)(2,1)S(1)}, bf16[2,528,128]{2,1,0:T(8,128)(2,1)S(1)}, u32[]{:S(2)}, u32[]{:S(2)}) %collective-permute-start.10) | collective-permute-done | bytes 270368 | tf_op jit(solution)/shard_map/ppermute | solution.py:625
  43.9 1.1 %owner.1 = (bf16[2,256,256]{2,1,0:T(8,128)(2,1)S(1)}, f32[8,256]{1,0:T(8,128)S(1)}, f32[8,16,128]{2,1,0:T(8,128)S(1)}, f32[32,1,128]{2,1,0:T(1,128)}) custom-call(f32[1,64]{1,0:T(1,128)S(1)} %bitcast.4, f32[1,64]{1,0:T(1,128)S(1)} %bitcast.7, bf16[8,256,256]{2,1,0:T(8,128)(2,1)S(1)} %copy-done, bf16[2,528,128]{2,1,0:T(8,128)(2,1)S(1)} %get-tuple-element.32.rest_0_, ...), custom_call_target="tpu_custom_call" | custom-call | tf_op jit(solution)/shard_map/owner/pallas_call | solution.py:483
  45.0 5.1 %all-to-all-start = ((f32[32,1,128]{2,1,0:T(1,128)}), f32[32,1,128]{2,1,0:T(1,128)S(1)}, u32[]{:S(2)}, u32[]{:S(2)}) async-start(f32[32,1,128]{2,1,0:T(1,128)} %get-tuple-element.45), calls=%async_computation | async-start | bytes 32768 | tf_op jit(solution)/shard_map/all_to_all | solution.py:636
  50.1 2.5 %last.1 = bf16[8,256,256]{2,1,0:T(8,128)(2,1)} custom-call(f32[1,64]{1,0:T(1,128)S(1)} %bitcast.5, f32[1,64]{1,0:T(1,128)S(1)} %bitcast.8, f32[8,256]{1,0:T(8,128)S(1)} %get-tuple-element.41.weight, f32[8,16,128]{2,1,0:T(8,128)S(1)} %get-tuple-element.42.label_ref, bf16[6,256,256]{2,1,0:T(8,128)(2,1)S(1)} %get-tuple-element.38.rest_6_.early_spectra, ...), custom_call_target="tpu_custom_call" | custom-call | flops 4194304 | bytes 4194304 | tf_op jit(solution)/shard_map/last/pallas_call | solution.py:577
  52.6 4.6 %all-to-all-done = f32[32,1,128]{2,1,0:T(1,128)S(1)} async-done(((f32[32,1,128]{2,1,0:T(1,128)}), f32[32,1,128]{2,1,0:T(1,128)S(1)}, u32[]{:S(2)}, u32[]{:S(2)}) %all-to-all-start) | async-done | bytes 16416 | tf_op jit(solution)/shard_map/all_to_all | solution.py:636
  57.2 0.6 reduce_sum.9
  (13 shorter events, 0.3 us)
Async XLA Ops:
  0.6 41.1 %copy-start = (bf16[8,256,256]{2,1,0:T(8,128)(2,1)S(1)}, bf16[8,256,256]{2,1,0:T(8,128)(2,1)}, u32[]{:S(2)}) copy-start(bf16[8,256,256]{2,1,0:T(8,128)(2,1)} %current_hbm.1) | copy-start | bytes 3145732
  0.6 41.1 %copy-start.2 = (f32[64]{0:T(128)S(1)}, f32[64]{0:T(128)}, u32[]{:S(2)}) copy-start(f32[64]{0:T(128)} %param.15) | copy-start | bytes 772
  0.7 41.1 %copy-start.1 = (f32[64]{0:T(128)S(1)}, f32[64]{0:T(128)}, u32[]{:S(2)}) copy-start(f32[64]{0:T(128)} %param.14) | copy-start | bytes 772
  2.3 13.3 %collective-permute-start.1 = (bf16[528,128]{1,0:T(8,128)(2,1)S(1)}, bf16[528,128]{1,0:T(8,128)(2,1)S(1)}, u32[]{:S(2)}, u32[]{:S(2)}) collective-permute-start(bf16[528,128]{1,0:T(8,128)(2,1)S(1)} %get-tuple-element.25), channel_id=1, source_target_pairs={{0,6},{1,7},{2,4},{3,5},{4,2},{5,3},{6,0},{7,1},{8,14},{9,15},{10,... | collective-permute-start | bytes 405512 | tf_op jit(solution)/shard_map/ppermute | solution.py:599
  7.5 19.5 %collective-permute-start.2 = (bf16[528,128]{1,0:T(8,128)(2,1)S(1)}, bf16[528,128]{1,0:T(8,128)(2,1)S(1)}, u32[]{:S(2)}, u32[]{:S(2)}) collective-permute-start(bf16[528,128]{1,0:T(8,128)(2,1)S(1)} %get-tuple-element.26), channel_id=1, source_target_pairs={{0,5},{1,4},{2,7},{3,6},{4,1},{5,0},{6,3},{7,2},{8,13},{9,12},{10,... | collective-permute-start | bytes 405512 | tf_op jit(solution)/shard_map/ppermute | solution.py:599
  8.3 19.0 %collective-permute-start = (bf16[528,128]{1,0:T(8,128)(2,1)S(1)}, bf16[528,128]{1,0:T(8,128)(2,1)S(1)}, u32[]{:S(2)}, u32[]{:S(2)}) collective-permute-start(bf16[528,128]{1,0:T(8,128)(2,1)S(1)} %get-tuple-element.24.rest_0_), channel_id=1, source_target_pairs={{0,7},{1,6},{2,5},{3,4},{4,3},{5,2},{6,1},{7,0},{8,15},{9,14},{10,... | collective-permute-start | bytes 405512 | tf_op jit(solution)/shard_map/ppermute | solution.py:599
  12.7 18.2 %collective-permute-start.3 = (bf16[528,128]{1,0:T(8,128)(2,1)S(1)}, bf16[528,128]{1,0:T(8,128)(2,1)S(1)}, u32[]{:S(2)}, u32[]{:S(2)}) collective-permute-start(bf16[528,128]{1,0:T(8,128)(2,1)S(1)} %get-tuple-element.27), channel_id=1, source_target_pairs={{0,4},{1,5},{2,6},{3,7},{4,0},{5,1},{6,2},{7,3},{8,12},{9,13},{10,... | collective-permute-start | bytes 405512 | tf_op jit(solution)/shard_map/ppermute | solution.py:599
  14.3 16.6 %collective-permute-start.4 = (bf16[528,128]{1,0:T(8,128)(2,1)S(1)}, bf16[528,128]{1,0:T(8,128)(2,1)S(1)}, u32[]{:S(2)}, u32[]{:S(2)}) collective-permute-start(bf16[528,128]{1,0:T(8,128)(2,1)S(1)} %get-tuple-element.28), channel_id=1, source_target_pairs={{0,3},{1,2},{2,1},{3,0},{4,7},{5,6},{6,5},{7,4},{8,11},{9,10},{10,... | collective-permute-start | bytes 405512 | tf_op jit(solution)/shard_map/ppermute | solution.py:599
  15.7 15.3 %collective-permute-start.5 = (bf16[528,128]{1,0:T(8,128)(2,1)S(1)}, bf16[528,128]{1,0:T(8,128)(2,1)S(1)}, u32[]{:S(2)}, u32[]{:S(2)}) collective-permute-start(bf16[528,128]{1,0:T(8,128)(2,1)S(1)} %get-tuple-element.29), channel_id=1, source_target_pairs={{0,2},{1,3},{2,0},{3,1},{4,6},{5,7},{6,4},{7,5},{8,10},{9,11},{10,... | collective-permute-start | bytes 405512 | tf_op jit(solution)/shard_map/ppermute | solution.py:599
  27.0 5.0 %collective-permute-start.6 = (bf16[528,128]{1,0:T(8,128)(2,1)S(1)}, bf16[528,128]{1,0:T(8,128)(2,1)S(1)}, u32[]{:S(2)}, u32[]{:S(2)}) collective-permute-start(bf16[528,128]{1,0:T(8,128)(2,1)S(1)} %get-tuple-element.30), channel_id=1, source_target_pairs={{0,1},{1,0},{2,3},{3,2},{4,5},{5,4},{6,7},{7,6},{8,9},{9,8},{10,11... | collective-permute-start | bytes 405512 | tf_op jit(solution)/shard_map/ppermute | solution.py:599
  32.5 9.3 %collective-permute-start.9 = (bf16[2,528,128]{2,1,0:T(8,128)(2,1)S(1)}, bf16[2,528,128]{2,1,0:T(8,128)(2,1)S(1)}, u32[]{:S(2)}, u32[]{:S(2)}) collective-permute-start(bf16[2,528,128]{2,1,0:T(8,128)(2,1)S(1)} %get-tuple-element.35), channel_id=1, source_target_pairs={{0,16},{8,24},{16,0},{24,8},{1,17},{9,25},{17,1},{25,9},{2,18},{10... | collective-permute-start | bytes 811016 | tf_op jit(solution)/shard_map/ppermute | solution.py:625
  33.7 10.2 %collective-permute-start.10 = (bf16[2,528,128]{2,1,0:T(8,128)(2,1)S(1)}, bf16[2,528,128]{2,1,0:T(8,128)(2,1)S(1)}, u32[]{:S(2)}, u32[]{:S(2)}) collective-permute-start(bf16[2,528,128]{2,1,0:T(8,128)(2,1)S(1)} %get-tuple-element.36), channel_id=1, source_target_pairs={{0,24},{8,16},{16,8},{24,0},{1,25},{9,17},{17,9},{25,1},{2,26},{10... | collective-permute-start | bytes 811016 | tf_op jit(solution)/shard_map/ppermute | solution.py:625
  33.7 2.0 %collective-permute-start.7 = (bf16[1,528,128]{2,1,0:T(8,128)(2,1)S(1)}, bf16[1,528,128]{2,1,0:T(8,128)(2,1)S(1)}, u32[]{:S(2)}, u32[]{:S(2)}) collective-permute-start(bf16[1,528,128]{2,1,0:T(8,128)(2,1)S(1)} %get-tuple-element.33), channel_id=1, source_target_pairs={{0,8},{8,0},{16,24},{24,16},{1,9},{9,1},{17,25},{25,17},{2,10},{10... | collective-permute-start | bytes 405512 | tf_op jit(solution)/shard_map/ppermute | solution.py:625
  34.7 1.4 %collective-permute-start.8 = (bf16[1,528,128]{2,1,0:T(8,128)(2,1)S(1)}, bf16[1,528,128]{2,1,0:T(8,128)(2,1)S(1)}, u32[]{:S(2)}, u32[]{:S(2)}) collective-permute-start(bf16[1,528,128]{2,1,0:T(8,128)(2,1)S(1)} %get-tuple-element.34), channel_id=1, source_target_pairs={{0,8},{8,0},{16,24},{24,16},{1,9},{9,1},{17,25},{25,17},{2,10},{10... | collective-permute-start | bytes 405512 | tf_op jit(solution)/shard_map/ppermute | solution.py:625
  45.0 12.2 %all-to-all-start = ((f32[32,1,128]{2,1,0:T(1,128)}), f32[32,1,128]{2,1,0:T(1,128)S(1)}, u32[]{:S(2)}, u32[]{:S(2)}) async-start(f32[32,1,128]{2,1,0:T(1,128)} %get-tuple-element.45), calls=%async_computation | async-start | bytes 32768 | tf_op jit(solution)/shard_map/all_to_all | solution.py:636

commit v10 on v8

--- a/solution.py
+++ b/solution.py
@@ -608,7 +608,7 @@
     basis = jnp.asarray(hartley(side), BF16)
     operands = (bin_place, particle_bin, ctf_group, offsets, images, basis)
     operands = tuple(map(in_hbm, operands))
-    far = 3 * bin_count // 8
+    far = bin_count // 4
     rest = bin_count - far
     sent_far = home_call(bin_count, own_bins, rest, far, operands)
     sent_near = home_call(bin_count, own_bins, 0, rest, operands, after=(sent_far[-1],))

time: 58.3 us -> 57.7 us (0.990)
  starting transfers between devices: 25.4 us -> 27.1 us
  waiting for transfers between devices: 18.7 us -> 17.5 us
  Pallas kernels: 12.6 us -> 11.5 us
    pallas_call x1, Pallas kernels: 2.86 us -> 1.84 us  [owner_call(): pl.pallas_call(functools.partial(owner_kernel, bin_count, steps), out_sha...]
    ppermute x7, starting transfers between devices: 18.9 us -> 19.8 us  [exchange(): lax.ppermute(blocks[k], axis, [(i, i ^ k) for i in range(size)])]
    all_to_all x1, starting transfers between devices: 4.28 us -> 5.16 us  [body(): lax.all_to_all(board, ('mic', 'bin'), split_axis=0, concat_axis=0, tiled=...]
    ppermute x7, waiting for transfers between devices: 7.65 us -> 6.79 us  [exchange(): lax.ppermute(blocks[k], axis, [(i, i ^ k) for i in range(size)])]
  transfers between devices with their start and end apart: 12 -> 12, of which waited for: 8 -> 7; matrix products, arithmetic and copies ran while one was open for 0% -> 0% of each run, Pallas kernels for 13% -> 12%
where the time goes in v10:
time: 57.7 us; the launch traced here: 57.4 us
  starting transfers between devices  27.1 us (47%)
  waiting for transfers between devices  17.5 us (30%)
  Pallas kernels  11.5 us (20%)
  between operations  0.72 us (1%)
    ppermute x7, starting transfers between devices, exchange(): lax.ppermute(blocks[k], axis, [(i, i ^ k) for i in range(size)])  19.8 us
    ppermute x4, waiting for transfers between devices, body(): lax.ppermute(block, 'mic', pairs)  6.93 us
    ppermute x7, waiting for transfers between devices, exchange(): lax.ppermute(blocks[k], axis, [(i, i ^ k) for i in range(size)])  6.79 us
    all_to_all x1, starting transfers between devices, body(): lax.all_to_all(board, ('mic', 'bin'), split_axis=0, concat_axis=0, tiled=...  5.16 us
    pallas_call x2, Pallas kernels, home_call(): pl.pallas_call(functools.partial(home_kernel, bin_count, own_bins, first,...  4.11 us
    all_to_all x1, waiting for transfers between devices, body(): lax.all_to_all(board, ('mic', 'bin'), split_axis=0, concat_axis=0, tiled=...  3.78 us
    pallas_call x1, Pallas kernels, last_call(): pl.pallas_call(last_kernel, out_shape=jax.ShapeDtypeStruct(references.sha...  3.32 us
    ppermute x4, starting transfers between devices, body(): lax.ppermute(block, 'mic', pairs)  2.21 us
  transfers between devices with their start and end apart: 12, of which 7 were waited for; matrix products, arithmetic and copies ran while one was open for 0% of the time, Pallas kernels for 12%

profile of v10, /device:TPU:0, one launch (start us, length us, event | category | flops | bytes accessed | tf_op | source)
XLA Modules:
  0.0 57.4 jit_solution(15081930690516810743)
XLA Ops:
  0.7 2.1 %home.2 = (bf16[520,128]{1,0:T(8,128)(2,1)S(1)}, bf16[520,128]{1,0:T(8,128)(2,1)S(1)}) custom-call(s32[256]{0:T(256)} %place_hbm.3, s32[4]{0:T(128)} %bin_hbm.3, s32[4]{0:T(128)} %group_hbm.3, s32[2,4]{1,0:T(2,128)} %offset_hbm.3, bf16[4,256,256]{2,1,0:T(8,128)(2,1)} %image_hbm.3, bf16[256,256]{1,0:T(8,128)(2,1)} %constant.4.clone.basis_hbm), custom_call_target="tpu_custom_call" | custom-call | tf_op jit(solution)/shard_map/home/pallas_call | solution.py:116
  2.8 4.3 %collective-permute-start.1 = (bf16[520,128]{1,0:T(8,128)(2,1)S(1)}, bf16[520,128]{1,0:T(8,128)(2,1)S(1)}, u32[]{:S(2)}, u32[]{:S(2)}) collective-permute-start(bf16[520,128]{1,0:T(8,128)(2,1)S(1)} %get-tuple-element.25), channel_id=1, source_target_pairs={{0,6},{1,7},{2,4},{3,5},{4,2},{5,3},{6,0},{7,1},{8,14},{9,15},{10,... | collective-permute-start | bytes 399368 | tf_op jit(solution)/shard_map/ppermute | solution.py:597
  7.1 1.9 %collective-permute-start = (bf16[520,128]{1,0:T(8,128)(2,1)S(1)}, bf16[520,128]{1,0:T(8,128)(2,1)S(1)}, u32[]{:S(2)}, u32[]{:S(2)}) collective-permute-start(bf16[520,128]{1,0:T(8,128)(2,1)S(1)} %get-tuple-element.24.rest_0_), channel_id=1, source_target_pairs={{0,7},{1,6},{2,5},{3,4},{4,3},{5,2},{6,1},{7,0},{8,15},{9,14},{10,... | collective-permute-start | bytes 399368 | tf_op jit(solution)/shard_map/ppermute | solution.py:597
  9.0 2.0 %home.3 = (bf16[520,128]{1,0:T(8,128)(2,1)S(1)}, bf16[520,128]{1,0:T(8,128)(2,1)S(1)}, bf16[520,128]{1,0:T(8,128)(2,1)S(1)}, bf16[520,128]{1,0:T(8,128)(2,1)S(1)...) custom-call(s32[256]{0:T(256)} %place_hbm.3, s32[4]{0:T(128)} %bin_hbm.3, s32[4]{0:T(128)} %group_hbm.3, ...), custom_call_target="tpu_custom_call" | custom-call | tf_op jit(solution)/shard_map/home/pallas_call | solution.py:116
  11.0 0.9 %collective-permute-start.2 = (bf16[520,128]{1,0:T(8,128)(2,1)S(1)}, bf16[520,128]{1,0:T(8,128)(2,1)S(1)}, u32[]{:S(2)}, u32[]{:S(2)}) collective-permute-start(bf16[520,128]{1,0:T(8,128)(2,1)S(1)} %get-tuple-element.26), channel_id=1, source_target_pairs={{0,5},{1,4},{2,7},{3,6},{4,1},{5,0},{6,3},{7,2},{8,13},{9,12},{10,... | collective-permute-start | bytes 399368 | tf_op jit(solution)/shard_map/ppermute | solution.py:597
  11.9 1.2 %collective-permute-start.3 = (bf16[520,128]{1,0:T(8,128)(2,1)S(1)}, bf16[520,128]{1,0:T(8,128)(2,1)S(1)}, u32[]{:S(2)}, u32[]{:S(2)}) collective-permute-start(bf16[520,128]{1,0:T(8,128)(2,1)S(1)} %get-tuple-element.27), channel_id=1, source_target_pairs={{0,4},{1,5},{2,6},{3,7},{4,0},{5,1},{6,2},{7,3},{8,12},{9,13},{10,... | collective-permute-start | bytes 399368 | tf_op jit(solution)/shard_map/ppermute | solution.py:597
  13.1 3.2 %collective-permute-start.4 = (bf16[520,128]{1,0:T(8,128)(2,1)S(1)}, bf16[520,128]{1,0:T(8,128)(2,1)S(1)}, u32[]{:S(2)}, u32[]{:S(2)}) collective-permute-start(bf16[520,128]{1,0:T(8,128)(2,1)S(1)} %get-tuple-element.28), channel_id=1, source_target_pairs={{0,3},{1,2},{2,1},{3,0},{4,7},{5,6},{6,5},{7,4},{8,11},{9,10},{10,... | collective-permute-start | bytes 399368 | tf_op jit(solution)/shard_map/ppermute | solution.py:597
  16.3 6.8 %collective-permute-start.5 = (bf16[520,128]{1,0:T(8,128)(2,1)S(1)}, bf16[520,128]{1,0:T(8,128)(2,1)S(1)}, u32[]{:S(2)}, u32[]{:S(2)}) collective-permute-start(bf16[520,128]{1,0:T(8,128)(2,1)S(1)} %get-tuple-element.29), channel_id=1, source_target_pairs={{0,2},{1,3},{2,0},{3,1},{4,6},{5,7},{6,4},{7,5},{8,10},{9,11},{10,... | collective-permute-start | bytes 399368 | tf_op jit(solution)/shard_map/ppermute | solution.py:597
  23.1 1.4 %collective-permute-start.6 = (bf16[520,128]{1,0:T(8,128)(2,1)S(1)}, bf16[520,128]{1,0:T(8,128)(2,1)S(1)}, u32[]{:S(2)}, u32[]{:S(2)}) collective-permute-start(bf16[520,128]{1,0:T(8,128)(2,1)S(1)} %get-tuple-element.30), channel_id=1, source_target_pairs={{0,1},{1,0},{2,3},{3,2},{4,5},{5,4},{6,7},{7,6},{8,9},{9,8},{10,11... | collective-permute-start | bytes 399368 | tf_op jit(solution)/shard_map/ppermute | solution.py:597
  24.6 4.7 %collective-permute-done.2.rest_2_ = bf16[520,128]{1,0:T(8,128)(2,1)S(1)} collective-permute-done((bf16[520,128]{1,0:T(8,128)(2,1)S(1)}, bf16[520,128]{1,0:T(8,128)(2,1)S(1)}, u32[]{:S(2)}, u32[]{:S(2)}) %collective-permute-start.2) | collective-permute-done | bytes 133152 | tf_op jit(solution)/shard_map/ppermute | solution.py:597
  29.2 1.3 %collective-permute-done.3.rest_3_ = bf16[520,128]{1,0:T(8,128)(2,1)S(1)} collective-permute-done((bf16[520,128]{1,0:T(8,128)(2,1)S(1)}, bf16[520,128]{1,0:T(8,128)(2,1)S(1)}, u32[]{:S(2)}, u32[]{:S(2)}) %collective-permute-start.3) | collective-permute-done | bytes 133152 | tf_op jit(solution)/shard_map/ppermute | solution.py:597
  30.5 0.8 %collective-permute-done.5.rest_5_ = bf16[520,128]{1,0:T(8,128)(2,1)S(1)} collective-permute-done((bf16[520,128]{1,0:T(8,128)(2,1)S(1)}, bf16[520,128]{1,0:T(8,128)(2,1)S(1)}, u32[]{:S(2)}, u32[]{:S(2)}) %collective-permute-start.5) | collective-permute-done | bytes 133152 | tf_op jit(solution)/shard_map/ppermute | solution.py:597
  31.4 0.4 middle.1
  31.8 1.2 %collective-permute-start.9 = (bf16[2,520,128]{2,1,0:T(8,128)(2,1)S(1)}, bf16[2,520,128]{2,1,0:T(8,128)(2,1)S(1)}, u32[]{:S(2)}, u32[]{:S(2)}) collective-permute-start(bf16[2,520,128]{2,1,0:T(8,128)(2,1)S(1)} %get-tuple-element.35), channel_id=1, source_target_pairs={{0,16},{8,24},{16,0},{24,8},{1,17},{9,25},{17,1},{25,9},{2,18},{10... | collective-permute-start | bytes 798728 | tf_op jit(solution)/shard_map/ppermute | solution.py:623
  33.1 1.0 %collective-permute-start.7 = (bf16[1,520,128]{2,1,0:T(8,128)(2,1)S(1)}, bf16[1,520,128]{2,1,0:T(8,128)(2,1)S(1)}, u32[]{:S(2)}, u32[]{:S(2)}) collective-permute-start(bf16[1,520,128]{2,1,0:T(8,128)(2,1)S(1)} %get-tuple-element.33), channel_id=1, source_target_pairs={{0,8},{8,0},{16,24},{24,16},{1,9},{9,1},{17,25},{25,17},{2,10},{10... | collective-permute-start | bytes 399368 | tf_op jit(solution)/shard_map/ppermute | solution.py:623
  34.0 1.0 %collective-permute-done.7.rest_1_ = bf16[1,520,128]{2,1,0:T(8,128)(2,1)S(1)} collective-permute-done((bf16[1,520,128]{2,1,0:T(8,128)(2,1)S(1)}, bf16[1,520,128]{2,1,0:T(8,128)(2,1)S(1)}, u32[]{:S(2)}, u32[]{:S(2)}) %collective-permute-start.7) | collective-permute-done | bytes 133152 | tf_op jit(solution)/shard_map/ppermute | solution.py:623
  35.0 0.4 collective-permute-done.8.rest_2_
  35.4 5.6 %collective-permute-done.9.rest_3_ = bf16[2,520,128]{2,1,0:T(8,128)(2,1)S(1)} collective-permute-done((bf16[2,520,128]{2,1,0:T(8,128)(2,1)S(1)}, bf16[2,520,128]{2,1,0:T(8,128)(2,1)S(1)}, u32[]{:S(2)}, u32[]{:S(2)}) %collective-permute-start.9) | collective-permute-done | bytes 266272 | tf_op jit(solution)/shard_map/ppermute | solution.py:623
  41.0 1.8 %ready.1 = (f32[6,256,256]{2,1,0:T(8,128)S(1)}, bf16[6,256,256]{2,1,0:T(8,128)(2,1)S(1)}, f32[8,256]{1,0:T(8,128)S(1)}, bf16[8,256,256]{2,1,0:T(8,128)(2,1)S(1)}, f32[3,8,256]{2,1,0:T(8,128)S(1)}) custom-call(f32[1,64]{1,0:T(1,128)S(1)} %bitcast.3, f32[1,64]{1,0:T(1,128)S(1)} %bitcast.6, bf16[8,256,256]{2,1,0:T(8,128)(2,1)S(1)} %copy-done, ...), custom_call_target="tpu_custom_call" | custom-call | tf_op jit(solution)/shard_map/ready/pallas_call | solution.py:389
  42.7 1.8 %owner.1 = (bf16[2,256,256]{2,1,0:T(8,128)(2,1)S(1)}, f32[8,256]{1,0:T(8,128)S(1)}, f32[8,8,128]{2,1,0:T(8,128)S(1)}, f32[32,1,128]{2,1,0:T(1,128)}) custom-call(f32[1,64]{1,0:T(1,128)S(1)} %bitcast.4, f32[1,64]{1,0:T(1,128)S(1)} %bitcast.7, bf16[8,256,256]{2,1,0:T(8,128)(2,1)S(1)} %copy-done, bf16[2,520,128]{2,1,0:T(8,128)(2,1)S(1)} %get-tuple-element.32.rest_0_, ...), custom_call_target="tpu_custom_call" | custom-call | tf_op jit(solution)/shard_map/owner/pallas_call | solution.py:481
  44.6 5.2 %all-to-all-start = ((f32[32,1,128]{2,1,0:T(1,128)}), f32[32,1,128]{2,1,0:T(1,128)S(1)}, u32[]{:S(2)}, u32[]{:S(2)}) async-start(f32[32,1,128]{2,1,0:T(1,128)} %get-tuple-element.45), calls=%async_computation | async-start | bytes 32768 | tf_op jit(solution)/shard_map/all_to_all | solution.py:634
  49.7 3.3 %last.1 = bf16[8,256,256]{2,1,0:T(8,128)(2,1)} custom-call(f32[1,64]{1,0:T(1,128)S(1)} %bitcast.5, f32[1,64]{1,0:T(1,128)S(1)} %bitcast.8, f32[8,256]{1,0:T(8,128)S(1)} %get-tuple-element.41.weight, f32[8,8,128]{2,1,0:T(8,128)S(1)} %get-tuple-element.42.label_ref, bf16[6,256,256]{2,1,0:T(8,128)(2,1)S(1)} %get-tuple-element.38.rest_6_.early_spectra, ...), custom_call_target="tpu_custom_call" | custom-call | flops 4194304 | bytes 4194304 | tf_op jit(solution)/shard_map/last/pallas_call | solution.py:575
  53.1 3.8 %all-to-all-done = f32[32,1,128]{2,1,0:T(1,128)S(1)} async-done(((f32[32,1,128]{2,1,0:T(1,128)}), f32[32,1,128]{2,1,0:T(1,128)S(1)}, u32[]{:S(2)}, u32[]{:S(2)}) %all-to-all-start) | async-done | bytes 16416 | tf_op jit(solution)/shard_map/all_to_all | solution.py:634
  56.9 0.6 reduce_sum.9
  (13 shorter events, 0.0 us)
Async XLA Ops:
  0.6 40.3 %copy-start = (bf16[8,256,256]{2,1,0:T(8,128)(2,1)S(1)}, bf16[8,256,256]{2,1,0:T(8,128)(2,1)}, u32[]{:S(2)}) copy-start(bf16[8,256,256]{2,1,0:T(8,128)(2,1)} %current_hbm.1) | copy-start | bytes 3145732
  0.6 40.3 %copy-start.2 = (f32[64]{0:T(128)S(1)}, f32[64]{0:T(128)}, u32[]{:S(2)}) copy-start(f32[64]{0:T(128)} %param.15) | copy-start | bytes 772
  0.7 40.3 %copy-start.1 = (f32[64]{0:T(128)S(1)}, f32[64]{0:T(128)}, u32[]{:S(2)}) copy-start(f32[64]{0:T(128)} %param.14) | copy-start | bytes 772
  2.8 13.6 %collective-permute-start.1 = (bf16[520,128]{1,0:T(8,128)(2,1)S(1)}, bf16[520,128]{1,0:T(8,128)(2,1)S(1)}, u32[]{:S(2)}, u32[]{:S(2)}) collective-permute-start(bf16[520,128]{1,0:T(8,128)(2,1)S(1)} %get-tuple-element.25), channel_id=1, source_target_pairs={{0,6},{1,7},{2,4},{3,5},{4,2},{5,3},{6,0},{7,1},{8,14},{9,15},{10,... | collective-permute-start | bytes 399368 | tf_op jit(solution)/shard_map/ppermute | solution.py:597
  7.1 16.0 %collective-permute-start = (bf16[520,128]{1,0:T(8,128)(2,1)S(1)}, bf16[520,128]{1,0:T(8,128)(2,1)S(1)}, u32[]{:S(2)}, u32[]{:S(2)}) collective-permute-start(bf16[520,128]{1,0:T(8,128)(2,1)S(1)} %get-tuple-element.24.rest_0_), channel_id=1, source_target_pairs={{0,7},{1,6},{2,5},{3,4},{4,3},{5,2},{6,1},{7,0},{8,15},{9,14},{10,... | collective-permute-start | bytes 399368 | tf_op jit(solution)/shard_map/ppermute | solution.py:597
  11.0 18.2 %collective-permute-start.2 = (bf16[520,128]{1,0:T(8,128)(2,1)S(1)}, bf16[520,128]{1,0:T(8,128)(2,1)S(1)}, u32[]{:S(2)}, u32[]{:S(2)}) collective-permute-start(bf16[520,128]{1,0:T(8,128)(2,1)S(1)} %get-tuple-element.26), channel_id=1, source_target_pairs={{0,5},{1,4},{2,7},{3,6},{4,1},{5,0},{6,3},{7,2},{8,13},{9,12},{10,... | collective-permute-start | bytes 399368 | tf_op jit(solution)/shard_map/ppermute | solution.py:597
  11.9 18.6 %collective-permute-start.3 = (bf16[520,128]{1,0:T(8,128)(2,1)S(1)}, bf16[520,128]{1,0:T(8,128)(2,1)S(1)}, u32[]{:S(2)}, u32[]{:S(2)}) collective-permute-start(bf16[520,128]{1,0:T(8,128)(2,1)S(1)} %get-tuple-element.27), channel_id=1, source_target_pairs={{0,4},{1,5},{2,6},{3,7},{4,0},{5,1},{6,2},{7,3},{8,12},{9,13},{10,... | collective-permute-start | bytes 399368 | tf_op jit(solution)/shard_map/ppermute | solution.py:597
  13.1 17.4 %collective-permute-start.4 = (bf16[520,128]{1,0:T(8,128)(2,1)S(1)}, bf16[520,128]{1,0:T(8,128)(2,1)S(1)}, u32[]{:S(2)}, u32[]{:S(2)}) collective-permute-start(bf16[520,128]{1,0:T(8,128)(2,1)S(1)} %get-tuple-element.28), channel_id=1, source_target_pairs={{0,3},{1,2},{2,1},{3,0},{4,7},{5,6},{6,5},{7,4},{8,11},{9,10},{10,... | collective-permute-start | bytes 399368 | tf_op jit(solution)/shard_map/ppermute | solution.py:597
  16.3 15.0 %collective-permute-start.5 = (bf16[520,128]{1,0:T(8,128)(2,1)S(1)}, bf16[520,128]{1,0:T(8,128)(2,1)S(1)}, u32[]{:S(2)}, u32[]{:S(2)}) collective-permute-start(bf16[520,128]{1,0:T(8,128)(2,1)S(1)} %get-tuple-element.29), channel_id=1, source_target_pairs={{0,2},{1,3},{2,0},{3,1},{4,6},{5,7},{6,4},{7,5},{8,10},{9,11},{10,... | collective-permute-start | bytes 399368 | tf_op jit(solution)/shard_map/ppermute | solution.py:597
  23.1 8.2 %collective-permute-start.6 = (bf16[520,128]{1,0:T(8,128)(2,1)S(1)}, bf16[520,128]{1,0:T(8,128)(2,1)S(1)}, u32[]{:S(2)}, u32[]{:S(2)}) collective-permute-start(bf16[520,128]{1,0:T(8,128)(2,1)S(1)} %get-tuple-element.30), channel_id=1, source_target_pairs={{0,1},{1,0},{2,3},{3,2},{4,5},{5,4},{6,7},{7,6},{8,9},{9,8},{10,11... | collective-permute-start | bytes 399368 | tf_op jit(solution)/shard_map/ppermute | solution.py:597
  31.8 9.1 %collective-permute-start.9 = (bf16[2,520,128]{2,1,0:T(8,128)(2,1)S(1)}, bf16[2,520,128]{2,1,0:T(8,128)(2,1)S(1)}, u32[]{:S(2)}, u32[]{:S(2)}) collective-permute-start(bf16[2,520,128]{2,1,0:T(8,128)(2,1)S(1)} %get-tuple-element.35), channel_id=1, source_target_pairs={{0,16},{8,24},{16,0},{24,8},{1,17},{9,25},{17,1},{25,9},{2,18},{10... | collective-permute-start | bytes 798728 | tf_op jit(solution)/shard_map/ppermute | solution.py:623
  33.0 9.7 %collective-permute-start.10 = (bf16[2,520,128]{2,1,0:T(8,128)(2,1)S(1)}, bf16[2,520,128]{2,1,0:T(8,128)(2,1)S(1)}, u32[]{:S(2)}, u32[]{:S(2)}) collective-permute-start(bf16[2,520,128]{2,1,0:T(8,128)(2,1)S(1)} %get-tuple-element.36), channel_id=1, source_target_pairs={{0,24},{8,16},{16,8},{24,0},{1,25},{9,17},{17,9},{25,1},{2,26},{10... | collective-permute-start | bytes 798728 | tf_op jit(solution)/shard_map/ppermute | solution.py:623
  33.1 1.9 %collective-permute-start.7 = (bf16[1,520,128]{2,1,0:T(8,128)(2,1)S(1)}, bf16[1,520,128]{2,1,0:T(8,128)(2,1)S(1)}, u32[]{:S(2)}, u32[]{:S(2)}) collective-permute-start(bf16[1,520,128]{2,1,0:T(8,128)(2,1)S(1)} %get-tuple-element.33), channel_id=1, source_target_pairs={{0,8},{8,0},{16,24},{24,16},{1,9},{9,1},{17,25},{25,17},{2,10},{10... | collective-permute-start | bytes 399368 | tf_op jit(solution)/shard_map/ppermute | solution.py:623
  34.0 1.4 %collective-permute-start.8 = (bf16[1,520,128]{2,1,0:T(8,128)(2,1)S(1)}, bf16[1,520,128]{2,1,0:T(8,128)(2,1)S(1)}, u32[]{:S(2)}, u32[]{:S(2)}) collective-permute-start(bf16[1,520,128]{2,1,0:T(8,128)(2,1)S(1)} %get-tuple-element.34), channel_id=1, source_target_pairs={{0,8},{8,0},{16,24},{24,16},{1,9},{9,1},{17,25},{25,17},{2,10},{10... | collective-permute-start | bytes 399368 | tf_op jit(solution)/shard_map/ppermute | solution.py:623
  44.6 12.3 %all-to-all-start = ((f32[32,1,128]{2,1,0:T(1,128)}), f32[32,1,128]{2,1,0:T(1,128)S(1)}, u32[]{:S(2)}, u32[]{:S(2)}) async-start(f32[32,1,128]{2,1,0:T(1,128)} %get-tuple-element.45), calls=%async_computation | async-start | bytes 32768 | tf_op jit(solution)/shard_map/all_to_all | solution.py:634

commit v11 on v8

--- a/solution.py
+++ b/solution.py
@@ -149,21 +149,25 @@
     counts = [jnp.int32(0)] * mic_count
     for block, target in zip(arrived, targets):
         step_of = (target - 1) ^ here
+
+        @pl.when(target > 0)
+        def _(block=block, step_of=step_of, counts=tuple(counts)):
+            for step in range(mic_count):
+                if len(outs[step]) == 1:
+
+                    @pl.when(step_of == step)
+                    def _(step=step):
+                        outs[step][0][counts[step]] = block[...]
+
+                else:
+                    for j, out in enumerate(outs[step]):
+
+                        @pl.when((step_of == step) & (counts[step] == j))
+                        def _(out=out):
+                            out[0] = block[...]
+
         for step in range(mic_count):
             chosen = (target > 0) & (step_of == step)
-            if len(outs[step]) == 1:
-
-                @pl.when(chosen)
-                def _(block=block, out=outs[step][0], slot=counts[step]):
-                    out[slot] = block[...]
-
-            else:
-                for j, out in enumerate(outs[step]):
-
-                    @pl.when(chosen & (counts[step] == j))
-                    def _(block=block, out=out):
-                        out[0] = block[...]
-
             counts[step] = counts[step] + chosen.astype(jnp.int32)
 
 

time: 58.3 us -> 58.2 us (level)
  Pallas kernels: 12.6 us -> 9.93 us
  waiting for transfers between devices: 18.7 us -> 21.2 us
  starting transfers between devices: 25.4 us -> 26 us
    pallas_call x1, Pallas kernels: 2.86 us -> 1.14 us  [owner_call(): pl.pallas_call(functools.partial(owner_kernel, bin_count, steps), out_sha...]
    all_to_all x1, starting transfers between devices: 4.28 us -> 5.69 us  [body(): lax.all_to_all(board, ('mic', 'bin'), split_axis=0, concat_axis=0, tiled=...]
    ppermute x7, waiting for transfers between devices: 7.65 us -> 8.56 us  [exchange(): lax.ppermute(blocks[k], axis, [(i, i ^ k) for i in range(size)])]
    ppermute x7, starting transfers between devices: 18.9 us -> 18.1 us  [exchange(): lax.ppermute(blocks[k], axis, [(i, i ^ k) for i in range(size)])]
    ppermute x4, waiting for transfers between devices: 7.43 us -> 8.21 us  [body(): lax.ppermute(block, 'mic', pairs)]
    pallas_call x1, Pallas kernels: 3.46 us -> 2.7 us  [last_call(): pl.pallas_call(last_kernel, out_shape=jax.ShapeDtypeStruct(references.sha...]
    all_to_all x1, waiting for transfers between devices: 3.64 us -> 4.4 us  [body(): lax.all_to_all(board, ('mic', 'bin'), split_axis=0, concat_axis=0, tiled=...]
  transfers between devices with their start and end apart: 12 -> 12, of which waited for: 8 -> 8; matrix products, arithmetic and copies ran while one was open for 0% -> 0% of each run, Pallas kernels for 13% -> 11%
where the time goes in v11:
time: 58.2 us; the launch traced here: 58.4 us
  starting transfers between devices  26 us (45%)
  waiting for transfers between devices  21.2 us (36%)
  Pallas kernels  9.93 us (17%)
  between operations  0.72 us (1%)
    ppermute x7, starting transfers between devices, exchange(): lax.ppermute(blocks[k], axis, [(i, i ^ k) for i in range(size)])  18.1 us
    ppermute x7, waiting for transfers between devices, exchange(): lax.ppermute(blocks[k], axis, [(i, i ^ k) for i in range(size)])  8.56 us
    ppermute x4, waiting for transfers between devices, body(): lax.ppermute(block, 'mic', pairs)  8.21 us
    all_to_all x1, starting transfers between devices, body(): lax.all_to_all(board, ('mic', 'bin'), split_axis=0, concat_axis=0, tiled=...  5.69 us
    all_to_all x1, waiting for transfers between devices, body(): lax.all_to_all(board, ('mic', 'bin'), split_axis=0, concat_axis=0, tiled=...  4.4 us
    pallas_call x2, Pallas kernels, home_call(): pl.pallas_call(functools.partial(home_kernel, bin_count, own_bins, first,...  4.11 us
    pallas_call x1, Pallas kernels, last_call(): pl.pallas_call(last_kernel, out_shape=jax.ShapeDtypeStruct(references.sha...  2.7 us
    ppermute x4, starting transfers between devices, body(): lax.ppermute(block, 'mic', pairs)  2.21 us
  transfers between devices with their start and end apart: 12, of which 8 were waited for; matrix products, arithmetic and copies ran while one was open for 0% of the time, Pallas kernels for 11%

profile of v11, /device:TPU:0, one launch (start us, length us, event | category | flops | bytes accessed | tf_op | source)
XLA Modules:
  0.0 58.4 jit_solution(13721924504082413927)
XLA Ops:
  0.7 2.1 %home.2 = (bf16[520,128]{1,0:T(8,128)(2,1)S(1)}, bf16[520,128]{1,0:T(8,128)(2,1)S(1)}, bf16[520,128]{1,0:T(8,128)(2,1)S(1)}) custom-call(s32[256]{0:T(256)} %place_hbm.3, s32[4]{0:T(128)} %bin_hbm.3, s32[4]{0:T(128)} %group_hbm.3, s32[2,4]{1,0:T(2,128)} %offset_hbm.3, bf16[4,256,256]{2,1,0:T(8,128)(2,1)} %image_hbm.3, bf16[256,256]{1,0:T(8,128)(2,1)} %constant.4.clone.basis_hbm), custom_call_target="tpu_custom_call" | custom-call | tf_op jit(solution)/shard_map/home/pallas_call | solution.py:116
  2.7 4.7 %collective-permute-start.1 = (bf16[520,128]{1,0:T(8,128)(2,1)S(1)}, bf16[520,128]{1,0:T(8,128)(2,1)S(1)}, u32[]{:S(2)}, u32[]{:S(2)}) collective-permute-start(bf16[520,128]{1,0:T(8,128)(2,1)S(1)} %get-tuple-element.25), channel_id=1, source_target_pairs={{0,6},{1,7},{2,4},{3,5},{4,2},{5,3},{6,0},{7,1},{8,14},{9,15},{10,... | collective-permute-start | bytes 399368 | tf_op jit(solution)/shard_map/ppermute | solution.py:601
  7.4 0.4 collective-permute-start.2
  7.9 2.8 %collective-permute-start = (bf16[520,128]{1,0:T(8,128)(2,1)S(1)}, bf16[520,128]{1,0:T(8,128)(2,1)S(1)}, u32[]{:S(2)}, u32[]{:S(2)}) collective-permute-start(bf16[520,128]{1,0:T(8,128)(2,1)S(1)} %get-tuple-element.24.rest_0_), channel_id=1, source_target_pairs={{0,7},{1,6},{2,5},{3,4},{4,3},{5,2},{6,1},{7,0},{8,15},{9,14},{10,... | collective-permute-start | bytes 399368 | tf_op jit(solution)/shard_map/ppermute | solution.py:601
  10.7 2.0 %home.3 = (bf16[520,128]{1,0:T(8,128)(2,1)S(1)}, bf16[520,128]{1,0:T(8,128)(2,1)S(1)}, bf16[520,128]{1,0:T(8,128)(2,1)S(1)}, bf16[520,128]{1,0:T(8,128)(2,1)S(1)}, bf16[520,128]{1,0:T(8,128)(2,1)S(1)}) custom-call(s32[256]{0:T(256)} %place_hbm.3, s32[4]{0:T(128)} %bin_hbm.3, s32[4]{0:T(128)} %group_hbm.3, s32[2,4]{1,0:T(2,128)} %offset_hbm.3, ...), custom_call_target="tpu_custom_call" | custom-call | tf_op jit(solution)/shard_map/home/pallas_call | solution.py:116
  12.7 0.7 %collective-permute-start.3 = (bf16[520,128]{1,0:T(8,128)(2,1)S(1)}, bf16[520,128]{1,0:T(8,128)(2,1)S(1)}, u32[]{:S(2)}, u32[]{:S(2)}) collective-permute-start(bf16[520,128]{1,0:T(8,128)(2,1)S(1)} %get-tuple-element.27), channel_id=1, source_target_pairs={{0,4},{1,5},{2,6},{3,7},{4,0},{5,1},{6,2},{7,3},{8,12},{9,13},{10,... | collective-permute-start | bytes 399368 | tf_op jit(solution)/shard_map/ppermute | solution.py:601
  13.5 2.2 %collective-permute-start.4 = (bf16[520,128]{1,0:T(8,128)(2,1)S(1)}, bf16[520,128]{1,0:T(8,128)(2,1)S(1)}, u32[]{:S(2)}, u32[]{:S(2)}) collective-permute-start(bf16[520,128]{1,0:T(8,128)(2,1)S(1)} %get-tuple-element.28), channel_id=1, source_target_pairs={{0,3},{1,2},{2,1},{3,0},{4,7},{5,6},{6,5},{7,4},{8,11},{9,10},{10,... | collective-permute-start | bytes 399368 | tf_op jit(solution)/shard_map/ppermute | solution.py:601
  15.7 7.1 %collective-permute-start.5 = (bf16[520,128]{1,0:T(8,128)(2,1)S(1)}, bf16[520,128]{1,0:T(8,128)(2,1)S(1)}, u32[]{:S(2)}, u32[]{:S(2)}) collective-permute-start(bf16[520,128]{1,0:T(8,128)(2,1)S(1)} %get-tuple-element.29), channel_id=1, source_target_pairs={{0,2},{1,3},{2,0},{3,1},{4,6},{5,7},{6,4},{7,5},{8,10},{9,11},{10,... | collective-permute-start | bytes 399368 | tf_op jit(solution)/shard_map/ppermute | solution.py:601
  22.7 3.7 %collective-permute-done.2.rest_2_ = bf16[520,128]{1,0:T(8,128)(2,1)S(1)} collective-permute-done((bf16[520,128]{1,0:T(8,128)(2,1)S(1)}, bf16[520,128]{1,0:T(8,128)(2,1)S(1)}, u32[]{:S(2)}, u32[]{:S(2)}) %collective-permute-start.2) | collective-permute-done | bytes 133152 | tf_op jit(solution)/shard_map/ppermute | solution.py:601
  26.5 3.5 %collective-permute-done.3.rest_3_ = bf16[520,128]{1,0:T(8,128)(2,1)S(1)} collective-permute-done((bf16[520,128]{1,0:T(8,128)(2,1)S(1)}, bf16[520,128]{1,0:T(8,128)(2,1)S(1)}, u32[]{:S(2)}, u32[]{:S(2)}) %collective-permute-start.3) | collective-permute-done | bytes 133152 | tf_op jit(solution)/shard_map/ppermute | solution.py:601
  30.1 1.4 %collective-permute-done.6.rest_6_ = bf16[520,128]{1,0:T(8,128)(2,1)S(1)} collective-permute-done((bf16[520,128]{1,0:T(8,128)(2,1)S(1)}, bf16[520,128]{1,0:T(8,128)(2,1)S(1)}, u32[]{:S(2)}, u32[]{:S(2)}) %collective-permute-start.6) | collective-permute-done | bytes 133152 | tf_op jit(solution)/shard_map/ppermute | solution.py:601
  31.4 0.3 middle.1
  31.8 1.6 %collective-permute-start.9 = (bf16[2,520,128]{2,1,0:T(8,128)(2,1)S(1)}, bf16[2,520,128]{2,1,0:T(8,128)(2,1)S(1)}, u32[]{:S(2)}, u32[]{:S(2)}) collective-permute-start(bf16[2,520,128]{2,1,0:T(8,128)(2,1)S(1)} %get-tuple-element.35), channel_id=1, source_target_pairs={{0,16},{8,24},{16,0},{24,8},{1,17},{9,25},{17,1},{25,9},{2,18},{10... | collective-permute-start | bytes 798728 | tf_op jit(solution)/shard_map/ppermute | solution.py:627
  33.3 0.6 %collective-permute-start.7 = (bf16[1,520,128]{2,1,0:T(8,128)(2,1)S(1)}, bf16[1,520,128]{2,1,0:T(8,128)(2,1)S(1)}, u32[]{:S(2)}, u32[]{:S(2)}) collective-permute-start(bf16[1,520,128]{2,1,0:T(8,128)(2,1)S(1)} %get-tuple-element.33), channel_id=1, source_target_pairs={{0,8},{8,0},{16,24},{24,16},{1,9},{9,1},{17,25},{25,17},{2,10},{10... | collective-permute-start | bytes 399368 | tf_op jit(solution)/shard_map/ppermute | solution.py:627
  34.0 1.0 %collective-permute-done.7.rest_1_ = bf16[1,520,128]{2,1,0:T(8,128)(2,1)S(1)} collective-permute-done((bf16[1,520,128]{2,1,0:T(8,128)(2,1)S(1)}, bf16[1,520,128]{2,1,0:T(8,128)(2,1)S(1)}, u32[]{:S(2)}, u32[]{:S(2)}) %collective-permute-start.7) | collective-permute-done | bytes 133152 | tf_op jit(solution)/shard_map/ppermute | solution.py:627
  35.0 0.4 collective-permute-done.8.rest_2_
  35.3 5.8 %collective-permute-done.9.rest_3_ = bf16[2,520,128]{2,1,0:T(8,128)(2,1)S(1)} collective-permute-done((bf16[2,520,128]{2,1,0:T(8,128)(2,1)S(1)}, bf16[2,520,128]{2,1,0:T(8,128)(2,1)S(1)}, u32[]{:S(2)}, u32[]{:S(2)}) %collective-permute-start.9) | collective-permute-done | bytes 266272 | tf_op jit(solution)/shard_map/ppermute | solution.py:627
  41.2 1.6 %ready.1 = (f32[6,256,256]{2,1,0:T(8,128)S(1)}, bf16[6,256,256]{2,1,0:T(8,128)(2,1)S(1)}, f32[8,256]{1,0:T(8,128)S(1)}, bf16[8,256,256]{2,1,0:T(8,128)(2,1)S(1)}, f32[3,8,256]{2,1,0:T(8,128)S(1)}) custom-call(f32[1,64]{1,0:T(1,128)S(1)} %bitcast.3, f32[1,64]{1,0:T(1,128)S(1)} %bitcast.6, bf16[8,256,256]{2,1,0:T(8,128)(2,1)S(1)} %copy-done, ...), custom_call_target="tpu_custom_call" | custom-call | tf_op jit(solution)/shard_map/ready/pallas_call | solution.py:393
  42.8 1.0 %collective-permute-done.10.rest_4_.late_ref = bf16[2,520,128]{2,1,0:T(8,128)(2,1)S(1)} collective-permute-done((bf16[2,520,128]{2,1,0:T(8,128)(2,1)S(1)}, bf16[2,520,128]{2,1,0:T(8,128)(2,1)S(1)}, u32[]{:S(2)}, u32[]{:S(2)}) %collective-permute-start.10) | collective-permute-done | bytes 266272 | tf_op jit(solution)/shard_map/ppermute | solution.py:627
  43.8 1.1 %owner.1 = (bf16[2,256,256]{2,1,0:T(8,128)(2,1)S(1)}, f32[8,256]{1,0:T(8,128)S(1)}, f32[8,8,128]{2,1,0:T(8,128)S(1)}, f32[32,1,128]{2,1,0:T(1,128)}) custom-call(f32[1,64]{1,0:T(1,128)S(1)} %bitcast.4, f32[1,64]{1,0:T(1,128)S(1)} %bitcast.7, bf16[8,256,256]{2,1,0:T(8,128)(2,1)S(1)} %copy-done, bf16[2,520,128]{2,1,0:T(8,128)(2,1)S(1)} %get-tuple-element.32.rest_0_, ...), custom_call_target="tpu_custom_call" | custom-call | tf_op jit(solution)/shard_map/owner/pallas_call | solution.py:485
  45.0 5.7 %all-to-all-start = ((f32[32,1,128]{2,1,0:T(1,128)}), f32[32,1,128]{2,1,0:T(1,128)S(1)}, u32[]{:S(2)}, u32[]{:S(2)}) async-start(f32[32,1,128]{2,1,0:T(1,128)} %get-tuple-element.45), calls=%async_computation | async-start | bytes 32768 | tf_op jit(solution)/shard_map/all_to_all | solution.py:638
  50.7 2.7 %last.1 = bf16[8,256,256]{2,1,0:T(8,128)(2,1)} custom-call(f32[1,64]{1,0:T(1,128)S(1)} %bitcast.5, f32[1,64]{1,0:T(1,128)S(1)} %bitcast.8, f32[8,256]{1,0:T(8,128)S(1)} %get-tuple-element.41.weight, f32[8,8,128]{2,1,0:T(8,128)S(1)} %get-tuple-element.42.label_ref, bf16[6,256,256]{2,1,0:T(8,128)(2,1)S(1)} %get-tuple-element.38.rest_6_.early_spectra, ...), custom_call_target="tpu_custom_call" | custom-call | flops 4194304 | bytes 4194304 | tf_op jit(solution)/shard_map/last/pallas_call | solution.py:579
  53.4 4.4 %all-to-all-done = f32[32,1,128]{2,1,0:T(1,128)S(1)} async-done(((f32[32,1,128]{2,1,0:T(1,128)}), f32[32,1,128]{2,1,0:T(1,128)S(1)}, u32[]{:S(2)}, u32[]{:S(2)}) %all-to-all-start) | async-done | bytes 16416 | tf_op jit(solution)/shard_map/all_to_all | solution.py:638
  57.8 0.6 reduce_sum.9
  (13 shorter events, 0.1 us)
Async XLA Ops:
  0.6 40.5 %copy-start = (bf16[8,256,256]{2,1,0:T(8,128)(2,1)S(1)}, bf16[8,256,256]{2,1,0:T(8,128)(2,1)}, u32[]{:S(2)}) copy-start(bf16[8,256,256]{2,1,0:T(8,128)(2,1)} %current_hbm.1) | copy-start | bytes 3145732
  0.6 40.5 %copy-start.2 = (f32[64]{0:T(128)S(1)}, f32[64]{0:T(128)}, u32[]{:S(2)}) copy-start(f32[64]{0:T(128)} %param.15) | copy-start | bytes 772
  0.7 40.5 %copy-start.1 = (f32[64]{0:T(128)S(1)}, f32[64]{0:T(128)}, u32[]{:S(2)}) copy-start(f32[64]{0:T(128)} %param.14) | copy-start | bytes 772
  2.7 12.9 %collective-permute-start.1 = (bf16[520,128]{1,0:T(8,128)(2,1)S(1)}, bf16[520,128]{1,0:T(8,128)(2,1)S(1)}, u32[]{:S(2)}, u32[]{:S(2)}) collective-permute-start(bf16[520,128]{1,0:T(8,128)(2,1)S(1)} %get-tuple-element.25), channel_id=1, source_target_pairs={{0,6},{1,7},{2,4},{3,5},{4,2},{5,3},{6,0},{7,1},{8,14},{9,15},{10,... | collective-permute-start | bytes 399368 | tf_op jit(solution)/shard_map/ppermute | solution.py:601
  7.4 19.0 %collective-permute-start.2 = (bf16[520,128]{1,0:T(8,128)(2,1)S(1)}, bf16[520,128]{1,0:T(8,128)(2,1)S(1)}, u32[]{:S(2)}, u32[]{:S(2)}) collective-permute-start(bf16[520,128]{1,0:T(8,128)(2,1)S(1)} %get-tuple-element.26), channel_id=1, source_target_pairs={{0,5},{1,4},{2,7},{3,6},{4,1},{5,0},{6,3},{7,2},{8,13},{9,12},{10,... | collective-permute-start | bytes 399368 | tf_op jit(solution)/shard_map/ppermute | solution.py:601
  7.9 18.7 %collective-permute-start = (bf16[520,128]{1,0:T(8,128)(2,1)S(1)}, bf16[520,128]{1,0:T(8,128)(2,1)S(1)}, u32[]{:S(2)}, u32[]{:S(2)}) collective-permute-start(bf16[520,128]{1,0:T(8,128)(2,1)S(1)} %get-tuple-element.24.rest_0_), channel_id=1, source_target_pairs={{0,7},{1,6},{2,5},{3,4},{4,3},{5,2},{6,1},{7,0},{8,15},{9,14},{10,... | collective-permute-start | bytes 399368 | tf_op jit(solution)/shard_map/ppermute | solution.py:601
  12.7 17.3 %collective-permute-start.3 = (bf16[520,128]{1,0:T(8,128)(2,1)S(1)}, bf16[520,128]{1,0:T(8,128)(2,1)S(1)}, u32[]{:S(2)}, u32[]{:S(2)}) collective-permute-start(bf16[520,128]{1,0:T(8,128)(2,1)S(1)} %get-tuple-element.27), channel_id=1, source_target_pairs={{0,4},{1,5},{2,6},{3,7},{4,0},{5,1},{6,2},{7,3},{8,12},{9,13},{10,... | collective-permute-start | bytes 399368 | tf_op jit(solution)/shard_map/ppermute | solution.py:601
  13.5 16.6 %collective-permute-start.4 = (bf16[520,128]{1,0:T(8,128)(2,1)S(1)}, bf16[520,128]{1,0:T(8,128)(2,1)S(1)}, u32[]{:S(2)}, u32[]{:S(2)}) collective-permute-start(bf16[520,128]{1,0:T(8,128)(2,1)S(1)} %get-tuple-element.28), channel_id=1, source_target_pairs={{0,3},{1,2},{2,1},{3,0},{4,7},{5,6},{6,5},{7,4},{8,11},{9,10},{10,... | collective-permute-start | bytes 399368 | tf_op jit(solution)/shard_map/ppermute | solution.py:601
  15.7 14.4 %collective-permute-start.5 = (bf16[520,128]{1,0:T(8,128)(2,1)S(1)}, bf16[520,128]{1,0:T(8,128)(2,1)S(1)}, u32[]{:S(2)}, u32[]{:S(2)}) collective-permute-start(bf16[520,128]{1,0:T(8,128)(2,1)S(1)} %get-tuple-element.29), channel_id=1, source_target_pairs={{0,2},{1,3},{2,0},{3,1},{4,6},{5,7},{6,4},{7,5},{8,10},{9,11},{10,... | collective-permute-start | bytes 399368 | tf_op jit(solution)/shard_map/ppermute | solution.py:601
  26.4 5.0 %collective-permute-start.6 = (bf16[520,128]{1,0:T(8,128)(2,1)S(1)}, bf16[520,128]{1,0:T(8,128)(2,1)S(1)}, u32[]{:S(2)}, u32[]{:S(2)}) collective-permute-start(bf16[520,128]{1,0:T(8,128)(2,1)S(1)} %get-tuple-element.30), channel_id=1, source_target_pairs={{0,1},{1,0},{2,3},{3,2},{4,5},{5,4},{6,7},{7,6},{8,9},{9,8},{10,11... | collective-permute-start | bytes 399368 | tf_op jit(solution)/shard_map/ppermute | solution.py:601
  31.8 9.4 %collective-permute-start.9 = (bf16[2,520,128]{2,1,0:T(8,128)(2,1)S(1)}, bf16[2,520,128]{2,1,0:T(8,128)(2,1)S(1)}, u32[]{:S(2)}, u32[]{:S(2)}) collective-permute-start(bf16[2,520,128]{2,1,0:T(8,128)(2,1)S(1)} %get-tuple-element.35), channel_id=1, source_target_pairs={{0,16},{8,24},{16,0},{24,8},{1,17},{9,25},{17,1},{25,9},{2,18},{10... | collective-permute-start | bytes 798728 | tf_op jit(solution)/shard_map/ppermute | solution.py:627
  33.3 10.5 %collective-permute-start.10 = (bf16[2,520,128]{2,1,0:T(8,128)(2,1)S(1)}, bf16[2,520,128]{2,1,0:T(8,128)(2,1)S(1)}, u32[]{:S(2)}, u32[]{:S(2)}) collective-permute-start(bf16[2,520,128]{2,1,0:T(8,128)(2,1)S(1)} %get-tuple-element.36), channel_id=1, source_target_pairs={{0,24},{8,16},{16,8},{24,0},{1,25},{9,17},{17,9},{25,1},{2,26},{10... | collective-permute-start | bytes 798728 | tf_op jit(solution)/shard_map/ppermute | solution.py:627
  33.3 1.6 %collective-permute-start.7 = (bf16[1,520,128]{2,1,0:T(8,128)(2,1)S(1)}, bf16[1,520,128]{2,1,0:T(8,128)(2,1)S(1)}, u32[]{:S(2)}, u32[]{:S(2)}) collective-permute-start(bf16[1,520,128]{2,1,0:T(8,128)(2,1)S(1)} %get-tuple-element.33), channel_id=1, source_target_pairs={{0,8},{8,0},{16,24},{24,16},{1,9},{9,1},{17,25},{25,17},{2,10},{10... | collective-permute-start | bytes 399368 | tf_op jit(solution)/shard_map/ppermute | solution.py:627
  34.0 1.4 %collective-permute-start.8 = (bf16[1,520,128]{2,1,0:T(8,128)(2,1)S(1)}, bf16[1,520,128]{2,1,0:T(8,128)(2,1)S(1)}, u32[]{:S(2)}, u32[]{:S(2)}) collective-permute-start(bf16[1,520,128]{2,1,0:T(8,128)(2,1)S(1)} %get-tuple-element.34), channel_id=1, source_target_pairs={{0,8},{8,0},{16,24},{24,16},{1,9},{9,1},{17,25},{25,17},{2,10},{10... | collective-permute-start | bytes 399368 | tf_op jit(solution)/shard_map/ppermute | solution.py:627
  45.0 12.8 %all-to-all-start = ((f32[32,1,128]{2,1,0:T(1,128)}), f32[32,1,128]{2,1,0:T(1,128)S(1)}, u32[]{:S(2)}, u32[]{:S(2)}) async-start(f32[32,1,128]{2,1,0:T(1,128)} %get-tuple-element.45), calls=%async_computation | async-start | bytes 32768 | tf_op jit(solution)/shard_map/all_to_all | solution.py:638
